TPU v7x, 32 devices: a whole 2x2x4 slice. The times are simulated.
32 devices in a mesh: dp: 8 (over z, x), tensor: 4 (over y, core).
Axes of the slice: x: 2, y: 2, z: 4, core: 2. Of those that a mesh axis runs over, the one named last changes fastest.
Arguments:
- tokens: bfloat16 [8192, 1024], P(('dp', 'tensor')), may hold values from -6 to 6
- cotangent: bfloat16 [8192, 1024], P(('dp', 'tensor')), may hold values from -6 to 6
- seq_lengths: int32 [8], P('dp'), may hold values from 256 to 1024, as said below
- block_owner: int32 [192], replicated, may hold values from 0 to 191, as said below
- master_blocks: float32 [4, 192, 128, 128], P('tensor', 'dp')
- first_moment: float32 [4, 192, 128, 128], P('tensor', 'dp')
- second_moment: float32 [4, 192, 128, 128], P('tensor', 'dp'), as said below
- left_stats: float32 [4, 192, 128, 128], P('tensor', 'dp'), as said below
- right_stats: float32 [4, 192, 128, 128], P('tensor', 'dp'), as said below
- left_basis: float32 [4, 192, 128, 128], P('tensor', 'dp'), as said below
- right_basis: float32 [4, 192, 128, 128], P('tensor', 'dp'), as said below
- vector_master: float32 [12288], replicated
- vector_first: float32 [12288], replicated
- vector_second: float32 [12288], replicated, as said below
Outputs:
- layer_output: bfloat16 [8192, 1024], P(('dp', 'tensor'))
- token_grad: bfloat16 [8192, 1024], P(('dp', 'tensor'))
- new_first: float32 [4, 192, 128, 128], P('tensor', 'dp')
- new_second: float32 [4, 192, 128, 128], P('tensor', 'dp')
- new_master: float32 [4, 192, 128, 128], P('tensor', 'dp')
- new_left_stats: float32 [4, 192, 128, 128], P('tensor', 'dp')
- new_right_stats: float32 [4, 192, 128, 128], P('tensor', 'dp')
- new_left_basis: float32 [4, 192, 128, 128], P('tensor', 'dp')
- new_right_basis: float32 [4, 192, 128, 128], P('tensor', 'dp')
- vector_new_first: float32 [12288], replicated
- vector_new_second: float32 [12288], replicated
- vector_new_master: float32 [12288], replicated
Inputs may be any that keep to these rules, and one draw needn't show every extreme that they name: `seq_lengths`: valid tokens of each sequence; some sequence is exactly 1024 long. `block_owner`: a permutation: every slot holds exactly one canonical block, the same for every tensor index. `second_moment`: positive entries. `vector_second`: positive entries. `left_stats`: each block symmetric positive definite. `right_stats`: each block symmetric positive definite. `left_basis`: each block invertible. `right_basis`: each block invertible.
All inputs are finite; a program needn't handle non-finite values.
Results may differ from a plain program's by a relative error of at most 0.018.
Values may be sent and summed in bfloat16 or wider, within the bound.
No kernel may reach another device: no remote copies, remote signals or barrier semaphores. Data moves between devices by JAX's collectives and lax.ppermute only.
A program may use at most 192 MiB of HBM per device.

v0:
```python
import math

import jax
import jax.numpy as jnp
from jax import lax
from jax.sharding import PartitionSpec as P

D = 1024
FF = 4096
HEAD_DIM = 64
BLK = 128
STEP = 10


norm_eps = 1e-05
adam_eps = 1e-08
moment_decay = 0.5
weight_decay = 0.01
vector_rate = 0.25
masked_score = -1000000000.0
highest = lax.Precision.HIGHEST
bfloat = jnp.bfloat16
single = jnp.float32


def matmul_high(left, right):
    return jnp.matmul(left, right, precision=highest)


def gelu_exact(inputs):
    return jax.nn.gelu(inputs, approximate=False)


def block_counts(tensors):
    return (D * D // (tensors * BLK * BLK), D * FF // (tensors * BLK * BLK))


def to_matrix(pieces, row_count, col_count):
    shaped = pieces.reshape(row_count // BLK, col_count // BLK, BLK, BLK)
    return shaped.swapaxes(1, 2).reshape(row_count, col_count)


def to_blocks(matrix):
    row_count, col_count = matrix.shape
    shaped = matrix.reshape(row_count // BLK, BLK, col_count // BLK, BLK)
    return shaped.swapaxes(1, 2).reshape(row_count * col_count // (BLK * BLK), BLK, BLK)


def rate_values(canon_index, tensors, seq_len):
    attn_count, ffn_count = block_counts(tensors)
    out_std = math.sqrt(seq_len / (3.0 * D))
    inner = jnp.where(canon_index < 4 * attn_count + ffn_count, D ** (-0.5), FF ** (-0.5))
    inner = jnp.where(canon_index < 4 * attn_count, out_std, inner)
    return jnp.where(canon_index < 3 * attn_count, D ** (-0.5), inner).astype(single)


def renew_basis(stats, basis):
    product = matmul_high(stats, basis)
    gram = matmul_high(product.swapaxes(-1, -2), product)
    factor = jnp.linalg.cholesky(gram)
    solved = jax.scipy.linalg.solve_triangular(factor, product.swapaxes(-1, -2), lower=True)
    return solved.swapaxes(-1, -2)


def norm_forward(inputs, gain, shift):
    centred = inputs - jnp.mean(inputs, -1, keepdims=True)
    inv_std = lax.rsqrt(jnp.mean(centred * centred, -1, keepdims=True) + norm_eps)
    normed = centred * inv_std
    return (normed * gain + shift, normed, inv_std)


def norm_backward(grad_in, normed, inv_std, gain):
    scaled = grad_in * gain
    mean_grad = jnp.mean(scaled, -1, keepdims=True)
    mean_cross = jnp.mean(scaled * normed, -1, keepdims=True)
    return (
        inv_std * (scaled - mean_grad - normed * mean_cross),
        jnp.sum(grad_in * normed, 0),
        jnp.sum(grad_in, 0),
    )


def body(
    tokens,
    cotangent,
    seq_lengths,
    block_owner,
    master_blocks,
    first_moment,
    second_moment,
    left_stats,
    right_stats,
    left_basis,
    right_basis,
    vector_master,
    vector_first,
    vector_second,
):
    tensors = lax.axis_size("tensor")
    data_ranks = lax.axis_size("dp")
    tensor_rank = lax.axis_index("tensor")
    local_rows = tokens.shape[0]
    seq_len = local_rows * tensors
    slice_width = D // tensors
    hidden_width = FF // tensors
    local_heads = slice_width // HEAD_DIM
    block_total = block_owner.shape[0]
    slots_here = master_blocks.shape[1]
    length = seq_lengths[0]
    score_scale = HEAD_DIM ** (-0.5)
    gathered = lax.all_gather(master_blocks[0].astype(bfloat), "dp", axis=0, tiled=True)
    canonical = jnp.take(gathered, block_owner, axis=0)
    attn_count, ffn_count = block_counts(tensors)
    up_start = 4 * attn_count
    w_query = to_matrix(canonical[0:attn_count], D, slice_width)
    w_key = to_matrix(canonical[attn_count : 2 * attn_count], D, slice_width)
    w_value = to_matrix(canonical[2 * attn_count : 3 * attn_count], D, slice_width)
    w_out = to_matrix(canonical[3 * attn_count : up_start], slice_width, D)
    w_up = to_matrix(canonical[up_start : up_start + ffn_count], D, hidden_width)
    w_down = to_matrix(canonical[up_start + ffn_count : up_start + 2 * ffn_count], hidden_width, D)
    w_qkv = jnp.concatenate([w_query, w_key, w_value], axis=1)
    gain_one, shift_one = (vector_master[0:D], vector_master[D : 2 * D])
    gain_two, shift_two = (vector_master[2 * D : 3 * D], vector_master[3 * D : 4 * D])
    bias_query = lax.dynamic_slice_in_dim(
        vector_master, 4 * D + tensor_rank * slice_width, slice_width
    )
    bias_value = lax.dynamic_slice_in_dim(
        vector_master, 5 * D + tensor_rank * slice_width, slice_width
    )
    bias_out = vector_master[6 * D : 7 * D]
    bias_up = lax.dynamic_slice_in_dim(
        vector_master, 7 * D + tensor_rank * hidden_width, hidden_width
    )
    bias_down = vector_master[7 * D + FF : 8 * D + FF]
    positions = tensor_rank * local_rows + jnp.arange(local_rows)
    row_valid = (positions < length).astype(single)[:, None]
    full_tokens = lax.all_gather(tokens, "tensor", axis=0, tiled=True)
    bias_qkv = jnp.concatenate([bias_query, jnp.zeros((slice_width,), single), bias_value])
    projected = (jnp.dot(full_tokens, w_qkv, preferred_element_type=single) + bias_qkv).astype(
        bfloat
    )
    heads_q = projected[:, 0:slice_width].reshape(seq_len, local_heads, HEAD_DIM)
    heads_k = projected[:, slice_width : 2 * slice_width].reshape(seq_len, local_heads, HEAD_DIM)
    heads_v = projected[:, 2 * slice_width : 3 * slice_width].reshape(
        seq_len, local_heads, HEAD_DIM
    )
    block_rows = min(512, seq_len)
    block_starts = jnp.arange(seq_len // block_rows, dtype=jnp.int32) * block_rows
    key_valid = jnp.arange(seq_len) < length

    def masked_scores(query_block):
        raw = (
            jnp.einsum("qhd,khd->hqk", query_block, heads_k, preferred_element_type=single)
            * score_scale
        )
        return jnp.where(key_valid, raw, masked_score)

    def forward_block(nothing, row_start):
        query_block = lax.dynamic_slice_in_dim(heads_q, row_start, block_rows, 0)
        scores = masked_scores(query_block)
        row_max = jnp.max(scores, -1, keepdims=True)
        shifted = jnp.exp(scores - row_max)
        row_total = jnp.sum(shifted, -1, keepdims=True)
        weights = (shifted / row_total).astype(bfloat)
        mixed = jnp.einsum("hqk,khd->qhd", weights, heads_v, preferred_element_type=single)
        return (nothing, (mixed.astype(bfloat), (row_max + jnp.log(row_total))[..., 0]))

    unused, (attended, log_totals) = lax.scan(forward_block, None, block_starts)
    attended_flat = attended.reshape(seq_len, slice_width)
    rows_here = attended_flat
    branch = (
        lax.psum_scatter(
            jnp.dot(rows_here, w_out, preferred_element_type=single),
            "tensor",
            scatter_dimension=0,
            tiled=True,
        )
        + bias_out
    )
    hidden, normed_one, inv_one = norm_forward(tokens.astype(single) + branch, gain_one, shift_one)
    full_hidden = lax.all_gather(hidden.astype(bfloat), "tensor", axis=0, tiled=True)
    up_proj = jnp.dot(full_hidden, w_up, preferred_element_type=single) + bias_up
    act_float, gelu_pull = jax.vjp(gelu_exact, up_proj)
    activation = act_float.astype(bfloat)
    rows_here = activation
    down_proj = (
        lax.psum_scatter(
            jnp.dot(rows_here, w_down, preferred_element_type=single),
            "tensor",
            scatter_dimension=0,
            tiled=True,
        )
        + bias_down
    )
    result, normed_two, inv_two = norm_forward(hidden + down_proj, gain_two, shift_two)
    layer_output = result.astype(bfloat)
    grad_out = cotangent.astype(single) * row_valid
    grad_second, dgain_two, dshift_two = norm_backward(grad_out, normed_two, inv_two, gain_two)
    grad_down = grad_second.astype(bfloat)
    dbias_down = jnp.sum(grad_down.astype(single), 0)
    full_grad_down = lax.all_gather(grad_down, "tensor", axis=0, tiled=True)
    grad_act = jnp.einsum("sd,fd->sf", full_grad_down, w_down, preferred_element_type=single)
    grad_up = gelu_pull(grad_act)[0].astype(bfloat)
    dw_down = jnp.einsum("sf,sd->fd", activation, full_grad_down, preferred_element_type=single)
    dw_up = jnp.einsum("sd,sf->df", full_hidden, grad_up, preferred_element_type=single)
    dbias_up = jnp.sum(grad_up.astype(single), 0)
    rows_here = grad_up
    grad_hidden = (
        lax.psum_scatter(
            jnp.einsum("sf,df->sd", rows_here, w_up, preferred_element_type=single),
            "tensor",
            scatter_dimension=0,
            tiled=True,
        )
        + grad_second
    )
    grad_summed, dgain_one, dshift_one = norm_backward(grad_hidden, normed_one, inv_one, gain_one)
    grad_branch = grad_summed.astype(bfloat)
    dbias_out = jnp.sum(grad_branch.astype(single), 0)
    full_grad_branch = lax.all_gather(grad_branch, "tensor", axis=0, tiled=True)
    dw_out = jnp.einsum("sa,sd->ad", attended_flat, full_grad_branch, preferred_element_type=single)
    grad_attended = jnp.einsum(
        "sd,ad->sa", full_grad_branch, w_out, preferred_element_type=single
    ).astype(bfloat)
    grad_heads = grad_attended.reshape(seq_len, local_heads, HEAD_DIM)

    def backward_block(totals, inputs):
        key_total, value_total = totals
        row_start, log_total = inputs
        query_block = lax.dynamic_slice_in_dim(heads_q, row_start, block_rows, 0)
        grad_block = lax.dynamic_slice_in_dim(grad_heads, row_start, block_rows, 0)
        probs_full = jnp.exp(masked_scores(query_block) - log_total[..., None])
        value_total = value_total + jnp.einsum(
            "hqk,qhd->khd", probs_full.astype(bfloat), grad_block, preferred_element_type=single
        )
        grad_probs = jnp.einsum("qhd,khd->hqk", grad_block, heads_v, preferred_element_type=single)
        row_cross = jnp.sum(grad_probs * probs_full, -1, keepdims=True)
        grad_scores = (probs_full * (grad_probs - row_cross)).astype(bfloat)
        grad_query = (
            jnp.einsum("hqk,khd->qhd", grad_scores, heads_k, preferred_element_type=single)
            * score_scale
        )
        key_total = (
            key_total
            + jnp.einsum("hqk,qhd->khd", grad_scores, query_block, preferred_element_type=single)
            * score_scale
        )
        return ((key_total, value_total), grad_query.astype(bfloat))

    zero_heads = jnp.zeros((seq_len, local_heads, HEAD_DIM), single)
    (key_total, value_total), grad_query = lax.scan(
        backward_block, (zero_heads, zero_heads), (block_starts, log_totals)
    )
    grad_qkv = jnp.concatenate(
        [
            grad_query.reshape(seq_len, slice_width),
            key_total.reshape(seq_len, slice_width).astype(bfloat),
            value_total.reshape(seq_len, slice_width).astype(bfloat),
        ],
        axis=1,
    )
    dw_qkv = jnp.einsum("sd,sc->dc", full_tokens, grad_qkv, preferred_element_type=single)
    dbias_query = jnp.sum(grad_qkv[:, 0:slice_width].astype(single), 0)
    dbias_value = jnp.sum(grad_qkv[:, 2 * slice_width : 3 * slice_width].astype(single), 0)
    rows_here = grad_qkv
    token_grad = (
        lax.psum_scatter(
            jnp.einsum("sc,dc->sd", rows_here, w_qkv, preferred_element_type=single).astype(
                jnp.bfloat16
            ),
            "tensor",
            scatter_dimension=0,
            tiled=True,
        ).astype(jnp.float32)
        + grad_summed
    ).astype(bfloat)
    grad_blocks = jnp.concatenate(
        [
            to_blocks(dw_qkv[:, 0:slice_width]),
            to_blocks(dw_qkv[:, slice_width : 2 * slice_width]),
            to_blocks(dw_qkv[:, 2 * slice_width : 3 * slice_width]),
            to_blocks(dw_out),
            to_blocks(dw_up),
            to_blocks(dw_down),
        ],
        axis=0,
    )
    vector_grad = jnp.concatenate(
        [
            dgain_one,
            dshift_one,
            dgain_two,
            dshift_two,
            jnp.zeros((2 * D,), single),
            dbias_out,
            jnp.zeros((FF,), single),
            dbias_down,
        ]
    )
    vector_grad = lax.dynamic_update_slice_in_dim(
        vector_grad, dbias_query, 4 * D + tensor_rank * slice_width, 0
    )
    vector_grad = lax.dynamic_update_slice_in_dim(
        vector_grad, dbias_value, 5 * D + tensor_rank * slice_width, 0
    )
    vector_grad = lax.dynamic_update_slice_in_dim(
        vector_grad, dbias_up, 7 * D + tensor_rank * hidden_width, 0
    )
    grad_scale = 1.0 / math.sqrt(seq_len * data_ranks)
    inverse = (
        jnp.zeros((block_total,), jnp.int32)
        .at[block_owner]
        .set(jnp.arange(block_total, dtype=jnp.int32))
    )
    own_canon = lax.dynamic_slice_in_dim(inverse, lax.axis_index("dp") * slots_here, slots_here)
    summed_all = lax.psum(grad_blocks, "dp")
    own_grad = jnp.take(summed_all, own_canon, axis=0)
    own_grad = own_grad * grad_scale
    vector_sum = lax.psum(vector_grad, ("dp", "tensor")) * grad_scale
    rates = rate_values(own_canon, tensors, seq_len)[:, None, None]
    left_q = left_basis[0]
    right_q = right_basis[0]
    rotated = matmul_high(left_q.swapaxes(-1, -2), matmul_high(own_grad, right_q))
    fresh_first = moment_decay * first_moment[0] + (1.0 - moment_decay) * rotated
    fresh_second = moment_decay * second_moment[0] + (1.0 - moment_decay) * rotated * rotated
    correction = 1.0 - moment_decay**STEP
    direction = fresh_first / correction / (jnp.sqrt(fresh_second / correction) + adam_eps)
    turned = matmul_high(left_q, matmul_high(direction, right_q.swapaxes(-1, -2)))
    fresh_master = master_blocks[0] - rates * (turned + weight_decay * master_blocks[0])
    fresh_left = (
        moment_decay * left_stats[0]
        + (1.0 - moment_decay) * matmul_high(own_grad, own_grad.swapaxes(-1, -2)) / BLK
    )
    fresh_right = (
        moment_decay * right_stats[0]
        + (1.0 - moment_decay) * matmul_high(own_grad.swapaxes(-1, -2), own_grad) / BLK
    )
    basis_left = renew_basis(fresh_left, left_q)
    basis_right = renew_basis(fresh_right, right_q)
    vec_first = moment_decay * vector_first + (1.0 - moment_decay) * vector_sum
    vec_second = moment_decay * vector_second + (1.0 - moment_decay) * vector_sum * vector_sum
    vec_master = vector_master - vector_rate * (vec_first / correction) / (
        jnp.sqrt(vec_second / correction) + adam_eps
    )
    return (
        layer_output,
        token_grad,
        fresh_first[None],
        fresh_second[None],
        fresh_master[None],
        fresh_left[None],
        fresh_right[None],
        basis_left[None],
        basis_right[None],
        vec_first,
        vec_second,
        vec_master,
    )


def solution(mesh):
    return jax.shard_map(
        body,
        mesh=mesh,
        in_specs=(
            P(("dp", "tensor"), None),
            P(("dp", "tensor"), None),
            P("dp"),
            P(),
            P("tensor", "dp", None, None),
            P("tensor", "dp", None, None),
            P("tensor", "dp", None, None),
            P("tensor", "dp", None, None),
            P("tensor", "dp", None, None),
            P("tensor", "dp", None, None),
            P("tensor", "dp", None, None),
            P(),
            P(),
            P(),
        ),
        out_specs=(
            P(("dp", "tensor"), None),
            P(("dp", "tensor"), None),
            P("tensor", "dp", None, None),
            P("tensor", "dp", None, None),
            P("tensor", "dp", None, None),
            P("tensor", "dp", None, None),
            P("tensor", "dp", None, None),
            P("tensor", "dp", None, None),
            P("tensor", "dp", None, None),
            P(),
            P(),
            P(),
        ),
        check_vma=False,
    )
```

profile of v0, /device:TPU:0, one launch (start us, length us, event | category | flops | bytes accessed | tf_op | source)
XLA Modules:
  0.0 2070.8 jit_solution(2761109126094623686)
XLA Ops:
  14.3 100.4 %all-gather.6.cloned.1.call-done = bf16[192,128,128]{2,1,0:T(8,128)(2,1)} async-done(((bf16[24,128,128]{2,1,0:T(8,128)(2,1)}), bf16[192,128,128]{2,1,0:T(8,128)(2,1)}) %all-gather.6.cloned.1.call-update) | async-done | bytes 6291472 | tf_op jit(solution)/shard_map/all_gather | solution.py:111
  114.6 10.8 gather_fusion
  142.1 20.1 while.28
  168.9 43.8 %reduce-scatter.5.cloned.1.call-done = f32[256,1024]{1,0:T(8,128)} async-done(((f32[1024,1024]{1,0:T(8,128)}), f32[256,1024]{1,0:T(8,128)}) %reduce-scatter.5.cloned.1.call-update) | async-done | bytes 1048592 | tf_op jit(solution)/shard_map/reduce_scatter | solution.py:172
  224.0 14.4 all-gather.10.cloned.1.call-done
  238.4 15.5 multiply_convert_fusion.1
  255.2 4.3 fusion.50
  260.5 43.8 %reduce-scatter.7.cloned.1.call-done = f32[256,1024]{1,0:T(8,128)} async-done(((f32[1024,1024]{1,0:T(8,128)}), f32[256,1024]{1,0:T(8,128)}) %reduce-scatter.7.cloned.1.call-update) | async-done | bytes 1048592 | tf_op jit(solution)/shard_map/reduce_scatter | solution.py:187
  309.2 22.7 %all-gather.12.cloned.1.call-done = bf16[1024,1024]{1,0:T(8,128)(2,1)} async-done(((bf16[256,1024]{1,0:T(8,128)(2,1)}), bf16[1024,1024]{1,0:T(8,128)(2,1)}) %all-gather.12.cloned.1.call-update) | async-done | bytes 2097168 | tf_op jit(solution)/shard_map/all_gather | solution.py:201
  331.9 9.1 convert_reduce_fusion
  342.4 4.3 fusion.54
  346.7 44.6 %reduce-scatter.9.cloned.1.call-done = f32[256,1024]{1,0:T(8,128)} async-done(((f32[1024,1024]{1,0:T(8,128)}), f32[256,1024]{1,0:T(8,128)}) %reduce-scatter.9.cloned.1.call-update) | async-done | bytes 1048592 | tf_op jit(solution)/shard_map/reduce_scatter | solution.py:209
  391.4 4.1 multiply_reduce_fusion.2
  398.1 22.3 %all-gather.14.cloned.1.call-done = bf16[1024,1024]{1,0:T(8,128)(2,1)} async-done(((bf16[256,1024]{1,0:T(8,128)(2,1)}), bf16[1024,1024]{1,0:T(8,128)(2,1)}) %all-gather.14.cloned.1.call-update) | async-done | bytes 2097168 | tf_op jit(solution)/shard_map/all_gather | solution.py:220
  424.4 45.1 %while.29 = (s32[]{:T(128)}, f32[1024,4,64]{0,2,1:T(8,128)S(1)}, f32[1024,4,64]{0,2,1:T(8,128)}, bf16[2,512,4,64]{1,3,2,0:T(8,128)(2,1)}, s32[2]{0:T(128)S(1)}, ...) while((s32[]{:T(128)}, f32[1024,4,64]{0,2,1:T(8,128)S(1)}, ...), condition=%wide.region_17.18_spmd.clone, body=%wide.region_15.17_spmd.clone.sunk | while | flops 1375206400 | bytes 164426176 | solution.py:251
  463.3 4.1 fusion.220
  471.9 4.7 convolution_convert_fusion
  476.8 4.6 convolution_bitcast_fusion.1
  539.8 44.8 %psum.15 = f32[12288]{0:T(1024)S(1)} all-reduce(f32[12288]{0:T(1024)S(1)} %dynamic_update_slice.22), channel_id=1, replica_groups=mesh['dp'=8,'tensor'=4] {'dp','tensor'}, use_global_device_ids=true, to_apply=%region_32.35 | all-reduce | flops 12288 | bytes 98304 | tf_op jit(solution)/shard_map/psum | solution.py:319
  587.3 336.5 %all-reduce.2.cloned.1.call-done = f32[192,128,128]{2,1,0:T(8,128)} async-done(((f32[192,128,128]{2,1,0:T(8,128)}), f32[192,128,128]{2,1,0:T(8,128)}) %all-reduce.2.cloned.1.call-update) | async-done | bytes 12582928 | tf_op jit(solution)/shard_map/psum | solution.py:316
  923.8 5.2 gather_fusion.1
  929.1 4.2 fusion.84
  947.2 6.4 fusion.73
  956.6 5.2 bitcast_add_fusion.3
  968.8 4.4 bitcast_add_fusion.2
  989.4 282.8 %custom-call.12 = f32[24,128,128]{2,1,0:T(8,128)} custom-call(f32[24,128,128]{2,1,0:T(8,128)} %fusion.66), custom_call_target="Cholesky" | custom-call | tf_op jit(solution)/shard_map/jit(cholesky)/cholesky | solution.py:60
  1272.2 5.7 fusion.153
  1284.2 283.2 %custom-call.10 = f32[24,128,128]{2,1,0:T(8,128)} custom-call(f32[24,128,128]{2,1,0:T(8,128)} %fusion.70), custom_call_target="Cholesky" | custom-call | tf_op jit(solution)/shard_map/jit(cholesky)/cholesky | solution.py:60
  1572.3 237.2 %custom-call.11 = f32[24,1,128,128]{2,3,1,0:T(8,128)} custom-call(f32[24,1,128,128]{3,2,1,0:T(8,128)} %get-tuple-element.323), custom_call_target="InvertDiagBlocksLowerTriangular" | custom-call | tf_op jit(solution)/shard_map/jit(_solve_triangular)/vmap()/triangular_solve | solution.py:61
  1809.5 5.7 fusion.91
  1818.2 237.3 %custom-call.13 = f32[24,1,128,128]{2,3,1,0:T(8,128)} custom-call(f32[24,1,128,128]{3,2,1,0:T(8,128)} %get-tuple-element.322), custom_call_target="InvertDiagBlocksLowerTriangular" | custom-call | tf_op jit(solution)/shard_map/jit(_solve_triangular)/vmap()/triangular_solve | solution.py:61
  2055.5 5.2 fusion.96
  (314 shorter events, 229.7 us)
Async XLA Ops:
  7.2 926.1 %copy-start = (f32[1,24,128,128]{3,2,1,0:T(8,128)S(1)}, f32[1,24,128,128]{3,2,1,0:T(8,128)}, u32[]{:S(2)}) copy-start(f32[1,24,128,128]{3,2,1,0:T(8,128)} %param.30) | copy-start | bytes 4718596
  7.2 107.4 %all-gather.6.cloned.1.call-start = ((), (), s32[]{:S(2)}) async-start(), calls=%async_computation.4 | async-start | bytes 7077888 | tf_op jit(solution)/shard_map/all_gather | solution.py:111
  9.2 4.3 copy-start.42
  9.3 4.4 copy-start.54
  12.8 124.5 %all-gather.8.cloned.1.call-start = ((), (), s32[]{:S(2)}) async-start(), calls=%async_computation.5 | async-start | bytes 2621440 | tf_op jit(solution)/shard_map/all_gather | solution.py:137
  13.5 199.2 %reduce-scatter.5.cloned.1.call-start = ((), (), s32[]{:S(2)}) async-start(), calls=%async_computation.6 | async-start | bytes 5242880 | tf_op jit(solution)/shard_map/reduce_scatter | solution.py:172
  162.2 6.0 copy-start.4
  162.2 6.0 copy-start.7
  168.3 70.1 %all-gather.10.cloned.1.call-start = ((), (), s32[]{:S(2)}) async-start(), calls=%async_computation.7 | async-start | bytes 2621440 | tf_op jit(solution)/shard_map/all_gather | solution.py:181
  215.6 88.6 %reduce-scatter.7.cloned.1.call-start = ((), (), s32[]{:S(2)}) async-start(), calls=%async_computation.8 | async-start | bytes 5242880 | tf_op jit(solution)/shard_map/reduce_scatter | solution.py:187
  238.4 16.9 copy-start.34
  259.6 72.4 %all-gather.12.cloned.1.call-start = ((), (), s32[]{:S(2)}) async-start(), calls=%async_computation.9 | async-start | bytes 2621440 | tf_op jit(solution)/shard_map/all_gather | solution.py:201
  309.2 82.2 %reduce-scatter.9.cloned.1.call-start = ((), (), s32[]{:S(2)}) async-start(), calls=%async_computation.10 | async-start | bytes 5242880 | tf_op jit(solution)/shard_map/reduce_scatter | solution.py:209
  331.9 10.4 copy-start.33
  346.7 73.7 %all-gather.14.cloned.1.call-start = ((), (), s32[]{:S(2)}) async-start(), calls=%async_computation.11 | async-start | bytes 2621440 | tf_op jit(solution)/shard_map/all_gather | solution.py:220
  397.6 187.7 %reduce-scatter.11.cloned.1.call-start = ((), (), s32[]{:S(2)}) async-start(), calls=%async_computation.12 | async-start | bytes 2621440 | tf_op jit(solution)/shard_map/reduce_scatter | solution.py:267
  436.5 4.7 copy-start.2
  436.5 4.8 copy-start.31
  458.5 4.7 copy-start.2
  458.5 4.8 copy-start.31
  463.3 4.1 copy-start.3
  463.3 4.1 copy-start.23
  476.6 447.2 %all-reduce.2.cloned.1.call-start = ((), (), s32[]{:S(2)}) async-start(), calls=%async_computation.13 | async-start | bytes 25165824 | tf_op jit(solution)/shard_map/psum | solution.py:316
  482.5 3.8 copy-start.58
  518.8 3.7 copy-start.10
  535.2 4.4 copy-start.53
  535.2 49.4 %copy-start.43 = (f32[12288]{0:T(1024)S(1)}, f32[12288]{0:T(1024)}, u32[]{:S(2)}) copy-start(f32[12288]{0:T(1024)} %param.32) | copy-start | bytes 147460
  535.2 49.4 %copy-start.44 = (f32[12288]{0:T(1024)S(1)}, f32[12288]{0:T(1024)}, u32[]{:S(2)}) copy-start(f32[12288]{0:T(1024)} %param.34) | copy-start | bytes 147460
  535.2 49.4 %copy-start.45 = (f32[12288]{0:T(1024)S(1)}, f32[12288]{0:T(1024)}, u32[]{:S(2)}) copy-start(f32[12288]{0:T(1024)} %param.33) | copy-start | bytes 147460
  535.2 50.1 %copy-start.29 = (f32[256,1024]{1,0:T(8,128)S(1)}, f32[256,1024]{1,0:T(8,128)}, u32[]{:S(2)}) copy-start(f32[256,1024]{1,0:T(8,128)} %get-tuple-element.284) | copy-start | bytes 3145732
  961.9 3.9 copy-start.13
  968.8 4.4 copy-start.16
  (48 other events, 112.3 us)
Sparse Core Ops, SparseCore 0:
  12.9 101.7 all-gather.5
  116.2 20.7 all-gather.7
  168.4 44.2 reduce-scatter.4
  215.7 22.5 all-gather.9
  259.7 44.4 reduce-scatter.6
  309.3 22.5 all-gather.11
  346.8 44.5 reduce-scatter.8
  397.8 22.5 all-gather.13
  476.7 31.4 reduce-scatter.10
  524.9 398.9 all-reduce.1
where the time goes:
time: 2080 us; the launch traced here: 2070 us
  other arithmetic  1090 us (52%)
  waiting for transfers between devices  629 us (30%)
  matrix products  146 us (7%)
  local copies, waits for them, and re-layouts  135 us (6%)
  blocking collectives  44.8 us (2%)
    another operation x6, other arithmetic, renew_basis(): factor = jnp.linalg.cholesky(gram)  569 us
    another operation x4, other arithmetic, renew_basis(): jax.scipy.linalg.solve_triangular(factor, product.swapaxes(-1, -2), lower...  477 us
    psum x1, waiting for transfers between devices, body(): summed_all = lax.psum(grad_blocks, 'dp')  337 us
    all_gather x1, waiting for transfers between devices, body(): lax.all_gather(master_blocks[0].astype(bfloat), 'dp', axis=0, tiled=True)  100 us
    unnamed x134, local copies, waits for them, and re-layouts  64.3 us
    psum x1, blocking collectives, body(): vector_sum = lax.psum(vector_grad, ('dp', 'tensor')) * grad_scale  44.8 us
    reduce_scatter x1, waiting for transfers between devices, body(): lax.psum_scatter(jnp.einsum('sf,df->sd', rows_here, w_up, preferred_eleme...  44.6 us
    reduce_scatter x1, waiting for transfers between devices, body(): lax.psum_scatter(jnp.dot(rows_here, w_out, preferred_element_type=single)...  43.8 us
  transfers between devices with their start and end apart: 10, of which 8 were waited for; matrix products, arithmetic and copies ran while one was open for 4% of the time, Pallas kernels for 0%

commit v1 on v0

--- a/solution.py
+++ b/solution.py
@@ -1,8 +1,11 @@
+import functools
 import math
 
 import jax
 import jax.numpy as jnp
 from jax import lax
+from jax.experimental import pallas as pl
+from jax.experimental.pallas import tpu as pltpu
 from jax.sharding import PartitionSpec as P
 
 D = 1024
@@ -27,6 +30,123 @@
     return jnp.matmul(left, right, precision=highest)
 
 
+def mm(a,b,ca=1,cb=0,prec=highest):
+    return lax.dot_general(a,b,(((ca,),(cb,)),((),())),precision=prec,preferred_element_type=single)
+
+def adam_kernel(rates_ref, g_ref, m_ref, v_ref, w_ref, sl_ref, sr_ref, l_ref, r_ref,
+                mo_ref, vo_ref, wo_ref, slo_ref, sro_ref, gram_ref, at_ref, *, per):
+    i = pl.program_id(0)
+    corr = 1.0 - 0.5**STEP
+    for q in range(per):
+        g=g_ref[q]; l=l_ref[q]; r=r_ref[q]
+        rot = mm(l, mm(g, r), 0, 0)
+        nm = 0.5*m_ref[q] + 0.5*rot
+        nv = 0.5*v_ref[q] + 0.5*rot*rot
+        mo_ref[q]=nm; vo_ref[q]=nv
+        d = (nm/corr)/(jnp.sqrt(nv/corr)+1e-8)
+        turned = mm(l, mm(d, r, 1, 1))
+        rate = rates_ref[i*per+q]
+        w = w_ref[q]
+        wo_ref[q] = w - rate*(turned + 0.01*w)
+        sl = 0.5*sl_ref[q] + (0.5/BLK)*mm(g,g,1,1)
+        sr = 0.5*sr_ref[q] + (0.5/BLK)*mm(g,g,0,0)
+        slo_ref[q]=sl; sro_ref[q]=sr
+        for side,(s,b) in enumerate(((sl,l),(sr,r))):
+            at = mm(b, s, 0, 0)
+            gram = mm(at, at, 1, 1)
+            gram_ref[side, q]=gram
+            at_ref[side, q]=at
+
+def adam(g,m,v,w,sl,sr,l,r,rates,per=2):
+    n=g.shape[0]
+    blk=lambda: pl.BlockSpec((per,BLK,BLK),lambda i,*_:(i,0,0))
+    sd=jax.ShapeDtypeStruct((n,BLK,BLK),single)
+    return pl.pallas_call(functools.partial(adam_kernel,per=per),
+        grid_spec=pltpu.PrefetchScalarGridSpec(num_scalar_prefetch=1,grid=(n//per,),
+            in_specs=[blk() for _ in range(8)],
+            out_specs=[blk() for _ in range(5)]+[pl.BlockSpec((2,per,BLK,BLK),lambda i,*_:(0,i,0,0))]*2),
+        out_shape=[sd]*5+[jax.ShapeDtypeStruct((2,n,BLK,BLK),single)]*2,
+        compiler_params=pltpu.CompilerParams(vmem_limit_bytes=48*2**20),
+        name="adam")(rates,g,m,v,w,sl,sr,l,r)
+
+PB=32
+def factor_panel(rows):
+    nb=PB//8
+    T=[[rows[j][8*ib:8*ib+8] if ib>=j//8 else None for ib in range(nb)] for j in range(PB)]
+    batch=rows[0].shape[1]
+    sub=lax.broadcasted_iota(jnp.int32,(8,batch),0)
+    X=[[None]*nb for _ in range(PB)]
+    zero=jnp.zeros((8,batch),single)
+    for k in range(PB):
+        kb,ks=divmod(k,8)
+        piv=T[k][kb][ks:ks+1]
+        y=lax.rsqrt(piv)
+        y=y*(1.5-0.5*piv*y*y)
+        yb=jnp.broadcast_to(y,(8,batch))
+        col=[T[k][ib]*yb if ib>=kb else None for ib in range(nb)]
+        unit=jnp.where(sub==ks,yb,0.0)
+        xk=[]
+        for cb in range(kb+1):
+            v=X[k][cb]
+            if cb==kb:
+                xk.append(unit if v is None else jnp.where(sub==ks,yb,v*yb))
+            else:
+                xk.append(zero if v is None else v*yb)
+        X[k]=xk+[zero]*(nb-kb-1)
+        for j in range(k+1,PB):
+            jb,js=divmod(j,8)
+            s=jnp.broadcast_to(col[jb][js:js+1],(8,batch))
+            for ib in range(jb,nb):
+                T[j][ib]=T[j][ib]-s*col[ib]
+            for cb in range(kb+1):
+                t=s*xk[cb]
+                X[j][cb]= -t if X[j][cb] is None else X[j][cb]-t
+    return X
+
+def chol_kernel(g_in_ref, at_in_ref, q_ref, g_ref, at_ref, xs_ref, *, n, unroll):
+    g_ref[...]=g_in_ref[...]
+    at_ref[...]=at_in_ref[...]
+    pad=jnp.zeros((BLK-PB,n),single)
+    for p in range(BLK//PB):
+        rows=[]
+        for j in range(PB):
+            t=g_ref[pl.ds(p*PB+j,n,stride=BLK),:]
+            rows.append(t.T[p*PB:(p+1)*PB])
+        X=factor_panel(rows)
+        for i in range(PB):
+            xi=jnp.concatenate(X[i]+[pad],axis=0)
+            xs_ref[pl.ds(i,n,stride=PB),:]=xi.T
+        def step(m,_):
+            xm=xs_ref[pl.ds(pl.multiple_of(m*PB,PB),PB),0:PB]
+            base=pl.multiple_of(m*BLK,BLK)
+            ra=mm(xm,at_ref[pl.ds(base+p*PB,PB),:])
+            at_ref[pl.ds(base+p*PB,PB),:]=ra
+            if p<BLK//PB-1:
+                first=(p+1)*PB
+                rest=pl.ds(base+first,BLK-first)
+                rg=mm(xm,g_ref[pl.ds(base+p*PB,PB),:])
+                lead=rg[:,first:]
+                g_ref[rest,:]=g_ref[rest,:]-mm(lead,rg,0,0)
+                at_ref[rest,:]=at_ref[rest,:]-mm(lead,ra,0,0)
+            return 0
+        lax.fori_loop(0,n,step,0,unroll=unroll)
+    def fin(m,_):
+        base=pl.multiple_of(m*BLK,BLK)
+        q_ref[m]=at_ref[pl.ds(base,BLK),:].T
+        return 0
+    lax.fori_loop(0,n,fin,0,unroll=unroll)
+
+def chol(gram,at,unroll=4):
+    n=gram.shape[0]*gram.shape[1]
+    q=pl.pallas_call(functools.partial(chol_kernel,n=n,unroll=unroll),
+        in_specs=[pl.BlockSpec(memory_space=pltpu.VMEM)]*2,out_specs=pl.BlockSpec(memory_space=pltpu.VMEM),
+        out_shape=jax.ShapeDtypeStruct((n,BLK,BLK),single),
+        scratch_shapes=[pltpu.VMEM((n*BLK,BLK),single),pltpu.VMEM((n*BLK,BLK),single),pltpu.VMEM((n*PB,BLK),single)],
+        compiler_params=pltpu.CompilerParams(vmem_limit_bytes=48*2**20),
+        name="chol")(gram.reshape(n*BLK,BLK),at.reshape(n*BLK,BLK))
+    return q
+
+
 def gelu_exact(inputs):
     return jax.nn.gelu(inputs, approximate=False)
 
@@ -52,14 +172,6 @@
     inner = jnp.where(canon_index < 4 * attn_count + ffn_count, D ** (-0.5), FF ** (-0.5))
     inner = jnp.where(canon_index < 4 * attn_count, out_std, inner)
     return jnp.where(canon_index < 3 * attn_count, D ** (-0.5), inner).astype(single)
-
-
-def renew_basis(stats, basis):
-    product = matmul_high(stats, basis)
-    gram = matmul_high(product.swapaxes(-1, -2), product)
-    factor = jnp.linalg.cholesky(gram)
-    solved = jax.scipy.linalg.solve_triangular(factor, product.swapaxes(-1, -2), lower=True)
-    return solved.swapaxes(-1, -2)
 
 
 def norm_forward(inputs, gain, shift):
@@ -170,11 +282,11 @@
     rows_here = attended_flat
     branch = (
         lax.psum_scatter(
-            jnp.dot(rows_here, w_out, preferred_element_type=single),
+            jnp.dot(rows_here, w_out, preferred_element_type=single).astype(bfloat),
             "tensor",
             scatter_dimension=0,
             tiled=True,
-        )
+        ).astype(single)
         + bias_out
     )
     hidden, normed_one, inv_one = norm_forward(tokens.astype(single) + branch, gain_one, shift_one)
@@ -185,11 +297,11 @@
     rows_here = activation
     down_proj = (
         lax.psum_scatter(
-            jnp.dot(rows_here, w_down, preferred_element_type=single),
+            jnp.dot(rows_here, w_down, preferred_element_type=single).astype(bfloat),
             "tensor",
             scatter_dimension=0,
             tiled=True,
-        )
+        ).astype(single)
         + bias_down
     )
     result, normed_two, inv_two = norm_forward(hidden + down_proj, gain_two, shift_two)
@@ -207,11 +319,11 @@
     rows_here = grad_up
     grad_hidden = (
         lax.psum_scatter(
-            jnp.einsum("sf,df->sd", rows_here, w_up, preferred_element_type=single),
+            jnp.einsum("sf,df->sd", rows_here, w_up, preferred_element_type=single).astype(bfloat),
             "tensor",
             scatter_dimension=0,
             tiled=True,
-        )
+        ).astype(single)
         + grad_second
     )
     grad_summed, dgain_one, dshift_one = norm_backward(grad_hidden, normed_one, inv_one, gain_one)
@@ -313,30 +425,16 @@
         .set(jnp.arange(block_total, dtype=jnp.int32))
     )
     own_canon = lax.dynamic_slice_in_dim(inverse, lax.axis_index("dp") * slots_here, slots_here)
-    summed_all = lax.psum(grad_blocks, "dp")
-    own_grad = jnp.take(summed_all, own_canon, axis=0)
-    own_grad = own_grad * grad_scale
     vector_sum = lax.psum(vector_grad, ("dp", "tensor")) * grad_scale
-    rates = rate_values(own_canon, tensors, seq_len)[:, None, None]
-    left_q = left_basis[0]
-    right_q = right_basis[0]
-    rotated = matmul_high(left_q.swapaxes(-1, -2), matmul_high(own_grad, right_q))
-    fresh_first = moment_decay * first_moment[0] + (1.0 - moment_decay) * rotated
-    fresh_second = moment_decay * second_moment[0] + (1.0 - moment_decay) * rotated * rotated
+    sent = jnp.take((grad_blocks * grad_scale).astype(bfloat), inverse, axis=0)
+    own_grad = lax.psum_scatter(sent, "dp", scatter_dimension=0, tiled=True).astype(single)
+    rates = rate_values(own_canon, tensors, seq_len)
     correction = 1.0 - moment_decay**STEP
-    direction = fresh_first / correction / (jnp.sqrt(fresh_second / correction) + adam_eps)
-    turned = matmul_high(left_q, matmul_high(direction, right_q.swapaxes(-1, -2)))
-    fresh_master = master_blocks[0] - rates * (turned + weight_decay * master_blocks[0])
-    fresh_left = (
-        moment_decay * left_stats[0]
-        + (1.0 - moment_decay) * matmul_high(own_grad, own_grad.swapaxes(-1, -2)) / BLK
-    )
-    fresh_right = (
-        moment_decay * right_stats[0]
-        + (1.0 - moment_decay) * matmul_high(own_grad.swapaxes(-1, -2), own_grad) / BLK
-    )
-    basis_left = renew_basis(fresh_left, left_q)
-    basis_right = renew_basis(fresh_right, right_q)
+    fresh_first, fresh_second, fresh_master, fresh_left, fresh_right, gram, product = adam(
+        own_grad, first_moment[0], second_moment[0], master_blocks[0], left_stats[0], right_stats[0],
+        left_basis[0], right_basis[0], rates, per=2 if slots_here % 2 == 0 else 1)
+    bases = chol(gram, product)
+    basis_left, basis_right = bases[:slots_here], bases[slots_here:]
     vec_first = moment_decay * vector_first + (1.0 - moment_decay) * vector_sum
     vec_second = moment_decay * vector_second + (1.0 - moment_decay) * vector_sum * vector_sum
     vec_master = vector_master - vector_rate * (vec_first / correction) / (

time: 2080 us -> 746 us (0.36)
  other arithmetic: 1090 us -> 65.1 us
  waiting for transfers between devices: 629 us -> 323 us
  Pallas kernels: 0 us -> 115 us
  matrix products: 146 us -> 86.2 us
  local copies, waits for them, and re-layouts: 135 us -> 79.7 us
    another operation x10 -> x0, other arithmetic: 1050 us -> none  [the longest x6 569 us: renew_basis(): factor = jnp.linalg.cholesky(gram)]
    psum x1 -> x0, waiting for transfers between devices: 337 us -> none  [body(): summed_all = lax.psum(grad_blocks, 'dp')]
    pallas_call x0 -> x2, Pallas kernels: none -> 115 us  [the longest x1 69.9 us: chol(): pl.pallas_call(functools.partial(chol_kernel, n=n, unroll=unroll), in_spe...]
    reduce_scatter x0 -> x1, waiting for transfers between devices: none -> 70.3 us  [body(): lax.psum_scatter(sent, 'dp', scatter_dimension=0, tiled=True).astype(single)]
    unnamed x134 -> x92, local copies, waits for them, and re-layouts: 64.3 us -> 18.8 us
    dot_general x12 -> x2, matrix products: 49.3 us -> 5.7 us  [the longest x1 3.62 us: body(): jnp.dot(rows_here, w_down, preferred_element_type=single).astype(bfloat)]
  transfers between devices with their start and end apart: 10 -> 10, of which waited for: 8 -> 9; matrix products, arithmetic and copies ran while one was open for 4% -> 14% of each run, Pallas kernels for 0% -> 0%
where the time goes in v1:
time: 746 us; the launch traced here: 736 us
  waiting for transfers between devices  323 us (43%)
  Pallas kernels  115 us (15%)
  matrix products  86.2 us (12%)
  local copies, waits for them, and re-layouts  79.7 us (11%)
  other arithmetic  65.1 us (9%)
  blocking collectives  43.2 us (6%)
  between operations  16 us (2%)
    all_gather x1, waiting for transfers between devices, body(): lax.all_gather(master_blocks[0].astype(bfloat), 'dp', axis=0, tiled=True)  99.8 us
    reduce_scatter x1, waiting for transfers between devices, body(): lax.psum_scatter(sent, 'dp', scatter_dimension=0, tiled=True).astype(single)  70.3 us
    pallas_call x1, Pallas kernels, chol(): pl.pallas_call(functools.partial(chol_kernel, n=n, unroll=unroll), in_spe...  69.9 us
    pallas_call x1, Pallas kernels, adam(): pl.pallas_call(functools.partial(adam_kernel, per=per), grid_spec=pltpu.P...  44.8 us
    psum x1, blocking collectives, body(): vector_sum = lax.psum(vector_grad, ('dp', 'tensor')) * grad_scale  43.2 us
    reduce_scatter x1, waiting for transfers between devices, body(): lax.psum_scatter(jnp.einsum('sf,df->sd', rows_here, w_up, preferred_eleme...  31.5 us
    reduce_scatter x1, waiting for transfers between devices, body(): lax.psum_scatter(jnp.dot(rows_here, w_out, preferred_element_type=single)...  31.3 us
    reduce_scatter x1, waiting for transfers between devices, body(): lax.psum_scatter(jnp.dot(rows_here, w_down, preferred_element_type=single...  30.7 us
  transfers between devices with their start and end apart: 10, of which 9 were waited for; matrix products, arithmetic and copies ran while one was open for 14% of the time, Pallas kernels for 0%

profile of v1, /device:TPU:0, one launch (start us, length us, event | category | flops | bytes accessed | tf_op | source)
XLA Modules:
  0.0 736.2 jit_solution(14537741930557742780)
XLA Ops:
  12.7 99.8 %all-gather.6.cloned.1.call-done = bf16[192,128,128]{2,1,0:T(8,128)(2,1)} async-done(((bf16[24,128,128]{2,1,0:T(8,128)(2,1)}), bf16[192,128,128]{2,1,0:T(8,128)(2,1)}) %all-gather.6.cloned.1.call-update) | async-done | bytes 6291472 | tf_op jit(solution)/shard_map/all_gather | solution.py:223
  112.5 10.8 %gather_fusion = bf16[192,128,128]{2,1,0:T(8,128)(2,1)} fusion(bf16[192,128,128]{2,1,0:T(8,128)(2,1)} %all-gather.6.cloned.1.call-done, s32[1024]{0:T(1024)S(1)} %pad_clamp_fusion.1), kind=kCustom, calls=%fused_computation.clone | custom fusion | bytes 12583680 | tf_op jit(solution)/shard_map/jit(_take)/gather | solution.py:224
  123.3 6.1 broadcast_select_fusion.1
  134.9 3.4 fusion.68
  138.5 18.5 %while.28 = (s32[]{:T(128)}, bf16[2,512,4,64]{1,3,2,0:T(8,128)(2,1)S(1)}, f32[2,4,512]{2,1,0:T(4,128)S(1)}, s32[2]{0:T(128)S(1)}, bf16[1024,4,64]{0,2,1:T(8,128)...) while((s32[]{:T(128)}, ...), condition=%wide.region_3.5_spmd.clone, body=%wide.region_0.4_spmd.clone.sunk | while | flops 562166784 | bytes 26808500 | solution.py:280
  161.6 31.3 %reduce-scatter.6.cloned.1.call-done = bf16[256,1024]{1,0:T(8,128)(2,1)} async-done(((bf16[1024,1024]{1,0:T(8,128)(2,1)}), bf16[256,1024]{1,0:T(8,128)(2,1)}) %reduce-scatter.6.cloned.1.call-update) | async-done | bytes 524304 | tf_op jit(solution)/shard_map/reduce_scatter | solution.py:284
  206.2 14.4 %all-gather.10.cloned.1.call-done = bf16[1024,1024]{1,0:T(8,128)(2,1)} async-done(((bf16[256,1024]{1,0:T(8,128)(2,1)}), bf16[1024,1024]{1,0:T(8,128)(2,1)}) %all-gather.10.cloned.1.call-update) | async-done | bytes 2097168 | tf_op jit(solution)/shard_map/all_gather | solution.py:293
  220.6 15.6 %multiply_convert_fusion.2 = (bf16[1024,1024]{1,0:T(8,128)(2,1)S(1)}, f32[1024,1024]{1,0:T(8,128)}, f32[1024,1024]{1,0:T(8,128)}) fusion(f32[1024]{0:T(1024)S(1)} %get-tuple-element.274, bf16[1024,1024]{1,0:T(8,128)(2,1)} %all-gather.10.cloned.1.call-done, bf16[128,8,8,128]{3,2,1,0:T(8,128)(2,1)} %bitcast.263), kind=kOutput, calls=%fused_computation.57 | convolution fusion | flops 2216689664 | bytes 14684160 | tf_op jit(solution)/shard_map/dot_general | solution.py:294
  237.5 3.6 fusion.61
  242.0 30.7 %reduce-scatter.8.cloned.1.call-done = bf16[256,1024]{1,0:T(8,128)(2,1)} async-done(((bf16[1024,1024]{1,0:T(8,128)(2,1)}), bf16[256,1024]{1,0:T(8,128)(2,1)}) %reduce-scatter.8.cloned.1.call-update) | async-done | bytes 524304 | tf_op jit(solution)/shard_map/reduce_scatter | solution.py:299
  279.4 22.7 %all-gather.12.cloned.1.call-done = bf16[1024,1024]{1,0:T(8,128)(2,1)} async-done(((bf16[256,1024]{1,0:T(8,128)(2,1)}), bf16[1024,1024]{1,0:T(8,128)(2,1)}) %all-gather.12.cloned.1.call-update) | async-done | bytes 2097168 | tf_op jit(solution)/shard_map/all_gather | solution.py:313
  302.1 9.1 %convert_reduce_fusion = (f32[1024]{0:T(1024)}, bf16[1024,1024]{1,0:T(8,128)(2,1)S(1)}) fusion(f32[1024,1024]{1,0:T(8,128)} %get-tuple-element.252, bf16[1024,1024]{1,0:T(8,128)(2,1)} %all-gather.12.cloned.1.call-done, bf16[128,8,8,128]{3,2,1,0:T(8,128)(2,1)} %bitcast.265, f32[1024,1024]{1,0:T(8,128)} %get-tuple-element.281, f32[1024]{0:T(1024)S(1)} %get-tuple-element.274), kind=kOutput, calls=%fused_computation.55 | convolution fusion | flops 2165308416 | bytes 14688256 | tf_op jit(solution)/shard_map/sd,fd->sf/dot_general | solution.py:314
  312.5 3.7 fusion.58
  316.2 31.5 %reduce-scatter.10.cloned.1.call-done = bf16[256,1024]{1,0:T(8,128)(2,1)} async-done(((bf16[1024,1024]{1,0:T(8,128)(2,1)}), bf16[256,1024]{1,0:T(8,128)(2,1)}) %reduce-scatter.10.cloned.1.call-update) | async-done | bytes 524304 | tf_op jit(solution)/shard_map/reduce_scatter | solution.py:321
  350.4 3.6 convert_reduce_fusion.4
  357.0 19.7 %all-gather.14.cloned.1.call-done = bf16[1024,1024]{1,0:T(8,128)(2,1)} async-done(((bf16[256,1024]{1,0:T(8,128)(2,1)}), bf16[1024,1024]{1,0:T(8,128)(2,1)}) %all-gather.14.cloned.1.call-update) | async-done | bytes 2097168 | tf_op jit(solution)/shard_map/all_gather | solution.py:332
  376.8 3.1 convolution_convert_fusion.2
  380.0 40.5 %while.29 = (s32[]{:T(128)}, f32[1024,4,64]{0,2,1:T(8,128)S(1)}, f32[1024,4,64]{0,2,1:T(8,128)}, bf16[2,512,4,64]{1,3,2,0:T(8,128)(2,1)S(1)}, s32[2]{0:T(128)S(1...) while((s32[]{:T(128)}, f32[1024,4,64]{0,2,1:T(8,128)S(1)}, ...), condition=%wide.region_17.19_spmd.clone, body=%wide.region_15.18_spmd.clone.sunk | while | flops 1375206400 | bytes 158134656 | solution.py:363
  387.1 3.5 multiply_convert_fusion.4
  390.7 3.4 fusion.147
  406.8 3.5 multiply_convert_fusion.4
  410.3 3.4 fusion.147
  415.0 4.1 fusion.148
  422.8 3.2 convolution_convert_fusion.1
  426.2 4.6 convolution_bitcast_fusion.1
  465.1 9.0 %multiply_convert_fusion.1 = bf16[192,128,128]{2,1,0:T(8,128)(2,1)} fusion(f32[192,128,128]{2,1,0:T(8,128)} %constant_dynamic-update-slice_fusion), kind=kLoop, calls=%fused_computation.50 | loop fusion | flops 6291456 | bytes 18874368 | tf_op jit(solution)/shard_map/convert_element_type | solution.py:429
  474.1 11.0 %gather_fusion.1 = bf16[192,128,128]{2,1,0:T(8,128)(2,1)} fusion(bf16[192,128,128]{2,1,0:T(8,128)(2,1)} %multiply_convert_fusion.1, s32[1024]{0:T(1024)} %pad_clamp_fusion), kind=kCustom, calls=%fused_computation.1.clone | custom fusion | bytes 12583680 | tf_op jit(solution)/shard_map/jit(_take)/gather | solution.py:429
  485.1 6.1 broadcast_select_fusion
  494.4 43.2 %psum.7 = f32[12288]{0:T(1024)S(1)} all-reduce(f32[12288]{0:T(1024)S(1)} %dynamic_update_slice.22), channel_id=1, replica_groups=mesh['dp'=8,'tensor'=4] {'dp','tensor'}, use_global_device_ids=true, to_apply=%region_30.32 | all-reduce | flops 12288 | bytes 98304 | tf_op jit(solution)/shard_map/psum | solution.py:428
  540.6 70.3 %reduce-scatter.14.cloned.1.call-done = bf16[24,128,128]{2,1,0:T(8,128)(2,1)} async-done(((bf16[192,128,128]{2,1,0:T(8,128)(2,1)}), bf16[24,128,128]{2,1,0:T(8,128)(2,1)}) %reduce-scatter.14.cloned.1.call-update) | async-done | bytes 786448 | tf_op jit(solution)/shard_map/reduce_scatter | solution.py:430
  612.2 44.8 %adam.1 = (f32[24,128,128]{2,1,0:T(8,128)}, f32[24,128,128]{2,1,0:T(8,128)}, f32[24,128,128]{2,1,0:T(8,128)}, f32[24,128,128]{2,1,0:T(8,128)}, f32[24,128,128]{2...) custom-call(f32[24]{0:T(128)S(1)} %compare_select_fusion.4.rates_ref, ...), custom_call_target="tpu_custom_call" | custom-call | tf_op jit(solution)/shard_map/adam/pallas_call | solution.py:64
  657.0 69.9 %chol.1 = f32[48,128,128]{2,1,0:T(8,128)S(1)} custom-call(f32[6144,128]{1,0:T(8,128)} %bitcast.260, f32[6144,128]{1,0:T(8,128)} %bitcast.261), custom_call_target="tpu_custom_call" | custom-call | tf_op jit(solution)/shard_map/chol/pallas_call | solution.py:141
  (231 shorter events, 123.7 us)
Async XLA Ops:
  7.2 105.3 %all-gather.6.cloned.1.call-start = ((), (), s32[]{:S(2)}) async-start(), calls=%async_computation.5 | async-start | bytes 7077888 | tf_op jit(solution)/shard_map/all_gather | solution.py:223
  9.7 125.2 %all-gather.8.cloned.1.call-start = ((), (), s32[]{:S(2)}) async-start(), calls=%async_computation.6 | async-start | bytes 2621440 | tf_op jit(solution)/shard_map/all_gather | solution.py:249
  10.4 182.5 %reduce-scatter.6.cloned.1.call-start = ((), (), s32[]{:S(2)}) async-start(), calls=%async_computation.7 | async-start | bytes 2621440 | tf_op jit(solution)/shard_map/reduce_scatter | solution.py:284
  12.0 111.4 %copy-start.30 = (s32[192]{0:T(256)}, s32[192]{0:T(256)S(1)}, u32[]{:S(2)}) copy-start(s32[192]{0:T(256)S(1)} %compare_select_fusion.1) | copy-start | bytes 2308
  157.0 4.6 copy-start.20
  157.1 35.9 %copy-start.5 = (bf16[256,1024]{1,0:T(8,128)(2,1)S(1)}, bf16[256,1024]{1,0:T(8,128)(2,1)}, u32[]{:S(2)}) copy-start(bf16[256,1024]{1,0:T(8,128)(2,1)} %param.20) | copy-start | bytes 1572868
  157.7 37.9 %copy-start.9 = (bf16[32,8,2,512]{3,1,2,0:T(8,128)(2,1)}, bf16[32,8,2,512]{3,1,2,0:T(8,128)(2,1)S(1)}, u32[]{:S(2)}) copy-start(bf16[32,8,2,512]{3,1,2,0:T(8,128)(2,1)S(1)} %copy.60) | copy-start | bytes 1572868
  161.4 59.2 %all-gather.10.cloned.1.call-start = ((), (), s32[]{:S(2)}) async-start(), calls=%async_computation.8 | async-start | bytes 2621440 | tf_op jit(solution)/shard_map/all_gather | solution.py:293
  197.8 74.9 %reduce-scatter.8.cloned.1.call-start = ((), (), s32[]{:S(2)}) async-start(), calls=%async_computation.9 | async-start | bytes 2621440 | tf_op jit(solution)/shard_map/reduce_scatter | solution.py:299
  220.6 16.9 %copy-start.16 = (bf16[8,8,128,128]{3,1,2,0:T(8,128)(2,1)S(1)}, bf16[8,8,128,128]{3,1,2,0:T(8,128)(2,1)}, u32[]{:S(2)}) copy-start(bf16[8,8,128,128]{3,1,2,0:T(8,128)(2,1)} %copy.47) | copy-start | bytes 6291460
  237.5 35.2 %copy-start.6 = (bf16[256,1024]{1,0:T(8,128)(2,1)S(1)}, bf16[256,1024]{1,0:T(8,128)(2,1)}, u32[]{:S(2)}) copy-start(bf16[256,1024]{1,0:T(8,128)(2,1)} %reduce-scatter.6.cloned.1.call-done) | copy-start | bytes 1572868
  241.1 61.0 %all-gather.12.cloned.1.call-start = ((), (), s32[]{:S(2)}) async-start(), calls=%async_computation.10 | async-start | bytes 2621440 | tf_op jit(solution)/shard_map/all_gather | solution.py:313
  272.7 4.2 copy-start.17
  279.3 68.5 %reduce-scatter.10.cloned.1.call-start = ((), (), s32[]{:S(2)}) async-start(), calls=%async_computation.11 | async-start | bytes 2621440 | tf_op jit(solution)/shard_map/reduce_scatter | solution.py:321
  302.1 10.4 %copy-start.15 = (bf16[8,8,128,128]{3,1,2,0:T(8,128)(2,1)S(1)}, bf16[8,8,128,128]{3,1,2,0:T(8,128)(2,1)}, u32[]{:S(2)}) copy-start(bf16[8,8,128,128]{3,1,2,0:T(8,128)(2,1)} %copy.46) | copy-start | bytes 6291460
  316.2 60.6 %all-gather.14.cloned.1.call-start = ((), (), s32[]{:S(2)}) async-start(), calls=%async_computation.12 | async-start | bytes 2621440 | tf_op jit(solution)/shard_map/all_gather | solution.py:332
  354.0 184.3 %reduce-scatter.12.cloned.1.call-start = ((), (), s32[]{:S(2)}) async-start(), calls=%async_computation.13 | async-start | bytes 2621440 | tf_op jit(solution)/shard_map/reduce_scatter | solution.py:379
  355.8 24.1 %copy-start.32 = (s32[192]{0:T(256)}, s32[192]{0:T(256)S(1)}, u32[]{:S(2)}) copy-start(s32[192]{0:T(256)S(1)} %scatter_custom_fusion) | copy-start | bytes 2308
  390.7 4.6 copy-start.3
  390.7 4.7 copy-start.14
  410.3 4.6 copy-start.3
  410.3 4.7 copy-start.14
  415.0 4.1 copy-start.4
  420.5 5.5 copy-start.11
  426.0 184.8 %reduce-scatter.14.cloned.1.call-start = ((), (), s32[]{:S(2)}) async-start(), calls=%async_computation.14 | async-start | bytes 7077888 | tf_op jit(solution)/shard_map/reduce_scatter | solution.py:430
  452.9 4.5 copy-start.10
  474.1 11.0 %copy-start.34 = (pred[192]{0:T(512)(128)(4,1)S(1)}, pred[192]{0:T(512)(128)(4,1)}, u32[]{:S(2)}) copy-start(pred[192]{0:T(512)(128)(4,1)} %compare_and_fusion) | copy-start | bytes 580
  491.2 46.3 %copy-start.21 = (f32[12288]{0:T(1024)S(1)}, f32[12288]{0:T(1024)}, u32[]{:S(2)}) copy-start(f32[12288]{0:T(1024)} %param.31) | copy-start | bytes 147460
  491.2 46.3 %copy-start.22 = (f32[12288]{0:T(1024)S(1)}, f32[12288]{0:T(1024)}, u32[]{:S(2)}) copy-start(f32[12288]{0:T(1024)} %param.33) | copy-start | bytes 147460
  491.2 46.3 %copy-start.23 = (f32[12288]{0:T(1024)S(1)}, f32[12288]{0:T(1024)}, u32[]{:S(2)}) copy-start(f32[12288]{0:T(1024)} %param.32) | copy-start | bytes 147460
  491.3 120.9 %copy-start = (f32[1,24,128,128]{3,2,1,0:T(8,128)S(1)}, f32[1,24,128,128]{3,2,1,0:T(8,128)}, u32[]{:S(2)}) copy-start(f32[1,24,128,128]{3,2,1,0:T(8,128)} %param.25) | copy-start | bytes 4718596
  491.3 120.9 %copy-start.1 = (f32[1,24,128,128]{3,2,1,0:T(8,128)S(1)}, f32[1,24,128,128]{3,2,1,0:T(8,128)}, u32[]{:S(2)}) copy-start(f32[1,24,128,128]{3,2,1,0:T(8,128)} %param.26) | copy-start | bytes 4718596
  (23 other events, 48.7 us)
Sparse Core Ops, SparseCore 0:
  10.8 101.7 all-gather.5
  114.1 20.7 all-gather.7
  161.5 31.4 reduce-scatter.5
  197.9 22.5 all-gather.9
  241.2 31.4 reduce-scatter.7
  279.4 22.5 all-gather.11
  316.3 31.4 reduce-scatter.9
  354.1 22.5 all-gather.13
  426.1 31.3 reduce-scatter.11
  491.4 119.3 reduce-scatter.13

commit v2 on v1

--- a/solution.py
+++ b/solution.py
@@ -30,7 +30,7 @@
     return jnp.matmul(left, right, precision=highest)
 
 
-def mm(a,b,ca=1,cb=0,prec=highest):
+def mm(a, b, ca=1, cb=0, prec=highest):
     return lax.dot_general(a,b,(((ca,),(cb,)),((),())),precision=prec,preferred_element_type=single)
 
 def adam_kernel(rates_ref, g_ref, m_ref, v_ref, w_ref, sl_ref, sr_ref, l_ref, r_ref,
@@ -155,11 +155,6 @@
     return (D * D // (tensors * BLK * BLK), D * FF // (tensors * BLK * BLK))
 
 
-def to_matrix(pieces, row_count, col_count):
-    shaped = pieces.reshape(row_count // BLK, col_count // BLK, BLK, BLK)
-    return shaped.swapaxes(1, 2).reshape(row_count, col_count)
-
-
 def to_blocks(matrix):
     row_count, col_count = matrix.shape
     shaped = matrix.reshape(row_count // BLK, BLK, col_count // BLK, BLK)
@@ -185,11 +180,117 @@
     scaled = grad_in * gain
     mean_grad = jnp.mean(scaled, -1, keepdims=True)
     mean_cross = jnp.mean(scaled * normed, -1, keepdims=True)
-    return (
-        inv_std * (scaled - mean_grad - normed * mean_cross),
-        jnp.sum(grad_in * normed, 0),
-        jnp.sum(grad_in, 0),
-    )
+    return inv_std * (scaled - mean_grad - normed * mean_cross)
+
+
+def swap(value, axis, bit):
+    count = lax.axis_size(axis)
+    return lax.ppermute(value, axis, [(i, i ^ bit) for i in range(count)])
+
+
+def ring(value):
+    count = lax.axis_size("dp")
+    return lax.ppermute(value, "dp", [(i, (i + 2) % count) for i in range(count)])
+
+
+def total_of(value):
+    for axis in ("tensor", "dp"):
+        bit = 1
+        while bit < lax.axis_size(axis):
+            value = value + swap(value, axis, bit)
+            bit *= 2
+    return value
+
+
+def gather_slots(local, parts):
+    size = local.shape[0] // parts
+    hops = lax.axis_size("dp") // 2
+    pieces = [[[None] * parts for _ in range(2)] for _ in range(hops)]
+    for part in range(parts):
+        shard = local[part * size : (part + 1) * size]
+        for hop in range(hops):
+            pieces[hop][0][part] = shard
+            pieces[hop][1][part] = swap(shard, "dp", 1)
+            if hop < hops - 1:
+                shard = ring(shard)
+    return [piece for pair in pieces for flip in pair for piece in flip]
+
+
+def scatter_slots(sent, slots, parts):
+    hops = lax.axis_size("dp") // 2
+    size = slots // parts
+    shaped = sent.reshape(hops, 2, slots, BLK, BLK)
+    done = []
+    for part in range(parts):
+        piece = shaped[:, :, part * size : (part + 1) * size]
+        carried = None
+        for hop in range(hops - 1, -1, -1):
+            mine = piece[hop, 0].astype(single) + swap(piece[hop, 1], "dp", 1).astype(single)
+            if carried is not None:
+                mine = mine + carried.astype(single)
+            if hop > 0:
+                carried = ring(mine.astype(bfloat))
+        done.append(mine)
+    return done
+
+
+def assemble_kernel(source_ref, *refs, sizes, layouts):
+    count = len(sizes)
+    pieces, outs, (held, sems) = refs[:count], refs[count:-2], refs[-2:]
+    copies, start = [], 0
+    for index, size in enumerate(sizes):
+        copies.append(pltpu.make_async_copy(pieces[index], held.at[start : start + size], sems.at[index]))
+        start += size
+    for copy in copies:
+        copy.start()
+    for copy in copies:
+        copy.wait()
+    canon = 0
+    for target, rows, cols, row_at, col_at in layouts:
+        for row in range(rows):
+            for col in range(cols):
+                outs[target][
+                    (row_at + row) * BLK : (row_at + row + 1) * BLK,
+                    (col_at + col) * BLK : (col_at + col + 1) * BLK,
+                ] = held[source_ref[canon]]
+                canon += 1
+
+
+def assemble(source, pieces, shapes, layouts):
+    sizes = [piece.shape[0] for piece in pieces]
+    return pl.pallas_call(
+        functools.partial(assemble_kernel, sizes=sizes, layouts=layouts),
+        grid_spec=pltpu.PrefetchScalarGridSpec(
+            num_scalar_prefetch=1,
+            grid=(1,),
+            in_specs=[pl.BlockSpec(memory_space=pl.ANY)] * len(pieces),
+            out_specs=[pl.BlockSpec(shape, lambda i, *_: (0, 0)) for shape in shapes],
+            scratch_shapes=[
+                pltpu.VMEM((sum(sizes), BLK, BLK), bfloat),
+                pltpu.SemaphoreType.DMA((len(sizes),)),
+            ],
+        ),
+        out_shape=[jax.ShapeDtypeStruct(shape, bfloat) for shape in shapes],
+        compiler_params=pltpu.CompilerParams(vmem_limit_bytes=40 * 2**20),
+        name="assemble",
+    )(source, *pieces)
+
+
+def reduce_pair(part_a, part_b):
+    half = part_a.shape[0] // 2
+    chip = []
+    for part in (part_a, part_b):
+        got = swap(part[half:].astype(bfloat), "tensor", 1)
+        chip.append((part[:half] + got.astype(single)).astype(bfloat))
+    from_b = swap(chip[1], "tensor", 2)
+    from_a = swap(chip[0], "tensor", 2)
+    full_a = chip[0].astype(single) + from_b.astype(single)
+    full_b = chip[1].astype(single) + from_a.astype(single)
+    return full_a, full_b
+
+
+def with_peer(rows):
+    return jnp.concatenate([rows, swap(rows, "tensor", 1)], axis=0)
 
 
 def body(
@@ -211,6 +312,7 @@
     tensors = lax.axis_size("tensor")
     data_ranks = lax.axis_size("dp")
     tensor_rank = lax.axis_index("tensor")
+    data_rank = lax.axis_index("dp")
     local_rows = tokens.shape[0]
     seq_len = local_rows * tensors
     slice_width = D // tensors
@@ -220,17 +322,44 @@
     slots_here = master_blocks.shape[1]
     length = seq_lengths[0]
     score_scale = HEAD_DIM ** (-0.5)
-    gathered = lax.all_gather(master_blocks[0].astype(bfloat), "dp", axis=0, tiled=True)
-    canonical = jnp.take(gathered, block_owner, axis=0)
     attn_count, ffn_count = block_counts(tensors)
-    up_start = 4 * attn_count
-    w_query = to_matrix(canonical[0:attn_count], D, slice_width)
-    w_key = to_matrix(canonical[attn_count : 2 * attn_count], D, slice_width)
-    w_value = to_matrix(canonical[2 * attn_count : 3 * attn_count], D, slice_width)
-    w_out = to_matrix(canonical[3 * attn_count : up_start], slice_width, D)
-    w_up = to_matrix(canonical[up_start : up_start + ffn_count], D, hidden_width)
-    w_down = to_matrix(canonical[up_start + ffn_count : up_start + 2 * ffn_count], hidden_width, D)
-    w_qkv = jnp.concatenate([w_query, w_key, w_value], axis=1)
+    permuted = data_ranks <= 16
+    hops = data_ranks // 2
+    parts = 3 if permuted else 1
+
+    holder, slot = block_owner // slots_here, block_owner % slots_here
+    flip = (holder % 2) ^ (data_rank % 2)
+    down = (data_rank // 2 - holder // 2) % hops
+    up = (holder // 2 - data_rank // 2) % hops
+    source = (down * 2 + flip) * slots_here + slot
+    target = (up * 2 + flip) * slots_here + slot
+    if not permuted:
+        source = target = block_owner
+    canon_ids = jnp.arange(block_total, dtype=jnp.int32)
+    inverse = jnp.zeros((block_total,), jnp.int32).at[block_owner].set(canon_ids)
+    sent_order = jnp.zeros((block_total,), jnp.int32).at[target].set(canon_ids)
+
+    local_weights = master_blocks[0].astype(bfloat)
+    if permuted:
+        pieces = gather_slots(local_weights, parts)
+    else:
+        pieces = [lax.all_gather(local_weights, "dp", axis=0, tiled=True)]
+    cols = slice_width // BLK
+    wide = hidden_width // BLK
+    full = D // BLK
+    w_qkv, w_out, w_up, w_down = assemble(
+        source,
+        pieces,
+        [(D, 3 * slice_width), (slice_width, D), (D, hidden_width), (hidden_width, D)],
+        [
+            (0, full, cols, 0, 0),
+            (0, full, cols, 0, cols),
+            (0, full, cols, 0, 2 * cols),
+            (1, cols, full, 0, 0),
+            (2, full, wide, 0, 0),
+            (3, wide, full, 0, 0),
+        ],
+    )
     gain_one, shift_one = (vector_master[0:D], vector_master[D : 2 * D])
     gain_two, shift_two = (vector_master[2 * D : 3 * D], vector_master[3 * D : 4 * D])
     bias_query = lax.dynamic_slice_in_dim(
@@ -244,9 +373,16 @@
         vector_master, 7 * D + tensor_rank * hidden_width, hidden_width
     )
     bias_down = vector_master[7 * D + FF : 8 * D + FF]
-    positions = tensor_rank * local_rows + jnp.arange(local_rows)
-    row_valid = (positions < length).astype(single)[:, None]
-    full_tokens = lax.all_gather(tokens, "tensor", axis=0, tiled=True)
+
+    tokens_b = swap(tokens, "tensor", 2)
+    cotangent_b = swap(cotangent, "tensor", 2)
+    full_tokens = jnp.concatenate([with_peer(tokens), with_peer(tokens_b)], axis=0)
+    quarters = tensor_rank ^ jnp.arange(4, dtype=jnp.int32)
+    positions = (quarters[:, None] * local_rows + jnp.arange(local_rows)[None, :]).reshape(-1)
+    key_valid = positions < length
+    row_valid = key_valid.astype(single)[:, None]
+    chunk = 2 * local_rows
+
     bias_qkv = jnp.concatenate([bias_query, jnp.zeros((slice_width,), single), bias_value])
     projected = (jnp.dot(full_tokens, w_qkv, preferred_element_type=single) + bias_qkv).astype(
         bfloat
@@ -256,9 +392,6 @@
     heads_v = projected[:, 2 * slice_width : 3 * slice_width].reshape(
         seq_len, local_heads, HEAD_DIM
     )
-    block_rows = min(512, seq_len)
-    block_starts = jnp.arange(seq_len // block_rows, dtype=jnp.int32) * block_rows
-    key_valid = jnp.arange(seq_len) < length
 
     def masked_scores(query_block):
         raw = (
@@ -267,125 +400,124 @@
         )
         return jnp.where(key_valid, raw, masked_score)
 
-    def forward_block(nothing, row_start):
-        query_block = lax.dynamic_slice_in_dim(heads_q, row_start, block_rows, 0)
-        scores = masked_scores(query_block)
+    attended, log_totals, branch_part = [None] * 2, [None] * 2, [None] * 2
+    for part in (1, 0):
+        scores = masked_scores(heads_q[part * chunk : (part + 1) * chunk])
         row_max = jnp.max(scores, -1, keepdims=True)
         shifted = jnp.exp(scores - row_max)
         row_total = jnp.sum(shifted, -1, keepdims=True)
         weights = (shifted / row_total).astype(bfloat)
         mixed = jnp.einsum("hqk,khd->qhd", weights, heads_v, preferred_element_type=single)
-        return (nothing, (mixed.astype(bfloat), (row_max + jnp.log(row_total))[..., 0]))
-
-    unused, (attended, log_totals) = lax.scan(forward_block, None, block_starts)
-    attended_flat = attended.reshape(seq_len, slice_width)
-    rows_here = attended_flat
-    branch = (
-        lax.psum_scatter(
-            jnp.dot(rows_here, w_out, preferred_element_type=single).astype(bfloat),
-            "tensor",
-            scatter_dimension=0,
-            tiled=True,
-        ).astype(single)
-        + bias_out
-    )
-    hidden, normed_one, inv_one = norm_forward(tokens.astype(single) + branch, gain_one, shift_one)
-    full_hidden = lax.all_gather(hidden.astype(bfloat), "tensor", axis=0, tiled=True)
-    up_proj = jnp.dot(full_hidden, w_up, preferred_element_type=single) + bias_up
-    act_float, gelu_pull = jax.vjp(gelu_exact, up_proj)
-    activation = act_float.astype(bfloat)
-    rows_here = activation
-    down_proj = (
-        lax.psum_scatter(
-            jnp.dot(rows_here, w_down, preferred_element_type=single).astype(bfloat),
-            "tensor",
-            scatter_dimension=0,
-            tiled=True,
-        ).astype(single)
-        + bias_down
-    )
-    result, normed_two, inv_two = norm_forward(hidden + down_proj, gain_two, shift_two)
-    layer_output = result.astype(bfloat)
-    grad_out = cotangent.astype(single) * row_valid
-    grad_second, dgain_two, dshift_two = norm_backward(grad_out, normed_two, inv_two, gain_two)
-    grad_down = grad_second.astype(bfloat)
-    dbias_down = jnp.sum(grad_down.astype(single), 0)
-    full_grad_down = lax.all_gather(grad_down, "tensor", axis=0, tiled=True)
-    grad_act = jnp.einsum("sd,fd->sf", full_grad_down, w_down, preferred_element_type=single)
-    grad_up = gelu_pull(grad_act)[0].astype(bfloat)
-    dw_down = jnp.einsum("sf,sd->fd", activation, full_grad_down, preferred_element_type=single)
-    dw_up = jnp.einsum("sd,sf->df", full_hidden, grad_up, preferred_element_type=single)
-    dbias_up = jnp.sum(grad_up.astype(single), 0)
-    rows_here = grad_up
-    grad_hidden = (
-        lax.psum_scatter(
-            jnp.einsum("sf,df->sd", rows_here, w_up, preferred_element_type=single).astype(bfloat),
-            "tensor",
-            scatter_dimension=0,
-            tiled=True,
-        ).astype(single)
-        + grad_second
-    )
-    grad_summed, dgain_one, dshift_one = norm_backward(grad_hidden, normed_one, inv_one, gain_one)
-    grad_branch = grad_summed.astype(bfloat)
-    dbias_out = jnp.sum(grad_branch.astype(single), 0)
-    full_grad_branch = lax.all_gather(grad_branch, "tensor", axis=0, tiled=True)
-    dw_out = jnp.einsum("sa,sd->ad", attended_flat, full_grad_branch, preferred_element_type=single)
-    grad_attended = jnp.einsum(
-        "sd,ad->sa", full_grad_branch, w_out, preferred_element_type=single
-    ).astype(bfloat)
-    grad_heads = grad_attended.reshape(seq_len, local_heads, HEAD_DIM)
-
-    def backward_block(totals, inputs):
-        key_total, value_total = totals
-        row_start, log_total = inputs
-        query_block = lax.dynamic_slice_in_dim(heads_q, row_start, block_rows, 0)
-        grad_block = lax.dynamic_slice_in_dim(grad_heads, row_start, block_rows, 0)
-        probs_full = jnp.exp(masked_scores(query_block) - log_total[..., None])
+        attended[part] = mixed.astype(bfloat).reshape(chunk, slice_width)
+        log_totals[part] = row_max + jnp.log(row_total)
+        branch_part[part] = jnp.dot(attended[part], w_out, preferred_element_type=single)
+    branches = reduce_pair(*branch_part)
+    hidden, normed_one, inv_one, full_hidden = [], [], [], []
+    up_proj, pulls, activation, down_part = [], [], [], []
+    for part, rows in enumerate((tokens, tokens_b)):
+        value, normed, inv = norm_forward(
+            rows.astype(single) + (branches[part] + bias_out), gain_one, shift_one
+        )
+        hidden.append(value)
+        normed_one.append(normed)
+        inv_one.append(inv)
+        full_hidden.append(with_peer(value.astype(bfloat)))
+        up_proj.append(jnp.dot(full_hidden[part], w_up, preferred_element_type=single) + bias_up)
+        act_float, gelu_pull = jax.vjp(gelu_exact, up_proj[part])
+        pulls.append(gelu_pull)
+        activation.append(act_float.astype(bfloat))
+        down_part.append(jnp.dot(activation[part], w_down, preferred_element_type=single))
+    downs = reduce_pair(*down_part)
+    grad_second, full_grad_down = [None] * 2, [None] * 2
+    grad_up, hidden_part = [None] * 2, [None] * 2
+    for part in (1, 0):
+        result, normed_two, inv_two = norm_forward(
+            hidden[part] + (downs[part] + bias_down), gain_two, shift_two
+        )
+        cot = (cotangent, cotangent_b)[part].astype(single)
+        grad_out = cot * row_valid[part * chunk : part * chunk + local_rows]
+        grad_second[part] = norm_backward(grad_out, normed_two, inv_two, gain_two)
+        grad_down = grad_second[part].astype(bfloat)
+        if part == 0:
+            layer_output = result.astype(bfloat)
+            dgain_two = jnp.sum(grad_out * normed_two, 0)
+            dshift_two = jnp.sum(grad_out, 0)
+            dbias_down = jnp.sum(grad_down.astype(single), 0)
+        full_grad_down[part] = with_peer(grad_down)
+        grad_act = jnp.einsum(
+            "sd,fd->sf", full_grad_down[part], w_down, preferred_element_type=single
+        )
+        grad_up[part] = pulls[part](grad_act)[0].astype(bfloat)
+        hidden_part[part] = jnp.einsum(
+            "sf,df->sd", grad_up[part], w_up, preferred_element_type=single
+        )
+    hidden_sums = reduce_pair(*hidden_part)
+    activation = jnp.concatenate(activation, 0)
+    all_grad_down = jnp.concatenate(full_grad_down, 0)
+    all_hidden = jnp.concatenate(full_hidden, 0)
+    all_grad_up = jnp.concatenate(grad_up, 0)
+    dw_down = jnp.einsum("sf,sd->fd", activation, all_grad_down, preferred_element_type=single)
+    dw_up = jnp.einsum("sd,sf->df", all_hidden, all_grad_up, preferred_element_type=single)
+    dbias_up = jnp.sum(all_grad_up.astype(single), 0)
+    full_grad_branch, grad_query = [], []
+    key_total = value_total = 0.0
+    for part in (0, 1):
+        grad_hidden = hidden_sums[part] + grad_second[part]
+        grad_rows = norm_backward(grad_hidden, normed_one[part], inv_one[part], gain_one)
+        grad_branch = grad_rows.astype(bfloat)
+        if part == 0:
+            grad_summed = grad_rows
+            dgain_one = jnp.sum(grad_hidden * normed_one[0], 0)
+            dshift_one = jnp.sum(grad_hidden, 0)
+            dbias_out = jnp.sum(grad_branch.astype(single), 0)
+        full_grad_branch.append(with_peer(grad_branch))
+        grad_attended = jnp.einsum(
+            "sd,ad->sa", full_grad_branch[part], w_out, preferred_element_type=single
+        ).astype(bfloat)
+        grad_block = grad_attended.reshape(chunk, local_heads, HEAD_DIM)
+        query_block = heads_q[part * chunk : (part + 1) * chunk]
+        probs_full = jnp.exp(masked_scores(query_block) - log_totals[part])
         value_total = value_total + jnp.einsum(
             "hqk,qhd->khd", probs_full.astype(bfloat), grad_block, preferred_element_type=single
         )
         grad_probs = jnp.einsum("qhd,khd->hqk", grad_block, heads_v, preferred_element_type=single)
         row_cross = jnp.sum(grad_probs * probs_full, -1, keepdims=True)
         grad_scores = (probs_full * (grad_probs - row_cross)).astype(bfloat)
-        grad_query = (
-            jnp.einsum("hqk,khd->qhd", grad_scores, heads_k, preferred_element_type=single)
-            * score_scale
+        grad_query.append(
+            (
+                jnp.einsum("hqk,khd->qhd", grad_scores, heads_k, preferred_element_type=single)
+                * score_scale
+            ).astype(bfloat)
         )
         key_total = (
             key_total
             + jnp.einsum("hqk,qhd->khd", grad_scores, query_block, preferred_element_type=single)
             * score_scale
         )
-        return ((key_total, value_total), grad_query.astype(bfloat))
-
-    zero_heads = jnp.zeros((seq_len, local_heads, HEAD_DIM), single)
-    (key_total, value_total), grad_query = lax.scan(
-        backward_block, (zero_heads, zero_heads), (block_starts, log_totals)
-    )
     grad_qkv = jnp.concatenate(
         [
-            grad_query.reshape(seq_len, slice_width),
+            jnp.concatenate(grad_query, 0).reshape(seq_len, slice_width),
             key_total.reshape(seq_len, slice_width).astype(bfloat),
             value_total.reshape(seq_len, slice_width).astype(bfloat),
         ],
         axis=1,
     )
+    all_attended = jnp.concatenate(attended, 0)
+    all_grad_branch = jnp.concatenate(full_grad_branch, 0)
+    dw_out = jnp.einsum(
+        "sa,sd->ad", all_attended, all_grad_branch, preferred_element_type=single
+    )
     dw_qkv = jnp.einsum("sd,sc->dc", full_tokens, grad_qkv, preferred_element_type=single)
     dbias_query = jnp.sum(grad_qkv[:, 0:slice_width].astype(single), 0)
     dbias_value = jnp.sum(grad_qkv[:, 2 * slice_width : 3 * slice_width].astype(single), 0)
-    rows_here = grad_qkv
-    token_grad = (
-        lax.psum_scatter(
-            jnp.einsum("sc,dc->sd", rows_here, w_qkv, preferred_element_type=single).astype(
-                jnp.bfloat16
-            ),
-            "tensor",
-            scatter_dimension=0,
-            tiled=True,
-        ).astype(jnp.float32)
-        + grad_summed
-    ).astype(bfloat)
+    token_part = jnp.einsum("sc,dc->sd", grad_qkv, w_qkv, preferred_element_type=single)
+    chip_rows = []
+    for part in (1, 0):
+        rows = token_part[part * chunk : (part + 1) * chunk]
+        got = swap(rows[local_rows:].astype(bfloat), "tensor", 1)
+        chip_rows.append(rows[:local_rows] + got.astype(single))
+    across = swap(chip_rows[0].astype(bfloat), "tensor", 2)
+    token_grad = (chip_rows[1] + across.astype(single) + grad_summed).astype(bfloat)
     grad_blocks = jnp.concatenate(
         [
             to_blocks(dw_qkv[:, 0:slice_width]),
@@ -419,22 +551,32 @@
         vector_grad, dbias_up, 7 * D + tensor_rank * hidden_width, 0
     )
     grad_scale = 1.0 / math.sqrt(seq_len * data_ranks)
-    inverse = (
-        jnp.zeros((block_total,), jnp.int32)
-        .at[block_owner]
-        .set(jnp.arange(block_total, dtype=jnp.int32))
-    )
-    own_canon = lax.dynamic_slice_in_dim(inverse, lax.axis_index("dp") * slots_here, slots_here)
-    vector_sum = lax.psum(vector_grad, ("dp", "tensor")) * grad_scale
-    sent = jnp.take((grad_blocks * grad_scale).astype(bfloat), inverse, axis=0)
-    own_grad = lax.psum_scatter(sent, "dp", scatter_dimension=0, tiled=True).astype(single)
+    own_canon = lax.dynamic_slice_in_dim(inverse, data_rank * slots_here, slots_here)
+    vector_sum = total_of(vector_grad) * grad_scale
+    sent = (grad_blocks * grad_scale).astype(bfloat)
+    sent = sent.at[sent_order].get(mode="promise_in_bounds")
+    if permuted:
+        done = scatter_slots(sent, slots_here, 2)
+    else:
+        done = [lax.psum_scatter(sent, "dp", scatter_dimension=0, tiled=True).astype(single)]
     rates = rate_values(own_canon, tensors, seq_len)
     correction = 1.0 - moment_decay**STEP
-    fresh_first, fresh_second, fresh_master, fresh_left, fresh_right, gram, product = adam(
-        own_grad, first_moment[0], second_moment[0], master_blocks[0], left_stats[0], right_stats[0],
-        left_basis[0], right_basis[0], rates, per=2 if slots_here % 2 == 0 else 1)
-    bases = chol(gram, product)
-    basis_left, basis_right = bases[:slots_here], bases[slots_here:]
+    states = [
+        first_moment[0], second_moment[0], master_blocks[0], left_stats[0], right_stats[0],
+        left_basis[0], right_basis[0],
+    ]
+    fresh, start = [], 0
+    for own_grad in done:
+        size = own_grad.shape[0]
+        here = slice(start, start + size)
+        start += size
+        *updated, gram, product = adam(
+            own_grad, *[state[here] for state in states], rates[here], per=2 if size % 2 == 0 else 1
+        )
+        bases = chol(gram, product)
+        fresh.append(updated + [bases[:size], bases[size:]])
+    fresh = [jnp.concatenate(column, 0) for column in zip(*fresh)]
+    fresh_first, fresh_second, fresh_master, fresh_left, fresh_right, basis_left, basis_right = fresh
     vec_first = moment_decay * vector_first + (1.0 - moment_decay) * vector_sum
     vec_second = moment_decay * vector_second + (1.0 - moment_decay) * vector_sum * vector_sum
     vec_master = vector_master - vector_rate * (vec_first / correction) / (

time: 746 us -> 545 us (0.73)
  waiting for transfers between devices: 323 us -> 143 us
  starting transfers between devices: 0.97 us -> 58.9 us
  blocking collectives: 43.2 us -> 0 us
  matrix products: 86.2 us -> 71.5 us
  between operations: 16 us -> 3.18 us
    reduce_scatter x5 -> x0, waiting for transfers between devices: 164 us -> none  [the longest x1 70.3 us: body(): lax.psum_scatter(sent, 'dp', scatter_dimension=0, tiled=True).astype(single)]
    all_gather x5 -> x0, waiting for transfers between devices: 158 us -> none  [the longest x1 99.8 us: body(): lax.all_gather(master_blocks[0].astype(bfloat), 'dp', axis=0, tiled=True)]
    ppermute x0 -> x65, waiting for transfers between devices: none -> 143 us  [the longest x50 98.6 us: swap(): return lax.ppermute(value, axis, [(i, i ^ bit) for i in range(count)])]
    ppermute x0 -> x65, starting transfers between devices: none -> 58.9 us  [the longest x50 45.3 us: swap(): return lax.ppermute(value, axis, [(i, i ^ bit) for i in range(count)])]
    psum x1 -> x0, blocking collectives: 43.2 us -> none  [body(): vector_sum = lax.psum(vector_grad, ('dp', 'tensor')) * grad_scale]
    unnamed x92 -> x178, local copies, waits for them, and re-layouts: 18.8 us -> 32.4 us
    select_n x4 -> x2, other arithmetic: 12.8 us -> 0.57 us  [the longest x1 0.57 us: body(): sent_order = jnp.zeros((block_total,), jnp.int32).at[target].set(canon_ids)]
    dot_general x20 -> x26, matrix products: 75.1 us -> 64.2 us  [the longest x2 14.9 us: body(): jnp.einsum('qhd,khd->hqk', grad_block, heads_v, preferred_element_type=si...]
  transfers between devices with their start and end apart: 10 -> 65, of which waited for: 9 -> 30; matrix products, arithmetic and copies ran while one was open for 14% -> 15% of each run, Pallas kernels for 0% -> 11%
where the time goes in v2:
time: 545 us; the launch traced here: 540 us
  waiting for transfers between devices  143 us (26%)
  Pallas kernels  122 us (22%)
  local copies, waits for them, and re-layouts  78.1 us (14%)
  matrix products  71.5 us (13%)
  other arithmetic  64 us (12%)
  starting transfers between devices  58.9 us (11%)
    ppermute x50, waiting for transfers between devices, swap(): return lax.ppermute(value, axis, [(i, i ^ bit) for i in range(count)])  98.6 us
    pallas_call x2, Pallas kernels, chol(): pl.pallas_call(functools.partial(chol_kernel, n=n, unroll=unroll), in_spe...  70.1 us
    pallas_call x2, Pallas kernels, adam(): pl.pallas_call(functools.partial(adam_kernel, per=per), grid_spec=pltpu.P...  47.5 us
    ppermute x50, starting transfers between devices, swap(): return lax.ppermute(value, axis, [(i, i ^ bit) for i in range(count)])  45.3 us
    ppermute x15, waiting for transfers between devices, ring(): lax.ppermute(value, 'dp', [(i, (i + 2) % count) for i in range(count)])  44.7 us
    unnamed x178, local copies, waits for them, and re-layouts  32.4 us
    dot_general x2, matrix products, body(): jnp.einsum('qhd,khd->hqk', grad_block, heads_v, preferred_element_type=si...  14.9 us
    reshape x9, local copies, waits for them, and re-layouts, to_blocks(): shaped = matrix.reshape(row_count // BLK, BLK, col_count // BLK, BLK)  14.6 us
  transfers between devices with their start and end apart: 65, of which 30 were waited for; matrix products, arithmetic and copies ran while one was open for 15% of the time, Pallas kernels for 11%

profile of v2, /device:TPU:0, one launch (start us, length us, event | category | flops | bytes accessed | tf_op | source)
XLA Modules:
  0.0 540.5 jit_solution(685370386425442876)
XLA Ops:
  8.9 3.6 collective-permute-done.3.refs_3_
  14.6 3.5 collective-permute-done.4.refs_4_
  39.6 3.7 collective-permute-done.12.refs_12_
  45.7 3.2 collective-permute-done.13.refs_13_
  48.9 5.7 %collective-permute-done.14.refs_14_ = bf16[8,128,128]{2,1,0:T(8,128)(2,1)} collective-permute-done((bf16[8,128,128]{2,1,0:T(8,128)(2,1)S(1)}, bf16[8,128,128]{2,1,0:T(8,128)(2,1)}, u32[]{:S(2)}, u32[]{:S(2)}) %collective-permute-start.14) | collective-permute-done | bytes 262176 | tf_op jit(solution)/shard_map/ppermute | solution.py:193
  56.9 3.3 collective-permute-done.18.refs_18_
  61.9 4.0 collective-permute-done.19.refs_19_
  76.6 3.9 collective-permute-done.22.refs_22_
  85.1 4.0 assemble.1
  95.4 3.8 fusion.1
  110.1 12.3 %collective-permute-done.26 = bf16[256,1024]{1,0:T(8,128)(2,1)S(1)} collective-permute-done((bf16[256,1024]{1,0:T(8,128)(2,1)S(1)}, bf16[256,1024]{1,0:T(8,128)(2,1)S(1)}, u32[]{:S(2)}, u32[]{:S(2)}) %collective-permute-start.26) | collective-permute-done | bytes 524320 | tf_op jit(solution)/shard_map/ppermute | solution.py:188
  127.2 11.2 %collective-permute-done.29 = bf16[256,1024]{1,0:T(8,128)(2,1)S(1)} collective-permute-done((bf16[256,1024]{1,0:T(8,128)(2,1)S(1)}, bf16[256,1024]{1,0:T(8,128)(2,1)S(1)}, u32[]{:S(2)}, u32[]{:S(2)}) %collective-permute-start.29) | collective-permute-done | bytes 524320 | tf_op jit(solution)/shard_map/ppermute | solution.py:188
  147.2 10.8 %multiply_convert_fusion.3 = (bf16[512,1024]{1,0:T(8,128)(2,1)S(1)}, f32[512,1024]{1,0:T(8,128)S(1)}, bf16[512,1024]{1,0:T(8,128)(2,1)S(1)}, f32[512,1024]{1,0:T(8,128)S(1)}, f32[512,1024]{1,0:T(8,128)S(1)}) fusion(f32[1024]{0:T(1024)S(1)} %get-tuple-element.136, f32[512,1024]{1,0:T(8,128)S(1)} %fusion.78, bf16[1024,1024]{1,0:T(8,128)(2,1)S(1)} %copy-done.11, ...), kind=kOutput, calls=%fused_computation.64 | convolution fusion | flops 1145044992 | bytes 13635584 | tf_op jit(solution)/shard_map/dot_general | solution.py:425
  164.1 11.5 %collective-permute-done.35 = bf16[256,1024]{1,0:T(8,128)(2,1)S(1)} collective-permute-done((bf16[256,1024]{1,0:T(8,128)(2,1)S(1)}, bf16[256,1024]{1,0:T(8,128)(2,1)S(1)}, u32[]{:S(2)}, u32[]{:S(2)}) %collective-permute-start.35) | collective-permute-done | bytes 524320 | tf_op jit(solution)/shard_map/ppermute | solution.py:188
  176.9 12.4 %collective-permute-done.32 = bf16[256,1024]{1,0:T(8,128)(2,1)S(1)} collective-permute-done((bf16[256,1024]{1,0:T(8,128)(2,1)S(1)}, bf16[256,1024]{1,0:T(8,128)(2,1)S(1)}, u32[]{:S(2)}, u32[]{:S(2)}) %collective-permute-start.32) | collective-permute-done | bytes 524320 | tf_op jit(solution)/shard_map/ppermute | solution.py:188
  204.9 3.6 convolution_bitcast_fusion.1
  222.7 12.0 %collective-permute-done.39 = bf16[256,1024]{1,0:T(8,128)(2,1)S(1)} collective-permute-done((bf16[256,1024]{1,0:T(8,128)(2,1)S(1)}, bf16[256,1024]{1,0:T(8,128)(2,1)S(1)}, u32[]{:S(2)}, u32[]{:S(2)}) %collective-permute-start.39) | collective-permute-done | bytes 524320 | tf_op jit(solution)/shard_map/ppermute | solution.py:188
  242.8 4.6 fusion.188
  247.5 10.3 %multiply_reduce_fusion = (f32[4,512]{1,0:T(4,128)S(1)}, f32[4,512]{1,0:T(4,128)S(1)}, f32[4,512,1024]{2,1,0:T(8,128)}) fusion(f32[4,512]{1,0:T(4,128)S(1)} %get-tuple-element.164, f32[4,512,1024]{2,1,0:T(8,128)} %copy-done.17, pred[1024]{0:T(1024)(128)(4,1)S(1)} %lt.74, f32[4,512,1024]{2,1,0:T(8,128)} %fusion.188, f32[4,512]{1,0:T(4,128)S(1)} %get-tuple-element.165, ...), kind=kOutput, calls=%fused_computation.5 | convolution fusion | flops 289402880 | bytes 34374656 | tf_op jit(solution)/shard_map/qhd,khd->hqk/dot_general | solution.py:483
  257.8 10.0 %multiply_convert_fusion.1 = (bf16[4,512,1024]{2,1,0:T(8,128)(2,1)S(1)}, bf16[4,512,1024]{2,1,0:T(8,128)(2,1)S(1)}) fusion(f32[4,512,1024]{2,1,0:T(8,128)} %get-tuple-element.159, f32[4,512]{1,0:T(4,128)S(1)} %get-tuple-element.62, f32[4,512]{1,0:T(4,128)S(1)} %get-tuple-element.164, f32[4,512,1024]{2,1,0:T(8,128)} %copy-done.17, pred[1024]{0:T(1024)(128)(4,1)S(1)} %lt.74, ...), kind=kLoop, calls=%fused_computation.4 | loop fusion | flops 25165824 | bytes 41976832 | tf_op jit(solution)/shard_map/convert_element_type | solution.py:485
  301.7 9.0 %multiply_convert_fusion = bf16[192,128,128]{2,1,0:T(8,128)(2,1)} fusion(f32[192,128,128]{2,1,0:T(8,128)} %constant_dynamic-update-slice_fusion.4), kind=kLoop, calls=%fused_computation.3 | loop fusion | flops 6291456 | bytes 18874368 | tf_op jit(solution)/shard_map/convert_element_type | solution.py:556
  310.7 10.9 %gather_fusion = bf16[192,128,128]{2,1,0:T(8,128)(2,1)} fusion(bf16[192,128,128]{2,1,0:T(8,128)(2,1)} %multiply_convert_fusion, s32[1024]{0:T(1024)S(1)} %pad_clamp_fusion), kind=kCustom, calls=%fused_computation | custom fusion | bytes 12583680 | tf_op jit(solution)/shard_map/gather | solution.py:557
  321.7 3.7 slice_bitcast_fusion.28
  333.0 4.6 collective-permute-done.49
  340.5 5.4 %collective-permute-done.48 = bf16[12,128,128]{2,1,0:T(8,128)(2,1)S(1)} collective-permute-done((bf16[12,128,128]{2,1,0:T(8,128)(2,1)S(1)}, bf16[12,128,128]{2,1,0:T(8,128)(2,1)S(1)}, u32[]{:S(2)}, u32[]{:S(2)}) %collective-permute-start.48) | collective-permute-done | bytes 393248 | tf_op jit(solution)/shard_map/ppermute | solution.py:188
  346.0 5.0 collective-permute-done.50
  356.1 8.2 %collective-permute-done.51 = bf16[12,128,128]{2,1,0:T(8,128)(2,1)} collective-permute-done((bf16[12,128,128]{2,1,0:T(8,128)(2,1)}, bf16[12,128,128]{2,1,0:T(8,128)(2,1)}, u32[]{:S(2)}, u32[]{:S(2)}) %collective-permute-start.51) | collective-permute-done | bytes 393248 | tf_op jit(solution)/shard_map/ppermute | solution.py:193
  397.9 6.0 %collective-permute-done.58 = bf16[12,128,128]{2,1,0:T(8,128)(2,1)S(1)} collective-permute-done((bf16[12,128,128]{2,1,0:T(8,128)(2,1)S(1)}, bf16[12,128,128]{2,1,0:T(8,128)(2,1)S(1)}, u32[]{:S(2)}, u32[]{:S(2)}) %collective-permute-start.58) | collective-permute-done | bytes 393248 | tf_op jit(solution)/shard_map/ppermute | solution.py:193
  406.7 23.8 %adam.2 = (f32[12,128,128]{2,1,0:T(8,128)S(1)}, f32[12,128,128]{2,1,0:T(8,128)S(1)}, f32[12,128,128]{2,1,0:T(8,128)S(1)}, f32[12,128,128]{2,1,0:T(8,128)S(1)}, f...) custom-call(f32[12]{0:T(128)S(1)} %get-tuple-element.155.rates_ref, ...), custom_call_target="tpu_custom_call" | custom-call | tf_op jit(solution)/shard_map/adam/pallas_call | solution.py:64
  433.4 34.9 %chol.2 = f32[24,128,128]{2,1,0:T(8,128)S(1)} custom-call(f32[3072,128]{1,0:T(8,128)S(1)} %bitcast.206, f32[3072,128]{1,0:T(8,128)S(1)} %bitcast.207), custom_call_target="tpu_custom_call" | custom-call | tf_op jit(solution)/shard_map/chol/pallas_call | solution.py:141
  469.6 23.6 %adam.3 = (f32[12,128,128]{2,1,0:T(8,128)S(1)}, f32[12,128,128]{2,1,0:T(8,128)S(1)}, f32[12,128,128]{2,1,0:T(8,128)S(1)}, f32[12,128,128]{2,1,0:T(8,128)S(1)}, f...) custom-call(f32[12]{0:T(128)S(1)} %get-tuple-element.156.rates_ref, ...), custom_call_target="tpu_custom_call" | custom-call | tf_op jit(solution)/shard_map/adam/pallas_call | solution.py:64
  496.1 35.2 %chol.3 = f32[24,128,128]{2,1,0:T(8,128)S(1)} custom-call(f32[3072,128]{1,0:T(8,128)S(1)} %bitcast.208, f32[3072,128]{1,0:T(8,128)S(1)} %bitcast.209), custom_call_target="tpu_custom_call" | custom-call | tf_op jit(solution)/shard_map/chol/pallas_call | solution.py:141
  (428 shorter events, 229.6 us)
Async XLA Ops:
  5.4 17.5 %collective-permute-start.5 = (bf16[8,128,128]{2,1,0:T(8,128)(2,1)S(1)}, bf16[8,128,128]{2,1,0:T(8,128)(2,1)S(1)}, u32[]{:S(2)}, u32[]{:S(2)}) collective-permute-start(bf16[8,128,128]{2,1,0:T(8,128)(2,1)S(1)} %get-tuple-element.131.refs_2_), channel_id=1, source_target_pairs={{0,4},{4,0},{8,12},{12,8},{16,20},{20,16},{24,28},{28,24},{1,5},{5... | collective-permute-start | bytes 786440 | tf_op jit(solution)/shard_map/ppermute | solution.py:188
  7.3 24.9 %collective-permute-start = (bf16[256,1024]{1,0:T(8,128)(2,1)}, bf16[256,1024]{1,0:T(8,128)(2,1)}, u32[]{:S(2)}, u32[]{:S(2)}) collective-permute-start(bf16[256,1024]{1,0:T(8,128)(2,1)} %param.14), channel_id=1, source_target_pairs={{0,1},{1,0},{2,3},{3,2},{4,5},{5,4},{6,7},{7,6},{8,9},{9,8},{10,11... | collective-permute-start | bytes 1572872 | tf_op jit(solution)/shard_map/ppermute | solution.py:188
  7.3 26.4 %collective-permute-start.1 = (bf16[256,1024]{1,0:T(8,128)(2,1)}, bf16[256,1024]{1,0:T(8,128)(2,1)}, u32[]{:S(2)}, u32[]{:S(2)}) collective-permute-start(bf16[256,1024]{1,0:T(8,128)(2,1)} %param.14), channel_id=1, source_target_pairs={{0,2},{1,3},{2,0},{3,1},{4,6},{5,7},{6,4},{7,5},{8,10},{9,11},{10,... | collective-permute-start | bytes 1572872 | tf_op jit(solution)/shard_map/ppermute | solution.py:188
  26.6 12.9 %collective-permute-start.10 = (bf16[8,128,128]{2,1,0:T(8,128)(2,1)S(1)}, bf16[8,128,128]{2,1,0:T(8,128)(2,1)S(1)}, u32[]{:S(2)}, u32[]{:S(2)}) collective-permute-start(bf16[8,128,128]{2,1,0:T(8,128)(2,1)S(1)} %collective-permute-done.7.refs_7_), channel_id=1, source_target_pairs={{0,4},{4,0},{8,12},{12,8},{16,20},{20,16},{24,28},{28,24},{1,5},{5... | collective-permute-start | bytes 786440 | tf_op jit(solution)/shard_map/ppermute | solution.py:188
  32.2 16.7 %collective-permute-start.13 = (bf16[8,128,128]{2,1,0:T(8,128)(2,1)S(1)}, bf16[8,128,128]{2,1,0:T(8,128)(2,1)S(1)}, u32[]{:S(2)}, u32[]{:S(2)}) collective-permute-start(bf16[8,128,128]{2,1,0:T(8,128)(2,1)S(1)} %collective-permute-done.7.refs_7_), channel_id=1, source_target_pairs={{0,8},{4,12},{8,16},{12,20},{16,24},{20,28},{24,0},{28,4},{1,9},{5... | collective-permute-start | bytes 786440 | tf_op jit(solution)/shard_map/ppermute | solution.py:193
  35.3 19.4 %collective-permute-start.14 = (bf16[8,128,128]{2,1,0:T(8,128)(2,1)S(1)}, bf16[8,128,128]{2,1,0:T(8,128)(2,1)}, u32[]{:S(2)}, u32[]{:S(2)}) collective-permute-start(bf16[8,128,128]{2,1,0:T(8,128)(2,1)S(1)} %collective-permute-done.8.refs_8_), channel_id=1, source_target_pairs={{0,8},{4,12},{8,16},{12,20},{16,24},{20,28},{24,0},{28,4},{1,9},{5... | collective-permute-start | bytes 786440 | tf_op jit(solution)/shard_map/ppermute | solution.py:193
  39.5 31.0 %collective-permute-start.2 = (bf16[256,1024]{1,0:T(8,128)(2,1)}, bf16[256,1024]{1,0:T(8,128)(2,1)}, u32[]{:S(2)}, u32[]{:S(2)}) collective-permute-start(bf16[256,1024]{1,0:T(8,128)(2,1)} %collective-permute-done.1), channel_id=1, source_target_pairs={{0,1},{1,0},{2,3},{3,2},{4,5},{5,4},{6,7},{7,6},{8,9},{9,8},{10,11... | collective-permute-start | bytes 1572872 | tf_op jit(solution)/shard_map/ppermute | solution.py:188
  45.7 14.6 %collective-permute-start.18 = (bf16[8,128,128]{2,1,0:T(8,128)(2,1)S(1)}, bf16[8,128,128]{2,1,0:T(8,128)(2,1)}, u32[]{:S(2)}, u32[]{:S(2)}) collective-permute-start(bf16[8,128,128]{2,1,0:T(8,128)(2,1)S(1)} %collective-permute-done.12.refs_12_), channel_id=1, source_target_pairs={{0,8},{4,12},{8,16},{12,20},{16,24},{20,28},{24,0},{28,4},{1,9},{5... | collective-permute-start | bytes 786440 | tf_op jit(solution)/shard_map/ppermute | solution.py:193
  48.9 17.0 %collective-permute-start.19 = (bf16[8,128,128]{2,1,0:T(8,128)(2,1)S(1)}, bf16[8,128,128]{2,1,0:T(8,128)(2,1)}, u32[]{:S(2)}, u32[]{:S(2)}) collective-permute-start(bf16[8,128,128]{2,1,0:T(8,128)(2,1)S(1)} %collective-permute-done.13.refs_13_), channel_id=1, source_target_pairs={{0,8},{4,12},{8,16},{12,20},{16,24},{20,28},{24,0},{28,4},{1,9},{5... | collective-permute-start | bytes 786440 | tf_op jit(solution)/shard_map/ppermute | solution.py:193
  54.6 14.3 %collective-permute-start.20 = (bf16[8,128,128]{2,1,0:T(8,128)(2,1)}, bf16[8,128,128]{2,1,0:T(8,128)(2,1)}, u32[]{:S(2)}, u32[]{:S(2)}) collective-permute-start(bf16[8,128,128]{2,1,0:T(8,128)(2,1)} %collective-permute-done.14.refs_14_), channel_id=1, source_target_pairs={{0,8},{4,12},{8,16},{12,20},{16,24},{20,28},{24,0},{28,4},{1,9},{5... | collective-permute-start | bytes 786440 | tf_op jit(solution)/shard_map/ppermute | solution.py:193
  55.3 21.3 %collective-permute-start.16 = (bf16[8,128,128]{2,1,0:T(8,128)(2,1)S(1)}, bf16[8,128,128]{2,1,0:T(8,128)(2,1)S(1)}, u32[]{:S(2)}, u32[]{:S(2)}) collective-permute-start(bf16[8,128,128]{2,1,0:T(8,128)(2,1)S(1)} %collective-permute-done.13.refs_13_), channel_id=1, source_target_pairs={{0,4},{4,0},{8,12},{12,8},{16,20},{20,16},{24,28},{28,24},{1,5},{5... | collective-permute-start | bytes 786440 | tf_op jit(solution)/shard_map/ppermute | solution.py:188
  60.2 16.3 %collective-permute-start.17 = (bf16[8,128,128]{2,1,0:T(8,128)(2,1)}, bf16[8,128,128]{2,1,0:T(8,128)(2,1)S(1)}, u32[]{:S(2)}, u32[]{:S(2)}) collective-permute-start(bf16[8,128,128]{2,1,0:T(8,128)(2,1)} %collective-permute-done.14.refs_14_), channel_id=1, source_target_pairs={{0,4},{4,0},{8,12},{12,8},{16,20},{20,16},{24,28},{28,24},{1,5},{5... | collective-permute-start | bytes 786440 | tf_op jit(solution)/shard_map/ppermute | solution.py:188
  108.4 13.9 %collective-permute-start.26 = (bf16[256,1024]{1,0:T(8,128)(2,1)S(1)}, bf16[256,1024]{1,0:T(8,128)(2,1)S(1)}, u32[]{:S(2)}, u32[]{:S(2)}) collective-permute-start(bf16[256,1024]{1,0:T(8,128)(2,1)S(1)} %fusion.76), channel_id=1, source_target_pairs={{0,2},{1,3},{2,0},{3,1},{4,6},{5,7},{6,4},{7,5},{8,10},{9,11},{10,... | collective-permute-start | bytes 1572872 | tf_op jit(solution)/shard_map/ppermute | solution.py:188
  125.2 13.1 %collective-permute-start.29 = (bf16[256,1024]{1,0:T(8,128)(2,1)S(1)}, bf16[256,1024]{1,0:T(8,128)(2,1)S(1)}, u32[]{:S(2)}, u32[]{:S(2)}) collective-permute-start(bf16[256,1024]{1,0:T(8,128)(2,1)S(1)} %get-tuple-element.88), channel_id=1, source_target_pairs={{0,2},{1,3},{2,0},{3,1},{4,6},{5,7},{6,4},{7,5},{8,10},{9,11},{10,... | collective-permute-start | bytes 1572872 | tf_op jit(solution)/shard_map/ppermute | solution.py:188
  141.2 48.8 %collective-permute-start.36 = (bf16[256,1024]{1,0:T(8,128)(2,1)}, bf16[256,1024]{1,0:T(8,128)(2,1)}, u32[]{:S(2)}, u32[]{:S(2)}) collective-permute-start(bf16[256,1024]{1,0:T(8,128)(2,1)} %param.15), channel_id=1, source_target_pairs={{0,2},{1,3},{2,0},{3,1},{4,6},{5,7},{6,4},{7,5},{8,10},{9,11},{10,... | collective-permute-start | bytes 1572872 | tf_op jit(solution)/shard_map/ppermute | solution.py:188
  161.6 14.0 %collective-permute-start.35 = (bf16[256,1024]{1,0:T(8,128)(2,1)S(1)}, bf16[256,1024]{1,0:T(8,128)(2,1)S(1)}, u32[]{:S(2)}, u32[]{:S(2)}) collective-permute-start(bf16[256,1024]{1,0:T(8,128)(2,1)S(1)} %fusion.75), channel_id=1, source_target_pairs={{0,2},{1,3},{2,0},{3,1},{4,6},{5,7},{6,4},{7,5},{8,10},{9,11},{10,... | collective-permute-start | bytes 1572872 | tf_op jit(solution)/shard_map/ppermute | solution.py:188
  176.1 13.1 %collective-permute-start.32 = (bf16[256,1024]{1,0:T(8,128)(2,1)S(1)}, bf16[256,1024]{1,0:T(8,128)(2,1)S(1)}, u32[]{:S(2)}, u32[]{:S(2)}) collective-permute-start(bf16[256,1024]{1,0:T(8,128)(2,1)S(1)} %get-tuple-element.81), channel_id=1, source_target_pairs={{0,2},{1,3},{2,0},{3,1},{4,6},{5,7},{6,4},{7,5},{8,10},{9,11},{10,... | collective-permute-start | bytes 1572872 | tf_op jit(solution)/shard_map/ppermute | solution.py:188
  203.5 15.0 %collective-permute-start.38 = (bf16[256,1024]{1,0:T(8,128)(2,1)S(1)}, bf16[256,1024]{1,0:T(8,128)(2,1)S(1)}, u32[]{:S(2)}, u32[]{:S(2)}) collective-permute-start(bf16[256,1024]{1,0:T(8,128)(2,1)S(1)} %slice.526), channel_id=1, source_target_pairs={{0,1},{1,0},{2,3},{3,2},{4,5},{5,4},{6,7},{7,6},{8,9},{9,8},{10,11... | collective-permute-start | bytes 1572872 | tf_op jit(solution)/shard_map/ppermute | solution.py:188
  204.4 14.1 %collective-permute-start.41 = (bf16[256,1024]{1,0:T(8,128)(2,1)S(1)}, bf16[256,1024]{1,0:T(8,128)(2,1)S(1)}, u32[]{:S(2)}, u32[]{:S(2)}) collective-permute-start(bf16[256,1024]{1,0:T(8,128)(2,1)S(1)} %fusion.73), channel_id=1, source_target_pairs={{0,2},{1,3},{2,0},{3,1},{4,6},{5,7},{6,4},{7,5},{8,10},{9,11},{10,... | collective-permute-start | bytes 1572872 | tf_op jit(solution)/shard_map/ppermute | solution.py:188
  220.7 14.1 %collective-permute-start.39 = (bf16[256,1024]{1,0:T(8,128)(2,1)S(1)}, bf16[256,1024]{1,0:T(8,128)(2,1)S(1)}, u32[]{:S(2)}, u32[]{:S(2)}) collective-permute-start(bf16[256,1024]{1,0:T(8,128)(2,1)S(1)} %get-tuple-element.77), channel_id=1, source_target_pairs={{0,2},{1,3},{2,0},{3,1},{4,6},{5,7},{6,4},{7,5},{8,10},{9,11},{10,... | collective-permute-start | bytes 1572872 | tf_op jit(solution)/shard_map/ppermute | solution.py:188
  222.7 16.7 %collective-permute-start.42 = (bf16[256,1024]{1,0:T(8,128)(2,1)S(1)}, bf16[256,1024]{1,0:T(8,128)(2,1)S(1)}, u32[]{:S(2)}, u32[]{:S(2)}) collective-permute-start(bf16[256,1024]{1,0:T(8,128)(2,1)S(1)} %multiply_convert_fusion.5), channel_id=1, source_target_pairs={{0,1},{1,0},{2,3},{3,2},{4,5},{5,4},{6,7},{7,6},{8,9},{9,8},{10,11... | collective-permute-start | bytes 1572872 | tf_op jit(solution)/shard_map/ppermute | solution.py:188
  332.4 13.5 %collective-permute-start.48 = (bf16[12,128,128]{2,1,0:T(8,128)(2,1)S(1)}, bf16[12,128,128]{2,1,0:T(8,128)(2,1)S(1)}, u32[]{:S(2)}, u32[]{:S(2)}) collective-permute-start(bf16[12,128,128]{2,1,0:T(8,128)(2,1)S(1)} %copy-done.59), channel_id=1, source_target_pairs={{0,4},{4,0},{8,12},{12,8},{16,20},{20,16},{24,28},{28,24},{1,5},{5... | collective-permute-start | bytes 1179656 | tf_op jit(solution)/shard_map/ppermute | solution.py:188
  339.0 17.1 %collective-permute-start.47 = (bf16[12,128,128]{2,1,0:T(8,128)(2,1)}, bf16[12,128,128]{2,1,0:T(8,128)(2,1)}, u32[]{:S(2)}, u32[]{:S(2)}) collective-permute-start(bf16[12,128,128]{2,1,0:T(8,128)(2,1)} %get-tuple-element.102), channel_id=1, source_target_pairs={{0,4},{4,0},{8,12},{12,8},{16,20},{20,16},{24,28},{28,24},{1,5},{5... | collective-permute-start | bytes 1179656 | tf_op jit(solution)/shard_map/ppermute | solution.py:188
  352.9 26.4 %collective-permute-start.46 = (bf16[12,128,128]{2,1,0:T(8,128)(2,1)}, bf16[12,128,128]{2,1,0:T(8,128)(2,1)}, u32[]{:S(2)}, u32[]{:S(2)}) collective-permute-start(bf16[12,128,128]{2,1,0:T(8,128)(2,1)} %get-tuple-element.95), channel_id=1, source_target_pairs={{0,4},{4,0},{8,12},{12,8},{16,20},{20,16},{24,28},{28,24},{1,5},{5... | collective-permute-start | bytes 1179656 | tf_op jit(solution)/shard_map/ppermute | solution.py:188
  354.4 25.0 %collective-permute-start.56 = (bf16[12,128,128]{2,1,0:T(8,128)(2,1)}, bf16[12,128,128]{2,1,0:T(8,128)(2,1)}, u32[]{:S(2)}, u32[]{:S(2)}) collective-permute-start(bf16[12,128,128]{2,1,0:T(8,128)(2,1)} %get-tuple-element.96), channel_id=1, source_target_pairs={{0,4},{4,0},{8,12},{12,8},{16,20},{20,16},{24,28},{28,24},{1,5},{5... | collective-permute-start | bytes 1179656 | tf_op jit(solution)/shard_map/ppermute | solution.py:188
  356.0 13.0 %collective-permute-start.60 = (f32[12288]{0:T(1024)S(1)}, f32[12288]{0:T(1024)S(1)}, u32[]{:S(2)}, u32[]{:S(2)}) collective-permute-start(f32[12288]{0:T(1024)S(1)} %dynamic_update_slice.11), channel_id=1, source_target_pairs={{0,1},{1,0},{2,3},{3,2},{4,5},{5,4},{6,7},{7,6},{8,9},{9,8},{10,11... | collective-permute-start | bytes 147464 | tf_op jit(solution)/shard_map/ppermute | solution.py:188
  365.7 13.7 %collective-permute-start.52 = (bf16[12,128,128]{2,1,0:T(8,128)(2,1)S(1)}, bf16[12,128,128]{2,1,0:T(8,128)(2,1)S(1)}, u32[]{:S(2)}, u32[]{:S(2)}) collective-permute-start(bf16[12,128,128]{2,1,0:T(8,128)(2,1)S(1)} %fusion.120), channel_id=1, source_target_pairs={{0,8},{4,12},{8,16},{12,20},{16,24},{20,28},{24,0},{28,4},{1,9},{5... | collective-permute-start | bytes 1179656 | tf_op jit(solution)/shard_map/ppermute | solution.py:193
  370.3 16.1 %collective-permute-start.44 = (bf16[256,1024]{1,0:T(8,128)(2,1)S(1)}, bf16[256,1024]{1,0:T(8,128)(2,1)S(1)}, u32[]{:S(2)}, u32[]{:S(2)}) collective-permute-start(bf16[256,1024]{1,0:T(8,128)(2,1)S(1)} %get-tuple-element.107), channel_id=1, source_target_pairs={{0,1},{1,0},{2,3},{3,2},{4,5},{5,4},{6,7},{7,6},{8,9},{9,8},{10,11... | collective-permute-start | bytes 1572872 | tf_op jit(solution)/shard_map/ppermute | solution.py:188
  383.2 22.4 %collective-permute-start.43 = (bf16[256,1024]{1,0:T(8,128)(2,1)S(1)}, bf16[256,1024]{1,0:T(8,128)(2,1)S(1)}, u32[]{:S(2)}, u32[]{:S(2)}) collective-permute-start(bf16[256,1024]{1,0:T(8,128)(2,1)S(1)} %get-tuple-element.106), channel_id=1, source_target_pairs={{0,1},{1,0},{2,3},{3,2},{4,5},{5,4},{6,7},{7,6},{8,9},{9,8},{10,11... | collective-permute-start | bytes 1572872 | tf_op jit(solution)/shard_map/ppermute | solution.py:188
  386.4 82.1 %collective-permute-start.53 = (bf16[12,128,128]{2,1,0:T(8,128)(2,1)S(1)}, bf16[12,128,128]{2,1,0:T(8,128)(2,1)S(1)}, u32[]{:S(2)}, u32[]{:S(2)}) collective-permute-start(bf16[12,128,128]{2,1,0:T(8,128)(2,1)S(1)} %copy-done.56), channel_id=1, source_target_pairs={{0,4},{4,0},{8,12},{12,8},{16,20},{20,16},{24,28},{28,24},{1,5},{5... | collective-permute-start | bytes 1179656 | tf_op jit(solution)/shard_map/ppermute | solution.py:188
  390.8 14.8 %collective-permute-start.45 = (bf16[256,1024]{1,0:T(8,128)(2,1)S(1)}, bf16[256,1024]{1,0:T(8,128)(2,1)S(1)}, u32[]{:S(2)}, u32[]{:S(2)}) collective-permute-start(bf16[256,1024]{1,0:T(8,128)(2,1)S(1)} %fusion.68), channel_id=1, source_target_pairs={{0,2},{1,3},{2,0},{3,1},{4,6},{5,7},{6,4},{7,5},{8,10},{9,11},{10,... | collective-permute-start | bytes 1572872 | tf_op jit(solution)/shard_map/ppermute | solution.py:188
  405.0 63.4 %collective-permute-start.59 = (bf16[12,128,128]{2,1,0:T(8,128)(2,1)S(1)}, bf16[12,128,128]{2,1,0:T(8,128)(2,1)S(1)}, u32[]{:S(2)}, u32[]{:S(2)}) collective-permute-start(bf16[12,128,128]{2,1,0:T(8,128)(2,1)S(1)} %fusion.114), channel_id=1, source_target_pairs={{0,8},{4,12},{8,16},{12,20},{16,24},{20,28},{24,0},{28,4},{1,9},{5... | collective-permute-start | bytes 1179656 | tf_op jit(solution)/shard_map/ppermute | solution.py:193
  (113 other events, 850.0 us)

commit v3 on v2

--- a/solution.py
+++ b/solution.py
@@ -21,130 +21,265 @@
 weight_decay = 0.01
 vector_rate = 0.25
 masked_score = -1000000000.0
-highest = lax.Precision.HIGHEST
 bfloat = jnp.bfloat16
 single = jnp.float32
 
 
-def matmul_high(left, right):
-    return jnp.matmul(left, right, precision=highest)
-
-
-def mm(a, b, ca=1, cb=0, prec=highest):
-    return lax.dot_general(a,b,(((ca,),(cb,)),((),())),precision=prec,preferred_element_type=single)
-
-def adam_kernel(rates_ref, g_ref, m_ref, v_ref, w_ref, sl_ref, sr_ref, l_ref, r_ref,
-                mo_ref, vo_ref, wo_ref, slo_ref, sro_ref, gram_ref, at_ref, *, per):
-    i = pl.program_id(0)
-    corr = 1.0 - 0.5**STEP
-    for q in range(per):
-        g=g_ref[q]; l=l_ref[q]; r=r_ref[q]
-        rot = mm(l, mm(g, r), 0, 0)
-        nm = 0.5*m_ref[q] + 0.5*rot
-        nv = 0.5*v_ref[q] + 0.5*rot*rot
-        mo_ref[q]=nm; vo_ref[q]=nv
-        d = (nm/corr)/(jnp.sqrt(nv/corr)+1e-8)
-        turned = mm(l, mm(d, r, 1, 1))
-        rate = rates_ref[i*per+q]
-        w = w_ref[q]
-        wo_ref[q] = w - rate*(turned + 0.01*w)
-        sl = 0.5*sl_ref[q] + (0.5/BLK)*mm(g,g,1,1)
-        sr = 0.5*sr_ref[q] + (0.5/BLK)*mm(g,g,0,0)
-        slo_ref[q]=sl; sro_ref[q]=sr
-        for side,(s,b) in enumerate(((sl,l),(sr,r))):
-            at = mm(b, s, 0, 0)
-            gram = mm(at, at, 1, 1)
-            gram_ref[side, q]=gram
-            at_ref[side, q]=at
-
-def adam(g,m,v,w,sl,sr,l,r,rates,per=2):
-    n=g.shape[0]
-    blk=lambda: pl.BlockSpec((per,BLK,BLK),lambda i,*_:(i,0,0))
-    sd=jax.ShapeDtypeStruct((n,BLK,BLK),single)
-    return pl.pallas_call(functools.partial(adam_kernel,per=per),
-        grid_spec=pltpu.PrefetchScalarGridSpec(num_scalar_prefetch=1,grid=(n//per,),
-            in_specs=[blk() for _ in range(8)],
-            out_specs=[blk() for _ in range(5)]+[pl.BlockSpec((2,per,BLK,BLK),lambda i,*_:(0,i,0,0))]*2),
-        out_shape=[sd]*5+[jax.ShapeDtypeStruct((2,n,BLK,BLK),single)]*2,
-        compiler_params=pltpu.CompilerParams(vmem_limit_bytes=48*2**20),
-        name="adam")(rates,g,m,v,w,sl,sr,l,r)
-
-PB=32
+PANEL = 32
+
+
+def dot_of(left, right, left_dim, right_dim):
+    return lax.dot_general(
+        left, right, (((left_dim,), (right_dim,)), ((), ())), preferred_element_type=single
+    )
+
+
+def split_two(value):
+    high = value.astype(bfloat)
+    return high, (value - high.astype(single)).astype(bfloat)
+
+
+def split_three(value):
+    high = value.astype(bfloat)
+    rest = value - high.astype(single)
+    mid = rest.astype(bfloat)
+    return high, mid, (rest - mid.astype(single)).astype(bfloat)
+
+
+def dot_three(left, right, left_dim, right_dim):
+    stacked_left = jnp.concatenate([left[0], left[0], left[1]], axis=left_dim)
+    stacked_right = jnp.concatenate([right[0], right[1], right[0]], axis=right_dim)
+    return dot_of(stacked_left, stacked_right, left_dim, right_dim)
+
+
+def dot_two(pair, other, pair_dim, other_dim, swapped=False):
+    stacked = jnp.concatenate(pair, axis=pair_dim)
+    twice = jnp.concatenate([other, other], axis=other_dim)
+    if swapped:
+        return dot_of(twice, stacked, other_dim, pair_dim)
+    return dot_of(stacked, twice, pair_dim, other_dim)
+
+
+def gram_six(pieces):
+    high, mid, low = pieces
+    left = jnp.concatenate([high, high, high, mid, mid, low], axis=1)
+    right = jnp.concatenate([high, mid, low, high, mid, high], axis=1)
+    return dot_of(left, right, 1, 1)
+
+
+def adam_kernel(
+    rates_ref, grad_ref, first_ref, second_ref, master_ref, left_stat_ref, right_stat_ref,
+    left_ref, right_ref, new_first_ref, new_second_ref, new_master_ref, new_left_ref,
+    new_right_ref, gram_ref, product_ref, *, per,
+):
+    step = pl.program_id(0)
+    correction = 1.0 - moment_decay**STEP
+    for item in range(per):
+        grad = grad_ref[item]
+        left, right = split_two(left_ref[item]), split_two(right_ref[item])
+        rotated = dot_two(left, dot_two(right, grad, 0, 1, True).astype(bfloat), 0, 0)
+        new_first = moment_decay * first_ref[item] + (1.0 - moment_decay) * rotated
+        new_second = moment_decay * second_ref[item] + (1.0 - moment_decay) * rotated * rotated
+        new_first_ref[item] = new_first
+        new_second_ref[item] = new_second
+        direction = (new_first / correction) / (jnp.sqrt(new_second / correction) + 1e-8)
+        turned = dot_two(right, direction.astype(bfloat), 1, 1, True)
+        turned = dot_two(left, turned.astype(bfloat), 1, 0)
+        master = master_ref[item]
+        new_master_ref[item] = master - rates_ref[step * per + item] * (turned + 0.01 * master)
+        scale = (1.0 - moment_decay) / BLK
+        new_left = moment_decay * left_stat_ref[item] + scale * dot_of(grad, grad, 1, 1)
+        new_right = moment_decay * right_stat_ref[item] + scale * dot_of(grad, grad, 0, 0)
+        new_left_ref[item] = new_left
+        new_right_ref[item] = new_right
+        for side, (stats, basis) in enumerate(((new_left, left), (new_right, right))):
+            product = dot_three(basis, split_two(stats), 0, 0)
+            product_ref[side, item] = product
+            gram_ref[side, item] = gram_six(split_three(product))
+
+
+def adam(grads, first, second, master, left_stats, right_stats, left, right, rates, per):
+    count = grads.shape[0]
+    block = pl.BlockSpec((per, BLK, BLK), lambda i, *_: (i, 0, 0))
+    pair = pl.BlockSpec((2, per, BLK, BLK), lambda i, *_: (0, i, 0, 0))
+    one = jax.ShapeDtypeStruct((count, BLK, BLK), single)
+    two = jax.ShapeDtypeStruct((2, count, BLK, BLK), single)
+    return pl.pallas_call(
+        functools.partial(adam_kernel, per=per),
+        grid_spec=pltpu.PrefetchScalarGridSpec(
+            num_scalar_prefetch=1,
+            grid=(count // per,),
+            in_specs=[block] * 8,
+            out_specs=[block] * 5 + [pair] * 2,
+        ),
+        out_shape=[one] * 5 + [two] * 2,
+        compiler_params=pltpu.CompilerParams(vmem_limit_bytes=48 * 2**20),
+        name="adam",
+    )(rates, grads, first, second, master, left_stats, right_stats, left, right)
+
+
 def factor_panel(rows):
-    nb=PB//8
-    T=[[rows[j][8*ib:8*ib+8] if ib>=j//8 else None for ib in range(nb)] for j in range(PB)]
-    batch=rows[0].shape[1]
-    sub=lax.broadcasted_iota(jnp.int32,(8,batch),0)
-    X=[[None]*nb for _ in range(PB)]
-    zero=jnp.zeros((8,batch),single)
-    for k in range(PB):
-        kb,ks=divmod(k,8)
-        piv=T[k][kb][ks:ks+1]
-        y=lax.rsqrt(piv)
-        y=y*(1.5-0.5*piv*y*y)
-        yb=jnp.broadcast_to(y,(8,batch))
-        col=[T[k][ib]*yb if ib>=kb else None for ib in range(nb)]
-        unit=jnp.where(sub==ks,yb,0.0)
-        xk=[]
-        for cb in range(kb+1):
-            v=X[k][cb]
-            if cb==kb:
-                xk.append(unit if v is None else jnp.where(sub==ks,yb,v*yb))
-            else:
-                xk.append(zero if v is None else v*yb)
-        X[k]=xk+[zero]*(nb-kb-1)
-        for j in range(k+1,PB):
-            jb,js=divmod(j,8)
-            s=jnp.broadcast_to(col[jb][js:js+1],(8,batch))
-            for ib in range(jb,nb):
-                T[j][ib]=T[j][ib]-s*col[ib]
-            for cb in range(kb+1):
-                t=s*xk[cb]
-                X[j][cb]= -t if X[j][cb] is None else X[j][cb]-t
-    return X
-
-def chol_kernel(g_in_ref, at_in_ref, q_ref, g_ref, at_ref, xs_ref, *, n, unroll):
-    g_ref[...]=g_in_ref[...]
-    at_ref[...]=at_in_ref[...]
-    pad=jnp.zeros((BLK-PB,n),single)
-    for p in range(BLK//PB):
-        rows=[]
-        for j in range(PB):
-            t=g_ref[pl.ds(p*PB+j,n,stride=BLK),:]
-            rows.append(t.T[p*PB:(p+1)*PB])
-        X=factor_panel(rows)
-        for i in range(PB):
-            xi=jnp.concatenate(X[i]+[pad],axis=0)
-            xs_ref[pl.ds(i,n,stride=PB),:]=xi.T
-        def step(m,_):
-            xm=xs_ref[pl.ds(pl.multiple_of(m*PB,PB),PB),0:PB]
-            base=pl.multiple_of(m*BLK,BLK)
-            ra=mm(xm,at_ref[pl.ds(base+p*PB,PB),:])
-            at_ref[pl.ds(base+p*PB,PB),:]=ra
-            if p<BLK//PB-1:
-                first=(p+1)*PB
-                rest=pl.ds(base+first,BLK-first)
-                rg=mm(xm,g_ref[pl.ds(base+p*PB,PB),:])
-                lead=rg[:,first:]
-                g_ref[rest,:]=g_ref[rest,:]-mm(lead,rg,0,0)
-                at_ref[rest,:]=at_ref[rest,:]-mm(lead,ra,0,0)
-            return 0
-        lax.fori_loop(0,n,step,0,unroll=unroll)
-    def fin(m,_):
-        base=pl.multiple_of(m*BLK,BLK)
-        q_ref[m]=at_ref[pl.ds(base,BLK),:].T
-        return 0
-    lax.fori_loop(0,n,fin,0,unroll=unroll)
-
-def chol(gram,at,unroll=4):
-    n=gram.shape[0]*gram.shape[1]
-    q=pl.pallas_call(functools.partial(chol_kernel,n=n,unroll=unroll),
-        in_specs=[pl.BlockSpec(memory_space=pltpu.VMEM)]*2,out_specs=pl.BlockSpec(memory_space=pltpu.VMEM),
-        out_shape=jax.ShapeDtypeStruct((n,BLK,BLK),single),
-        scratch_shapes=[pltpu.VMEM((n*BLK,BLK),single),pltpu.VMEM((n*BLK,BLK),single),pltpu.VMEM((n*PB,BLK),single)],
-        compiler_params=pltpu.CompilerParams(vmem_limit_bytes=48*2**20),
-        name="chol")(gram.reshape(n*BLK,BLK),at.reshape(n*BLK,BLK))
-    return q
+    pieces = PANEL // 8
+    batch = rows[0].shape[1]
+    work = [
+        [rows[j][8 * i : 8 * i + 8] if i >= j // 8 else None for i in range(pieces)]
+        for j in range(PANEL)
+    ]
+    sublane = lax.broadcasted_iota(jnp.int32, (8, batch), 0)
+    zero = jnp.zeros((8, batch), single)
+    inverse = [[None] * pieces for _ in range(PANEL)]
+    for k in range(PANEL):
+        group, lane = divmod(k, 8)
+        pivot = work[k][group][lane : lane + 1]
+        root = lax.rsqrt(pivot)
+        root = root * (1.5 - 0.5 * pivot * root * root)
+        root = jnp.broadcast_to(root, (8, batch))
+        column = [work[k][i] * root if i >= group else None for i in range(pieces)]
+        done = []
+        for i in range(group + 1):
+            value = inverse[k][i]
+            value = zero if value is None else value * root
+            done.append(jnp.where(sublane == lane, root, value) if i == group else value)
+        inverse[k] = done + [zero] * (pieces - group - 1)
+        for j in range(k + 1, PANEL):
+            row_group, row_lane = divmod(j, 8)
+            factor = jnp.broadcast_to(column[row_group][row_lane : row_lane + 1], (8, batch))
+            for i in range(row_group, pieces):
+                work[j][i] = work[j][i] - factor * column[i]
+            for i in range(group + 1):
+                term = factor * done[i]
+                inverse[j][i] = -term if inverse[j][i] is None else inverse[j][i] - term
+    return inverse
+
+
+def renew_kernel(
+    gram_in_ref, product_in_ref, left_ref, right_ref, gram_ref, product_ref, inverse_ref, *, count, unroll
+):
+    gram_ref[...] = gram_in_ref[...]
+    product_ref[...] = product_in_ref[...]
+    lane = lax.broadcasted_iota(jnp.int32, (PANEL, BLK), 1)
+    for panel in range(BLK // PANEL):
+        top = panel * PANEL
+        last = panel == BLK // PANEL - 1
+        rows = []
+        for j in range(PANEL):
+            row = gram_ref[pl.ds(top + j, count, stride=BLK), :]
+            rows.append(row.T[top : top + PANEL])
+        inverse = factor_panel(rows)
+        for i in range(PANEL):
+            row = jnp.concatenate(inverse[i], 0)
+            inverse_ref[pl.ds(i, count, stride=PANEL), :] = jnp.concatenate([row] * 4, 0).T
+
+        def step(item, nothing):
+            base = pl.multiple_of(item * BLK, BLK)
+            here = pl.ds(pl.multiple_of(item * PANEL, PANEL), PANEL)
+            high, mid, low = split_three(inverse_ref[here, :])
+            none = jnp.zeros_like(high)
+            left = jnp.concatenate(
+                [
+                    jnp.where(lane < 3 * PANEL, high, none),
+                    jnp.where(lane < 2 * PANEL, mid, none),
+                    jnp.where(lane < PANEL, low, none),
+                ],
+                0,
+            )[:, : 3 * PANEL]
+            rows_at = pl.ds(base + top, PANEL)
+            whole = product_ref[rows_at, :]
+            if not last:
+                whole = jnp.concatenate([gram_ref[rows_at, :], whole], 1)
+            solved = dot_of(left, jnp.concatenate(split_three(whole), 0), 1, 0)
+            solved = solved[:PANEL] + (solved[PANEL : 2 * PANEL] + solved[2 * PANEL :])
+            product_ref[rows_at, :] = solved[:, -BLK:]
+            if not last:
+                high, mid, low = split_three(solved)
+                left = jnp.concatenate([high, high, high, mid, mid, low], 0)[:, top + PANEL : BLK]
+                right = jnp.concatenate([high, mid, low, high, mid, high], 0)
+                update = dot_of(left, right, 0, 0)
+                rest = pl.ds(base + top + PANEL, BLK - top - PANEL)
+                gram_ref[rest, :] = gram_ref[rest, :] - update[:, :BLK]
+                product_ref[rest, :] = product_ref[rest, :] - update[:, BLK:]
+            return nothing
+
+        lax.fori_loop(0, count, step, 0, unroll=math.gcd(count, unroll))
+
+    half = count // 2
+    for side, basis_ref in enumerate((left_ref, right_ref)):
+
+        def finish(item, nothing):
+            base = pl.multiple_of((side * half + item) * BLK, BLK)
+            basis_ref[item] = product_ref[pl.ds(base, BLK), :].T
+            return nothing
+
+        lax.fori_loop(0, half, finish, 0, unroll=math.gcd(half, unroll))
+
+
+def renew(gram, product, unroll=16):
+    count = gram.shape[0] * gram.shape[1]
+    whole = pl.BlockSpec(memory_space=pltpu.VMEM)
+    return pl.pallas_call(
+        functools.partial(renew_kernel, count=count, unroll=unroll),
+        in_specs=[whole] * 2,
+        out_specs=[whole] * 2,
+        out_shape=[jax.ShapeDtypeStruct((count // 2, BLK, BLK), single)] * 2,
+        scratch_shapes=[pltpu.VMEM((count * BLK, BLK), single)] * 2
+        + [pltpu.VMEM((count * PANEL, BLK), single)],
+        compiler_params=pltpu.CompilerParams(vmem_limit_bytes=48 * 2**20),
+        name="renew",
+    )(gram.reshape(count * BLK, BLK), product.reshape(count * BLK, BLK))
+
+
+def pack_kernel(target_ref, *refs, jobs, scale):
+    count = 2 * len(jobs)
+    inputs, out_ref, held_ref, sem = refs[:count], refs[-3], refs[-2], refs[-1]
+    copies = []
+    for index, (layout, rows, cols) in enumerate(jobs):
+        left_ref, right_ref = inputs[2 * index], inputs[2 * index + 1]
+        for row in range(0, rows, 2):
+            span = min(2, rows - row)
+            weights = dot_of(left_ref[:, row * BLK : (row + span) * BLK], right_ref[...], 0, 0)
+            weights = (weights * scale).astype(bfloat)
+            for i in range(span):
+                for col in range(cols):
+                    place = len(copies)
+                    held_ref[place] = weights[
+                        i * BLK : (i + 1) * BLK, col * BLK : (col + 1) * BLK
+                    ]
+                    copy = pltpu.make_async_copy(
+                        held_ref.at[place], out_ref.at[target_ref[layout(row + i, col)]], sem
+                    )
+                    copy.start()
+                    copies.append(copy)
+    pltpu.make_async_copy(held_ref, out_ref.at[pl.ds(0, len(copies))], sem).wait()
+
+
+def pack(target, pairs, layouts, scale, total, earlier=None):
+    jobs = [
+        (layout, left.shape[1] // BLK, right.shape[1] // BLK)
+        for (left, right), layout in zip(pairs, layouts)
+    ]
+    operands = [value for pair in pairs for value in pair]
+    blocks = sum(rows * cols for _, rows, cols in jobs)
+    whole = pl.BlockSpec(memory_space=pltpu.VMEM)
+    some = pl.BlockSpec(memory_space=pl.ANY)
+    more = [] if earlier is None else [earlier]
+    flops = sum(2 * left.shape[0] * left.shape[1] * right.shape[1] for left, right in pairs)
+    return pl.pallas_call(
+        functools.partial(pack_kernel, jobs=jobs, scale=scale),
+        grid_spec=pltpu.PrefetchScalarGridSpec(
+            num_scalar_prefetch=1,
+            grid=(),
+            in_specs=[whole] * len(operands) + [some] * len(more),
+            out_specs=some,
+            scratch_shapes=[pltpu.VMEM((blocks, BLK, BLK), bfloat), pltpu.SemaphoreType.DMA],
+        ),
+        out_shape=jax.ShapeDtypeStruct((total, BLK, BLK), bfloat),
+        input_output_aliases={1 + len(operands): 0} if more else {},
+        cost_estimate=pl.CostEstimate(
+            flops=flops, bytes_accessed=blocks * BLK * BLK * 4, transcendentals=0
+        ),
+        compiler_params=pltpu.CompilerParams(vmem_limit_bytes=48 * 2**20),
+        name="pack",
+    )(target, *operands, *more)
 
 
 def gelu_exact(inputs):
@@ -153,12 +288,6 @@
 
 def block_counts(tensors):
     return (D * D // (tensors * BLK * BLK), D * FF // (tensors * BLK * BLK))
-
-
-def to_blocks(matrix):
-    row_count, col_count = matrix.shape
-    shaped = matrix.reshape(row_count // BLK, BLK, col_count // BLK, BLK)
-    return shaped.swapaxes(1, 2).reshape(row_count * col_count // (BLK * BLK), BLK, BLK)
 
 
 def rate_values(canon_index, tensors, seq_len):
@@ -230,8 +359,8 @@
                 mine = mine + carried.astype(single)
             if hop > 0:
                 carried = ring(mine.astype(bfloat))
-        done.append(mine)
-    return done
+        done.append(mine.astype(bfloat))
+    return jnp.concatenate(done, 0)
 
 
 def assemble_kernel(source_ref, *refs, sizes, layouts):
@@ -337,7 +466,6 @@
         source = target = block_owner
     canon_ids = jnp.arange(block_total, dtype=jnp.int32)
     inverse = jnp.zeros((block_total,), jnp.int32).at[block_owner].set(canon_ids)
-    sent_order = jnp.zeros((block_total,), jnp.int32).at[target].set(canon_ids)
 
     local_weights = master_blocks[0].astype(bfloat)
     if permuted:
@@ -456,8 +584,18 @@
     all_grad_down = jnp.concatenate(full_grad_down, 0)
     all_hidden = jnp.concatenate(full_hidden, 0)
     all_grad_up = jnp.concatenate(grad_up, 0)
-    dw_down = jnp.einsum("sf,sd->fd", activation, all_grad_down, preferred_element_type=single)
-    dw_up = jnp.einsum("sd,sf->df", all_hidden, all_grad_up, preferred_element_type=single)
+    grad_scale = 1.0 / math.sqrt(seq_len * data_ranks)
+    up_start = 4 * attn_count
+    sent = pack(
+        target,
+        [(all_hidden, all_grad_up), (activation, all_grad_down)],
+        [
+            lambda row, col: up_start + row * wide + col,
+            lambda row, col: up_start + ffn_count + row * full + col,
+        ],
+        grad_scale,
+        block_total,
+    )
     dbias_up = jnp.sum(all_grad_up.astype(single), 0)
     full_grad_branch, grad_query = [], []
     key_total = value_total = 0.0
@@ -504,10 +642,17 @@
     )
     all_attended = jnp.concatenate(attended, 0)
     all_grad_branch = jnp.concatenate(full_grad_branch, 0)
-    dw_out = jnp.einsum(
-        "sa,sd->ad", all_attended, all_grad_branch, preferred_element_type=single
-    )
-    dw_qkv = jnp.einsum("sd,sc->dc", full_tokens, grad_qkv, preferred_element_type=single)
+    sent = pack(
+        target,
+        [(full_tokens, grad_qkv), (all_attended, all_grad_branch)],
+        [
+            lambda row, col: col // cols * attn_count + row * cols + col % cols,
+            lambda row, col: 3 * attn_count + row * full + col,
+        ],
+        grad_scale,
+        block_total,
+        sent,
+    )
     dbias_query = jnp.sum(grad_qkv[:, 0:slice_width].astype(single), 0)
     dbias_value = jnp.sum(grad_qkv[:, 2 * slice_width : 3 * slice_width].astype(single), 0)
     token_part = jnp.einsum("sc,dc->sd", grad_qkv, w_qkv, preferred_element_type=single)
@@ -518,17 +663,6 @@
         chip_rows.append(rows[:local_rows] + got.astype(single))
     across = swap(chip_rows[0].astype(bfloat), "tensor", 2)
     token_grad = (chip_rows[1] + across.astype(single) + grad_summed).astype(bfloat)
-    grad_blocks = jnp.concatenate(
-        [
-            to_blocks(dw_qkv[:, 0:slice_width]),
-            to_blocks(dw_qkv[:, slice_width : 2 * slice_width]),
-            to_blocks(dw_qkv[:, 2 * slice_width : 3 * slice_width]),
-            to_blocks(dw_out),
-            to_blocks(dw_up),
-            to_blocks(dw_down),
-        ],
-        axis=0,
-    )
     vector_grad = jnp.concatenate(
         [
             dgain_one,
@@ -550,33 +684,19 @@
     vector_grad = lax.dynamic_update_slice_in_dim(
         vector_grad, dbias_up, 7 * D + tensor_rank * hidden_width, 0
     )
-    grad_scale = 1.0 / math.sqrt(seq_len * data_ranks)
     own_canon = lax.dynamic_slice_in_dim(inverse, data_rank * slots_here, slots_here)
     vector_sum = total_of(vector_grad) * grad_scale
-    sent = (grad_blocks * grad_scale).astype(bfloat)
-    sent = sent.at[sent_order].get(mode="promise_in_bounds")
     if permuted:
-        done = scatter_slots(sent, slots_here, 2)
+        own_grad = scatter_slots(sent, slots_here, 2)
     else:
-        done = [lax.psum_scatter(sent, "dp", scatter_dimension=0, tiled=True).astype(single)]
+        own_grad = lax.psum_scatter(sent, "dp", scatter_dimension=0, tiled=True)
     rates = rate_values(own_canon, tensors, seq_len)
     correction = 1.0 - moment_decay**STEP
-    states = [
-        first_moment[0], second_moment[0], master_blocks[0], left_stats[0], right_stats[0],
-        left_basis[0], right_basis[0],
-    ]
-    fresh, start = [], 0
-    for own_grad in done:
-        size = own_grad.shape[0]
-        here = slice(start, start + size)
-        start += size
-        *updated, gram, product = adam(
-            own_grad, *[state[here] for state in states], rates[here], per=2 if size % 2 == 0 else 1
-        )
-        bases = chol(gram, product)
-        fresh.append(updated + [bases[:size], bases[size:]])
-    fresh = [jnp.concatenate(column, 0) for column in zip(*fresh)]
-    fresh_first, fresh_second, fresh_master, fresh_left, fresh_right, basis_left, basis_right = fresh
+    fresh_first, fresh_second, fresh_master, fresh_left, fresh_right, gram, product = adam(
+        own_grad, first_moment[0], second_moment[0], master_blocks[0], left_stats[0],
+        right_stats[0], left_basis[0], right_basis[0], rates, per=math.gcd(slots_here, 4)
+    )
+    basis_left, basis_right = renew(gram, product)
     vec_first = moment_decay * vector_first + (1.0 - moment_decay) * vector_sum
     vec_second = moment_decay * vector_second + (1.0 - moment_decay) * vector_sum * vector_sum
     vec_master = vector_master - vector_rate * (vec_first / correction) / (

time: 545 us -> 455 us (0.83)
  Pallas kernels: 122 us -> 62 us
  local copies, waits for them, and re-layouts: 78.1 us -> 29.4 us
  waiting for transfers between devices: 143 us -> 169 us
    pallas_call x2 -> x3, Pallas kernels: 70.1 us -> 34.9 us  [the longest x1 21.2 us: renew(): pl.pallas_call(functools.partial(renew_kernel, count=count, unroll=unroll...]
    ppermute x50, waiting for transfers between devices: 98.6 us -> 128 us  [swap(): return lax.ppermute(value, axis, [(i, i ^ bit) for i in range(count)])]
    pallas_call x2 -> x1, Pallas kernels: 47.5 us -> 23.1 us  [adam(): pl.pallas_call(functools.partial(adam_kernel, per=per), grid_spec=pltpu.P...]
    unnamed x178 -> x242, local copies, waits for them, and re-layouts: 32.4 us -> 14.9 us
    reshape x9 -> x3, local copies, waits for them, and re-layouts: 14.6 us -> 2.69 us  [the longest x2 1.69 us: body(): attended[part] = mixed.astype(bfloat).reshape(chunk, slice_width)]
    gather x1 -> x0, local copies, waits for them, and re-layouts: 10.9 us -> none  [body(): sent = sent.at[sent_order].get(mode='promise_in_bounds')]
    concatenate x0 -> x8, other arithmetic: none -> 10.6 us  [the longest x1 3.19 us: body(): activation = jnp.concatenate(activation, 0)]
    broadcast_in_dim x7 -> x0, other arithmetic: 8.83 us -> none  [the longest x1 1.3 us: body(): fresh_right[None]]
  transfers between devices with their start and end apart: 65 -> 65, of which waited for: 30 -> 36; matrix products, arithmetic and copies ran while one was open for 15% -> 13% of each run, Pallas kernels for 11% -> 2%
where the time goes in v3:
time: 455 us; the launch traced here: 451 us
  waiting for transfers between devices  169 us (37%)
  matrix products  70.7 us (16%)
  Pallas kernels  62 us (14%)
  other arithmetic  60.9 us (13%)
  starting transfers between devices  55.5 us (12%)
  local copies, waits for them, and re-layouts  29.4 us (6%)
    ppermute x50, waiting for transfers between devices, swap(): return lax.ppermute(value, axis, [(i, i ^ bit) for i in range(count)])  128 us
    ppermute x50, starting transfers between devices, swap(): return lax.ppermute(value, axis, [(i, i ^ bit) for i in range(count)])  46.9 us
    ppermute x15, waiting for transfers between devices, ring(): lax.ppermute(value, 'dp', [(i, (i + 2) % count) for i in range(count)])  41.7 us
    pallas_call x1, Pallas kernels, adam(): pl.pallas_call(functools.partial(adam_kernel, per=per), grid_spec=pltpu.P...  23.1 us
    pallas_call x1, Pallas kernels, renew(): pl.pallas_call(functools.partial(renew_kernel, count=count, unroll=unroll...  21.2 us
    dot_general x2, matrix products, body(): jnp.einsum('qhd,khd->hqk', grad_block, heads_v, preferred_element_type=si...  15.4 us
    unnamed x242, local copies, waits for them, and re-layouts  14.9 us
    pallas_call x2, Pallas kernels, pack(): pl.pallas_call(functools.partial(pack_kernel, jobs=jobs, scale=scale), gr...  13.7 us
  transfers between devices with their start and end apart: 65, of which 36 were waited for; matrix products, arithmetic and copies ran while one was open for 13% of the time, Pallas kernels for 2%

profile of v3, /device:TPU:0, one launch (start us, length us, event | category | flops | bytes accessed | tf_op | source)
XLA Modules:
  0.0 451.1 jit_solution(15385996646044353380)
XLA Ops:
  10.0 4.6 %collective-permute-done.8.refs_8_ = bf16[8,128,128]{2,1,0:T(8,128)(2,1)S(1)} collective-permute-done((bf16[8,128,128]{2,1,0:T(8,128)(2,1)S(1)}, bf16[8,128,128]{2,1,0:T(8,128)(2,1)S(1)}, u32[]{:S(2)}, u32[]{:S(2)}) %collective-permute-start.8) | collective-permute-done | bytes 262176 | tf_op jit(solution)/shard_map/ppermute | solution.py:322
  16.3 3.9 collective-permute-done.7.refs_7_
  35.2 4.3 collective-permute-done.13.refs_13_
  47.0 3.8 collective-permute-done.20.refs_20_
  52.8 3.5 collective-permute-done.19.refs_19_
  65.9 5.6 %collective-permute-done.23.refs_23_ = bf16[8,128,128]{2,1,0:T(8,128)(2,1)S(1)} collective-permute-done((bf16[8,128,128]{2,1,0:T(8,128)(2,1)}, bf16[8,128,128]{2,1,0:T(8,128)(2,1)S(1)}, u32[]{:S(2)}, u32[]{:S(2)}) %collective-permute-start.23) | collective-permute-done | bytes 262176 | tf_op jit(solution)/shard_map/ppermute | solution.py:317
  79.3 4.1 assemble.1
  89.7 3.8 fusion.1
  104.7 12.3 %collective-permute-done.26 = bf16[256,1024]{1,0:T(8,128)(2,1)} collective-permute-done((bf16[256,1024]{1,0:T(8,128)(2,1)S(1)}, bf16[256,1024]{1,0:T(8,128)(2,1)}, u32[]{:S(2)}, u32[]{:S(2)}) %collective-permute-start.26) | collective-permute-done | bytes 524320 | tf_op jit(solution)/shard_map/ppermute | solution.py:317
  120.9 11.3 %collective-permute-done.29 = bf16[256,1024]{1,0:T(8,128)(2,1)S(1)} collective-permute-done((bf16[256,1024]{1,0:T(8,128)(2,1)S(1)}, bf16[256,1024]{1,0:T(8,128)(2,1)S(1)}, u32[]{:S(2)}, u32[]{:S(2)}) %collective-permute-start.29) | collective-permute-done | bytes 524320 | tf_op jit(solution)/shard_map/ppermute | solution.py:317
  137.6 11.8 %multiply_convert_fusion.2 = (bf16[512,1024]{1,0:T(8,128)(2,1)S(1)}, f32[512,1024]{1,0:T(8,128)}, bf16[512,1024]{1,0:T(8,128)(2,1)S(1)}, f32[512,1024]{1,0:T(8,128)}, f32[512,1024]{1,0:T(8,128)}) fusion(f32[1024]{0:T(1024)S(1)} %get-tuple-element.105, f32[512,1024]{1,0:T(8,128)S(1)} %fusion.50, bf16[1024,1024]{1,0:T(8,128)(2,1)S(1)} %copy-done.21, ...), kind=kOutput, calls=%fused_computation.38 | convolution fusion | flops 1145044992 | bytes 13635584 | tf_op jit(solution)/shard_map/dot_general | solution.py:553
  155.1 12.7 %collective-permute-done.35 = bf16[256,1024]{1,0:T(8,128)(2,1)S(1)} collective-permute-done((bf16[256,1024]{1,0:T(8,128)(2,1)S(1)}, bf16[256,1024]{1,0:T(8,128)(2,1)S(1)}, u32[]{:S(2)}, u32[]{:S(2)}) %collective-permute-start.35) | collective-permute-done | bytes 524320 | tf_op jit(solution)/shard_map/ppermute | solution.py:317
  170.2 19.3 %collective-permute-done.32 = bf16[256,1024]{1,0:T(8,128)(2,1)S(1)} collective-permute-done((bf16[256,1024]{1,0:T(8,128)(2,1)S(1)}, bf16[256,1024]{1,0:T(8,128)(2,1)S(1)}, u32[]{:S(2)}, u32[]{:S(2)}) %collective-permute-start.32) | collective-permute-done | bytes 524320 | tf_op jit(solution)/shard_map/ppermute | solution.py:317
  202.3 3.2 add_convert_fusion.2
  217.5 8.3 %pack.2.refs_4_ = bf16[192,128,128]{2,1,0:T(8,128)(2,1)} custom-call(s32[192]{0:T(256)S(1)} %get-tuple-element.119.target_ref, bf16[1024,1024]{1,0:T(8,128)(2,1)S(1)} %pad_maximum_fusion.1.refs_0_, bf16[1024,1024]{1,0:T(8,128)(2,1)S(1)} %pad_maximum_fusion.2.refs_1_, bf16[1024,1024]{1,0:T(8,128)(2,1)} %pad_maximum_fusion.3.refs_2_, ...), custom_call_target="tpu_custom_call" | custom-call | flops 4294967296 | bytes 8388608 | tf_op jit(solution)/shard_map/pack/pallas_call | solution.py:266
  225.8 3.8 collective-permute-done.41
  233.8 11.1 %collective-permute-done.39 = bf16[256,1024]{1,0:T(8,128)(2,1)S(1)} collective-permute-done((bf16[256,1024]{1,0:T(8,128)(2,1)S(1)}, bf16[256,1024]{1,0:T(8,128)(2,1)S(1)}, u32[]{:S(2)}, u32[]{:S(2)}) %collective-permute-start.39) | collective-permute-done | bytes 524320 | tf_op jit(solution)/shard_map/ppermute | solution.py:317
  251.3 4.6 %fusion.148 = f32[4,512,1024]{2,1,0:T(8,128)} fusion(bf16[512,4,64]{0,2,1:T(8,128)(2,1)S(1)} %bitcast.183, bf16[1024,4,64]{0,2,1:T(8,128)(2,1)S(1)} %bitcast.163), kind=kOutput, calls=%fused_computation.313 | convolution fusion | flops 268435456 | bytes 9175040 | tf_op jit(solution)/shard_map/qhd,khd->hqk/dot_general | solution.py:621
  256.0 10.8 %multiply_reduce_fusion = (f32[4,512]{1,0:T(4,128)S(1)}, f32[4,512]{1,0:T(4,128)S(1)}, f32[4,512,1024]{2,1,0:T(8,128)}) fusion(f32[4,512]{1,0:T(4,128)S(1)} %get-tuple-element.131, f32[4,512,1024]{2,1,0:T(8,128)} %copy-done.29, pred[1024]{0:T(1024)(128)(4,1)S(1)} %lt.68, f32[4,512,1024]{2,1,0:T(8,128)} %fusion.148, f32[4,512]{1,0:T(4,128)S(1)} %get-tuple-element.132, ...), kind=kOutput, calls=%fused_computation.2 | convolution fusion | flops 289402880 | bytes 34374656 | tf_op jit(solution)/shard_map/qhd,khd->hqk/dot_general | solution.py:621
  266.8 11.7 %multiply_convert_fusion = (bf16[4,512,1024]{2,1,0:T(8,128)(2,1)}, bf16[4,512,1024]{2,1,0:T(8,128)(2,1)S(1)}) fusion(f32[4,512,1024]{2,1,0:T(8,128)} %get-tuple-element.126, f32[4,512]{1,0:T(4,128)S(1)} %get-tuple-element.52, f32[4,512]{1,0:T(4,128)S(1)} %get-tuple-element.131, f32[4,512,1024]{2,1,0:T(8,128)} %copy-done.29, pred[1024]{0:T(1024)(128)(4,1)S(1)} %lt.68, ...), kind=kLoop, calls=%fused_computation.1 | loop fusion | flops 25165824 | bytes 41976832 | tf_op jit(solution)/shard_map/convert_element_type | solution.py:623
  287.3 4.5 fusion.38
  300.5 5.3 %pack.3 = bf16[192,128,128]{2,1,0:T(8,128)(2,1)} custom-call(s32[192]{0:T(256)S(1)} %get-tuple-element.119.target_ref, bf16[1024,1024]{1,0:T(8,128)(2,1)S(1)} %constant_dynamic-update-slice_fusion.refs_0_, bf16[1024,768]{1,0:T(8,128)(2,1)S(1)} %pad_maximum_fusion.5.refs_1_, ...), custom_call_target="tpu_custom_call", output_to_operand_aliasing={{}: (5, {})} | custom-call | flops 2147483648 | bytes 4194304 | tf_op jit(solution)/shard_map/pack/pallas_call | solution.py:266
  310.9 9.9 %collective-permute-done.49 = bf16[12,128,128]{2,1,0:T(8,128)(2,1)S(1)} collective-permute-done((bf16[12,128,128]{2,1,0:T(8,128)(2,1)S(1)}, bf16[12,128,128]{2,1,0:T(8,128)(2,1)S(1)}, u32[]{:S(2)}, u32[]{:S(2)}) %collective-permute-start.49) | collective-permute-done | bytes 393248 | tf_op jit(solution)/shard_map/ppermute | solution.py:317
  323.9 5.3 %collective-permute-done.48 = bf16[12,128,128]{2,1,0:T(8,128)(2,1)S(1)} collective-permute-done((bf16[12,128,128]{2,1,0:T(8,128)(2,1)S(1)}, bf16[12,128,128]{2,1,0:T(8,128)(2,1)S(1)}, u32[]{:S(2)}, u32[]{:S(2)}) %collective-permute-start.48) | collective-permute-done | bytes 393248 | tf_op jit(solution)/shard_map/ppermute | solution.py:317
  329.2 4.8 %collective-permute-done.50 = bf16[12,128,128]{2,1,0:T(8,128)(2,1)S(1)} collective-permute-done((bf16[12,128,128]{2,1,0:T(8,128)(2,1)S(1)}, bf16[12,128,128]{2,1,0:T(8,128)(2,1)S(1)}, u32[]{:S(2)}, u32[]{:S(2)}) %collective-permute-start.50) | collective-permute-done | bytes 393248 | tf_op jit(solution)/shard_map/ppermute | solution.py:322
  339.0 7.6 %collective-permute-done.51 = bf16[12,128,128]{2,1,0:T(8,128)(2,1)S(1)} collective-permute-done((bf16[12,128,128]{2,1,0:T(8,128)(2,1)S(1)}, bf16[12,128,128]{2,1,0:T(8,128)(2,1)S(1)}, u32[]{:S(2)}, u32[]{:S(2)}) %collective-permute-start.51) | collective-permute-done | bytes 393248 | tf_op jit(solution)/shard_map/ppermute | solution.py:322
  347.8 3.9 fusion.140
  351.7 4.3 collective-permute-done.56
  378.2 5.9 %collective-permute-done.63 = f32[12288]{0:T(1024)S(1)} collective-permute-done((f32[12288]{0:T(1024)S(1)}, f32[12288]{0:T(1024)S(1)}, u32[]{:S(2)}, u32[]{:S(2)}) %collective-permute-start.63) | collective-permute-done | bytes 49184 | tf_op jit(solution)/shard_map/ppermute | solution.py:317
  391.5 8.8 %collective-permute-done.45 = bf16[256,1024]{1,0:T(8,128)(2,1)S(1)} collective-permute-done((bf16[256,1024]{1,0:T(8,128)(2,1)S(1)}, bf16[256,1024]{1,0:T(8,128)(2,1)S(1)}, u32[]{:S(2)}, u32[]{:S(2)}) %collective-permute-start.45) | collective-permute-done | bytes 524320 | tf_op jit(solution)/shard_map/ppermute | solution.py:317
  404.8 23.1 %adam.1 = (f32[24,128,128]{2,1,0:T(8,128)}, f32[24,128,128]{2,1,0:T(8,128)}, f32[24,128,128]{2,1,0:T(8,128)}, f32[24,128,128]{2,1,0:T(8,128)}, f32[24,128,128]{2...) custom-call(f32[24]{0:T(128)S(1)} %compare_select_fusion.7.rates_ref, ...), custom_call_target="tpu_custom_call" | custom-call | tf_op jit(solution)/shard_map/adam/pallas_call | solution.py:107
  429.7 21.2 %renew.1 = (f32[24,128,128]{2,1,0:T(8,128)}, f32[24,128,128]{2,1,0:T(8,128)}) custom-call(f32[6144,128]{1,0:T(8,128)S(1)} %bitcast.142, f32[6144,128]{1,0:T(8,128)} %bitcast.170), custom_call_target="tpu_custom_call" | custom-call | tf_op jit(solution)/shard_map/renew/pallas_call | solution.py:219
  (470 shorter events, 188.9 us)
Async XLA Ops:
  6.9 13.3 %collective-permute-start.7 = (bf16[8,128,128]{2,1,0:T(8,128)(2,1)S(1)}, bf16[8,128,128]{2,1,0:T(8,128)(2,1)S(1)}, u32[]{:S(2)}, u32[]{:S(2)}) collective-permute-start(bf16[8,128,128]{2,1,0:T(8,128)(2,1)S(1)} %get-tuple-element.101.refs_1_), channel_id=1, source_target_pairs={{0,8},{4,12},{8,16},{12,20},{16,24},{20,28},{24,0},{28,4},{1,9},{5... | collective-permute-start | bytes 786440 | tf_op jit(solution)/shard_map/ppermute | solution.py:322
  8.5 20.1 %collective-permute-start = (bf16[256,1024]{1,0:T(8,128)(2,1)}, bf16[256,1024]{1,0:T(8,128)(2,1)}, u32[]{:S(2)}, u32[]{:S(2)}) collective-permute-start(bf16[256,1024]{1,0:T(8,128)(2,1)} %param.14), channel_id=1, source_target_pairs={{0,1},{1,0},{2,3},{3,2},{4,5},{5,4},{6,7},{7,6},{8,9},{9,8},{10,11... | collective-permute-start | bytes 1572872 | tf_op jit(solution)/shard_map/ppermute | solution.py:317
  8.5 20.8 %collective-permute-start.1 = (bf16[256,1024]{1,0:T(8,128)(2,1)}, bf16[256,1024]{1,0:T(8,128)(2,1)}, u32[]{:S(2)}, u32[]{:S(2)}) collective-permute-start(bf16[256,1024]{1,0:T(8,128)(2,1)} %param.14), channel_id=1, source_target_pairs={{0,2},{1,3},{2,0},{3,1},{4,6},{5,7},{6,4},{7,5},{8,10},{9,11},{10,... | collective-permute-start | bytes 1572872 | tf_op jit(solution)/shard_map/ppermute | solution.py:317
  29.2 14.8 %collective-permute-start.12 = (bf16[8,128,128]{2,1,0:T(8,128)(2,1)}, bf16[8,128,128]{2,1,0:T(8,128)(2,1)}, u32[]{:S(2)}, u32[]{:S(2)}) collective-permute-start(bf16[8,128,128]{2,1,0:T(8,128)(2,1)} %copy-done.12), channel_id=1, source_target_pairs={{0,8},{4,12},{8,16},{12,20},{16,24},{20,28},{24,0},{28,4},{1,9},{5... | collective-permute-start | bytes 786440 | tf_op jit(solution)/shard_map/ppermute | solution.py:322
  30.9 14.7 %collective-permute-start.9 = (bf16[8,128,128]{2,1,0:T(8,128)(2,1)}, bf16[8,128,128]{2,1,0:T(8,128)(2,1)S(1)}, u32[]{:S(2)}, u32[]{:S(2)}) collective-permute-start(bf16[8,128,128]{2,1,0:T(8,128)(2,1)} %copy-done.12), channel_id=1, source_target_pairs={{0,4},{4,0},{8,12},{12,8},{16,20},{20,16},{24,28},{28,24},{1,5},{5... | collective-permute-start | bytes 786440 | tf_op jit(solution)/shard_map/ppermute | solution.py:317
  35.1 25.2 %collective-permute-start.2 = (bf16[256,1024]{1,0:T(8,128)(2,1)}, bf16[256,1024]{1,0:T(8,128)(2,1)}, u32[]{:S(2)}, u32[]{:S(2)}) collective-permute-start(bf16[256,1024]{1,0:T(8,128)(2,1)} %collective-permute-done.1), channel_id=1, source_target_pairs={{0,1},{1,0},{2,3},{3,2},{4,5},{5,4},{6,7},{7,6},{8,9},{9,8},{10,11... | collective-permute-start | bytes 1572872 | tf_op jit(solution)/shard_map/ppermute | solution.py:317
  46.3 12.8 %collective-permute-start.18 = (bf16[8,128,128]{2,1,0:T(8,128)(2,1)}, bf16[8,128,128]{2,1,0:T(8,128)(2,1)}, u32[]{:S(2)}, u32[]{:S(2)}) collective-permute-start(bf16[8,128,128]{2,1,0:T(8,128)(2,1)} %collective-permute-done.12.refs_12_), channel_id=1, source_target_pairs={{0,8},{4,12},{8,16},{12,20},{16,24},{20,28},{24,0},{28,4},{1,9},{5... | collective-permute-start | bytes 786440 | tf_op jit(solution)/shard_map/ppermute | solution.py:322
  50.8 13.6 %collective-permute-start.16 = (bf16[8,128,128]{2,1,0:T(8,128)(2,1)}, bf16[8,128,128]{2,1,0:T(8,128)(2,1)S(1)}, u32[]{:S(2)}, u32[]{:S(2)}) collective-permute-start(bf16[8,128,128]{2,1,0:T(8,128)(2,1)} %collective-permute-done.13.refs_13_), channel_id=1, source_target_pairs={{0,4},{4,0},{8,12},{12,8},{16,20},{20,16},{24,28},{28,24},{1,5},{5... | collective-permute-start | bytes 786440 | tf_op jit(solution)/shard_map/ppermute | solution.py:317
  51.8 14.1 %collective-permute-start.15 = (bf16[8,128,128]{2,1,0:T(8,128)(2,1)}, bf16[8,128,128]{2,1,0:T(8,128)(2,1)S(1)}, u32[]{:S(2)}, u32[]{:S(2)}) collective-permute-start(bf16[8,128,128]{2,1,0:T(8,128)(2,1)} %collective-permute-done.12.refs_12_), channel_id=1, source_target_pairs={{0,4},{4,0},{8,12},{12,8},{16,20},{20,16},{24,28},{28,24},{1,5},{5... | collective-permute-start | bytes 786440 | tf_op jit(solution)/shard_map/ppermute | solution.py:317
  56.3 15.2 %collective-permute-start.23 = (bf16[8,128,128]{2,1,0:T(8,128)(2,1)}, bf16[8,128,128]{2,1,0:T(8,128)(2,1)S(1)}, u32[]{:S(2)}, u32[]{:S(2)}) collective-permute-start(bf16[8,128,128]{2,1,0:T(8,128)(2,1)} %collective-permute-done.20.refs_20_), channel_id=1, source_target_pairs={{0,4},{4,0},{8,12},{12,8},{16,20},{20,16},{24,28},{28,24},{1,5},{5... | collective-permute-start | bytes 786440 | tf_op jit(solution)/shard_map/ppermute | solution.py:317
  59.1 15.5 %collective-permute-start.22 = (bf16[8,128,128]{2,1,0:T(8,128)(2,1)}, bf16[8,128,128]{2,1,0:T(8,128)(2,1)S(1)}, u32[]{:S(2)}, u32[]{:S(2)}) collective-permute-start(bf16[8,128,128]{2,1,0:T(8,128)(2,1)} %collective-permute-done.19.refs_19_), channel_id=1, source_target_pairs={{0,4},{4,0},{8,12},{12,8},{16,20},{20,16},{24,28},{28,24},{1,5},{5... | collective-permute-start | bytes 786440 | tf_op jit(solution)/shard_map/ppermute | solution.py:317
  60.3 17.1 %collective-permute-start.21 = (bf16[8,128,128]{2,1,0:T(8,128)(2,1)}, bf16[8,128,128]{2,1,0:T(8,128)(2,1)S(1)}, u32[]{:S(2)}, u32[]{:S(2)}) collective-permute-start(bf16[8,128,128]{2,1,0:T(8,128)(2,1)} %collective-permute-done.18.refs_18_), channel_id=1, source_target_pairs={{0,4},{4,0},{8,12},{12,8},{16,20},{20,16},{24,28},{28,24},{1,5},{5... | collective-permute-start | bytes 786440 | tf_op jit(solution)/shard_map/ppermute | solution.py:317
  103.0 14.0 %collective-permute-start.26 = (bf16[256,1024]{1,0:T(8,128)(2,1)S(1)}, bf16[256,1024]{1,0:T(8,128)(2,1)}, u32[]{:S(2)}, u32[]{:S(2)}) collective-permute-start(bf16[256,1024]{1,0:T(8,128)(2,1)S(1)} %fusion.48), channel_id=1, source_target_pairs={{0,2},{1,3},{2,0},{3,1},{4,6},{5,7},{6,4},{7,5},{8,10},{9,11},{10,... | collective-permute-start | bytes 1572872 | tf_op jit(solution)/shard_map/ppermute | solution.py:317
  119.1 13.1 %collective-permute-start.29 = (bf16[256,1024]{1,0:T(8,128)(2,1)S(1)}, bf16[256,1024]{1,0:T(8,128)(2,1)S(1)}, u32[]{:S(2)}, u32[]{:S(2)}) collective-permute-start(bf16[256,1024]{1,0:T(8,128)(2,1)S(1)} %get-tuple-element.78), channel_id=1, source_target_pairs={{0,2},{1,3},{2,0},{3,1},{4,6},{5,7},{6,4},{7,5},{8,10},{9,11},{10,... | collective-permute-start | bytes 1572872 | tf_op jit(solution)/shard_map/ppermute | solution.py:317
  153.0 14.8 %collective-permute-start.35 = (bf16[256,1024]{1,0:T(8,128)(2,1)S(1)}, bf16[256,1024]{1,0:T(8,128)(2,1)S(1)}, u32[]{:S(2)}, u32[]{:S(2)}) collective-permute-start(bf16[256,1024]{1,0:T(8,128)(2,1)S(1)} %fusion.47), channel_id=1, source_target_pairs={{0,2},{1,3},{2,0},{3,1},{4,6},{5,7},{6,4},{7,5},{8,10},{9,11},{10,... | collective-permute-start | bytes 1572872 | tf_op jit(solution)/shard_map/ppermute | solution.py:317
  154.5 35.8 %collective-permute-start.36 = (bf16[256,1024]{1,0:T(8,128)(2,1)S(1)}, bf16[256,1024]{1,0:T(8,128)(2,1)S(1)}, u32[]{:S(2)}, u32[]{:S(2)}) collective-permute-start(bf16[256,1024]{1,0:T(8,128)(2,1)S(1)} %copy-done.44), channel_id=1, source_target_pairs={{0,2},{1,3},{2,0},{3,1},{4,6},{5,7},{6,4},{7,5},{8,10},{9,11},{10,... | collective-permute-start | bytes 1572872 | tf_op jit(solution)/shard_map/ppermute | solution.py:317
  168.4 21.1 %collective-permute-start.32 = (bf16[256,1024]{1,0:T(8,128)(2,1)S(1)}, bf16[256,1024]{1,0:T(8,128)(2,1)S(1)}, u32[]{:S(2)}, u32[]{:S(2)}) collective-permute-start(bf16[256,1024]{1,0:T(8,128)(2,1)S(1)} %get-tuple-element.71), channel_id=1, source_target_pairs={{0,2},{1,3},{2,0},{3,1},{4,6},{5,7},{6,4},{7,5},{8,10},{9,11},{10,... | collective-permute-start | bytes 1572872 | tf_op jit(solution)/shard_map/ppermute | solution.py:317
  212.3 13.5 %collective-permute-start.38 = (bf16[256,1024]{1,0:T(8,128)(2,1)}, bf16[256,1024]{1,0:T(8,128)(2,1)}, u32[]{:S(2)}, u32[]{:S(2)}) collective-permute-start(bf16[256,1024]{1,0:T(8,128)(2,1)} %slice.340), channel_id=1, source_target_pairs={{0,1},{1,0},{2,3},{3,2},{4,5},{5,4},{6,7},{7,6},{8,9},{9,8},{10,11... | collective-permute-start | bytes 1572872 | tf_op jit(solution)/shard_map/ppermute | solution.py:317
  215.7 13.9 %collective-permute-start.41 = (bf16[256,1024]{1,0:T(8,128)(2,1)S(1)}, bf16[256,1024]{1,0:T(8,128)(2,1)S(1)}, u32[]{:S(2)}, u32[]{:S(2)}) collective-permute-start(bf16[256,1024]{1,0:T(8,128)(2,1)S(1)} %fusion.45), channel_id=1, source_target_pairs={{0,2},{1,3},{2,0},{3,1},{4,6},{5,7},{6,4},{7,5},{8,10},{9,11},{10,... | collective-permute-start | bytes 1572872 | tf_op jit(solution)/shard_map/ppermute | solution.py:317
  231.8 13.1 %collective-permute-start.39 = (bf16[256,1024]{1,0:T(8,128)(2,1)S(1)}, bf16[256,1024]{1,0:T(8,128)(2,1)S(1)}, u32[]{:S(2)}, u32[]{:S(2)}) collective-permute-start(bf16[256,1024]{1,0:T(8,128)(2,1)S(1)} %get-tuple-element.67), channel_id=1, source_target_pairs={{0,2},{1,3},{2,0},{3,1},{4,6},{5,7},{6,4},{7,5},{8,10},{9,11},{10,... | collective-permute-start | bytes 1572872 | tf_op jit(solution)/shard_map/ppermute | solution.py:317
  233.7 14.6 %collective-permute-start.42 = (bf16[256,1024]{1,0:T(8,128)(2,1)S(1)}, bf16[256,1024]{1,0:T(8,128)(2,1)S(1)}, u32[]{:S(2)}, u32[]{:S(2)}) collective-permute-start(bf16[256,1024]{1,0:T(8,128)(2,1)S(1)} %multiply_convert_fusion.4), channel_id=1, source_target_pairs={{0,1},{1,0},{2,3},{3,2},{4,5},{5,4},{6,7},{7,6},{8,9},{9,8},{10,11... | collective-permute-start | bytes 1572872 | tf_op jit(solution)/shard_map/ppermute | solution.py:317
  310.3 18.9 %collective-permute-start.48 = (bf16[12,128,128]{2,1,0:T(8,128)(2,1)S(1)}, bf16[12,128,128]{2,1,0:T(8,128)(2,1)S(1)}, u32[]{:S(2)}, u32[]{:S(2)}) collective-permute-start(bf16[12,128,128]{2,1,0:T(8,128)(2,1)S(1)} %get-tuple-element.91), channel_id=1, source_target_pairs={{0,4},{4,0},{8,12},{12,8},{16,20},{20,16},{24,28},{28,24},{1,5},{5... | collective-permute-start | bytes 1179656 | tf_op jit(solution)/shard_map/ppermute | solution.py:317
  322.4 16.6 %collective-permute-start.47 = (bf16[12,128,128]{2,1,0:T(8,128)(2,1)S(1)}, bf16[12,128,128]{2,1,0:T(8,128)(2,1)S(1)}, u32[]{:S(2)}, u32[]{:S(2)}) collective-permute-start(bf16[12,128,128]{2,1,0:T(8,128)(2,1)S(1)} %get-tuple-element.92), channel_id=1, source_target_pairs={{0,4},{4,0},{8,12},{12,8},{16,20},{20,16},{24,28},{28,24},{1,5},{5... | collective-permute-start | bytes 1179656 | tf_op jit(solution)/shard_map/ppermute | solution.py:317
  335.5 16.2 %collective-permute-start.46 = (bf16[12,128,128]{2,1,0:T(8,128)(2,1)S(1)}, bf16[12,128,128]{2,1,0:T(8,128)(2,1)S(1)}, u32[]{:S(2)}, u32[]{:S(2)}) collective-permute-start(bf16[12,128,128]{2,1,0:T(8,128)(2,1)S(1)} %get-tuple-element.85), channel_id=1, source_target_pairs={{0,4},{4,0},{8,12},{12,8},{16,20},{20,16},{24,28},{28,24},{1,5},{5... | collective-permute-start | bytes 1179656 | tf_op jit(solution)/shard_map/ppermute | solution.py:317
  337.0 19.0 %collective-permute-start.56 = (bf16[12,128,128]{2,1,0:T(8,128)(2,1)S(1)}, bf16[12,128,128]{2,1,0:T(8,128)(2,1)S(1)}, u32[]{:S(2)}, u32[]{:S(2)}) collective-permute-start(bf16[12,128,128]{2,1,0:T(8,128)(2,1)S(1)} %get-tuple-element.86), channel_id=1, source_target_pairs={{0,4},{4,0},{8,12},{12,8},{16,20},{20,16},{24,28},{28,24},{1,5},{5... | collective-permute-start | bytes 1179656 | tf_op jit(solution)/shard_map/ppermute | solution.py:317
  337.5 30.9 %collective-permute-start.55 = (bf16[12,128,128]{2,1,0:T(8,128)(2,1)}, bf16[12,128,128]{2,1,0:T(8,128)(2,1)}, u32[]{:S(2)}, u32[]{:S(2)}) collective-permute-start(bf16[12,128,128]{2,1,0:T(8,128)(2,1)} %get-tuple-element.87), channel_id=1, source_target_pairs={{0,4},{4,0},{8,12},{12,8},{16,20},{20,16},{24,28},{28,24},{1,5},{5... | collective-permute-start | bytes 1179656 | tf_op jit(solution)/shard_map/ppermute | solution.py:317
  360.3 23.9 %collective-permute-start.44 = (bf16[256,1024]{1,0:T(8,128)(2,1)S(1)}, bf16[256,1024]{1,0:T(8,128)(2,1)S(1)}, u32[]{:S(2)}, u32[]{:S(2)}) collective-permute-start(bf16[256,1024]{1,0:T(8,128)(2,1)S(1)} %get-tuple-element.94), channel_id=1, source_target_pairs={{0,1},{1,0},{2,3},{3,2},{4,5},{5,4},{6,7},{7,6},{8,9},{9,8},{10,11... | collective-permute-start | bytes 1572872 | tf_op jit(solution)/shard_map/ppermute | solution.py:317
  364.3 21.8 %collective-permute-start.54 = (bf16[12,128,128]{2,1,0:T(8,128)(2,1)S(1)}, bf16[12,128,128]{2,1,0:T(8,128)(2,1)S(1)}, u32[]{:S(2)}, u32[]{:S(2)}) collective-permute-start(bf16[12,128,128]{2,1,0:T(8,128)(2,1)S(1)} %get-tuple-element.88), channel_id=1, source_target_pairs={{0,4},{4,0},{8,12},{12,8},{16,20},{20,16},{24,28},{28,24},{1,5},{5... | collective-permute-start | bytes 1179656 | tf_op jit(solution)/shard_map/ppermute | solution.py:317
  372.2 15.5 %collective-permute-start.58 = (bf16[12,128,128]{2,1,0:T(8,128)(2,1)}, bf16[12,128,128]{2,1,0:T(8,128)(2,1)}, u32[]{:S(2)}, u32[]{:S(2)}) collective-permute-start(bf16[12,128,128]{2,1,0:T(8,128)(2,1)} %fusion.84), channel_id=1, source_target_pairs={{0,8},{4,12},{8,16},{12,20},{16,24},{20,28},{24,0},{28,4},{1,9},{5... | collective-permute-start | bytes 1179656 | tf_op jit(solution)/shard_map/ppermute | solution.py:322
  376.7 26.1 %collective-permute-start.53 = (bf16[12,128,128]{2,1,0:T(8,128)(2,1)S(1)}, bf16[12,128,128]{2,1,0:T(8,128)(2,1)S(1)}, u32[]{:S(2)}, u32[]{:S(2)}) collective-permute-start(bf16[12,128,128]{2,1,0:T(8,128)(2,1)S(1)} %get-tuple-element.89), channel_id=1, source_target_pairs={{0,4},{4,0},{8,12},{12,8},{16,20},{20,16},{24,28},{28,24},{1,5},{5... | collective-permute-start | bytes 1179656 | tf_op jit(solution)/shard_map/ppermute | solution.py:317
  386.1 14.1 %collective-permute-start.45 = (bf16[256,1024]{1,0:T(8,128)(2,1)S(1)}, bf16[256,1024]{1,0:T(8,128)(2,1)S(1)}, u32[]{:S(2)}, u32[]{:S(2)}) collective-permute-start(bf16[256,1024]{1,0:T(8,128)(2,1)S(1)} %fusion.40), channel_id=1, source_target_pairs={{0,2},{1,3},{2,0},{3,1},{4,6},{5,7},{6,4},{7,5},{8,10},{9,11},{10,... | collective-permute-start | bytes 1572872 | tf_op jit(solution)/shard_map/ppermute | solution.py:317
  389.0 13.8 %collective-permute-start.59 = (bf16[12,128,128]{2,1,0:T(8,128)(2,1)S(1)}, bf16[12,128,128]{2,1,0:T(8,128)(2,1)S(1)}, u32[]{:S(2)}, u32[]{:S(2)}) collective-permute-start(bf16[12,128,128]{2,1,0:T(8,128)(2,1)S(1)} %fusion.86), channel_id=1, source_target_pairs={{0,8},{4,12},{8,16},{12,20},{16,24},{20,28},{24,0},{28,4},{1,9},{5... | collective-permute-start | bytes 1179656 | tf_op jit(solution)/shard_map/ppermute | solution.py:322
  (149 other events, 1552.8 us)

commit v4 on v3

--- a/solution.py
+++ b/solution.py
@@ -228,62 +228,536 @@
     )(gram.reshape(count * BLK, BLK), product.reshape(count * BLK, BLK))
 
 
+def whole_spec():
+    return pl.BlockSpec(memory_space=pltpu.VMEM)
+
+
+def fixed(shape):
+    return pl.BlockSpec(shape, lambda *_: (0,) * len(shape))
+
+
+def anywhere():
+    return pl.BlockSpec(memory_space=pl.ANY)
+
+
+def cost(flops, *arrays):
+    moved = sum(math.prod(a.shape) * jnp.dtype(a.dtype).itemsize for a in arrays)
+    return pl.CostEstimate(flops=flops // 16, bytes_accessed=moved // 16, transcendentals=0)
+
+
+def of(shape, dtype):
+    return jax.ShapeDtypeStruct(shape, dtype)
+
+
+def flip_rows(value):
+    return value.astype(single).T.astype(bfloat)
+
+
+def attend_kernel(q_ref, k_ref, v_ref, valid_ref, w_ref, *refs, heads, own):
+    attended_ref, lse_ref, branch_ref, flipped_ref, score_ref, prob_ref = refs[-6:]
+    keys, width = k_ref.shape
+    rows = q_ref.shape[0]
+    tile = 128
+
+    flipped_ref[...] = flip_rows(v_ref[...])
+    queries = flip_rows(q_ref[...]) * (HEAD_DIM ** (-0.5))
+    queries = queries.astype(bfloat)
+    head_of = lax.broadcasted_iota(jnp.int32, (width, rows), 0) // HEAD_DIM
+    mixed = []
+    for head in range(heads):
+        score_ref[...] = dot_of(
+            k_ref[...], jnp.where(head_of == head, queries, jnp.zeros_like(queries)), 1, 0
+        )
+
+        def masked(index):
+            here = pl.ds(pl.multiple_of(index * tile, tile), tile)
+            valid = valid_ref[here, :]
+            valid = jnp.concatenate([valid] * (rows // 128), 1)
+            return here, jnp.where(valid > 0.0, score_ref[here, :], masked_score)
+
+        def highest_of(index, best):
+            _, value = masked(index)
+            return jnp.maximum(best, jnp.max(value.reshape(tile // 8, 8, rows), 0))
+
+        best = lax.fori_loop(
+            0, keys // tile, highest_of, jnp.full((8, rows), -jnp.inf, single), unroll=True
+        )
+        best = jnp.max(best, 0, keepdims=True)
+
+        def weigh(index, total):
+            here, value = masked(index)
+            value = jnp.exp(value - best)
+            prob_ref[here, :] = value.astype(bfloat)
+            return total + jnp.sum(value.reshape(tile // 8, 8, rows), 0)
+
+        total = lax.fori_loop(
+            0, keys // tile, weigh, jnp.zeros((8, rows), single), unroll=True
+        )
+        total = jnp.sum(total, 0, keepdims=True)
+        out = dot_of(
+            flipped_ref[head * HEAD_DIM : (head + 1) * HEAD_DIM, :], prob_ref[...], 1, 0
+        )
+        mixed.append(out * (1.0 / total))
+        lse_ref[head : head + 1, :] = best + jnp.log(total)
+    attended = jnp.concatenate(mixed, 0).T.astype(bfloat)
+    attended_ref[...] = attended
+    branch = dot_of(attended, w_ref[...], 1, 0)
+    if own:
+        branch = branch + refs[0][...].astype(single)
+    branch_ref[...] = branch.astype(bfloat)
+
+
+def attend(projected, valid, w_out, block, received=None, after=()):
+    seq, width = projected.shape[0], w_out.shape[0]
+    rows = seq // 4
+    heads = width // HEAD_DIM
+    own = received is not None
+    more = [received] if own else []
+    out_shape = [of((rows, width), bfloat), of((heads, rows), single), of((rows, D), bfloat)]
+    return pl.pallas_call(
+        functools.partial(attend_kernel, heads=heads, own=own),
+        grid=(1,),
+        in_specs=[
+            pl.BlockSpec((rows, width), lambda i: (block, 0)),
+            pl.BlockSpec((seq, width), lambda i: (0, 1)),
+            pl.BlockSpec((seq, width), lambda i: (0, 2)),
+            fixed(valid.shape),
+            fixed(w_out.shape),
+        ] + [fixed(value.shape) for value in more] + [anywhere()] * len(after),
+        out_specs=[fixed(value.shape) for value in out_shape],
+        out_shape=out_shape,
+        scratch_shapes=[
+            pltpu.VMEM((width, seq), bfloat), pltpu.VMEM((seq, rows), single),
+            pltpu.VMEM((seq, rows), bfloat),
+        ],
+        cost_estimate=cost(2 * 2 * rows * seq * width * heads, projected, *out_shape),
+        compiler_params=pltpu.CompilerParams(vmem_limit_bytes=24 * 2**20),
+        name="attend",
+    )(projected, projected, projected, valid, w_out, *more, *after)
+
+
+def attend_back_kernel(*refs, heads, first, extra):
+    inputs = 11 if first else 13
+    refs = refs[:inputs] + refs[inputs + extra :]
+    if first:
+        (own_ref, peer_ref, w_ref, q_ref, k_ref, v_ref, att_own, att_peer, lse_own, lse_peer,
+         valid_ref, dq_ref, dk_ref, dv_ref, flipped_ref, grad_ref, score_ref, cross_ref, prob_ref, back_ref,
+         att_ref, log_ref, dk_sum, dv_sum) = refs
+    else:
+        (own_ref, peer_ref, w_ref, q_ref, k_ref, v_ref, att_own, att_peer, lse_own, lse_peer,
+         valid_ref, dk_in_ref, dv_in_ref, dq_ref, dk_ref, dv_ref, flipped_ref, grad_ref, score_ref,
+         cross_ref, prob_ref, back_ref, att_ref, log_ref, dk_sum, dv_sum) = refs
+    step = pl.program_id(0)
+    keys, width = k_ref.shape
+    rows = q_ref.shape[0]
+    scale = HEAD_DIM ** (-0.5)
+    tile = 128
+
+    @pl.when(step == 0)
+    def _():
+        flipped_ref[...] = flip_rows(k_ref[...])
+        grad_ref[...] = own_ref[...]
+        att_ref[...] = att_own[...]
+        log_ref[...] = lse_own[...]
+        if first:
+            dk_sum[...] = jnp.zeros_like(dk_sum)
+            dv_sum[...] = jnp.zeros_like(dv_sum)
+        else:
+            dk_sum[...] = dk_in_ref[...]
+            dv_sum[...] = dv_in_ref[...]
+
+    @pl.when(step == 1)
+    def _():
+        grad_ref[...] = peer_ref[...]
+        att_ref[...] = att_peer[...]
+        log_ref[...] = lse_peer[...]
+
+    grads = dot_of(grad_ref[...], w_ref[...], 1, 1).astype(bfloat)
+    flat = grads.astype(single).T
+    cross = flat * att_ref[...].astype(single).T
+    grads_t = flat.astype(bfloat)
+    queries = q_ref[...]
+    queries_t = (flip_rows(queries) * scale).astype(bfloat)
+    head_of = lax.broadcasted_iota(jnp.int32, (width, rows), 0) // HEAD_DIM
+    none = jnp.zeros_like(grads_t)
+    dq = []
+    for head in range(heads):
+        score_ref[...] = dot_of(k_ref[...], jnp.where(head_of == head, queries_t, none), 1, 0)
+        cross_ref[...] = dot_of(v_ref[...], jnp.where(head_of == head, grads_t, none), 1, 0)
+        lse = log_ref[head : head + 1, :]
+        mean = jnp.sum(cross[head * HEAD_DIM : (head + 1) * HEAD_DIM], 0, keepdims=True)
+        at = slice(head * rows, (head + 1) * rows)
+
+        def weigh(index, nothing):
+            here = pl.ds(pl.multiple_of(index * tile, tile), tile)
+            valid = jnp.concatenate([valid_ref[here, :]] * (rows // 128), 1)
+            value = jnp.where(valid > 0.0, score_ref[here, :], masked_score)
+            prob = jnp.exp(value - lse)
+            prob_ref[here, at] = prob.astype(bfloat)
+            back_ref[here, at] = (prob * (cross_ref[here, :] - mean)).astype(bfloat)
+            return nothing
+
+        lax.fori_loop(0, keys // tile, weigh, 0, unroll=True)
+        dq.append(
+            dot_of(flipped_ref[head * HEAD_DIM : (head + 1) * HEAD_DIM, :], back_ref[:, at], 1, 0)
+        )
+    dq_ref[...] = (jnp.concatenate(dq, 0).T * scale).astype(bfloat)
+    lane_head = lax.broadcasted_iota(jnp.int32, (rows, width), 1) // HEAD_DIM
+    query_rows = jnp.concatenate(
+        [jnp.where(lane_head == head, queries, jnp.zeros_like(queries)) for head in range(heads)], 0
+    )
+    grad_rows = jnp.concatenate(
+        [jnp.where(lane_head == head, grads, jnp.zeros_like(grads)) for head in range(heads)], 0
+    )
+
+    def total(index, nothing):
+        here = pl.ds(pl.multiple_of(index * 256, 256), 256)
+        dk_sum[here, :] = dk_sum[here, :] + dot_of(back_ref[here, :], query_rows, 1, 0) * scale
+        dv_sum[here, :] = dv_sum[here, :] + dot_of(prob_ref[here, :], grad_rows, 1, 0)
+        return nothing
+
+    lax.fori_loop(0, keys // 256, total, 0, unroll=True)
+
+    @pl.when(step == 1)
+    def _():
+        dk_ref[...] = dk_sum[...].astype(dk_ref.dtype)
+        dv_ref[...] = dv_sum[...].astype(dv_ref.dtype)
+
+
+def attend_back(own, peer, w_out, projected, attended, lse, valid, part, earlier=None, after=()):
+    seq, width = projected.shape[0], w_out.shape[0]
+    rows = seq // 4
+    heads = width // HEAD_DIM
+    first = earlier is None
+    kind = single if first else bfloat
+    more = [] if first else list(earlier)
+    out_shape = [of((2 * rows, width), bfloat), of((seq, width), kind), of((seq, width), kind)]
+    return pl.pallas_call(
+        functools.partial(attend_back_kernel, heads=heads, first=first, extra=len(after)),
+        grid=(2,),
+        in_specs=[
+            fixed(own.shape), fixed(peer.shape), fixed(w_out.shape),
+            pl.BlockSpec((rows, width), lambda i: (2 * part + i, 0)),
+            pl.BlockSpec((seq, width), lambda i: (0, 1)),
+            pl.BlockSpec((seq, width), lambda i: (0, 2)),
+            fixed((rows, width)), fixed((rows, width)), fixed((heads, rows)), fixed((heads, rows)),
+            fixed(valid.shape),
+        ] + [fixed((seq, width))] * len(more) + [anywhere()] * len(after),
+        out_specs=[
+            pl.BlockSpec((rows, width), lambda i: (i, 0)),
+            fixed((seq, width)), fixed((seq, width)),
+        ],
+        out_shape=out_shape,
+        scratch_shapes=[
+            pltpu.VMEM((width, seq), bfloat), pltpu.VMEM((rows, D), bfloat),
+            pltpu.VMEM((seq, rows), single), pltpu.VMEM((seq, rows), single),
+            pltpu.VMEM((seq, heads * rows), bfloat), pltpu.VMEM((seq, heads * rows), bfloat),
+            pltpu.VMEM((rows, width), bfloat), pltpu.VMEM((heads, rows), single),
+            pltpu.VMEM((seq, width), single), pltpu.VMEM((seq, width), single),
+        ],
+        cost_estimate=cost(2 * 2 * rows * seq * width * 5 * heads, projected, *out_shape),
+        compiler_params=pltpu.CompilerParams(vmem_limit_bytes=32 * 2**20),
+        name="attend_back",
+    )(own, peer, w_out, projected, projected, projected, *attended, *lse, valid, *more, *after)
+
+
+def gelu_pair(value):
+    size = jnp.abs(value)
+    ratio = 1.0 / (1.0 + (0.3275911 * 0.5**0.5) * size)
+    bell = jnp.exp(-0.5 * value * value)
+    series = 0.5 * 1.061405429 * ratio + 0.5 * -1.453152027
+    series = series * ratio + 0.5 * 1.421413741
+    series = series * ratio + 0.5 * -0.284496736
+    series = series * ratio + 0.5 * 0.254829592
+    tail = series * ratio * bell
+    below = jnp.where(value >= 0.0, 1.0 - tail, tail)
+    return value * below, below + value * bell * (1.0 / math.sqrt(2.0 * math.pi))
+
+
+def feed_kernel(rows_ref, up_ref, bias_ref, down_ref, *refs):
+    act_ref, slope_ref, out_ref, pre_ref, sum_ref = refs[-5:]
+    step = pl.program_id(0)
+    rows = rows_ref.shape[0]
+    tile = 32
+    pre_ref[...] = dot_of(rows_ref[...], up_ref[...], 1, 0)
+
+    def activate(index, nothing):
+        here = pl.ds(pl.multiple_of(index * tile, tile), tile)
+        value, slope = gelu_pair(pre_ref[here, :] + bias_ref[...])
+        act_ref[here, :] = value.astype(bfloat)
+        slope_ref[here, :] = slope.astype(bfloat)
+        return nothing
+
+    lax.fori_loop(0, rows // tile, activate, 0, unroll=4)
+    add_up(step, dot_of(act_ref[...], down_ref[...], 1, 0), sum_ref, out_ref)
+
+
+def add_up(step, more, sum_ref, out_ref):
+    last = pl.num_programs(0) - 1
+
+    @pl.when(step == 0)
+    def _():
+        sum_ref[...] = more
+
+    @pl.when((step > 0) & (step < last))
+    def _():
+        sum_ref[...] = sum_ref[...] + more
+
+    @pl.when(step == last)
+    def _():
+        out_ref[...] = (sum_ref[...] + more).astype(out_ref.dtype)
+
+
+def feed(block, w_up, bias, w_down, kind, after=()):
+    rows, hidden = block.shape[0], w_up.shape[1]
+    step = 256
+    out_shape = [of((rows, hidden), bfloat), of((rows, hidden), bfloat), of((rows, D), kind)]
+    return pl.pallas_call(
+        feed_kernel,
+        grid=(hidden // step,),
+        in_specs=[
+            fixed(block.shape),
+            pl.BlockSpec((D, step), lambda j: (0, j)),
+            pl.BlockSpec((1, step), lambda j: (0, j)),
+            pl.BlockSpec((step, D), lambda j: (j, 0)),
+        ] + [anywhere()] * len(after),
+        out_specs=[
+            pl.BlockSpec((rows, step), lambda j: (0, j)),
+            pl.BlockSpec((rows, step), lambda j: (0, j)),
+            fixed((rows, D)),
+        ],
+        out_shape=out_shape,
+        scratch_shapes=[pltpu.VMEM((rows, step), single), pltpu.VMEM((rows, D), single)],
+        cost_estimate=cost(4 * rows * D * hidden, w_up, w_down, *out_shape),
+        compiler_params=pltpu.CompilerParams(vmem_limit_bytes=20 * 2**20),
+        name="feed",
+    )(block, w_up, bias, w_down, *after)
+
+
+def feed_back_kernel(rows_ref, down_ref, up_ref, slope_ref, *refs):
+    grad_ref, bias_ref, out_ref, sum_ref = refs[-4:]
+    grads = dot_of(rows_ref[...], down_ref[...], 1, 1) * slope_ref[...].astype(single)
+    grads = grads.astype(bfloat)
+    grad_ref[...] = grads
+    bias_ref[...] = jnp.sum(grads.astype(single), 0, keepdims=True)
+    add_up(pl.program_id(0), dot_of(grads, up_ref[...], 1, 1), sum_ref, out_ref)
+
+
+def feed_back(block, w_down, w_up, slope, kind, after=()):
+    rows, hidden = block.shape[0], w_up.shape[1]
+    step = 256
+    out_shape = [of((rows, hidden), bfloat), of((1, hidden), single), of((rows, D), kind)]
+    return pl.pallas_call(
+        feed_back_kernel,
+        grid=(hidden // step,),
+        in_specs=[
+            fixed(block.shape),
+            pl.BlockSpec((step, D), lambda j: (j, 0)),
+            pl.BlockSpec((D, step), lambda j: (0, j)),
+            pl.BlockSpec((rows, step), lambda j: (0, j)),
+        ] + [anywhere()] * len(after),
+        out_specs=[
+            pl.BlockSpec((rows, step), lambda j: (0, j)),
+            pl.BlockSpec((1, step), lambda j: (0, j)),
+            fixed((rows, D)),
+        ],
+        out_shape=out_shape,
+        scratch_shapes=[pltpu.VMEM((rows, D), single)],
+        cost_estimate=cost(4 * rows * D * hidden, w_up, w_down, *out_shape),
+        compiler_params=pltpu.CompilerParams(vmem_limit_bytes=20 * 2**20),
+        name="feed_back",
+    )(block, w_down, w_up, slope, *after)
+
+
+def chip_kernel(keep_ref, got_ref, *refs):
+    refs[-1][...] = (keep_ref[...] + got_ref[...].astype(single)).astype(bfloat)
+
+
+def standardise(value):
+    centred = value - jnp.mean(value, -1, keepdims=True)
+    inv_std = lax.rsqrt(jnp.mean(centred * centred, -1, keepdims=True) + norm_eps)
+    return centred * inv_std, inv_std
+
+
+def through_norm(grads, normed, inv_std, gain):
+    scaled = grads * gain
+    mean_grad = jnp.mean(scaled, -1, keepdims=True)
+    mean_cross = jnp.mean(scaled * normed, -1, keepdims=True)
+    return inv_std * (scaled - mean_grad - normed * mean_cross)
+
+
+def gain_sums(grads, normed, rounded):
+    total = lambda value: jnp.sum(value, 0, keepdims=True)
+    blank = jnp.zeros((5, grads.shape[1]), single)
+    return jnp.concatenate(
+        [total(grads * normed), total(grads), total(rounded.astype(single)), blank], 0
+    )
+
+
+norm_tile = 64
+
+
+def norm_one_kernel(chip_ref, across_ref, rows_ref, vectors_ref, *refs):
+    normed_ref, inv_ref, hidden_ref = refs[-3:]
+    branch = chip_ref[...].astype(single) + across_ref[...].astype(single)
+    normed, inv_std = standardise(rows_ref[...].astype(single) + (branch + vectors_ref[2:3, :]))
+    normed_ref[...] = normed
+    inv_ref[...] = jnp.broadcast_to(inv_std, inv_ref.shape)
+    hidden_ref[...] = (normed * vectors_ref[0:1, :] + vectors_ref[1:2, :]).astype(bfloat)
+
+
+def norm_two_kernel(
+    chip_ref, across_ref, normed_ref, cot_ref, valid_ref, one_ref, two_ref, *refs
+):
+    out_ref, grad_ref, low_ref, sums_ref = refs[-4:]
+
+    @pl.when(pl.program_id(0) == 0)
+    def _():
+        sums_ref[...] = jnp.zeros_like(sums_ref)
+
+    hidden = normed_ref[...] * one_ref[0:1, :] + one_ref[1:2, :]
+    down = chip_ref[...].astype(single) + across_ref[...].astype(single)
+    normed, inv_std = standardise(hidden + (down + two_ref[2:3, :]))
+    gain = two_ref[0:1, :]
+    out_ref[...] = (normed * gain + two_ref[1:2, :]).astype(bfloat)
+    grads = cot_ref[...].astype(single) * valid_ref[:, 0:1]
+    back = through_norm(grads, normed, inv_std, gain)
+    grad_ref[...] = back
+    low = back.astype(bfloat)
+    low_ref[...] = low
+    sums_ref[...] += gain_sums(grads, normed, low)
+
+
+def norm_back_kernel(
+    chip_ref, across_ref, second_ref, normed_ref, inv_ref, one_ref, *refs
+):
+    grad_ref, low_ref, sums_ref = refs[-3:]
+
+    @pl.when(pl.program_id(0) == 0)
+    def _():
+        sums_ref[...] = jnp.zeros_like(sums_ref)
+
+    grads = chip_ref[...].astype(single) + across_ref[...].astype(single) + second_ref[...]
+    normed = normed_ref[...]
+    back = through_norm(grads, normed, inv_ref[:, 0:1], one_ref[0:1, :])
+    grad_ref[...] = back
+    low = back.astype(bfloat)
+    low_ref[...] = low
+    sums_ref[...] += gain_sums(grads, normed, low)
+
+
+def norm_call(kernel, name, rowed, fixed_in, row_outs, sums, after=()):
+    rows = rowed[0].shape[0]
+    by_row = lambda width: pl.BlockSpec((norm_tile, width), lambda i: (i, 0))
+    out_shape = [of((rows, width), kind) for width, kind in row_outs]
+    out_specs = [by_row(width) for width, _ in row_outs]
+    if sums:
+        out_shape.append(of((8, D), single))
+        out_specs.append(fixed((8, D)))
+    return pl.pallas_call(
+        kernel,
+        grid=(rows // norm_tile,),
+        in_specs=[by_row(value.shape[1]) for value in rowed]
+        + [fixed(value.shape) for value in fixed_in]
+        + [anywhere()] * len(after),
+        out_specs=out_specs,
+        out_shape=out_shape,
+        cost_estimate=cost(20 * rows * D, *rowed, *out_shape),
+        compiler_params=pltpu.CompilerParams(vmem_limit_bytes=16 * 2**20),
+        name=name,
+    )(*rowed, *fixed_in, *after)
+
+
+def token_back_kernel(*refs):
+    dq_refs, (dk_ref, dv_ref, w_ref), outs = refs[:2], refs[2:5], refs[5:]
+    width = dk_ref.shape[1]
+    rows = dk_ref.shape[0] // 4
+    for block in range(4):
+        here = slice(block * rows, (block + 1) * rows)
+        parts = [
+            dq_refs[block // 2][block % 2 * rows : (block % 2 + 1) * rows, :],
+            dk_ref[here, :], dv_ref[here, :],
+        ]
+        value = dot_of(jnp.concatenate(parts, 1), w_ref[...], 1, 1)
+        outs[block][...] = value.astype(outs[block].dtype)
+
+
+def token_back(dq_a, dq_b, dk, dv, w_qkv):
+    rows = dk.shape[0] // 4
+    out_shape = [of((rows, D), kind) for kind in (single, bfloat, single, bfloat)]
+    return pl.pallas_call(
+        token_back_kernel,
+        in_specs=[whole_spec()] * 5,
+        out_specs=[whole_spec()] * 4,
+        out_shape=out_shape,
+        cost_estimate=cost(8 * rows * D * w_qkv.shape[1], w_qkv, dk, *out_shape),
+        compiler_params=pltpu.CompilerParams(vmem_limit_bytes=24 * 2**20),
+        name="token_back",
+    )(dq_a, dq_b, dk, dv, w_qkv)
+
+
 def pack_kernel(target_ref, *refs, jobs, scale):
-    count = 2 * len(jobs)
-    inputs, out_ref, held_ref, sem = refs[:count], refs[-3], refs[-2], refs[-1]
-    copies = []
-    for index, (layout, rows, cols) in enumerate(jobs):
-        left_ref, right_ref = inputs[2 * index], inputs[2 * index + 1]
+    inputs, out_ref, held_ref, sem = refs[:-3], refs[-3], refs[-2], refs[-1]
+    place = 0
+    for lefts, rights, layout, rows, cols in jobs:
         for row in range(0, rows, 2):
             span = min(2, rows - row)
-            weights = dot_of(left_ref[:, row * BLK : (row + span) * BLK], right_ref[...], 0, 0)
+            weights = 0.0
+            for (left, left_at, size), (right, right_at, _) in zip(lefts, rights):
+                weights = weights + dot_of(
+                    inputs[left][left_at : left_at + size, row * BLK : (row + span) * BLK],
+                    inputs[right][right_at : right_at + size, :],
+                    0,
+                    0,
+                )
             weights = (weights * scale).astype(bfloat)
             for i in range(span):
                 for col in range(cols):
-                    place = len(copies)
                     held_ref[place] = weights[
                         i * BLK : (i + 1) * BLK, col * BLK : (col + 1) * BLK
                     ]
-                    copy = pltpu.make_async_copy(
+                    pltpu.make_async_copy(
                         held_ref.at[place], out_ref.at[target_ref[layout(row + i, col)]], sem
-                    )
-                    copy.start()
-                    copies.append(copy)
-    pltpu.make_async_copy(held_ref, out_ref.at[pl.ds(0, len(copies))], sem).wait()
-
-
-def pack(target, pairs, layouts, scale, total, earlier=None):
-    jobs = [
-        (layout, left.shape[1] // BLK, right.shape[1] // BLK)
-        for (left, right), layout in zip(pairs, layouts)
-    ]
-    operands = [value for pair in pairs for value in pair]
-    blocks = sum(rows * cols for _, rows, cols in jobs)
-    whole = pl.BlockSpec(memory_space=pltpu.VMEM)
+                    ).start()
+                    place += 1
+    pltpu.make_async_copy(held_ref, out_ref.at[pl.ds(0, place)], sem).wait()
+
+
+def pack(target, pairs, scale, total, earlier=None, after=()):
+    operands, jobs, blocks, flops = [], [], 0, 0
+
+    def segments(arrays, size):
+        found = []
+        for value in arrays:
+            if not any(value is other for other in operands):
+                operands.append(value)
+            index = [value is other for other in operands].index(True)
+            found += [(index, at, size) for at in range(0, value.shape[0], size)]
+        return found
+
+    for lefts, rights, layout in pairs:
+        size = min(value.shape[0] for value in lefts + rights)
+        rows, cols = lefts[0].shape[1] // BLK, rights[0].shape[1] // BLK
+        jobs.append((segments(lefts, size), segments(rights, size), layout, rows, cols))
+        blocks += rows * cols
+        flops += 2 * rows * cols * BLK * BLK * sum(value.shape[0] for value in lefts)
     some = pl.BlockSpec(memory_space=pl.ANY)
     more = [] if earlier is None else [earlier]
-    flops = sum(2 * left.shape[0] * left.shape[1] * right.shape[1] for left, right in pairs)
     return pl.pallas_call(
         functools.partial(pack_kernel, jobs=jobs, scale=scale),
         grid_spec=pltpu.PrefetchScalarGridSpec(
             num_scalar_prefetch=1,
             grid=(),
-            in_specs=[whole] * len(operands) + [some] * len(more),
+            in_specs=[whole_spec()] * len(operands) + [some] * (len(more) + len(after)),
             out_specs=some,
             scratch_shapes=[pltpu.VMEM((blocks, BLK, BLK), bfloat), pltpu.SemaphoreType.DMA],
         ),
-        out_shape=jax.ShapeDtypeStruct((total, BLK, BLK), bfloat),
+        out_shape=of((total, BLK, BLK), bfloat),
         input_output_aliases={1 + len(operands): 0} if more else {},
-        cost_estimate=pl.CostEstimate(
-            flops=flops, bytes_accessed=blocks * BLK * BLK * 4, transcendentals=0
-        ),
-        compiler_params=pltpu.CompilerParams(vmem_limit_bytes=48 * 2**20),
+        cost_estimate=cost(flops, *operands, of((blocks, BLK, BLK), bfloat)),
+        compiler_params=pltpu.CompilerParams(vmem_limit_bytes=32 * 2**20),
         name="pack",
-    )(target, *operands, *more)
-
-
-def gelu_exact(inputs):
-    return jax.nn.gelu(inputs, approximate=False)
+    )(target, *operands, *more, *after)
 
 
 def block_counts(tensors):
@@ -296,20 +770,6 @@
     inner = jnp.where(canon_index < 4 * attn_count + ffn_count, D ** (-0.5), FF ** (-0.5))
     inner = jnp.where(canon_index < 4 * attn_count, out_std, inner)
     return jnp.where(canon_index < 3 * attn_count, D ** (-0.5), inner).astype(single)
-
-
-def norm_forward(inputs, gain, shift):
-    centred = inputs - jnp.mean(inputs, -1, keepdims=True)
-    inv_std = lax.rsqrt(jnp.mean(centred * centred, -1, keepdims=True) + norm_eps)
-    normed = centred * inv_std
-    return (normed * gain + shift, normed, inv_std)
-
-
-def norm_backward(grad_in, normed, inv_std, gain):
-    scaled = grad_in * gain
-    mean_grad = jnp.mean(scaled, -1, keepdims=True)
-    mean_cross = jnp.mean(scaled * normed, -1, keepdims=True)
-    return inv_std * (scaled - mean_grad - normed * mean_cross)
 
 
 def swap(value, axis, bit):
@@ -405,21 +865,18 @@
     )(source, *pieces)
 
 
-def reduce_pair(part_a, part_b):
-    half = part_a.shape[0] // 2
-    chip = []
-    for part in (part_a, part_b):
-        got = swap(part[half:].astype(bfloat), "tensor", 1)
-        chip.append((part[:half] + got.astype(single)).astype(bfloat))
-    from_b = swap(chip[1], "tensor", 2)
-    from_a = swap(chip[0], "tensor", 2)
-    full_a = chip[0].astype(single) + from_b.astype(single)
-    full_b = chip[1].astype(single) + from_a.astype(single)
-    return full_a, full_b
-
-
-def with_peer(rows):
-    return jnp.concatenate([rows, swap(rows, "tensor", 1)], axis=0)
+def chip_sum(keep, send, after=()):
+    return norm_call(
+        chip_kernel, "chip_sum", [keep, peer_of(send)], [], [(D, bfloat)], False, after
+    )[0]
+
+
+def across(value):
+    return swap(value, "tensor", 2)
+
+
+def peer_of(value):
+    return swap(value, "tensor", 1)
 
 
 def body(
@@ -446,11 +903,9 @@
     seq_len = local_rows * tensors
     slice_width = D // tensors
     hidden_width = FF // tensors
-    local_heads = slice_width // HEAD_DIM
     block_total = block_owner.shape[0]
     slots_here = master_blocks.shape[1]
     length = seq_lengths[0]
-    score_scale = HEAD_DIM ** (-0.5)
     attn_count, ffn_count = block_counts(tensors)
     permuted = data_ranks <= 16
     hops = data_ranks // 2
@@ -504,7 +959,9 @@
 
     tokens_b = swap(tokens, "tensor", 2)
     cotangent_b = swap(cotangent, "tensor", 2)
-    full_tokens = jnp.concatenate([with_peer(tokens), with_peer(tokens_b)], axis=0)
+    full_tokens = jnp.concatenate(
+        [tokens, peer_of(tokens), tokens_b, peer_of(tokens_b)], axis=0
+    )
     quarters = tensor_rank ^ jnp.arange(4, dtype=jnp.int32)
     positions = (quarters[:, None] * local_rows + jnp.arange(local_rows)[None, :]).reshape(-1)
     key_valid = positions < length
@@ -515,154 +972,155 @@
     projected = (jnp.dot(full_tokens, w_qkv, preferred_element_type=single) + bias_qkv).astype(
         bfloat
     )
-    heads_q = projected[:, 0:slice_width].reshape(seq_len, local_heads, HEAD_DIM)
-    heads_k = projected[:, slice_width : 2 * slice_width].reshape(seq_len, local_heads, HEAD_DIM)
-    heads_v = projected[:, 2 * slice_width : 3 * slice_width].reshape(
-        seq_len, local_heads, HEAD_DIM
-    )
-
-    def masked_scores(query_block):
-        raw = (
-            jnp.einsum("qhd,khd->hqk", query_block, heads_k, preferred_element_type=single)
-            * score_scale
-        )
-        return jnp.where(key_valid, raw, masked_score)
-
-    attended, log_totals, branch_part = [None] * 2, [None] * 2, [None] * 2
-    for part in (1, 0):
-        scores = masked_scores(heads_q[part * chunk : (part + 1) * chunk])
-        row_max = jnp.max(scores, -1, keepdims=True)
-        shifted = jnp.exp(scores - row_max)
-        row_total = jnp.sum(shifted, -1, keepdims=True)
-        weights = (shifted / row_total).astype(bfloat)
-        mixed = jnp.einsum("hqk,khd->qhd", weights, heads_v, preferred_element_type=single)
-        attended[part] = mixed.astype(bfloat).reshape(chunk, slice_width)
-        log_totals[part] = row_max + jnp.log(row_total)
-        branch_part[part] = jnp.dot(attended[part], w_out, preferred_element_type=single)
-    branches = reduce_pair(*branch_part)
-    hidden, normed_one, inv_one, full_hidden = [], [], [], []
-    up_proj, pulls, activation, down_part = [], [], [], []
-    for part, rows in enumerate((tokens, tokens_b)):
-        value, normed, inv = norm_forward(
-            rows.astype(single) + (branches[part] + bias_out), gain_one, shift_one
-        )
-        hidden.append(value)
-        normed_one.append(normed)
-        inv_one.append(inv)
-        full_hidden.append(with_peer(value.astype(bfloat)))
-        up_proj.append(jnp.dot(full_hidden[part], w_up, preferred_element_type=single) + bias_up)
-        act_float, gelu_pull = jax.vjp(gelu_exact, up_proj[part])
-        pulls.append(gelu_pull)
-        activation.append(act_float.astype(bfloat))
-        down_part.append(jnp.dot(activation[part], w_down, preferred_element_type=single))
-    downs = reduce_pair(*down_part)
-    grad_second, full_grad_down = [None] * 2, [None] * 2
-    grad_up, hidden_part = [None] * 2, [None] * 2
-    for part in (1, 0):
-        result, normed_two, inv_two = norm_forward(
-            hidden[part] + (downs[part] + bias_down), gain_two, shift_two
-        )
-        cot = (cotangent, cotangent_b)[part].astype(single)
-        grad_out = cot * row_valid[part * chunk : part * chunk + local_rows]
-        grad_second[part] = norm_backward(grad_out, normed_two, inv_two, gain_two)
-        grad_down = grad_second[part].astype(bfloat)
-        if part == 0:
-            layer_output = result.astype(bfloat)
-            dgain_two = jnp.sum(grad_out * normed_two, 0)
-            dshift_two = jnp.sum(grad_out, 0)
-            dbias_down = jnp.sum(grad_down.astype(single), 0)
-        full_grad_down[part] = with_peer(grad_down)
-        grad_act = jnp.einsum(
-            "sd,fd->sf", full_grad_down[part], w_down, preferred_element_type=single
-        )
-        grad_up[part] = pulls[part](grad_act)[0].astype(bfloat)
-        hidden_part[part] = jnp.einsum(
-            "sf,df->sd", grad_up[part], w_up, preferred_element_type=single
-        )
-    hidden_sums = reduce_pair(*hidden_part)
-    activation = jnp.concatenate(activation, 0)
-    all_grad_down = jnp.concatenate(full_grad_down, 0)
-    all_hidden = jnp.concatenate(full_hidden, 0)
-    all_grad_up = jnp.concatenate(grad_up, 0)
+    one = jnp.stack([gain_one, shift_one, bias_out])
+    two = jnp.stack([gain_two, shift_two, bias_down])
+    valid = jnp.broadcast_to(row_valid, (seq_len, 128))
     grad_scale = 1.0 / math.sqrt(seq_len * data_ranks)
     up_start = 4 * attn_count
+
+    attended, lse, shares = [None] * 4, [None] * 4, [None] * 4
+    attended[3], lse[3], shares[3] = attend(projected, valid, w_out, 3, after=[cotangent_b])
+    attended[1], lse[1], shares[1] = attend(projected, valid, w_out, 1, after=[shares[3]])
+    for block in (2, 0):
+        attended[block], lse[block], shares[block] = attend(
+            projected, valid, w_out, block, peer_of(shares[block + 1]),
+            after=[shares[1] if block == 2 else shares[2]],
+        )
+    chip = [shares[0], shares[2]]
+    other = [across(chip[1]), across(chip[0])]
+
+    normed_one, inv_one = [None] * 2, [None] * 2
+    hidden, activation, slope, chip_two = [None] * 4, [None] * 4, [None] * 4, [None] * 2
+    bias_row = bias_up[None, :]
+
+    def norm_up(part, after):
+        normed_one[part], inv_one[part], hidden[2 * part] = norm_call(
+            norm_one_kernel, "norm_one", [chip[part], other[part], (tokens, tokens_b)[part]],
+            [one], [(D, single), (128, single), (D, bfloat)], False, after,
+        )
+        hidden[2 * part + 1] = peer_of(hidden[2 * part])
+
+    def feed_part(part, after):
+        block = 2 * part
+        activation[block], slope[block], keep = feed(
+            hidden[block], w_up, bias_row, w_down, single, after
+        )
+        block += 1
+        activation[block], slope[block], send = feed(
+            hidden[block], w_up, bias_row, w_down, bfloat, [keep]
+        )
+        return keep, send
+
+    norm_up(0, [chip[0]])
+    sums = feed_part(0, [])
+    norm_up(1, [sums[1]])
+    chip_two[0] = chip_sum(*sums, [hidden[2]])
+    sums = feed_part(1, [chip_two[0]])
+    chip_two[1] = chip_sum(*sums)
+    other = [across(chip_two[1]), across(chip_two[0])]
+
+    grad_second, grad_down, grad_up = [None] * 2, [None] * 4, [None] * 4
+    bias_parts, chip_three, outs, sums_two = [None] * 4, [None] * 2, [None] * 2, [None] * 2
+
+    def norm_down(part, after):
+        rows_valid = valid[part * chunk : part * chunk + local_rows]
+        outs[part], grad_second[part], grad_down[2 * part], sums_two[part] = norm_call(
+            norm_two_kernel, "norm_two",
+            [chip_two[part], other[part], normed_one[part], (cotangent, cotangent_b)[part],
+             rows_valid],
+            [one, two], [(D, bfloat), (D, single), (D, bfloat)], True, after,
+        )
+        grad_down[2 * part + 1] = peer_of(grad_down[2 * part])
+
+    def feed_back_part(part, after):
+        block = 2 * part
+        grad_up[block], bias_parts[block], keep = feed_back(
+            grad_down[block], w_down, w_up, slope[block], single, after
+        )
+        block += 1
+        grad_up[block], bias_parts[block], send = feed_back(
+            grad_down[block], w_down, w_up, slope[block], bfloat, [keep]
+        )
+        return keep, send
+
+    norm_down(1, [chip_two[1]])
+    sums = feed_back_part(1, [])
+    norm_down(0, [sums[1]])
+    chip_three[1] = chip_sum(*sums, [grad_down[0]])
+    sums = feed_back_part(0, [chip_three[1]])
+    chip_three[0] = chip_sum(*sums)
+    other = [across(chip_three[1]), across(chip_three[0])]
+    layer_output = outs[0]
+    dgain_two, dshift_two, dbias_down = sums_two[0][0], sums_two[0][1], sums_two[0][2]
+    dbias_up = (bias_parts[0] + bias_parts[1] + bias_parts[2] + bias_parts[3])[0]
     sent = pack(
         target,
-        [(all_hidden, all_grad_up), (activation, all_grad_down)],
         [
-            lambda row, col: up_start + row * wide + col,
-            lambda row, col: up_start + ffn_count + row * full + col,
+            (hidden, grad_up, lambda row, col: up_start + row * wide + col),
+            (activation, grad_down, lambda row, col: up_start + ffn_count + row * full + col),
         ],
         grad_scale,
         block_total,
-    )
-    dbias_up = jnp.sum(all_grad_up.astype(single), 0)
-    full_grad_branch, grad_query = [], []
-    key_total = value_total = 0.0
+        after=[chip_three[0]],
+    )
+
+    grad_branch, grad_query, back, grad_rows, sums_one = [None] * 4, [None] * 2, None, [0, 0], [0, 0]
+    after = [sent]
     for part in (0, 1):
-        grad_hidden = hidden_sums[part] + grad_second[part]
-        grad_rows = norm_backward(grad_hidden, normed_one[part], inv_one[part], gain_one)
-        grad_branch = grad_rows.astype(bfloat)
-        if part == 0:
-            grad_summed = grad_rows
-            dgain_one = jnp.sum(grad_hidden * normed_one[0], 0)
-            dshift_one = jnp.sum(grad_hidden, 0)
-            dbias_out = jnp.sum(grad_branch.astype(single), 0)
-        full_grad_branch.append(with_peer(grad_branch))
-        grad_attended = jnp.einsum(
-            "sd,ad->sa", full_grad_branch[part], w_out, preferred_element_type=single
-        ).astype(bfloat)
-        grad_block = grad_attended.reshape(chunk, local_heads, HEAD_DIM)
-        query_block = heads_q[part * chunk : (part + 1) * chunk]
-        probs_full = jnp.exp(masked_scores(query_block) - log_totals[part])
-        value_total = value_total + jnp.einsum(
-            "hqk,qhd->khd", probs_full.astype(bfloat), grad_block, preferred_element_type=single
-        )
-        grad_probs = jnp.einsum("qhd,khd->hqk", grad_block, heads_v, preferred_element_type=single)
-        row_cross = jnp.sum(grad_probs * probs_full, -1, keepdims=True)
-        grad_scores = (probs_full * (grad_probs - row_cross)).astype(bfloat)
-        grad_query.append(
-            (
-                jnp.einsum("hqk,khd->qhd", grad_scores, heads_k, preferred_element_type=single)
-                * score_scale
-            ).astype(bfloat)
-        )
-        key_total = (
-            key_total
-            + jnp.einsum("hqk,qhd->khd", grad_scores, query_block, preferred_element_type=single)
-            * score_scale
-        )
-    grad_qkv = jnp.concatenate(
-        [
-            jnp.concatenate(grad_query, 0).reshape(seq_len, slice_width),
-            key_total.reshape(seq_len, slice_width).astype(bfloat),
-            value_total.reshape(seq_len, slice_width).astype(bfloat),
-        ],
-        axis=1,
-    )
-    all_attended = jnp.concatenate(attended, 0)
-    all_grad_branch = jnp.concatenate(full_grad_branch, 0)
+        block = 2 * part
+        grad_rows[part], grad_branch[block], sums_one[part] = norm_call(
+            norm_back_kernel, "norm_back",
+            [chip_three[part], other[part], grad_second[part], normed_one[part], inv_one[part]],
+            [one], [(D, single), (D, bfloat)], True, after,
+        )
+        grad_branch[block + 1] = peer_of(grad_branch[block])
+        grad_query[part], *back = attend_back(
+            grad_branch[block], grad_branch[block + 1], w_out, projected,
+            attended[block : block + 2], lse[block : block + 2], valid, part, back,
+        )
+        after = [back[0]]
+    grad_summed, sums_one = grad_rows[0], sums_one[0]
+    dgain_one, dshift_one, dbias_out = sums_one[0], sums_one[1], sums_one[2]
+    grad_key, grad_value = back
     sent = pack(
         target,
-        [(full_tokens, grad_qkv), (all_attended, all_grad_branch)],
         [
-            lambda row, col: col // cols * attn_count + row * cols + col % cols,
-            lambda row, col: 3 * attn_count + row * full + col,
+            (
+                [full_tokens],
+                grad_query,
+                lambda row, col: row * cols + col,
+            ),
+            (
+                [full_tokens],
+                [grad_key],
+                lambda row, col: attn_count + row * cols + col,
+            ),
+            (
+                [full_tokens],
+                [grad_value],
+                lambda row, col: 2 * attn_count + row * cols + col,
+            ),
+            (
+                attended,
+                grad_branch,
+                lambda row, col: 3 * attn_count + row * full + col,
+            ),
         ],
         grad_scale,
         block_total,
         sent,
     )
-    dbias_query = jnp.sum(grad_qkv[:, 0:slice_width].astype(single), 0)
-    dbias_value = jnp.sum(grad_qkv[:, 2 * slice_width : 3 * slice_width].astype(single), 0)
-    token_part = jnp.einsum("sc,dc->sd", grad_qkv, w_qkv, preferred_element_type=single)
-    chip_rows = []
-    for part in (1, 0):
-        rows = token_part[part * chunk : (part + 1) * chunk]
-        got = swap(rows[local_rows:].astype(bfloat), "tensor", 1)
-        chip_rows.append(rows[:local_rows] + got.astype(single))
-    across = swap(chip_rows[0].astype(bfloat), "tensor", 2)
-    token_grad = (chip_rows[1] + across.astype(single) + grad_summed).astype(bfloat)
+    dbias_query = jnp.sum(grad_query[0].astype(single), 0) + jnp.sum(
+        grad_query[1].astype(single), 0
+    )
+    dbias_value = jnp.sum(grad_value.astype(single), 0)
+    keep_a, send_a, keep_b, send_b = token_back(
+        grad_query[0], grad_query[1], grad_key, grad_value, w_qkv
+    )
+    over = across(chip_sum(keep_b, send_b))
+    token_grad = (
+        chip_sum(keep_a, send_a).astype(single) + over.astype(single) + grad_summed
+    ).astype(bfloat)
     vector_grad = jnp.concatenate(
         [
             dgain_one,

time: 455 us -> 397 us (0.87)
  Pallas kernels: 62 us -> 156 us
  matrix products: 70.7 us -> 1.79 us
  other arithmetic: 60.9 us -> 11.9 us
  waiting for transfers between devices: 169 us -> 134 us
  starting transfers between devices: 55.5 us -> 62.1 us
    pallas_call x0 -> x27, Pallas kernels: none -> 85.6 us  [the longest x4 20.3 us: feed(): pl.pallas_call(feed_kernel, grid=(hidden // step,), in_specs=[fixed(block...]
    dot_general x25 -> x0, matrix products: 68.8 us -> none  [the longest x2 15.4 us: body(): jnp.einsum('qhd,khd->hqk', grad_block, heads_v, preferred_element_type=si...]
    ppermute x50, waiting for transfers between devices: 128 us -> 96.7 us  [swap(): return lax.ppermute(value, axis, [(i, i ^ bit) for i in range(count)])]
    reduce_sum x16 -> x3, other arithmetic: 19.1 us -> 0.32 us  [the longest x1 0.15 us: body(): dbias_value = jnp.sum(grad_value.astype(single), 0)]
    convert_element_type x8 -> x1, other arithmetic: 16.7 us -> 1.03 us  [body(): token_grad = (chip_sum(keep_a, send_a).astype(single) + over.astype(singl...]
    concatenate x8 -> x0, other arithmetic: 11.6 us -> none  [the longest x1 3.19 us: body(): activation = jnp.concatenate(activation, 0)]
    pallas_call x2, Pallas kernels: 13.7 us -> 22 us  [pack(): pl.pallas_call(functools.partial(pack_kernel, jobs=jobs, scale=scale), gr...]
    unnamed x242 -> x107, local copies, waits for them, and re-layouts: 14.9 us -> 16.2 us
  transfers between devices with their start and end apart: 65 -> 65, of which waited for: 36 -> 32; matrix products, arithmetic and copies ran while one was open for 13% -> 5% of each run, Pallas kernels for 2% -> 19%
where the time goes in v4:
time: 397 us; the launch traced here: 393 us
  Pallas kernels  156 us (39%)
  waiting for transfers between devices  134 us (34%)
  starting transfers between devices  62.1 us (16%)
  local copies, waits for them, and re-layouts  24.9 us (6%)
  other arithmetic  11.9 us (3%)
    ppermute x50, waiting for transfers between devices, swap(): return lax.ppermute(value, axis, [(i, i ^ bit) for i in range(count)])  96.7 us
    ppermute x50, starting transfers between devices, swap(): return lax.ppermute(value, axis, [(i, i ^ bit) for i in range(count)])  50.4 us
    ppermute x15, waiting for transfers between devices, ring(): lax.ppermute(value, 'dp', [(i, (i + 2) % count) for i in range(count)])  37.2 us
    pallas_call x1, Pallas kernels, adam(): pl.pallas_call(functools.partial(adam_kernel, per=per), grid_spec=pltpu.P...  23.1 us
    pallas_call x2, Pallas kernels, pack(): pl.pallas_call(functools.partial(pack_kernel, jobs=jobs, scale=scale), gr...  22 us
    pallas_call x1, Pallas kernels, renew(): pl.pallas_call(functools.partial(renew_kernel, count=count, unroll=unroll...  21.2 us
    pallas_call x4, Pallas kernels, feed(): pl.pallas_call(feed_kernel, grid=(hidden // step,), in_specs=[fixed(block...  20.3 us
    pallas_call x4, Pallas kernels, attend(): pl.pallas_call(functools.partial(attend_kernel, heads=heads, own=own), gr...  16.8 us
  transfers between devices with their start and end apart: 65, of which 32 were waited for; matrix products, arithmetic and copies ran while one was open for 5% of the time, Pallas kernels for 19%

profile of v4, /device:TPU:0, one launch (start us, length us, event | category | flops | bytes accessed | tf_op | source)
XLA Modules:
  0.0 393.3 jit_solution(10976202295194114185)
XLA Ops:
  16.3 4.0 %collective-permute-done.7.refs_7_ = bf16[8,128,128]{2,1,0:T(8,128)(2,1)} collective-permute-done((bf16[8,128,128]{2,1,0:T(8,128)(2,1)S(1)}, bf16[8,128,128]{2,1,0:T(8,128)(2,1)}, u32[]{:S(2)}, u32[]{:S(2)}) %collective-permute-start.7) | collective-permute-done | bytes 262176 | tf_op jit(solution)/shard_map/ppermute | solution.py:782
  20.3 5.6 %collective-permute-done.8.refs_8_ = bf16[8,128,128]{2,1,0:T(8,128)(2,1)} collective-permute-done((bf16[8,128,128]{2,1,0:T(8,128)(2,1)S(1)}, bf16[8,128,128]{2,1,0:T(8,128)(2,1)}, u32[]{:S(2)}, u32[]{:S(2)}) %collective-permute-start.8) | collective-permute-done | bytes 262176 | tf_op jit(solution)/shard_map/ppermute | solution.py:782
  46.7 4.7 %collective-permute-done.9.refs_9_ = bf16[8,128,128]{2,1,0:T(8,128)(2,1)S(1)} collective-permute-done((bf16[8,128,128]{2,1,0:T(8,128)(2,1)}, bf16[8,128,128]{2,1,0:T(8,128)(2,1)S(1)}, u32[]{:S(2)}, u32[]{:S(2)}) %collective-permute-start.9) | collective-permute-done | bytes 262176 | tf_op jit(solution)/shard_map/ppermute | solution.py:777
  55.6 6.0 %collective-permute-done.19.refs_19_ = bf16[8,128,128]{2,1,0:T(8,128)(2,1)} collective-permute-done((bf16[8,128,128]{2,1,0:T(8,128)(2,1)}, bf16[8,128,128]{2,1,0:T(8,128)(2,1)}, u32[]{:S(2)}, u32[]{:S(2)}) %collective-permute-start.19) | collective-permute-done | bytes 262176 | tf_op jit(solution)/shard_map/ppermute | solution.py:782
  72.1 4.6 %collective-permute-done.21.refs_21_ = bf16[8,128,128]{2,1,0:T(8,128)(2,1)S(1)} collective-permute-done((bf16[8,128,128]{2,1,0:T(8,128)(2,1)}, bf16[8,128,128]{2,1,0:T(8,128)(2,1)S(1)}, u32[]{:S(2)}, u32[]{:S(2)}) %collective-permute-start.21) | collective-permute-done | bytes 262176 | tf_op jit(solution)/shard_map/ppermute | solution.py:777
  89.0 4.0 %assemble.1 = (bf16[1024,768]{1,0:T(8,128)(2,1)S(1)}, bf16[256,1024]{1,0:T(8,128)(2,1)S(1)}, bf16[1024,1024]{1,0:T(8,128)(2,1)S(1)}, bf16[1024,1024]{1,0:T(8,128)(2,1)S(1)}) custom-call(s32[192]{0:T(256)S(1)} %get-tuple-element.196.source_ref, bf16[8,128,128]{2,1,0:T(8,128)(2,1)S(1)} %copy-done.23, bf16[8,128,128]{2,1,0:T(8,128)(2,1)S(1)} %copy-done.21, ...), custom_call_target="tpu_custom_call" | custom-call | tf_op jit(solution)/shard_map/assemble/pallas_call | solution.py:850
  99.2 4.2 %attend.5 = (bf16[256,256]{1,0:T(8,128)(2,1)S(1)}, f32[4,256]{1,0:T(4,128)S(1)}, bf16[256,1024]{1,0:T(8,128)(2,1)}) custom-call(bf16[1024,768]{1,0:T(8,128)(2,1)S(1)} %add_convert_fusion.q_ref.k_ref.v_ref.refs_3_.refs_4_.refs_5_, bf16[1024,768]{1,0:T(8,128)(2,1)S(1)} %add_convert_fusion.q_ref.k_ref.v_ref.refs_3_.refs_4_.refs_5_, ...), custom_call_target="tpu_custom_call" | custom-call | flops 67108864 | bytes 139520 | tf_op jit(solution)/shard_map/attend/pallas_call | solution.py:317
  103.9 4.2 %attend.6 = (bf16[256,256]{1,0:T(8,128)(2,1)S(1)}, f32[4,256]{1,0:T(4,128)S(1)}, bf16[256,1024]{1,0:T(8,128)(2,1)}) custom-call(bf16[1024,768]{1,0:T(8,128)(2,1)S(1)} %add_convert_fusion.q_ref.k_ref.v_ref.refs_3_.refs_4_.refs_5_, bf16[1024,768]{1,0:T(8,128)(2,1)S(1)} %add_convert_fusion.q_ref.k_ref.v_ref.refs_3_.refs_4_.refs_5_, ...), custom_call_target="tpu_custom_call" | custom-call | flops 67108864 | bytes 139520 | tf_op jit(solution)/shard_map/attend/pallas_call | solution.py:317
  110.6 5.0 %attend.7 = (bf16[256,256]{1,0:T(8,128)(2,1)S(1)}, f32[4,256]{1,0:T(4,128)S(1)}, bf16[256,1024]{1,0:T(8,128)(2,1)S(1)}) custom-call(bf16[1024,768]{1,0:T(8,128)(2,1)S(1)} %add_convert_fusion.q_ref.k_ref.v_ref.refs_3_.refs_4_.refs_5_, bf16[1024,768]{1,0:T(8,128)(2,1)S(1)} %add_convert_fusion.q_ref.k_ref.v_ref.refs_3_.refs_4_.refs_5_, ...), custom_call_target="tpu_custom_call" | custom-call | flops 67108864 | bytes 139520 | tf_op jit(solution)/shard_map/attend/pallas_call | solution.py:317
  115.7 6.5 %collective-permute-done.27.across_ref = bf16[256,1024]{1,0:T(8,128)(2,1)} collective-permute-done((bf16[256,1024]{1,0:T(8,128)(2,1)}, bf16[256,1024]{1,0:T(8,128)(2,1)}, u32[]{:S(2)}, u32[]{:S(2)}) %collective-permute-start.27) | collective-permute-done | bytes 524320 | tf_op jit(solution)/shard_map/ppermute | solution.py:777
  126.7 5.1 %feed.4 = (bf16[256,1024]{1,0:T(8,128)(2,1)S(1)}, bf16[256,1024]{1,0:T(8,128)(2,1)S(1)}, f32[256,1024]{1,0:T(8,128)S(1)}) custom-call(bf16[256,1024]{1,0:T(8,128)(2,1)S(1)} %get-tuple-element.93.rows_ref.refs_0_, bf16[1024,1024]{1,0:T(8,128)(2,1)S(1)} %copy-done.1, f32[1,1024]{1,0:T(1,128)S(1)} %bitcast.109, bf16[1024,1024]{1,0:T(8,128)(2,1)S(1)} %copy-done.3), custom_call_target="tpu_custom_call" | custom-call | flops 67108864 | bytes 393216 | tf_op jit(solution)/shard_map/feed/pallas_call | solution.py:515
  131.8 5.1 %feed.5 = (bf16[256,1024]{1,0:T(8,128)(2,1)S(1)}, bf16[256,1024]{1,0:T(8,128)(2,1)S(1)}, bf16[256,1024]{1,0:T(8,128)(2,1)S(1)}) custom-call(bf16[256,1024]{1,0:T(8,128)(2,1)S(1)} %collective-permute-done.28.rows_ref.refs_1_, bf16[1024,1024]{1,0:T(8,128)(2,1)S(1)} %copy-done.1, f32[1,1024]{1,0:T(1,128)S(1)} %bitcast.110, bf16[1024,1024]{1,0:T(8,128)(2,1)S(1)} %copy-done.3, ...), custom_call_target="tpu_custom_call" | custom-call | flops 67108864 | bytes 360448 | tf_op jit(solution)/shard_map/feed/pallas_call | solution.py:515
  142.1 5.1 %feed.6 = (bf16[256,1024]{1,0:T(8,128)(2,1)S(1)}, bf16[256,1024]{1,0:T(8,128)(2,1)S(1)}, f32[256,1024]{1,0:T(8,128)S(1)}) custom-call(bf16[256,1024]{1,0:T(8,128)(2,1)S(1)} %get-tuple-element.98.refs_0_.rows_ref.refs_2_, bf16[1024,1024]{1,0:T(8,128)(2,1)S(1)} %copy-done.1, f32[1,1024]{1,0:T(1,128)S(1)} %bitcast.111, bf16[1024,1024]{1,0:T(8,128)(2,1)S(1)} %copy-done.3, ...), custom_call_target="tpu_custom_call" | custom-call | flops 67108864 | bytes 393216 | tf_op jit(solution)/shard_map/feed/pallas_call | solution.py:515
  147.2 5.1 %feed.7 = (bf16[256,1024]{1,0:T(8,128)(2,1)S(1)}, bf16[256,1024]{1,0:T(8,128)(2,1)S(1)}, bf16[256,1024]{1,0:T(8,128)(2,1)S(1)}) custom-call(bf16[256,1024]{1,0:T(8,128)(2,1)S(1)} %collective-permute-done.31.rows_ref.refs_3_, bf16[1024,1024]{1,0:T(8,128)(2,1)S(1)} %copy-done.1, f32[1,1024]{1,0:T(1,128)S(1)} %bitcast.112, bf16[1024,1024]{1,0:T(8,128)(2,1)S(1)} %copy-done.3, ...), custom_call_target="tpu_custom_call" | custom-call | flops 67108864 | bytes 360448 | tf_op jit(solution)/shard_map/feed/pallas_call | solution.py:515
  154.8 12.0 %collective-permute-done.34.across_ref = bf16[256,1024]{1,0:T(8,128)(2,1)S(1)} collective-permute-done((bf16[256,1024]{1,0:T(8,128)(2,1)S(1)}, bf16[256,1024]{1,0:T(8,128)(2,1)S(1)}, u32[]{:S(2)}, u32[]{:S(2)}) %collective-permute-start.34) | collective-permute-done | bytes 524320 | tf_op jit(solution)/shard_map/ppermute | solution.py:777
  171.1 3.9 feed_back.4
  175.1 3.9 feed_back.5
  179.3 4.5 %collective-permute-done.33.across_ref = bf16[256,1024]{1,0:T(8,128)(2,1)S(1)} collective-permute-done((bf16[256,1024]{1,0:T(8,128)(2,1)S(1)}, bf16[256,1024]{1,0:T(8,128)(2,1)S(1)}, u32[]{:S(2)}, u32[]{:S(2)}) %collective-permute-start.33) | collective-permute-done | bytes 524320 | tf_op jit(solution)/shard_map/ppermute | solution.py:777
  186.5 3.9 %feed_back.6 = (bf16[256,1024]{1,0:T(8,128)(2,1)S(1)}, f32[1,1024]{1,0:T(1,128)S(1)}, f32[256,1024]{1,0:T(8,128)S(1)}) custom-call(bf16[256,1024]{1,0:T(8,128)(2,1)S(1)} %get-tuple-element.109.refs_0_.rows_ref.refs_12_, bf16[1024,1024]{1,0:T(8,128)(2,1)S(1)} %copy-done.3, bf16[1024,1024]{1,0:T(8,128)(2,1)S(1)} %copy-done.1, ...), custom_call_target="tpu_custom_call" | custom-call | flops 67108864 | bytes 360704 | tf_op jit(solution)/shard_map/feed_back/pallas_call | solution.py:550
  190.5 3.9 feed_back.7
  197.0 12.6 %pack.2.refs_0_.refs_13_ = bf16[192,128,128]{2,1,0:T(8,128)(2,1)S(1)} custom-call(s32[192]{0:T(256)S(1)} %get-tuple-element.197.target_ref, bf16[256,1024]{1,0:T(8,128)(2,1)S(1)} %get-tuple-element.93.rows_ref.refs_0_, bf16[256,1024]{1,0:T(8,128)(2,1)S(1)} %collective-permute-done.28.rows_ref.refs_1_, ...), custom_call_target="tpu_custom_call" | custom-call | flops 268435456 | bytes 786432 | tf_op jit(solution)/shard_map/pack/pallas_call | solution.py:746
  213.5 7.7 %attend_back.2 = (bf16[512,256]{1,0:T(8,128)(2,1)S(1)}, f32[1024,256]{1,0:T(8,128)S(1)}, f32[1024,256]{1,0:T(8,128)S(1)}) custom-call(bf16[256,1024]{1,0:T(8,128)(2,1)S(1)} %get-tuple-element.124.refs_0_.refs_9_, bf16[256,1024]{1,0:T(8,128)(2,1)S(1)} %collective-permute-done.40.refs_1_.refs_10_, bf16[256,1024]{1,0:T(8,128)(2,1)S(1)} %get-tuple-element.88.w_ref.refs_2_, ...), custom_call_target="tpu_custom_call" | custom-call | flops 335544320 | bytes 245760 | tf_op jit(solution)/shard_map/attend_back/pallas_call | solution.py:435
  221.3 4.7 %collective-permute-done.41.across_ref = bf16[256,1024]{1,0:T(8,128)(2,1)S(1)} collective-permute-done((bf16[256,1024]{1,0:T(8,128)(2,1)S(1)}, bf16[256,1024]{1,0:T(8,128)(2,1)S(1)}, u32[]{:S(2)}, u32[]{:S(2)}) %collective-permute-start.41) | collective-permute-done | bytes 524320 | tf_op jit(solution)/shard_map/ppermute | solution.py:777
  230.0 7.9 %attend_back.3 = (bf16[512,256]{1,0:T(8,128)(2,1)S(1)}, bf16[1024,256]{1,0:T(8,128)(2,1)S(1)}, bf16[1024,256]{1,0:T(8,128)(2,1)S(1)}) custom-call(bf16[256,1024]{1,0:T(8,128)(2,1)S(1)} %get-tuple-element.133.refs_0_.refs_11_, bf16[256,1024]{1,0:T(8,128)(2,1)S(1)} %collective-permute-done.42.refs_1_.refs_12_, ...), custom_call_target="tpu_custom_call" | custom-call | flops 335544320 | bytes 180224 | tf_op jit(solution)/shard_map/attend_back/pallas_call | solution.py:435
  238.0 9.4 %pack.3 = bf16[192,128,128]{2,1,0:T(8,128)(2,1)S(1)} custom-call(s32[192]{0:T(256)S(1)} %get-tuple-element.197.target_ref, bf16[1024,1024]{1,0:T(8,128)(2,1)S(1)} %copy-done.8, bf16[512,256]{1,0:T(8,128)(2,1)S(1)} %get-tuple-element.129.refs_0_.refs_1_, bf16[512,256]{1,0:T(8,128)(2,1)S(1)} %get-tuple-element.139.refs_1_.refs_2_, ...), custom_call_target="tpu_custom_call", output_to_operand_aliasing={{}: (14, {})} | custom-call | flops 134217728 | bytes 524288 | tf_op jit(solution)/shard_map/pack/pallas_call | solution.py:746
  251.0 9.9 %collective-permute-done.49 = bf16[12,128,128]{2,1,0:T(8,128)(2,1)S(1)} collective-permute-done((bf16[12,128,128]{2,1,0:T(8,128)(2,1)S(1)}, bf16[12,128,128]{2,1,0:T(8,128)(2,1)S(1)}, u32[]{:S(2)}, u32[]{:S(2)}) %collective-permute-start.49) | collective-permute-done | bytes 393248 | tf_op jit(solution)/shard_map/ppermute | solution.py:777
  262.6 6.6 %collective-permute-done.48 = bf16[12,128,128]{2,1,0:T(8,128)(2,1)S(1)} collective-permute-done((bf16[12,128,128]{2,1,0:T(8,128)(2,1)S(1)}, bf16[12,128,128]{2,1,0:T(8,128)(2,1)S(1)}, u32[]{:S(2)}, u32[]{:S(2)}) %collective-permute-start.48) | collective-permute-done | bytes 393248 | tf_op jit(solution)/shard_map/ppermute | solution.py:777
  277.7 5.2 %collective-permute-done.51 = bf16[12,128,128]{2,1,0:T(8,128)(2,1)S(1)} collective-permute-done((bf16[12,128,128]{2,1,0:T(8,128)(2,1)S(1)}, bf16[12,128,128]{2,1,0:T(8,128)(2,1)S(1)}, u32[]{:S(2)}, u32[]{:S(2)}) %collective-permute-start.51) | collective-permute-done | bytes 393248 | tf_op jit(solution)/shard_map/ppermute | solution.py:782
  286.1 8.4 %collective-permute-done.56 = bf16[12,128,128]{2,1,0:T(8,128)(2,1)S(1)} collective-permute-done((bf16[12,128,128]{2,1,0:T(8,128)(2,1)S(1)}, bf16[12,128,128]{2,1,0:T(8,128)(2,1)S(1)}, u32[]{:S(2)}, u32[]{:S(2)}) %collective-permute-start.56) | collective-permute-done | bytes 393248 | tf_op jit(solution)/shard_map/ppermute | solution.py:777
  335.2 8.2 %collective-permute-done.45 = bf16[256,1024]{1,0:T(8,128)(2,1)S(1)} collective-permute-done((bf16[256,1024]{1,0:T(8,128)(2,1)S(1)}, bf16[256,1024]{1,0:T(8,128)(2,1)S(1)}, u32[]{:S(2)}, u32[]{:S(2)}) %collective-permute-start.45) | collective-permute-done | bytes 524320 | tf_op jit(solution)/shard_map/ppermute | solution.py:777
  346.7 23.1 %adam.1 = (f32[24,128,128]{2,1,0:T(8,128)}, f32[24,128,128]{2,1,0:T(8,128)}, f32[24,128,128]{2,1,0:T(8,128)}, f32[24,128,128]{2,1,0:T(8,128)}, f32[24,128,128]{2...) custom-call(f32[24]{0:T(128)S(1)} %compare_select_fusion.7.rates_ref, ...), custom_call_target="tpu_custom_call" | custom-call | tf_op jit(solution)/shard_map/adam/pallas_call | solution.py:107
  371.6 21.2 %renew.1 = (f32[24,128,128]{2,1,0:T(8,128)}, f32[24,128,128]{2,1,0:T(8,128)}) custom-call(f32[6144,128]{1,0:T(8,128)S(1)} %bitcast.106, f32[6144,128]{1,0:T(8,128)} %bitcast.113), custom_call_target="tpu_custom_call" | custom-call | tf_op jit(solution)/shard_map/renew/pallas_call | solution.py:219
  (282 shorter events, 164.3 us)
Async XLA Ops:
  5.4 14.9 %collective-permute-start.7 = (bf16[8,128,128]{2,1,0:T(8,128)(2,1)S(1)}, bf16[8,128,128]{2,1,0:T(8,128)(2,1)}, u32[]{:S(2)}, u32[]{:S(2)}) collective-permute-start(bf16[8,128,128]{2,1,0:T(8,128)(2,1)S(1)} %get-tuple-element.176.refs_1_), channel_id=1, source_target_pairs={{0,8},{4,12},{8,16},{12,20},{16,24},{20,28},{24,0},{28,4},{1,9},{5... | collective-permute-start | bytes 786440 | tf_op jit(solution)/shard_map/ppermute | solution.py:782
  7.0 18.9 %collective-permute-start.8 = (bf16[8,128,128]{2,1,0:T(8,128)(2,1)S(1)}, bf16[8,128,128]{2,1,0:T(8,128)(2,1)}, u32[]{:S(2)}, u32[]{:S(2)}) collective-permute-start(bf16[8,128,128]{2,1,0:T(8,128)(2,1)S(1)} %get-tuple-element.175.refs_2_), channel_id=1, source_target_pairs={{0,8},{4,12},{8,16},{12,20},{16,24},{20,28},{24,0},{28,4},{1,9},{5... | collective-permute-start | bytes 786440 | tf_op jit(solution)/shard_map/ppermute | solution.py:782
  8.6 17.4 %collective-permute-start.3 = (bf16[8,128,128]{2,1,0:T(8,128)(2,1)S(1)}, bf16[8,128,128]{2,1,0:T(8,128)(2,1)S(1)}, u32[]{:S(2)}, u32[]{:S(2)}) collective-permute-start(bf16[8,128,128]{2,1,0:T(8,128)(2,1)S(1)} %get-tuple-element.177.refs_0_), channel_id=1, source_target_pairs={{0,4},{4,0},{8,12},{12,8},{16,20},{20,16},{24,28},{28,24},{1,5},{5... | collective-permute-start | bytes 786440 | tf_op jit(solution)/shard_map/ppermute | solution.py:777
  10.8 17.5 %collective-permute-start.4 = (bf16[8,128,128]{2,1,0:T(8,128)(2,1)S(1)}, bf16[8,128,128]{2,1,0:T(8,128)(2,1)S(1)}, u32[]{:S(2)}, u32[]{:S(2)}) collective-permute-start(bf16[8,128,128]{2,1,0:T(8,128)(2,1)S(1)} %get-tuple-element.176.refs_1_), channel_id=1, source_target_pairs={{0,4},{4,0},{8,12},{12,8},{16,20},{20,16},{24,28},{28,24},{1,5},{5... | collective-permute-start | bytes 786440 | tf_op jit(solution)/shard_map/ppermute | solution.py:777
  14.6 15.9 %collective-permute-start.5 = (bf16[8,128,128]{2,1,0:T(8,128)(2,1)S(1)}, bf16[8,128,128]{2,1,0:T(8,128)(2,1)S(1)}, u32[]{:S(2)}, u32[]{:S(2)}) collective-permute-start(bf16[8,128,128]{2,1,0:T(8,128)(2,1)S(1)} %get-tuple-element.175.refs_2_), channel_id=1, source_target_pairs={{0,4},{4,0},{8,12},{12,8},{16,20},{20,16},{24,28},{28,24},{1,5},{5... | collective-permute-start | bytes 786440 | tf_op jit(solution)/shard_map/ppermute | solution.py:777
  26.7 15.3 %collective-permute-start.14 = (bf16[8,128,128]{2,1,0:T(8,128)(2,1)}, bf16[8,128,128]{2,1,0:T(8,128)(2,1)}, u32[]{:S(2)}, u32[]{:S(2)}) collective-permute-start(bf16[8,128,128]{2,1,0:T(8,128)(2,1)} %collective-permute-done.8.refs_8_), channel_id=1, source_target_pairs={{0,8},{4,12},{8,16},{12,20},{16,24},{20,28},{24,0},{28,4},{1,9},{5... | collective-permute-start | bytes 786440 | tf_op jit(solution)/shard_map/ppermute | solution.py:782
  28.9 14.5 %collective-permute-start.10 = (bf16[8,128,128]{2,1,0:T(8,128)(2,1)}, bf16[8,128,128]{2,1,0:T(8,128)(2,1)}, u32[]{:S(2)}, u32[]{:S(2)}) collective-permute-start(bf16[8,128,128]{2,1,0:T(8,128)(2,1)} %collective-permute-done.7.refs_7_), channel_id=1, source_target_pairs={{0,4},{4,0},{8,12},{12,8},{16,20},{20,16},{24,28},{28,24},{1,5},{5... | collective-permute-start | bytes 786440 | tf_op jit(solution)/shard_map/ppermute | solution.py:777
  31.1 21.0 %collective-permute-start.1 = (bf16[256,1024]{1,0:T(8,128)(2,1)S(1)}, bf16[256,1024]{1,0:T(8,128)(2,1)S(1)}, u32[]{:S(2)}, u32[]{:S(2)}) collective-permute-start(bf16[256,1024]{1,0:T(8,128)(2,1)S(1)} %copy-done.10), channel_id=1, source_target_pairs={{0,2},{1,3},{2,0},{3,1},{4,6},{5,7},{6,4},{7,5},{8,10},{9,11},{10,... | collective-permute-start | bytes 1572872 | tf_op jit(solution)/shard_map/ppermute | solution.py:777
  32.7 21.0 %collective-permute-start = (bf16[256,1024]{1,0:T(8,128)(2,1)S(1)}, bf16[256,1024]{1,0:T(8,128)(2,1)S(1)}, u32[]{:S(2)}, u32[]{:S(2)}) collective-permute-start(bf16[256,1024]{1,0:T(8,128)(2,1)S(1)} %copy-done.10), channel_id=1, source_target_pairs={{0,1},{1,0},{2,3},{3,2},{4,5},{5,4},{6,7},{7,6},{8,9},{9,8},{10,11... | collective-permute-start | bytes 1572872 | tf_op jit(solution)/shard_map/ppermute | solution.py:777
  45.5 20.7 %collective-permute-start.15 = (bf16[8,128,128]{2,1,0:T(8,128)(2,1)}, bf16[8,128,128]{2,1,0:T(8,128)(2,1)}, u32[]{:S(2)}, u32[]{:S(2)}) collective-permute-start(bf16[8,128,128]{2,1,0:T(8,128)(2,1)} %copy-done.33), channel_id=1, source_target_pairs={{0,4},{4,0},{8,12},{12,8},{16,20},{20,16},{24,28},{28,24},{1,5},{5... | collective-permute-start | bytes 786440 | tf_op jit(solution)/shard_map/ppermute | solution.py:777
  52.1 14.2 %collective-permute-start.16 = (bf16[8,128,128]{2,1,0:T(8,128)(2,1)}, bf16[8,128,128]{2,1,0:T(8,128)(2,1)}, u32[]{:S(2)}, u32[]{:S(2)}) collective-permute-start(bf16[8,128,128]{2,1,0:T(8,128)(2,1)} %collective-permute-done.13.refs_13_), channel_id=1, source_target_pairs={{0,4},{4,0},{8,12},{12,8},{16,20},{20,16},{24,28},{28,24},{1,5},{5... | collective-permute-start | bytes 786440 | tf_op jit(solution)/shard_map/ppermute | solution.py:777
  54.9 14.5 %collective-permute-start.2 = (bf16[256,1024]{1,0:T(8,128)(2,1)S(1)}, bf16[256,1024]{1,0:T(8,128)(2,1)}, u32[]{:S(2)}, u32[]{:S(2)}) collective-permute-start(bf16[256,1024]{1,0:T(8,128)(2,1)S(1)} %collective-permute-done.1.rows_ref), channel_id=1, source_target_pairs={{0,1},{1,0},{2,3},{3,2},{4,5},{5,4},{6,7},{7,6},{8,9},{9,8},{10,11... | collective-permute-start | bytes 1572872 | tf_op jit(solution)/shard_map/ppermute | solution.py:777
  66.2 14.2 %collective-permute-start.22 = (bf16[8,128,128]{2,1,0:T(8,128)(2,1)}, bf16[8,128,128]{2,1,0:T(8,128)(2,1)S(1)}, u32[]{:S(2)}, u32[]{:S(2)}) collective-permute-start(bf16[8,128,128]{2,1,0:T(8,128)(2,1)} %collective-permute-done.19.refs_19_), channel_id=1, source_target_pairs={{0,4},{4,0},{8,12},{12,8},{16,20},{20,16},{24,28},{28,24},{1,5},{5... | collective-permute-start | bytes 786440 | tf_op jit(solution)/shard_map/ppermute | solution.py:777
  66.3 16.9 %collective-permute-start.23 = (bf16[8,128,128]{2,1,0:T(8,128)(2,1)S(1)}, bf16[8,128,128]{2,1,0:T(8,128)(2,1)S(1)}, u32[]{:S(2)}, u32[]{:S(2)}) collective-permute-start(bf16[8,128,128]{2,1,0:T(8,128)(2,1)S(1)} %collective-permute-done.20.refs_20_), channel_id=1, source_target_pairs={{0,4},{4,0},{8,12},{12,8},{16,20},{20,16},{24,28},{28,24},{1,5},{5... | collective-permute-start | bytes 786440 | tf_op jit(solution)/shard_map/ppermute | solution.py:777
  69.4 26.1 %collective-permute-start.24 = (bf16[256,1024]{1,0:T(8,128)(2,1)}, bf16[256,1024]{1,0:T(8,128)(2,1)S(1)}, u32[]{:S(2)}, u32[]{:S(2)}) collective-permute-start(bf16[256,1024]{1,0:T(8,128)(2,1)} %cot_ref.1), channel_id=1, source_target_pairs={{0,2},{1,3},{2,0},{3,1},{4,6},{5,7},{6,4},{7,5},{8,10},{9,11},{10,... | collective-permute-start | bytes 1572872 | tf_op jit(solution)/shard_map/ppermute | solution.py:777
  108.0 14.2 %collective-permute-start.27 = (bf16[256,1024]{1,0:T(8,128)(2,1)}, bf16[256,1024]{1,0:T(8,128)(2,1)}, u32[]{:S(2)}, u32[]{:S(2)}) collective-permute-start(bf16[256,1024]{1,0:T(8,128)(2,1)} %get-tuple-element.91.refs_1_.chip_ref), channel_id=1, source_target_pairs={{0,2},{1,3},{2,0},{3,1},{4,6},{5,7},{6,4},{7,5},{8,10},{9,11},{10,... | collective-permute-start | bytes 1572872 | tf_op jit(solution)/shard_map/ppermute | solution.py:777
  124.9 14.3 %collective-permute-start.30 = (bf16[256,1024]{1,0:T(8,128)(2,1)S(1)}, bf16[256,1024]{1,0:T(8,128)(2,1)S(1)}, u32[]{:S(2)}, u32[]{:S(2)}) collective-permute-start(bf16[256,1024]{1,0:T(8,128)(2,1)S(1)} %get-tuple-element.92.chip_ref.refs_0_), channel_id=1, source_target_pairs={{0,2},{1,3},{2,0},{3,1},{4,6},{5,7},{6,4},{7,5},{8,10},{9,11},{10,... | collective-permute-start | bytes 1572872 | tf_op jit(solution)/shard_map/ppermute | solution.py:777
  152.8 13.9 %collective-permute-start.34 = (bf16[256,1024]{1,0:T(8,128)(2,1)S(1)}, bf16[256,1024]{1,0:T(8,128)(2,1)S(1)}, u32[]{:S(2)}, u32[]{:S(2)}) collective-permute-start(bf16[256,1024]{1,0:T(8,128)(2,1)S(1)} %chip_sum.6.refs_0_.chip_ref), channel_id=1, source_target_pairs={{0,2},{1,3},{2,0},{3,1},{4,6},{5,7},{6,4},{7,5},{8,10},{9,11},{10,... | collective-permute-start | bytes 1572872 | tf_op jit(solution)/shard_map/ppermute | solution.py:777
  169.4 14.3 %collective-permute-start.33 = (bf16[256,1024]{1,0:T(8,128)(2,1)S(1)}, bf16[256,1024]{1,0:T(8,128)(2,1)S(1)}, u32[]{:S(2)}, u32[]{:S(2)}) collective-permute-start(bf16[256,1024]{1,0:T(8,128)(2,1)S(1)} %chip_sum.7.chip_ref.refs_0_), channel_id=1, source_target_pairs={{0,2},{1,3},{2,0},{3,1},{4,6},{5,7},{6,4},{7,5},{8,10},{9,11},{10,... | collective-permute-start | bytes 1572872 | tf_op jit(solution)/shard_map/ppermute | solution.py:777
  195.0 14.6 %collective-permute-start.39 = (bf16[256,1024]{1,0:T(8,128)(2,1)S(1)}, bf16[256,1024]{1,0:T(8,128)(2,1)S(1)}, u32[]{:S(2)}, u32[]{:S(2)}) collective-permute-start(bf16[256,1024]{1,0:T(8,128)(2,1)S(1)} %chip_sum.8.refs_0_.chip_ref), channel_id=1, source_target_pairs={{0,2},{1,3},{2,0},{3,1},{4,6},{5,7},{6,4},{7,5},{8,10},{9,11},{10,... | collective-permute-start | bytes 1572872 | tf_op jit(solution)/shard_map/ppermute | solution.py:777
  211.8 14.1 %collective-permute-start.41 = (bf16[256,1024]{1,0:T(8,128)(2,1)S(1)}, bf16[256,1024]{1,0:T(8,128)(2,1)S(1)}, u32[]{:S(2)}, u32[]{:S(2)}) collective-permute-start(bf16[256,1024]{1,0:T(8,128)(2,1)S(1)} %chip_sum.9.refs_16_.chip_ref), channel_id=1, source_target_pairs={{0,2},{1,3},{2,0},{3,1},{4,6},{5,7},{6,4},{7,5},{8,10},{9,11},{10,... | collective-permute-start | bytes 1572872 | tf_op jit(solution)/shard_map/ppermute | solution.py:777
  250.4 18.9 %collective-permute-start.48 = (bf16[12,128,128]{2,1,0:T(8,128)(2,1)S(1)}, bf16[12,128,128]{2,1,0:T(8,128)(2,1)S(1)}, u32[]{:S(2)}, u32[]{:S(2)}) collective-permute-start(bf16[12,128,128]{2,1,0:T(8,128)(2,1)S(1)} %get-tuple-element.173), channel_id=1, source_target_pairs={{0,4},{4,0},{8,12},{12,8},{16,20},{20,16},{24,28},{28,24},{1,5},{5... | collective-permute-start | bytes 1179656 | tf_op jit(solution)/shard_map/ppermute | solution.py:777
  261.0 16.6 %collective-permute-start.47 = (bf16[12,128,128]{2,1,0:T(8,128)(2,1)S(1)}, bf16[12,128,128]{2,1,0:T(8,128)(2,1)S(1)}, u32[]{:S(2)}, u32[]{:S(2)}) collective-permute-start(bf16[12,128,128]{2,1,0:T(8,128)(2,1)S(1)} %get-tuple-element.174), channel_id=1, source_target_pairs={{0,4},{4,0},{8,12},{12,8},{16,20},{20,16},{24,28},{28,24},{1,5},{5... | collective-permute-start | bytes 1179656 | tf_op jit(solution)/shard_map/ppermute | solution.py:777
  272.6 13.5 %collective-permute-start.46 = (bf16[12,128,128]{2,1,0:T(8,128)(2,1)S(1)}, bf16[12,128,128]{2,1,0:T(8,128)(2,1)S(1)}, u32[]{:S(2)}, u32[]{:S(2)}) collective-permute-start(bf16[12,128,128]{2,1,0:T(8,128)(2,1)S(1)} %get-tuple-element.167), channel_id=1, source_target_pairs={{0,4},{4,0},{8,12},{12,8},{16,20},{20,16},{24,28},{28,24},{1,5},{5... | collective-permute-start | bytes 1179656 | tf_op jit(solution)/shard_map/ppermute | solution.py:777
  274.1 20.4 %collective-permute-start.56 = (bf16[12,128,128]{2,1,0:T(8,128)(2,1)S(1)}, bf16[12,128,128]{2,1,0:T(8,128)(2,1)S(1)}, u32[]{:S(2)}, u32[]{:S(2)}) collective-permute-start(bf16[12,128,128]{2,1,0:T(8,128)(2,1)S(1)} %get-tuple-element.168), channel_id=1, source_target_pairs={{0,4},{4,0},{8,12},{12,8},{16,20},{20,16},{24,28},{28,24},{1,5},{5... | collective-permute-start | bytes 1179656 | tf_op jit(solution)/shard_map/ppermute | solution.py:777
  283.2 19.8 %collective-permute-start.55 = (bf16[12,128,128]{2,1,0:T(8,128)(2,1)S(1)}, bf16[12,128,128]{2,1,0:T(8,128)(2,1)S(1)}, u32[]{:S(2)}, u32[]{:S(2)}) collective-permute-start(bf16[12,128,128]{2,1,0:T(8,128)(2,1)S(1)} %get-tuple-element.169), channel_id=1, source_target_pairs={{0,4},{4,0},{8,12},{12,8},{16,20},{20,16},{24,28},{28,24},{1,5},{5... | collective-permute-start | bytes 1179656 | tf_op jit(solution)/shard_map/ppermute | solution.py:777
  295.0 34.3 %collective-permute-start.54 = (bf16[12,128,128]{2,1,0:T(8,128)(2,1)}, bf16[12,128,128]{2,1,0:T(8,128)(2,1)}, u32[]{:S(2)}, u32[]{:S(2)}) collective-permute-start(bf16[12,128,128]{2,1,0:T(8,128)(2,1)} %get-tuple-element.170), channel_id=1, source_target_pairs={{0,4},{4,0},{8,12},{12,8},{16,20},{20,16},{24,28},{28,24},{1,5},{5... | collective-permute-start | bytes 1179656 | tf_op jit(solution)/shard_map/ppermute | solution.py:777
  299.2 27.5 %collective-permute-start.44 = (bf16[256,1024]{1,0:T(8,128)(2,1)}, bf16[256,1024]{1,0:T(8,128)(2,1)S(1)}, u32[]{:S(2)}, u32[]{:S(2)}) collective-permute-start(bf16[256,1024]{1,0:T(8,128)(2,1)} %get-tuple-element.145), channel_id=1, source_target_pairs={{0,1},{1,0},{2,3},{3,2},{4,5},{5,4},{6,7},{7,6},{8,9},{9,8},{10,11... | collective-permute-start | bytes 1572872 | tf_op jit(solution)/shard_map/ppermute | solution.py:777
  307.1 23.8 %collective-permute-start.58 = (bf16[12,128,128]{2,1,0:T(8,128)(2,1)}, bf16[12,128,128]{2,1,0:T(8,128)(2,1)}, u32[]{:S(2)}, u32[]{:S(2)}) collective-permute-start(bf16[12,128,128]{2,1,0:T(8,128)(2,1)} %fusion.2), channel_id=1, source_target_pairs={{0,8},{4,12},{8,16},{12,20},{16,24},{20,28},{24,0},{28,4},{1,9},{5... | collective-permute-start | bytes 1179656 | tf_op jit(solution)/shard_map/ppermute | solution.py:782
  322.9 21.5 %collective-permute-start.53 = (bf16[12,128,128]{2,1,0:T(8,128)(2,1)}, bf16[12,128,128]{2,1,0:T(8,128)(2,1)S(1)}, u32[]{:S(2)}, u32[]{:S(2)}) collective-permute-start(bf16[12,128,128]{2,1,0:T(8,128)(2,1)} %get-tuple-element.171), channel_id=1, source_target_pairs={{0,4},{4,0},{8,12},{12,8},{16,20},{20,16},{24,28},{28,24},{1,5},{5... | collective-permute-start | bytes 1179656 | tf_op jit(solution)/shard_map/ppermute | solution.py:777
  329.3 14.1 %collective-permute-start.45 = (bf16[256,1024]{1,0:T(8,128)(2,1)S(1)}, bf16[256,1024]{1,0:T(8,128)(2,1)S(1)}, u32[]{:S(2)}, u32[]{:S(2)}) collective-permute-start(bf16[256,1024]{1,0:T(8,128)(2,1)S(1)} %chip_sum.11), channel_id=1, source_target_pairs={{0,2},{1,3},{2,0},{3,1},{4,6},{5,7},{6,4},{7,5},{8,10},{9,11},{10,... | collective-permute-start | bytes 1572872 | tf_op jit(solution)/shard_map/ppermute | solution.py:777
  332.3 12.8 %collective-permute-start.59 = (bf16[12,128,128]{2,1,0:T(8,128)(2,1)S(1)}, bf16[12,128,128]{2,1,0:T(8,128)(2,1)S(1)}, u32[]{:S(2)}, u32[]{:S(2)}) collective-permute-start(bf16[12,128,128]{2,1,0:T(8,128)(2,1)S(1)} %fusion.4), channel_id=1, source_target_pairs={{0,8},{4,12},{8,16},{12,20},{16,24},{20,28},{24,0},{28,4},{1,9},{5... | collective-permute-start | bytes 1179656 | tf_op jit(solution)/shard_map/ppermute | solution.py:782
  (81 other events, 761.4 us)

commit v5 on v4

--- a/solution.py
+++ b/solution.py
@@ -67,55 +67,48 @@
     return dot_of(left, right, 1, 1)
 
 
-def adam_kernel(
-    rates_ref, grad_ref, first_ref, second_ref, master_ref, left_stat_ref, right_stat_ref,
-    left_ref, right_ref, new_first_ref, new_second_ref, new_master_ref, new_left_ref,
-    new_right_ref, gram_ref, product_ref, *, per,
-):
-    step = pl.program_id(0)
+def adam_group(items, grads, states, rates, gram_ref, product_ref, count):
     correction = 1.0 - moment_decay**STEP
-    for item in range(per):
-        grad = grad_ref[item]
-        left, right = split_two(left_ref[item]), split_two(right_ref[item])
-        rotated = dot_two(left, dot_two(right, grad, 0, 1, True).astype(bfloat), 0, 0)
-        new_first = moment_decay * first_ref[item] + (1.0 - moment_decay) * rotated
-        new_second = moment_decay * second_ref[item] + (1.0 - moment_decay) * rotated * rotated
-        new_first_ref[item] = new_first
-        new_second_ref[item] = new_second
-        direction = (new_first / correction) / (jnp.sqrt(new_second / correction) + 1e-8)
-        turned = dot_two(right, direction.astype(bfloat), 1, 1, True)
-        turned = dot_two(left, turned.astype(bfloat), 1, 0)
-        master = master_ref[item]
-        new_master_ref[item] = master - rates_ref[step * per + item] * (turned + 0.01 * master)
-        scale = (1.0 - moment_decay) / BLK
-        new_left = moment_decay * left_stat_ref[item] + scale * dot_of(grad, grad, 1, 1)
-        new_right = moment_decay * right_stat_ref[item] + scale * dot_of(grad, grad, 0, 0)
-        new_left_ref[item] = new_left
-        new_right_ref[item] = new_right
-        for side, (stats, basis) in enumerate(((new_left, left), (new_right, right))):
-            product = dot_three(basis, split_two(stats), 0, 0)
-            product_ref[side, item] = product
-            gram_ref[side, item] = gram_six(split_three(product))
-
-
-def adam(grads, first, second, master, left_stats, right_stats, left, right, rates, per):
-    count = grads.shape[0]
-    block = pl.BlockSpec((per, BLK, BLK), lambda i, *_: (i, 0, 0))
-    pair = pl.BlockSpec((2, per, BLK, BLK), lambda i, *_: (0, i, 0, 0))
-    one = jax.ShapeDtypeStruct((count, BLK, BLK), single)
-    two = jax.ShapeDtypeStruct((2, count, BLK, BLK), single)
-    return pl.pallas_call(
-        functools.partial(adam_kernel, per=per),
-        grid_spec=pltpu.PrefetchScalarGridSpec(
-            num_scalar_prefetch=1,
-            grid=(count // per,),
-            in_specs=[block] * 8,
-            out_specs=[block] * 5 + [pair] * 2,
-        ),
-        out_shape=[one] * 5 + [two] * 2,
-        compiler_params=pltpu.CompilerParams(vmem_limit_bytes=48 * 2**20),
-        name="adam",
-    )(rates, grads, first, second, master, left_stats, right_stats, left, right)
+    scale = (1.0 - moment_decay) / BLK
+    first, second, master, left_stat, right_stat, left, right = zip(*states)
+    left_t = [split_two(value.T) for value in left]
+    right_t = [split_two(value.T) for value in right]
+    left = [split_two(value) for value in left]
+    right = [split_two(value) for value in right]
+    half = [dot_two(r, g, 0, 1, True).astype(bfloat) for r, g in zip(right, grads)]
+    new_left = [
+        moment_decay * old + scale * dot_of(g, g, 1, 1) for old, g in zip(left_stat, grads)
+    ]
+    new_right = [
+        moment_decay * old + scale * dot_of(g, g, 0, 0) for old, g in zip(right_stat, grads)
+    ]
+    rotated = [dot_two(t, value, 1, 0) for t, value in zip(left_t, half)]
+    sides = []
+    for stats, basis in ((new_left, left_t), (new_right, right_t)):
+        sides.append([dot_three(b, split_two(value), 1, 0) for b, value in zip(basis, stats)])
+    new_first = [moment_decay * old + (1.0 - moment_decay) * r for old, r in zip(first, rotated)]
+    new_second = [
+        moment_decay * old + (1.0 - moment_decay) * r * r for old, r in zip(second, rotated)
+    ]
+    direction = [
+        ((m / correction) / (jnp.sqrt(v / correction) + adam_eps)).astype(bfloat)
+        for m, v in zip(new_first, new_second)
+    ]
+    half = [
+        dot_two(t, value, 0, 1, True).astype(bfloat) for t, value in zip(right_t, direction)
+    ]
+    grams = [[gram_six(split_three(value)) for value in side] for side in sides]
+    turned = [dot_two(b, value, 1, 0) for b, value in zip(left, half)]
+    new_master = [
+        old - rate * (value + weight_decay * old)
+        for old, rate, value in zip(master, rates, turned)
+    ]
+    for side in range(2):
+        for item, product, gram in zip(items, sides[side], grams[side]):
+            here = pl.ds(pl.multiple_of((side * count + item) * BLK, BLK), BLK)
+            product_ref[here, :] = product
+            gram_ref[here, :] = gram
+    return list(zip(new_first, new_second, new_master, new_left, new_right))
 
 
 def factor_panel(rows):
@@ -152,11 +145,8 @@
     return inverse
 
 
-def renew_kernel(
-    gram_in_ref, product_in_ref, left_ref, right_ref, gram_ref, product_ref, inverse_ref, *, count, unroll
-):
-    gram_ref[...] = gram_in_ref[...]
-    product_ref[...] = product_in_ref[...]
+def renew(gram_ref, product_ref, inverse_ref, count):
+    group = math.gcd(count, 16)
     lane = lax.broadcasted_iota(jnp.int32, (PANEL, BLK), 1)
     for panel in range(BLK // PANEL):
         top = panel * PANEL
@@ -170,62 +160,142 @@
             row = jnp.concatenate(inverse[i], 0)
             inverse_ref[pl.ds(i, count, stride=PANEL), :] = jnp.concatenate([row] * 4, 0).T
 
-        def step(item, nothing):
-            base = pl.multiple_of(item * BLK, BLK)
-            here = pl.ds(pl.multiple_of(item * PANEL, PANEL), PANEL)
-            high, mid, low = split_three(inverse_ref[here, :])
-            none = jnp.zeros_like(high)
-            left = jnp.concatenate(
-                [
-                    jnp.where(lane < 3 * PANEL, high, none),
-                    jnp.where(lane < 2 * PANEL, mid, none),
-                    jnp.where(lane < PANEL, low, none),
-                ],
-                0,
-            )[:, : 3 * PANEL]
-            rows_at = pl.ds(base + top, PANEL)
-            whole = product_ref[rows_at, :]
+        def step(index, nothing):
+            bases = [pl.multiple_of((index * group + g) * BLK, BLK) for g in range(group)]
+            lefts, wholes = [], []
+            for g in range(group):
+                here = pl.ds(pl.multiple_of((index * group + g) * PANEL, PANEL), PANEL)
+                lefts.append(inverse_ref[here, :])
+                rows_at = pl.ds(bases[g] + top, PANEL)
+                whole = product_ref[rows_at, :]
+                if not last:
+                    whole = jnp.concatenate([gram_ref[rows_at, :], whole], 1)
+                wholes.append(whole)
+            rest = [pl.ds(base + top + PANEL, BLK - top - PANEL) for base in bases]
             if not last:
-                whole = jnp.concatenate([gram_ref[rows_at, :], whole], 1)
-            solved = dot_of(left, jnp.concatenate(split_three(whole), 0), 1, 0)
-            solved = solved[:PANEL] + (solved[PANEL : 2 * PANEL] + solved[2 * PANEL :])
-            product_ref[rows_at, :] = solved[:, -BLK:]
+                old = [(gram_ref[at, :], product_ref[at, :]) for at in rest]
+            lefts = [six_rows(split_three(left), lane) for left in lefts]
+            wholes = [jnp.concatenate(split_three(whole), 0) for whole in wholes]
+            solved = [dot_of(left, whole, 1, 0) for left, whole in zip(lefts, wholes)]
+            solved = [
+                value[:PANEL] + (value[PANEL : 2 * PANEL] + value[2 * PANEL :])
+                for value in solved
+            ]
             if not last:
-                high, mid, low = split_three(solved)
-                left = jnp.concatenate([high, high, high, mid, mid, low], 0)[:, top + PANEL : BLK]
-                right = jnp.concatenate([high, mid, low, high, mid, high], 0)
-                update = dot_of(left, right, 0, 0)
-                rest = pl.ds(base + top + PANEL, BLK - top - PANEL)
-                gram_ref[rest, :] = gram_ref[rest, :] - update[:, :BLK]
-                product_ref[rest, :] = product_ref[rest, :] - update[:, BLK:]
+                pieces = [split_three(value) for value in solved]
+                lefts = [
+                    jnp.concatenate([high, high, high, mid, mid, low], 0)[:, top + PANEL : BLK]
+                    for high, mid, low in pieces
+                ]
+                rights = [
+                    jnp.concatenate([high, mid, low, high, mid, high], 0)
+                    for high, mid, low in pieces
+                ]
+                update = [dot_of(left, right, 0, 0) for left, right in zip(lefts, rights)]
+            for g in range(group):
+                product_ref[pl.ds(bases[g] + top, PANEL), :] = solved[g][:, -BLK:]
+                if not last:
+                    gram_ref[rest[g], :] = old[g][0] - update[g][:, :BLK]
+                    product_ref[rest[g], :] = old[g][1] - update[g][:, BLK:]
             return nothing
 
-        lax.fori_loop(0, count, step, 0, unroll=math.gcd(count, unroll))
-
-    half = count // 2
-    for side, basis_ref in enumerate((left_ref, right_ref)):
-
-        def finish(item, nothing):
-            base = pl.multiple_of((side * half + item) * BLK, BLK)
-            basis_ref[item] = product_ref[pl.ds(base, BLK), :].T
-            return nothing
-
-        lax.fori_loop(0, half, finish, 0, unroll=math.gcd(half, unroll))
-
-
-def renew(gram, product, unroll=16):
-    count = gram.shape[0] * gram.shape[1]
-    whole = pl.BlockSpec(memory_space=pltpu.VMEM)
+        lax.fori_loop(0, count // group, step, 0)
+
+
+def six_rows(pieces, lane):
+    high, mid, low = pieces
+    none = jnp.zeros_like(high)
+    return jnp.concatenate(
+        [
+            jnp.where(lane < 3 * PANEL, high, none),
+            jnp.where(lane < 2 * PANEL, mid, none),
+            jnp.where(lane < PANEL, low, none),
+        ],
+        0,
+    )[:, : 3 * PANEL]
+
+
+def optimise_kernel(slots_ref, rates_ref, *refs, count, adds):
+    grads, states = refs[:adds], refs[adds : adds + 7]
+    outs = refs[-16:-9]
+    in_ref, out_ref, gram_ref, product_ref, inverse_ref, in_sems, out_sem, _ = refs[-8:]
+    for item in range(count):
+        for index, state in enumerate(states):
+            pltpu.make_async_copy(
+                state.at[slots_ref[item]], in_ref.at[item, index], in_sems.at[item]
+            ).start()
+
+    group = math.gcd(count, 4)
+
+    def update(step, nothing):
+        items = [step * group + index for index in range(group)]
+        gradients = []
+        for item in items:
+            pltpu.make_async_copy(in_ref.at[item], in_ref.at[item], in_sems.at[item]).wait()
+            grad = grads[0][item].astype(single)
+            for other in grads[1:]:
+                grad = grad + other[item].astype(single)
+            gradients.append(grad.astype(bfloat))
+        results = adam_group(
+            items, gradients, [[in_ref[item, index] for index in range(7)] for item in items],
+            [rates_ref[item] for item in items], gram_ref, product_ref, count,
+        )
+        for item, values in zip(items, results):
+            for index, value in enumerate(values):
+                out_ref[item, index] = value
+        for item in items:
+            for index in range(5):
+                pltpu.make_async_copy(
+                    out_ref.at[item, index], outs[index].at[slots_ref[item]], out_sem
+                ).start()
+        return nothing
+
+    lax.fori_loop(0, count // group, update, 0)
+    renew(gram_ref, product_ref, inverse_ref, 2 * count)
+
+    def finish(item, nothing):
+        for side in range(2):
+            base = pl.multiple_of((side * count + item) * BLK, BLK)
+            out_ref[item, 5 + side] = product_ref[pl.ds(base, BLK), :].T
+            pltpu.make_async_copy(
+                out_ref.at[item, 5 + side], outs[5 + side].at[slots_ref[item]], out_sem
+            ).start()
+        return nothing
+
+    lax.fori_loop(0, count, finish, 0, unroll=math.gcd(count, 4))
+    pltpu.make_async_copy(out_ref, out_ref, out_sem).wait()
+
+
+def optimise(slots, rates, grads, states, earlier=None, after=()):
+    count, total = slots.shape[0], states[0].shape[0]
+    more = [] if earlier is None else list(earlier)
+    skip = 2 + len(grads) + 7
     return pl.pallas_call(
-        functools.partial(renew_kernel, count=count, unroll=unroll),
-        in_specs=[whole] * 2,
-        out_specs=[whole] * 2,
-        out_shape=[jax.ShapeDtypeStruct((count // 2, BLK, BLK), single)] * 2,
-        scratch_shapes=[pltpu.VMEM((count * BLK, BLK), single)] * 2
-        + [pltpu.VMEM((count * PANEL, BLK), single)],
-        compiler_params=pltpu.CompilerParams(vmem_limit_bytes=48 * 2**20),
-        name="renew",
-    )(gram.reshape(count * BLK, BLK), product.reshape(count * BLK, BLK))
+        functools.partial(optimise_kernel, count=count, adds=len(grads)),
+        grid_spec=pltpu.PrefetchScalarGridSpec(
+            num_scalar_prefetch=2,
+            grid=(),
+            in_specs=[whole_spec()] * len(grads)
+            + [in_hbm()] * (7 + len(more))
+            + [anywhere()] * len(after),
+            out_specs=[in_hbm()] * 7 + [anywhere()],
+            scratch_shapes=[
+                pltpu.VMEM((count, 7, BLK, BLK), single),
+                pltpu.VMEM((count, 7, BLK, BLK), single),
+                pltpu.VMEM((2 * count * BLK, BLK), single),
+                pltpu.VMEM((2 * count * BLK, BLK), single),
+                pltpu.VMEM((2 * count * PANEL, BLK), single),
+                pltpu.SemaphoreType.DMA((count,)),
+                pltpu.SemaphoreType.DMA,
+                pltpu.SMEM((1,), jnp.int32),
+            ],
+        ),
+        out_shape=[of((total, BLK, BLK), single)] * 7 + [token_of()],
+        input_output_aliases={skip + index: index for index in range(7)} if more else {},
+        cost_estimate=cost(count * 40 * BLK**3, *grads, *states),
+        compiler_params=pltpu.CompilerParams(vmem_limit_bytes=56 * 2**20),
+        name="optimise",
+    )(slots, rates, *grads, *states, *more, *after)
 
 
 def whole_spec():
@@ -238,6 +308,14 @@
 
 def anywhere():
     return pl.BlockSpec(memory_space=pl.ANY)
+
+
+def token_of():
+    return of((8, 128), single)
+
+
+def in_hbm():
+    return pl.BlockSpec(memory_space=pltpu.HBM)
 
 
 def cost(flops, *arrays):
@@ -254,7 +332,7 @@
 
 
 def attend_kernel(q_ref, k_ref, v_ref, valid_ref, w_ref, *refs, heads, own):
-    attended_ref, lse_ref, branch_ref, flipped_ref, score_ref, prob_ref = refs[-6:]
+    attended_ref, lse_ref, branch_ref, _, flipped_ref, score_ref, prob_ref = refs[-7:]
     keys, width = k_ref.shape
     rows = q_ref.shape[0]
     tile = 128
@@ -313,7 +391,9 @@
     heads = width // HEAD_DIM
     own = received is not None
     more = [received] if own else []
-    out_shape = [of((rows, width), bfloat), of((heads, rows), single), of((rows, D), bfloat)]
+    out_shape = [
+        of((rows, width), bfloat), of((heads, rows), single), of((rows, D), bfloat), token_of()
+    ]
     return pl.pallas_call(
         functools.partial(attend_kernel, heads=heads, own=own),
         grid=(1,),
@@ -324,7 +404,7 @@
             fixed(valid.shape),
             fixed(w_out.shape),
         ] + [fixed(value.shape) for value in more] + [anywhere()] * len(after),
-        out_specs=[fixed(value.shape) for value in out_shape],
+        out_specs=[fixed(value.shape) for value in out_shape[:-1]] + [anywhere()],
         out_shape=out_shape,
         scratch_shapes=[
             pltpu.VMEM((width, seq), bfloat), pltpu.VMEM((seq, rows), single),
@@ -341,11 +421,11 @@
     refs = refs[:inputs] + refs[inputs + extra :]
     if first:
         (own_ref, peer_ref, w_ref, q_ref, k_ref, v_ref, att_own, att_peer, lse_own, lse_peer,
-         valid_ref, dq_ref, dk_ref, dv_ref, flipped_ref, grad_ref, score_ref, cross_ref, prob_ref, back_ref,
+         valid_ref, dq_ref, dk_ref, dv_ref, _, flipped_ref, grad_ref, score_ref, cross_ref, prob_ref, back_ref,
          att_ref, log_ref, dk_sum, dv_sum) = refs
     else:
         (own_ref, peer_ref, w_ref, q_ref, k_ref, v_ref, att_own, att_peer, lse_own, lse_peer,
-         valid_ref, dk_in_ref, dv_in_ref, dq_ref, dk_ref, dv_ref, flipped_ref, grad_ref, score_ref,
+         valid_ref, dk_in_ref, dv_in_ref, dq_ref, dk_ref, dv_ref, _, flipped_ref, grad_ref, score_ref,
          cross_ref, prob_ref, back_ref, att_ref, log_ref, dk_sum, dv_sum) = refs
     step = pl.program_id(0)
     keys, width = k_ref.shape
@@ -431,7 +511,9 @@
     first = earlier is None
     kind = single if first else bfloat
     more = [] if first else list(earlier)
-    out_shape = [of((2 * rows, width), bfloat), of((seq, width), kind), of((seq, width), kind)]
+    out_shape = [
+        of((2 * rows, width), bfloat), of((seq, width), kind), of((seq, width), kind), token_of()
+    ]
     return pl.pallas_call(
         functools.partial(attend_back_kernel, heads=heads, first=first, extra=len(after)),
         grid=(2,),
@@ -445,7 +527,7 @@
         ] + [fixed((seq, width))] * len(more) + [anywhere()] * len(after),
         out_specs=[
             pl.BlockSpec((rows, width), lambda i: (i, 0)),
-            fixed((seq, width)), fixed((seq, width)),
+            fixed((seq, width)), fixed((seq, width)), anywhere(),
         ],
         out_shape=out_shape,
         scratch_shapes=[
@@ -475,7 +557,7 @@
 
 
 def feed_kernel(rows_ref, up_ref, bias_ref, down_ref, *refs):
-    act_ref, slope_ref, out_ref, pre_ref, sum_ref = refs[-5:]
+    act_ref, slope_ref, out_ref, _, pre_ref, sum_ref = refs[-6:]
     step = pl.program_id(0)
     rows = rows_ref.shape[0]
     tile = 32
@@ -511,7 +593,9 @@
 def feed(block, w_up, bias, w_down, kind, after=()):
     rows, hidden = block.shape[0], w_up.shape[1]
     step = 256
-    out_shape = [of((rows, hidden), bfloat), of((rows, hidden), bfloat), of((rows, D), kind)]
+    out_shape = [
+        of((rows, hidden), bfloat), of((rows, hidden), bfloat), of((rows, D), kind), token_of()
+    ]
     return pl.pallas_call(
         feed_kernel,
         grid=(hidden // step,),
@@ -524,7 +608,7 @@
         out_specs=[
             pl.BlockSpec((rows, step), lambda j: (0, j)),
             pl.BlockSpec((rows, step), lambda j: (0, j)),
-            fixed((rows, D)),
+            fixed((rows, D)), anywhere(),
         ],
         out_shape=out_shape,
         scratch_shapes=[pltpu.VMEM((rows, step), single), pltpu.VMEM((rows, D), single)],
@@ -535,7 +619,7 @@
 
 
 def feed_back_kernel(rows_ref, down_ref, up_ref, slope_ref, *refs):
-    grad_ref, bias_ref, out_ref, sum_ref = refs[-4:]
+    grad_ref, bias_ref, out_ref, _, sum_ref = refs[-5:]
     grads = dot_of(rows_ref[...], down_ref[...], 1, 1) * slope_ref[...].astype(single)
     grads = grads.astype(bfloat)
     grad_ref[...] = grads
@@ -546,7 +630,9 @@
 def feed_back(block, w_down, w_up, slope, kind, after=()):
     rows, hidden = block.shape[0], w_up.shape[1]
     step = 256
-    out_shape = [of((rows, hidden), bfloat), of((1, hidden), single), of((rows, D), kind)]
+    out_shape = [
+        of((rows, hidden), bfloat), of((1, hidden), single), of((rows, D), kind), token_of()
+    ]
     return pl.pallas_call(
         feed_back_kernel,
         grid=(hidden // step,),
@@ -559,7 +645,7 @@
         out_specs=[
             pl.BlockSpec((rows, step), lambda j: (0, j)),
             pl.BlockSpec((1, step), lambda j: (0, j)),
-            fixed((rows, D)),
+            fixed((rows, D)), anywhere(),
         ],
         out_shape=out_shape,
         scratch_shapes=[pltpu.VMEM((rows, D), single)],
@@ -570,7 +656,7 @@
 
 
 def chip_kernel(keep_ref, got_ref, *refs):
-    refs[-1][...] = (keep_ref[...] + got_ref[...].astype(single)).astype(bfloat)
+    refs[-2][...] = (keep_ref[...] + got_ref[...].astype(single)).astype(bfloat)
 
 
 def standardise(value):
@@ -598,7 +684,7 @@
 
 
 def norm_one_kernel(chip_ref, across_ref, rows_ref, vectors_ref, *refs):
-    normed_ref, inv_ref, hidden_ref = refs[-3:]
+    normed_ref, inv_ref, hidden_ref = refs[-4:-1]
     branch = chip_ref[...].astype(single) + across_ref[...].astype(single)
     normed, inv_std = standardise(rows_ref[...].astype(single) + (branch + vectors_ref[2:3, :]))
     normed_ref[...] = normed
@@ -609,7 +695,7 @@
 def norm_two_kernel(
     chip_ref, across_ref, normed_ref, cot_ref, valid_ref, one_ref, two_ref, *refs
 ):
-    out_ref, grad_ref, low_ref, sums_ref = refs[-4:]
+    out_ref, grad_ref, low_ref, sums_ref = refs[-5:-1]
 
     @pl.when(pl.program_id(0) == 0)
     def _():
@@ -631,7 +717,7 @@
 def norm_back_kernel(
     chip_ref, across_ref, second_ref, normed_ref, inv_ref, one_ref, *refs
 ):
-    grad_ref, low_ref, sums_ref = refs[-3:]
+    grad_ref, low_ref, sums_ref = refs[-4:-1]
 
     @pl.when(pl.program_id(0) == 0)
     def _():
@@ -654,6 +740,8 @@
     if sums:
         out_shape.append(of((8, D), single))
         out_specs.append(fixed((8, D)))
+    out_shape.append(token_of())
+    out_specs.append(anywhere())
     return pl.pallas_call(
         kernel,
         grid=(rows // norm_tile,),
@@ -669,7 +757,7 @@
 
 
 def token_back_kernel(*refs):
-    dq_refs, (dk_ref, dv_ref, w_ref), outs = refs[:2], refs[2:5], refs[5:]
+    dq_refs, (dk_ref, dv_ref, w_ref), outs = refs[:2], refs[2:5], refs[-5:-1]
     width = dk_ref.shape[1]
     rows = dk_ref.shape[0] // 4
     for block in range(4):
@@ -682,82 +770,126 @@
         outs[block][...] = value.astype(outs[block].dtype)
 
 
-def token_back(dq_a, dq_b, dk, dv, w_qkv):
+def token_back(dq_a, dq_b, dk, dv, w_qkv, after=()):
     rows = dk.shape[0] // 4
-    out_shape = [of((rows, D), kind) for kind in (single, bfloat, single, bfloat)]
+    out_shape = [of((rows, D), kind) for kind in (single, bfloat, single, bfloat)] + [token_of()]
     return pl.pallas_call(
         token_back_kernel,
-        in_specs=[whole_spec()] * 5,
-        out_specs=[whole_spec()] * 4,
+        in_specs=[whole_spec()] * 5 + [anywhere()] * len(after),
+        out_specs=[whole_spec()] * 4 + [anywhere()],
         out_shape=out_shape,
         cost_estimate=cost(8 * rows * D * w_qkv.shape[1], w_qkv, dk, *out_shape),
         compiler_params=pltpu.CompilerParams(vmem_limit_bytes=24 * 2**20),
         name="token_back",
-    )(dq_a, dq_b, dk, dv, w_qkv)
-
-
-def pack_kernel(target_ref, *refs, jobs, scale):
-    inputs, out_ref, held_ref, sem = refs[:-3], refs[-3], refs[-2], refs[-1]
-    place = 0
+    )(dq_a, dq_b, dk, dv, w_qkv, *after)
+
+
+def pack_kernel(target_ref, *refs, jobs, scale, regions, count, resumed):
+    outs = refs[-4 - len(regions) : -4]
+    held_ref, sem, in_sem = refs[-3:]
+    if resumed:
+        start = pltpu.make_async_copy(refs[count], held_ref, in_sem)
+        start.start()
+    waited = not resumed
     for lefts, rights, layout, rows, cols in jobs:
+        right = jnp.concatenate([refs[index][...] for index in rights], 0)
         for row in range(0, rows, 2):
             span = min(2, rows - row)
-            weights = 0.0
-            for (left, left_at, size), (right, right_at, _) in zip(lefts, rights):
-                weights = weights + dot_of(
-                    inputs[left][left_at : left_at + size, row * BLK : (row + span) * BLK],
-                    inputs[right][right_at : right_at + size, :],
-                    0,
-                    0,
-                )
-            weights = (weights * scale).astype(bfloat)
+            left = jnp.concatenate(
+                [refs[index][:, row * BLK : (row + span) * BLK] for index in lefts], 0
+            )
+            weights = (dot_of(left, right, 0, 0) * scale).astype(bfloat)
+            if not waited:
+                start.wait()
+                waited = True
             for i in range(span):
                 for col in range(cols):
-                    held_ref[place] = weights[
+                    held_ref[target_ref[layout(row + i, col)]] = weights[
                         i * BLK : (i + 1) * BLK, col * BLK : (col + 1) * BLK
                     ]
-                    pltpu.make_async_copy(
-                        held_ref.at[place], out_ref.at[target_ref[layout(row + i, col)]], sem
-                    ).start()
-                    place += 1
-    pltpu.make_async_copy(held_ref, out_ref.at[pl.ds(0, place)], sem).wait()
-
-
-def pack(target, pairs, scale, total, earlier=None, after=()):
+    copies = [
+        pltpu.make_async_copy(held_ref.at[first : first + size], out, sem.at[index])
+        for index, ((first, size), out) in enumerate(zip(regions, outs))
+    ]
+    for copy in copies:
+        copy.start()
+    for copy in copies:
+        copy.wait()
+
+
+def pack(target, pairs, scale, regions, earlier=None, after=()):
     operands, jobs, blocks, flops = [], [], 0, 0
-
-    def segments(arrays, size):
+    total = target.shape[0]
+
+    def places(arrays):
         found = []
         for value in arrays:
             if not any(value is other for other in operands):
                 operands.append(value)
-            index = [value is other for other in operands].index(True)
-            found += [(index, at, size) for at in range(0, value.shape[0], size)]
+            found.append([value is other for other in operands].index(True))
         return found
 
     for lefts, rights, layout in pairs:
-        size = min(value.shape[0] for value in lefts + rights)
         rows, cols = lefts[0].shape[1] // BLK, rights[0].shape[1] // BLK
-        jobs.append((segments(lefts, size), segments(rights, size), layout, rows, cols))
+        jobs.append((places(lefts), places(rights), layout, rows, cols))
         blocks += rows * cols
         flops += 2 * rows * cols * BLK * BLK * sum(value.shape[0] for value in lefts)
-    some = pl.BlockSpec(memory_space=pl.ANY)
     more = [] if earlier is None else [earlier]
     return pl.pallas_call(
-        functools.partial(pack_kernel, jobs=jobs, scale=scale),
+        functools.partial(
+            pack_kernel, jobs=jobs, scale=scale, regions=regions, count=len(operands),
+            resumed=bool(more),
+        ),
         grid_spec=pltpu.PrefetchScalarGridSpec(
             num_scalar_prefetch=1,
             grid=(),
-            in_specs=[whole_spec()] * len(operands) + [some] * (len(more) + len(after)),
-            out_specs=some,
-            scratch_shapes=[pltpu.VMEM((blocks, BLK, BLK), bfloat), pltpu.SemaphoreType.DMA],
+            in_specs=[whole_spec()] * len(operands)
+            + [in_hbm()] * len(more)
+            + [anywhere()] * len(after),
+            out_specs=[in_hbm()] * len(regions) + [anywhere()],
+            scratch_shapes=[
+                pltpu.VMEM((total, BLK, BLK), bfloat),
+                pltpu.SemaphoreType.DMA((len(regions),)),
+                pltpu.SemaphoreType.DMA,
+            ],
         ),
-        out_shape=of((total, BLK, BLK), bfloat),
-        input_output_aliases={1 + len(operands): 0} if more else {},
+        out_shape=[of((size, BLK, BLK), bfloat) for _, size in regions] + [token_of()],
         cost_estimate=cost(flops, *operands, of((blocks, BLK, BLK), bfloat)),
-        compiler_params=pltpu.CompilerParams(vmem_limit_bytes=32 * 2**20),
+        compiler_params=pltpu.CompilerParams(vmem_limit_bytes=40 * 2**20),
         name="pack",
     )(target, *operands, *more, *after)
+
+
+def join_kernel(*refs, groups):
+    out_ref = refs[-2]
+    at = 0
+    for index, terms in enumerate(groups):
+        total = 0.0
+        for ref in refs[at : at + terms]:
+            value = ref[...].reshape(-1, BLK, BLK)
+            total = total + value.astype(single)
+        at += terms
+        size = total.shape[0]
+        out_ref[index * size : (index + 1) * size] = total.astype(bfloat)
+
+
+def join(hop, groups, after=()):
+    operands, specs = [], []
+    for keep, got, *carried in groups:
+        slots = keep.shape[0] // (lax.axis_size("dp") // 2)
+        block = pl.BlockSpec((slots, BLK, BLK), lambda i: (hop, 0, 0))
+        operands += [keep, got, *carried]
+        specs += [block] + [fixed((slots, BLK, BLK))] * (1 + len(carried))
+    out = of((slots * len(groups), BLK, BLK), bfloat)
+    return pl.pallas_call(
+        functools.partial(join_kernel, groups=[len(group) for group in groups]),
+        grid=(1,),
+        in_specs=specs + [anywhere()] * len(after),
+        out_specs=[fixed(out.shape), anywhere()],
+        out_shape=[out, token_of()],
+        cost_estimate=cost(1, out),
+        name="join",
+    )(*operands, *after)
 
 
 def block_counts(tensors):
@@ -782,21 +914,12 @@
     return lax.ppermute(value, "dp", [(i, (i + 2) % count) for i in range(count)])
 
 
-def total_of(value):
-    for axis in ("tensor", "dp"):
-        bit = 1
-        while bit < lax.axis_size(axis):
-            value = value + swap(value, axis, bit)
-            bit *= 2
-    return value
-
-
 def gather_slots(local, parts):
     size = local.shape[0] // parts
     hops = lax.axis_size("dp") // 2
     pieces = [[[None] * parts for _ in range(2)] for _ in range(hops)]
     for part in range(parts):
-        shard = local[part * size : (part + 1) * size]
+        shard = local[part * size : (part + 1) * size] if parts > 1 else local
         for hop in range(hops):
             pieces[hop][0][part] = shard
             pieces[hop][1][part] = swap(shard, "dp", 1)
@@ -805,27 +928,54 @@
     return [piece for pair in pieces for flip in pair for piece in flip]
 
 
-def scatter_slots(sent, slots, parts):
-    hops = lax.axis_size("dp") // 2
-    size = slots // parts
-    shaped = sent.reshape(hops, 2, slots, BLK, BLK)
-    done = []
-    for part in range(parts):
-        piece = shaped[:, :, part * size : (part + 1) * size]
-        carried = None
-        for hop in range(hops - 1, -1, -1):
-            mine = piece[hop, 0].astype(single) + swap(piece[hop, 1], "dp", 1).astype(single)
-            if carried is not None:
-                mine = mine + carried.astype(single)
-            if hop > 0:
-                carried = ring(mine.astype(bfloat))
-        done.append(mine.astype(bfloat))
-    return jnp.concatenate(done, 0)
+def vector_kernel(rank_ref, one_ref, two_ref, up_a, up_b, up_c, up_d, dq_a, dq_b, dv_ref, *refs):
+    out_ref = refs[-2]
+    rank = rank_ref[0]
+    out_ref[...] = jnp.zeros_like(out_ref)
+    out_ref[0:2, :] = one_ref[0:2, :]
+    out_ref[2:4, :] = two_ref[0:2, :]
+    out_ref[6:7, :] = one_ref[2:3, :]
+    out_ref[11:12, :] = two_ref[2:3, :]
+    width = dv_ref.shape[1]
+    query = jnp.sum(dq_a[...].astype(single), 0, keepdims=True) + jnp.sum(
+        dq_b[...].astype(single), 0, keepdims=True
+    )
+    value = jnp.sum(dv_ref[...].astype(single), 0, keepdims=True)
+    place = lax.broadcasted_iota(jnp.int32, (1, D), 1) // width == rank
+    for row, total in ((4, query), (5, value)):
+        wide = jnp.concatenate([total] * (D // width), 1)
+        out_ref[row : row + 1, :] = jnp.where(place, wide, 0.0)
+    bias = up_a[...] + up_b[...] + up_c[...] + up_d[...]
+    size = bias.shape[1]
+    for row in range(FF // D):
+        for part in range(D // size if size < D else 1):
+            here = (row * D + part * size) // size == rank
+            out_ref[7 + row : 8 + row, part * size : (part + 1) * size] = jnp.where(here, bias, 0.0)
+
+
+def vector_rows(rank, sums_one, sums_two, bias_parts, dq_a, dq_b, grad_value, after):
+    operands = [sums_one, sums_two, *bias_parts, dq_a, dq_b, grad_value]
+    return pl.pallas_call(
+        vector_kernel,
+        grid_spec=pltpu.PrefetchScalarGridSpec(
+            num_scalar_prefetch=1,
+            grid=(),
+            in_specs=[whole_spec()] * len(operands) + [anywhere()] * len(after),
+            out_specs=[whole_spec(), anywhere()],
+        ),
+        out_shape=[of((16, D), single), token_of()],
+        cost_estimate=cost(1, *operands),
+        name="vector_rows",
+    )(rank, *operands, *after)
+
+
+def hop_sum(value, axis, bit):
+    return value + swap(value, axis, bit)
 
 
 def assemble_kernel(source_ref, *refs, sizes, layouts):
     count = len(sizes)
-    pieces, outs, (held, sems) = refs[:count], refs[count:-2], refs[-2:]
+    pieces, outs, (held, sems) = refs[:count], refs[-2 - len(set(job[0] for job in layouts)) : -2], refs[-2:]
     copies, start = [], 0
     for index, size in enumerate(sizes):
         copies.append(pltpu.make_async_copy(pieces[index], held.at[start : start + size], sems.at[index]))
@@ -845,14 +995,14 @@
                 canon += 1
 
 
-def assemble(source, pieces, shapes, layouts):
+def assemble(source, pieces, shapes, layouts, after=()):
     sizes = [piece.shape[0] for piece in pieces]
     return pl.pallas_call(
         functools.partial(assemble_kernel, sizes=sizes, layouts=layouts),
         grid_spec=pltpu.PrefetchScalarGridSpec(
             num_scalar_prefetch=1,
             grid=(1,),
-            in_specs=[pl.BlockSpec(memory_space=pl.ANY)] * len(pieces),
+            in_specs=[in_hbm()] * len(pieces) + [anywhere()] * len(after),
             out_specs=[pl.BlockSpec(shape, lambda i, *_: (0, 0)) for shape in shapes],
             scratch_shapes=[
                 pltpu.VMEM((sum(sizes), BLK, BLK), bfloat),
@@ -862,13 +1012,13 @@
         out_shape=[jax.ShapeDtypeStruct(shape, bfloat) for shape in shapes],
         compiler_params=pltpu.CompilerParams(vmem_limit_bytes=40 * 2**20),
         name="assemble",
-    )(source, *pieces)
+    )(source, *pieces, *after)
 
 
 def chip_sum(keep, send, after=()):
     return norm_call(
         chip_kernel, "chip_sum", [keep, peer_of(send)], [], [(D, bfloat)], False, after
-    )[0]
+    )
 
 
 def across(value):
@@ -909,27 +1059,27 @@
     attn_count, ffn_count = block_counts(tensors)
     permuted = data_ranks <= 16
     hops = data_ranks // 2
-    parts = 3 if permuted else 1
-
+    canon_ids = jnp.arange(block_total, dtype=jnp.int32)
     holder, slot = block_owner // slots_here, block_owner % slots_here
-    flip = (holder % 2) ^ (data_rank % 2)
-    down = (data_rank // 2 - holder // 2) % hops
-    up = (holder // 2 - data_rank // 2) % hops
-    source = (down * 2 + flip) * slots_here + slot
-    target = (up * 2 + flip) * slots_here + slot
-    if not permuted:
-        source = target = block_owner
-    canon_ids = jnp.arange(block_total, dtype=jnp.int32)
-    inverse = jnp.zeros((block_total,), jnp.int32).at[block_owner].set(canon_ids)
-
-    local_weights = master_blocks[0].astype(bfloat)
+    source = target = block_owner
     if permuted:
-        pieces = gather_slots(local_weights, parts)
-    else:
-        pieces = [lax.all_gather(local_weights, "dp", axis=0, tiled=True)]
+        flip = (holder % 2) ^ (data_rank % 2)
+        down = (data_rank // 2 - holder // 2) % hops
+        up = (holder // 2 - data_rank // 2) % hops
+        source = (down * 2 + flip) * slots_here + slot
+        target = (flip * hops + up) * slots_here + slot
+    mine = block_owner[None, :] == data_rank * slots_here + jnp.arange(slots_here)[:, None]
+    own_canon = jnp.sum(jnp.where(mine, canon_ids[None, :], 0), 1)
+    own_slots = jnp.arange(slots_here, dtype=jnp.int32)
+
     cols = slice_width // BLK
     wide = hidden_width // BLK
     full = D // BLK
+    local_weights = master_blocks[0].astype(bfloat)
+    if permuted:
+        pieces = gather_slots(local_weights, 3)
+    else:
+        pieces = [lax.all_gather(local_weights, "dp", axis=0, tiled=True)]
     w_qkv, w_out, w_up, w_down = assemble(
         source,
         pieces,
@@ -979,12 +1129,14 @@
     up_start = 4 * attn_count
 
     attended, lse, shares = [None] * 4, [None] * 4, [None] * 4
-    attended[3], lse[3], shares[3] = attend(projected, valid, w_out, 3, after=[cotangent_b])
-    attended[1], lse[1], shares[1] = attend(projected, valid, w_out, 1, after=[shares[3]])
+    attended[3], lse[3], shares[3], token = attend(
+        projected, valid, w_out, 3, after=[cotangent_b]
+    )
+    attended[1], lse[1], shares[1], token = attend(projected, valid, w_out, 1, after=[token])
     for block in (2, 0):
-        attended[block], lse[block], shares[block] = attend(
+        attended[block], lse[block], shares[block], token = attend(
             projected, valid, w_out, block, peer_of(shares[block + 1]),
-            after=[shares[1] if block == 2 else shares[2]],
+            after=[token],
         )
     chip = [shares[0], shares[2]]
     other = [across(chip[1]), across(chip[0])]
@@ -994,167 +1146,154 @@
     bias_row = bias_up[None, :]
 
     def norm_up(part, after):
-        normed_one[part], inv_one[part], hidden[2 * part] = norm_call(
+        normed_one[part], inv_one[part], hidden[2 * part], token = norm_call(
             norm_one_kernel, "norm_one", [chip[part], other[part], (tokens, tokens_b)[part]],
             [one], [(D, single), (128, single), (D, bfloat)], False, after,
         )
         hidden[2 * part + 1] = peer_of(hidden[2 * part])
-
-    def feed_part(part, after):
+        return token
+
+    def feed_part(part, token):
         block = 2 * part
-        activation[block], slope[block], keep = feed(
-            hidden[block], w_up, bias_row, w_down, single, after
+        activation[block], slope[block], keep, token = feed(
+            hidden[block], w_up, bias_row, w_down, single, [token]
         )
         block += 1
-        activation[block], slope[block], send = feed(
-            hidden[block], w_up, bias_row, w_down, bfloat, [keep]
-        )
-        return keep, send
-
-    norm_up(0, [chip[0]])
-    sums = feed_part(0, [])
-    norm_up(1, [sums[1]])
-    chip_two[0] = chip_sum(*sums, [hidden[2]])
-    sums = feed_part(1, [chip_two[0]])
-    chip_two[1] = chip_sum(*sums)
-    other = [across(chip_two[1]), across(chip_two[0])]
+        activation[block], slope[block], send, token = feed(
+            hidden[block], w_up, bias_row, w_down, bfloat, [token]
+        )
+        return keep, send, token
+
+    token = norm_up(0, [token])
+    *sums, token = feed_part(0, token)
+    token = norm_up(1, [token])
+    chip_two[0], token = chip_sum(*sums, [token])
+    other = [None, across(chip_two[0])]
+    *sums, token = feed_part(1, token)
+    chip_two[1], token = chip_sum(*sums, [token])
+    other[0] = across(chip_two[1])
 
     grad_second, grad_down, grad_up = [None] * 2, [None] * 4, [None] * 4
     bias_parts, chip_three, outs, sums_two = [None] * 4, [None] * 2, [None] * 2, [None] * 2
 
-    def norm_down(part, after):
+    def norm_down(part, token):
         rows_valid = valid[part * chunk : part * chunk + local_rows]
-        outs[part], grad_second[part], grad_down[2 * part], sums_two[part] = norm_call(
+        outs[part], grad_second[part], grad_down[2 * part], sums_two[part], token = norm_call(
             norm_two_kernel, "norm_two",
             [chip_two[part], other[part], normed_one[part], (cotangent, cotangent_b)[part],
              rows_valid],
-            [one, two], [(D, bfloat), (D, single), (D, bfloat)], True, after,
+            [one, two], [(D, bfloat), (D, single), (D, bfloat)], True, [token],
         )
         grad_down[2 * part + 1] = peer_of(grad_down[2 * part])
-
-    def feed_back_part(part, after):
+        return token
+
+    def feed_back_part(part, token):
         block = 2 * part
-        grad_up[block], bias_parts[block], keep = feed_back(
-            grad_down[block], w_down, w_up, slope[block], single, after
+        grad_up[block], bias_parts[block], keep, token = feed_back(
+            grad_down[block], w_down, w_up, slope[block], single, [token]
         )
         block += 1
-        grad_up[block], bias_parts[block], send = feed_back(
-            grad_down[block], w_down, w_up, slope[block], bfloat, [keep]
-        )
-        return keep, send
-
-    norm_down(1, [chip_two[1]])
-    sums = feed_back_part(1, [])
-    norm_down(0, [sums[1]])
-    chip_three[1] = chip_sum(*sums, [grad_down[0]])
-    sums = feed_back_part(0, [chip_three[1]])
-    chip_three[0] = chip_sum(*sums)
-    other = [across(chip_three[1]), across(chip_three[0])]
+        grad_up[block], bias_parts[block], send, token = feed_back(
+            grad_down[block], w_down, w_up, slope[block], bfloat, [token]
+        )
+        return keep, send, token
+
+    token = norm_down(1, token)
+    *sums, token = feed_back_part(1, token)
+    token = norm_down(0, token)
+    chip_three[1], token = chip_sum(*sums, [token])
+    other = [across(chip_three[1]), None]
+    *sums, token = feed_back_part(0, token)
+    chip_three[0], token = chip_sum(*sums, [token])
+    other[1] = across(chip_three[0])
     layer_output = outs[0]
-    dgain_two, dshift_two, dbias_down = sums_two[0][0], sums_two[0][1], sums_two[0][2]
-    dbias_up = (bias_parts[0] + bias_parts[1] + bias_parts[2] + bias_parts[3])[0]
-    sent = pack(
+    *sent, token = pack(
         target,
         [
             (hidden, grad_up, lambda row, col: up_start + row * wide + col),
             (activation, grad_down, lambda row, col: up_start + ffn_count + row * full + col),
         ],
         grad_scale,
-        block_total,
-        after=[chip_three[0]],
+        [(0, block_total)],
+        after=[token],
     )
 
     grad_branch, grad_query, back, grad_rows, sums_one = [None] * 4, [None] * 2, None, [0, 0], [0, 0]
-    after = [sent]
     for part in (0, 1):
         block = 2 * part
-        grad_rows[part], grad_branch[block], sums_one[part] = norm_call(
+        grad_rows[part], grad_branch[block], sums_one[part], token = norm_call(
             norm_back_kernel, "norm_back",
             [chip_three[part], other[part], grad_second[part], normed_one[part], inv_one[part]],
-            [one], [(D, single), (D, bfloat)], True, after,
+            [one], [(D, single), (D, bfloat)], True, [token],
         )
         grad_branch[block + 1] = peer_of(grad_branch[block])
-        grad_query[part], *back = attend_back(
+        grad_query[part], *back, token = attend_back(
             grad_branch[block], grad_branch[block + 1], w_out, projected,
-            attended[block : block + 2], lse[block : block + 2], valid, part, back,
-        )
-        after = [back[0]]
+            attended[block : block + 2], lse[block : block + 2], valid, part, back, [token],
+        )
     grad_summed, sums_one = grad_rows[0], sums_one[0]
-    dgain_one, dshift_one, dbias_out = sums_one[0], sums_one[1], sums_one[2]
     grad_key, grad_value = back
-    sent = pack(
+    moved = hops * slots_here
+    regions = [(0, block_total)]
+    if permuted:
+        regions = [(0, moved)] + [
+            (moved + hop * slots_here, slots_here) for hop in range(hops)
+        ]
+    kept, *leaving, token = pack(
         target,
         [
-            (
-                [full_tokens],
-                grad_query,
-                lambda row, col: row * cols + col,
-            ),
-            (
-                [full_tokens],
-                [grad_key],
-                lambda row, col: attn_count + row * cols + col,
-            ),
-            (
-                [full_tokens],
-                [grad_value],
-                lambda row, col: 2 * attn_count + row * cols + col,
-            ),
-            (
-                attended,
-                grad_branch,
-                lambda row, col: 3 * attn_count + row * full + col,
-            ),
+            ([full_tokens], grad_query, lambda row, col: row * cols + col),
+            ([full_tokens], [grad_key], lambda row, col: attn_count + row * cols + col),
+            ([full_tokens], [grad_value], lambda row, col: 2 * attn_count + row * cols + col),
+            (attended, grad_branch, lambda row, col: 3 * attn_count + row * full + col),
         ],
         grad_scale,
-        block_total,
-        sent,
-    )
-    dbias_query = jnp.sum(grad_query[0].astype(single), 0) + jnp.sum(
-        grad_query[1].astype(single), 0
-    )
-    dbias_value = jnp.sum(grad_value.astype(single), 0)
-    keep_a, send_a, keep_b, send_b = token_back(
-        grad_query[0], grad_query[1], grad_key, grad_value, w_qkv
-    )
-    over = across(chip_sum(keep_b, send_b))
-    token_grad = (
-        chip_sum(keep_a, send_a).astype(single) + over.astype(single) + grad_summed
-    ).astype(bfloat)
-    vector_grad = jnp.concatenate(
-        [
-            dgain_one,
-            dshift_one,
-            dgain_two,
-            dshift_two,
-            jnp.zeros((2 * D,), single),
-            dbias_out,
-            jnp.zeros((FF,), single),
-            dbias_down,
-        ]
-    )
-    vector_grad = lax.dynamic_update_slice_in_dim(
-        vector_grad, dbias_query, 4 * D + tensor_rank * slice_width, 0
-    )
-    vector_grad = lax.dynamic_update_slice_in_dim(
-        vector_grad, dbias_value, 5 * D + tensor_rank * slice_width, 0
-    )
-    vector_grad = lax.dynamic_update_slice_in_dim(
-        vector_grad, dbias_up, 7 * D + tensor_rank * hidden_width, 0
-    )
-    own_canon = lax.dynamic_slice_in_dim(inverse, data_rank * slots_here, slots_here)
-    vector_sum = total_of(vector_grad) * grad_scale
+        regions,
+        sent[0],
+        [token],
+    )
+    vector_grad, token = vector_rows(
+        tensor_rank.astype(jnp.int32)[None], sums_one, sums_two[0], bias_parts, *grad_query,
+        grad_value, [token],
+    )
+    vector_grad = hop_sum(vector_grad, "tensor", 1)
+    keep_a, send_a, keep_b, send_b, token = token_back(
+        grad_query[0], grad_query[1], grad_key, grad_value, w_qkv, [token]
+    )
+    vector_grad = hop_sum(vector_grad, "tensor", 2)
+    chip_b = chip_sum(keep_b, send_b, [token])[0]
+    chip_a = chip_sum(keep_a, send_a, [token])[0]
+    over = across(chip_b)
+    token_grad = (chip_a.astype(single) + over.astype(single) + grad_summed).astype(bfloat)
+    bits = []
+    bit = 1
+    while bit < data_ranks:
+        bits.append(bit)
+        bit *= 2
+    bits = bits[1:] + bits[:1]
     if permuted:
-        own_grad = scatter_slots(sent, slots_here, 2)
+        carried, after = [], [token]
+        for bit in bits[:-1]:
+            vector_grad = hop_sum(vector_grad, "dp", bit)
+            after.append(vector_grad)
+        bits = bits[-1:]
+        for hop in range(hops - 1, -1, -1):
+            got = swap(leaving[hop], "dp", 1)
+            own_grad, token = join(hop, [[kept, got] + carried], after)
+            carried, after = [ring(own_grad)] if hop else [], [token]
     else:
-        own_grad = lax.psum_scatter(sent, "dp", scatter_dimension=0, tiled=True)
+        own_grad = lax.psum_scatter(kept, "dp", scatter_dimension=0, tiled=True)
+    for bit in bits:
+        vector_grad = hop_sum(vector_grad, "dp", bit)
+    vector_sum = vector_grad[: 8 + FF // D].reshape(-1) * grad_scale
     rates = rate_values(own_canon, tensors, seq_len)
     correction = 1.0 - moment_decay**STEP
-    fresh_first, fresh_second, fresh_master, fresh_left, fresh_right, gram, product = adam(
-        own_grad, first_moment[0], second_moment[0], master_blocks[0], left_stats[0],
-        right_stats[0], left_basis[0], right_basis[0], rates, per=math.gcd(slots_here, 4)
-    )
-    basis_left, basis_right = renew(gram, product)
+    states = [
+        first_moment[0], second_moment[0], master_blocks[0], left_stats[0], right_stats[0],
+        left_basis[0], right_basis[0],
+    ]
+    *fresh, _ = optimise(own_slots, rates, [own_grad], states)
+    fresh_first, fresh_second, fresh_master, fresh_left, fresh_right, basis_left, basis_right = fresh
     vec_first = moment_decay * vector_first + (1.0 - moment_decay) * vector_sum
     vec_second = moment_decay * vector_second + (1.0 - moment_decay) * vector_sum * vector_sum
     vec_master = vector_master - vector_rate * (vec_first / correction) / (

time: 397 us -> 369 us (0.929)
  starting transfers between devices: 62.1 us -> 52.1 us
  Pallas kernels: 156 us -> 147 us
  waiting for transfers between devices: 134 us -> 127 us
    ppermute x50 -> x46, waiting for transfers between devices: 96.7 us -> 66.3 us  [swap(): return lax.ppermute(value, axis, [(i, i ^ bit) for i in range(count)])]
    ppermute x15 -> x12, waiting for transfers between devices: 37.2 us -> 60.7 us  [ring(): lax.ppermute(value, 'dp', [(i, (i + 2) % count) for i in range(count)])]
    pallas_call x5 -> x9, Pallas kernels: 68.9 us -> 57.8 us  [the longest x1 27.3 us: optimise(): pl.pallas_call(functools.partial(optimise_kernel, count=count, adds=len(g...]
    ppermute x50 -> x46, starting transfers between devices: 50.4 us -> 42.3 us  [swap(): return lax.ppermute(value, axis, [(i, i ^ bit) for i in range(count)])]
    unnamed x107 -> x144, local copies, waits for them, and re-layouts: 16.2 us -> 20.4 us
    ppermute x15 -> x12, starting transfers between devices: 11.6 us -> 9.87 us  [ring(): lax.ppermute(value, 'dp', [(i, (i + 2) % count) for i in range(count)])]
  transfers between devices with their start and end apart: 65 -> 58, of which waited for: 32 -> 27; matrix products, arithmetic and copies ran while one was open for 5% -> 4% of each run, Pallas kernels for 19% -> 22%
where the time goes in v5:
time: 369 us; the launch traced here: 365 us
  Pallas kernels  147 us (40%)
  waiting for transfers between devices  127 us (34%)
  starting transfers between devices  52.1 us (14%)
  local copies, waits for them, and re-layouts  25.5 us (7%)
  other arithmetic  9.8 us (3%)
    ppermute x46, waiting for transfers between devices, swap(): return lax.ppermute(value, axis, [(i, i ^ bit) for i in range(count)])  66.3 us
    ppermute x12, waiting for transfers between devices, ring(): lax.ppermute(value, 'dp', [(i, (i + 2) % count) for i in range(count)])  60.7 us
    ppermute x46, starting transfers between devices, swap(): return lax.ppermute(value, axis, [(i, i ^ bit) for i in range(count)])  42.3 us
    pallas_call x1, Pallas kernels, optimise(): pl.pallas_call(functools.partial(optimise_kernel, count=count, adds=len(g...  27.3 us
    unnamed x144, local copies, waits for them, and re-layouts  20.4 us
    pallas_call x4, Pallas kernels, feed(): pl.pallas_call(feed_kernel, grid=(hidden // step,), in_specs=[fixed(block...  20.4 us
    pallas_call x4, Pallas kernels, attend(): pl.pallas_call(functools.partial(attend_kernel, heads=heads, own=own), gr...  16.6 us
    pallas_call x12, Pallas kernels, norm_call(): pl.pallas_call(kernel, grid=(rows // norm_tile,), in_specs=[by_row(value....  16.3 us
  transfers between devices with their start and end apart: 58, of which 27 were waited for; matrix products, arithmetic and copies ran while one was open for 4% of the time, Pallas kernels for 22%

profile of v5, /device:TPU:0, one launch (start us, length us, event | category | flops | bytes accessed | tf_op | source)
XLA Modules:
  0.0 365.5 jit_solution(3010758070010403649)
XLA Ops:
  16.4 3.9 %collective-permute-done.7.refs_7_ = bf16[8,128,128]{2,1,0:T(8,128)(2,1)} collective-permute-done((bf16[8,128,128]{2,1,0:T(8,128)(2,1)S(1)}, bf16[8,128,128]{2,1,0:T(8,128)(2,1)}, u32[]{:S(2)}, u32[]{:S(2)}) %collective-permute-start.7) | collective-permute-done | bytes 262176 | tf_op jit(solution)/shard_map/ppermute | solution.py:914
  20.3 5.6 %collective-permute-done.8.refs_8_ = bf16[8,128,128]{2,1,0:T(8,128)(2,1)} collective-permute-done((bf16[8,128,128]{2,1,0:T(8,128)(2,1)S(1)}, bf16[8,128,128]{2,1,0:T(8,128)(2,1)}, u32[]{:S(2)}, u32[]{:S(2)}) %collective-permute-start.8) | collective-permute-done | bytes 262176 | tf_op jit(solution)/shard_map/ppermute | solution.py:914
  46.7 4.7 %collective-permute-done.9.refs_9_ = bf16[8,128,128]{2,1,0:T(8,128)(2,1)S(1)} collective-permute-done((bf16[8,128,128]{2,1,0:T(8,128)(2,1)}, bf16[8,128,128]{2,1,0:T(8,128)(2,1)S(1)}, u32[]{:S(2)}, u32[]{:S(2)}) %collective-permute-start.9) | collective-permute-done | bytes 262176 | tf_op jit(solution)/shard_map/ppermute | solution.py:909
  55.1 6.5 %collective-permute-done.19.refs_19_ = bf16[8,128,128]{2,1,0:T(8,128)(2,1)} collective-permute-done((bf16[8,128,128]{2,1,0:T(8,128)(2,1)}, bf16[8,128,128]{2,1,0:T(8,128)(2,1)}, u32[]{:S(2)}, u32[]{:S(2)}) %collective-permute-start.19) | collective-permute-done | bytes 262176 | tf_op jit(solution)/shard_map/ppermute | solution.py:914
  72.2 4.5 %collective-permute-done.21.refs_21_ = bf16[8,128,128]{2,1,0:T(8,128)(2,1)S(1)} collective-permute-done((bf16[8,128,128]{2,1,0:T(8,128)(2,1)}, bf16[8,128,128]{2,1,0:T(8,128)(2,1)S(1)}, u32[]{:S(2)}, u32[]{:S(2)}) %collective-permute-start.21) | collective-permute-done | bytes 262176 | tf_op jit(solution)/shard_map/ppermute | solution.py:909
  83.3 4.2 %assemble.1 = (bf16[1024,768]{1,0:T(8,128)(2,1)S(1)}, bf16[256,1024]{1,0:T(8,128)(2,1)S(1)}, bf16[1024,1024]{1,0:T(8,128)(2,1)S(1)}, bf16[1024,1024]{1,0:T(8,128)(2,1)S(1)}) custom-call(s32[192]{0:T(256)S(1)} %get-tuple-element.274.source_ref, bf16[8,128,128]{2,1,0:T(8,128)(2,1)S(1)} %copy-done.32, bf16[8,128,128]{2,1,0:T(8,128)(2,1)S(1)} %copy-done.30, ...), custom_call_target="tpu_custom_call" | custom-call | tf_op jit(solution)/shard_map/assemble/pallas_call | solution.py:1000
  93.8 4.2 %attend.5 = (bf16[256,256]{1,0:T(8,128)(2,1)S(1)}, f32[4,256]{1,0:T(4,128)S(1)}, bf16[256,1024]{1,0:T(8,128)(2,1)}, f32[8,128]{1,0:T(8,128)S(1)}) custom-call(bf16[1024,768]{1,0:T(8,128)(2,1)S(1)} %add_convert_fusion.q_ref.k_ref.v_ref.refs_3_.refs_4_.refs_5_, bf16[1024,768]{1,0:T(8,128)(2,1)S(1)} %add_convert_fusion.q_ref.k_ref.v_ref.refs_3_.refs_4_.refs_5_, ...), custom_call_target="tpu_custom_call" | custom-call | flops 67108864 | bytes 139776 | tf_op jit(solution)/shard_map/attend/pallas_call | solution.py:397
  98.4 4.2 %attend.6 = (bf16[256,256]{1,0:T(8,128)(2,1)S(1)}, f32[4,256]{1,0:T(4,128)S(1)}, bf16[256,1024]{1,0:T(8,128)(2,1)}, f32[8,128]{1,0:T(8,128)S(1)}) custom-call(bf16[1024,768]{1,0:T(8,128)(2,1)S(1)} %add_convert_fusion.q_ref.k_ref.v_ref.refs_3_.refs_4_.refs_5_, bf16[1024,768]{1,0:T(8,128)(2,1)S(1)} %add_convert_fusion.q_ref.k_ref.v_ref.refs_3_.refs_4_.refs_5_, ...), custom_call_target="tpu_custom_call" | custom-call | flops 67108864 | bytes 139776 | tf_op jit(solution)/shard_map/attend/pallas_call | solution.py:397
  106.4 4.8 %attend.7 = (bf16[256,256]{1,0:T(8,128)(2,1)S(1)}, f32[4,256]{1,0:T(4,128)S(1)}, bf16[256,1024]{1,0:T(8,128)(2,1)S(1)}, f32[8,128]{1,0:T(8,128)S(1)}) custom-call(bf16[1024,768]{1,0:T(8,128)(2,1)S(1)} %add_convert_fusion.q_ref.k_ref.v_ref.refs_3_.refs_4_.refs_5_, bf16[1024,768]{1,0:T(8,128)(2,1)S(1)} %add_convert_fusion.q_ref.k_ref.v_ref.refs_3_.refs_4_.refs_5_, ...), custom_call_target="tpu_custom_call" | custom-call | flops 67108864 | bytes 139776 | tf_op jit(solution)/shard_map/attend/pallas_call | solution.py:397
  111.3 6.1 %collective-permute-done.27.across_ref = bf16[256,1024]{1,0:T(8,128)(2,1)} collective-permute-done((bf16[256,1024]{1,0:T(8,128)(2,1)}, bf16[256,1024]{1,0:T(8,128)(2,1)}, u32[]{:S(2)}, u32[]{:S(2)}) %collective-permute-start.27) | collective-permute-done | bytes 524320 | tf_op jit(solution)/shard_map/ppermute | solution.py:909
  121.8 5.1 %feed.4 = (bf16[256,1024]{1,0:T(8,128)(2,1)S(1)}, bf16[256,1024]{1,0:T(8,128)(2,1)S(1)}, f32[256,1024]{1,0:T(8,128)S(1)}, f32[8,128]{1,0:T(8,128)S(1)}) custom-call(bf16[256,1024]{1,0:T(8,128)(2,1)S(1)} %get-tuple-element.143.rows_ref.refs_0_, bf16[1024,1024]{1,0:T(8,128)(2,1)S(1)} %copy-done.1, f32[1,1024]{1,0:T(1,128)S(1)} %bitcast.32, ...), custom_call_target="tpu_custom_call" | custom-call | flops 67108864 | bytes 393472 | tf_op jit(solution)/shard_map/feed/pallas_call | solution.py:599
  127.0 5.1 %feed.5 = (bf16[256,1024]{1,0:T(8,128)(2,1)S(1)}, bf16[256,1024]{1,0:T(8,128)(2,1)S(1)}, bf16[256,1024]{1,0:T(8,128)(2,1)S(1)}, f32[8,128]{1,0:T(8,128)S(1)}) custom-call(bf16[256,1024]{1,0:T(8,128)(2,1)S(1)} %collective-permute-done.28.rows_ref.refs_1_, bf16[1024,1024]{1,0:T(8,128)(2,1)S(1)} %copy-done.1, f32[1,1024]{1,0:T(1,128)S(1)} %bitcast.33, ...), custom_call_target="tpu_custom_call" | custom-call | flops 67108864 | bytes 360704 | tf_op jit(solution)/shard_map/feed/pallas_call | solution.py:599
  137.3 5.1 %feed.6 = (bf16[256,1024]{1,0:T(8,128)(2,1)S(1)}, bf16[256,1024]{1,0:T(8,128)(2,1)S(1)}, f32[256,1024]{1,0:T(8,128)S(1)}, f32[8,128]{1,0:T(8,128)S(1)}) custom-call(bf16[256,1024]{1,0:T(8,128)(2,1)S(1)} %get-tuple-element.153.rows_ref.refs_2_, bf16[1024,1024]{1,0:T(8,128)(2,1)S(1)} %copy-done.1, f32[1,1024]{1,0:T(1,128)S(1)} %bitcast.34, ...), custom_call_target="tpu_custom_call" | custom-call | flops 67108864 | bytes 393472 | tf_op jit(solution)/shard_map/feed/pallas_call | solution.py:599
  142.4 5.1 %feed.7 = (bf16[256,1024]{1,0:T(8,128)(2,1)S(1)}, bf16[256,1024]{1,0:T(8,128)(2,1)S(1)}, bf16[256,1024]{1,0:T(8,128)(2,1)S(1)}, f32[8,128]{1,0:T(8,128)S(1)}) custom-call(bf16[256,1024]{1,0:T(8,128)(2,1)S(1)} %collective-permute-done.31.rows_ref.refs_3_, bf16[1024,1024]{1,0:T(8,128)(2,1)S(1)} %copy-done.1, f32[1,1024]{1,0:T(1,128)S(1)} %bitcast.35, ...), custom_call_target="tpu_custom_call" | custom-call | flops 67108864 | bytes 360704 | tf_op jit(solution)/shard_map/feed/pallas_call | solution.py:599
  150.0 12.0 %collective-permute-done.34.across_ref = bf16[256,1024]{1,0:T(8,128)(2,1)S(1)} collective-permute-done((bf16[256,1024]{1,0:T(8,128)(2,1)S(1)}, bf16[256,1024]{1,0:T(8,128)(2,1)S(1)}, u32[]{:S(2)}, u32[]{:S(2)}) %collective-permute-start.34) | collective-permute-done | bytes 524320 | tf_op jit(solution)/shard_map/ppermute | solution.py:909
  166.3 3.9 %feed_back.4 = (bf16[256,1024]{1,0:T(8,128)(2,1)S(1)}, f32[1,1024]{1,0:T(1,128)S(1)}, f32[256,1024]{1,0:T(8,128)S(1)}, f32[8,128]{1,0:T(8,128)S(1)}) custom-call(bf16[256,1024]{1,0:T(8,128)(2,1)S(1)} %get-tuple-element.163.rows_ref.refs_14_, bf16[1024,1024]{1,0:T(8,128)(2,1)S(1)} %copy-done.3, bf16[1024,1024]{1,0:T(8,128)(2,1)S(1)} %copy-done.1, ...), custom_call_target="tpu_custom_call" | custom-call | flops 67108864 | bytes 360960 | tf_op jit(solution)/shard_map/feed_back/pallas_call | solution.py:636
  170.3 3.9 %feed_back.5 = (bf16[256,1024]{1,0:T(8,128)(2,1)S(1)}, f32[1,1024]{1,0:T(1,128)S(1)}, bf16[256,1024]{1,0:T(8,128)(2,1)S(1)}, f32[8,128]{1,0:T(8,128)S(1)}) custom-call(bf16[256,1024]{1,0:T(8,128)(2,1)S(1)} %collective-permute-done.35.rows_ref.refs_15_, bf16[1024,1024]{1,0:T(8,128)(2,1)S(1)} %copy-done.3, bf16[1024,1024]{1,0:T(8,128)(2,1)S(1)} %copy-done.1, ...), custom_call_target="tpu_custom_call" | custom-call | flops 67108864 | bytes 328192 | tf_op jit(solution)/shard_map/feed_back/pallas_call | solution.py:636
  174.5 4.4 %collective-permute-done.33.across_ref = bf16[256,1024]{1,0:T(8,128)(2,1)S(1)} collective-permute-done((bf16[256,1024]{1,0:T(8,128)(2,1)S(1)}, bf16[256,1024]{1,0:T(8,128)(2,1)S(1)}, u32[]{:S(2)}, u32[]{:S(2)}) %collective-permute-start.33) | collective-permute-done | bytes 524320 | tf_op jit(solution)/shard_map/ppermute | solution.py:909
  182.2 3.9 %feed_back.6 = (bf16[256,1024]{1,0:T(8,128)(2,1)S(1)}, f32[1,1024]{1,0:T(1,128)S(1)}, f32[256,1024]{1,0:T(8,128)S(1)}, f32[8,128]{1,0:T(8,128)S(1)}) custom-call(bf16[256,1024]{1,0:T(8,128)(2,1)S(1)} %get-tuple-element.170.rows_ref.refs_12_, bf16[1024,1024]{1,0:T(8,128)(2,1)S(1)} %copy-done.3, bf16[1024,1024]{1,0:T(8,128)(2,1)S(1)} %copy-done.1, ...), custom_call_target="tpu_custom_call" | custom-call | flops 67108864 | bytes 360960 | tf_op jit(solution)/shard_map/feed_back/pallas_call | solution.py:636
  186.2 3.9 %feed_back.7 = (bf16[256,1024]{1,0:T(8,128)(2,1)S(1)}, f32[1,1024]{1,0:T(1,128)S(1)}, bf16[256,1024]{1,0:T(8,128)(2,1)S(1)}, f32[8,128]{1,0:T(8,128)S(1)}) custom-call(bf16[256,1024]{1,0:T(8,128)(2,1)S(1)} %collective-permute-done.37.rows_ref.refs_13_, bf16[1024,1024]{1,0:T(8,128)(2,1)S(1)} %copy-done.3, bf16[1024,1024]{1,0:T(8,128)(2,1)S(1)} %copy-done.1, ...), custom_call_target="tpu_custom_call" | custom-call | flops 67108864 | bytes 328192 | tf_op jit(solution)/shard_map/feed_back/pallas_call | solution.py:636
  192.7 8.0 %pack.2 = (bf16[192,128,128]{2,1,0:T(8,128)(2,1)}, f32[8,128]{1,0:T(8,128)S(1)}) custom-call(s32[192]{0:T(256)S(1)} %get-tuple-element.273.target_ref, bf16[256,1024]{1,0:T(8,128)(2,1)S(1)} %get-tuple-element.143.rows_ref.refs_0_, bf16[256,1024]{1,0:T(8,128)(2,1)S(1)} %collective-permute-done.28.rows_ref.refs_1_, ...), custom_call_target="tpu_custom_call" | custom-call | flops 268435456 | bytes 786432 | tf_op jit(solution)/shard_map/pack/pallas_call | solution.py:838
  200.6 3.9 %collective-permute-done.39.across_ref = bf16[256,1024]{1,0:T(8,128)(2,1)S(1)} collective-permute-done((bf16[256,1024]{1,0:T(8,128)(2,1)S(1)}, bf16[256,1024]{1,0:T(8,128)(2,1)S(1)}, u32[]{:S(2)}, u32[]{:S(2)}) %collective-permute-start.39) | collective-permute-done | bytes 524320 | tf_op jit(solution)/shard_map/ppermute | solution.py:909
  207.6 7.7 %attend_back.2 = (bf16[512,256]{1,0:T(8,128)(2,1)S(1)}, f32[1024,256]{1,0:T(8,128)S(1)}, f32[1024,256]{1,0:T(8,128)S(1)}, f32[8,128]{1,0:T(8,128)S(1)}) custom-call(bf16[256,1024]{1,0:T(8,128)(2,1)S(1)} %get-tuple-element.195.refs_0_.refs_9_, bf16[256,1024]{1,0:T(8,128)(2,1)S(1)} %collective-permute-done.40.refs_1_.refs_10_, ...), custom_call_target="tpu_custom_call" | custom-call | flops 335544320 | bytes 246016 | tf_op jit(solution)/shard_map/attend_back/pallas_call | solution.py:517
  215.4 4.7 %collective-permute-done.41.across_ref = bf16[256,1024]{1,0:T(8,128)(2,1)S(1)} collective-permute-done((bf16[256,1024]{1,0:T(8,128)(2,1)S(1)}, bf16[256,1024]{1,0:T(8,128)(2,1)S(1)}, u32[]{:S(2)}, u32[]{:S(2)}) %collective-permute-start.41) | collective-permute-done | bytes 524320 | tf_op jit(solution)/shard_map/ppermute | solution.py:909
  224.1 7.9 %attend_back.3 = (bf16[512,256]{1,0:T(8,128)(2,1)S(1)}, bf16[1024,256]{1,0:T(8,128)(2,1)S(1)}, bf16[1024,256]{1,0:T(8,128)(2,1)S(1)}, f32[8,128]{1,0:T(8,128)S(1)}) custom-call(bf16[256,1024]{1,0:T(8,128)(2,1)S(1)} %get-tuple-element.205.refs_0_.refs_11_, bf16[256,1024]{1,0:T(8,128)(2,1)S(1)} %collective-permute-done.42.refs_1_.refs_12_, ...), custom_call_target="tpu_custom_call" | custom-call | flops 335544320 | bytes 180480 | tf_op jit(solution)/shard_map/attend_back/pallas_call | solution.py:517
  232.1 7.6 %pack.3 = (bf16[96,128,128]{2,1,0:T(8,128)(2,1)S(1)}, bf16[24,128,128]{2,1,0:T(8,128)(2,1)S(1)}, bf16[24,128,128]{2,1,0:T(8,128)(2,1)}, bf16[24,128,128]{2,1,0:T...) custom-call(s32[192]{0:T(256)S(1)} %get-tuple-element.273.target_ref, ...), custom_call_target="tpu_custom_call" | custom-call | flops 134217728 | bytes 524288 | tf_op jit(solution)/shard_map/pack/pallas_call | solution.py:838
  254.3 4.3 %collective-permute-done.52 = f32[16,1024]{1,0:T(8,128)S(1)} collective-permute-done((f32[16,1024]{1,0:T(8,128)S(1)}, f32[16,1024]{1,0:T(8,128)S(1)}, u32[]{:S(2)}, u32[]{:S(2)}) %collective-permute-start.52) | collective-permute-done | bytes 65568 | tf_op jit(solution)/shard_map/ppermute | solution.py:909
  274.6 6.7 %collective-permute-done.48.refs_1_ = bf16[24,128,128]{2,1,0:T(8,128)(2,1)} collective-permute-done((bf16[24,128,128]{2,1,0:T(8,128)(2,1)}, bf16[24,128,128]{2,1,0:T(8,128)(2,1)}, u32[]{:S(2)}, u32[]{:S(2)}) %collective-permute-start.48) | collective-permute-done | bytes 786464 | tf_op jit(solution)/shard_map/ppermute | solution.py:909
  281.3 10.4 %collective-permute-done.54.refs_2_ = bf16[24,128,128]{2,1,0:T(8,128)(2,1)S(1)} collective-permute-done((bf16[24,128,128]{2,1,0:T(8,128)(2,1)}, bf16[24,128,128]{2,1,0:T(8,128)(2,1)S(1)}, u32[]{:S(2)}, u32[]{:S(2)}) %collective-permute-start.54) | collective-permute-done | bytes 786464 | tf_op jit(solution)/shard_map/ppermute | solution.py:914
  300.6 13.4 %collective-permute-done.55.refs_2_ = bf16[24,128,128]{2,1,0:T(8,128)(2,1)} collective-permute-done((bf16[24,128,128]{2,1,0:T(8,128)(2,1)}, bf16[24,128,128]{2,1,0:T(8,128)(2,1)}, u32[]{:S(2)}, u32[]{:S(2)}) %collective-permute-start.55) | collective-permute-done | bytes 786464 | tf_op jit(solution)/shard_map/ppermute | solution.py:914
  324.0 10.5 %collective-permute-done.56.refs_2_ = bf16[24,128,128]{2,1,0:T(8,128)(2,1)} collective-permute-done((bf16[24,128,128]{2,1,0:T(8,128)(2,1)}, bf16[24,128,128]{2,1,0:T(8,128)(2,1)}, u32[]{:S(2)}, u32[]{:S(2)}) %collective-permute-start.56) | collective-permute-done | bytes 786464 | tf_op jit(solution)/shard_map/ppermute | solution.py:914
  337.9 27.3 %optimise.1 = (f32[24,128,128]{2,1,0:T(8,128)}, f32[24,128,128]{2,1,0:T(8,128)}, f32[24,128,128]{2,1,0:T(8,128)}, f32[24,128,128]{2,1,0:T(8,128)}, f32[24,128,12...) custom-call(s32[24]{0:T(128)} %iota.22.slots_ref, ...), custom_call_target="tpu_custom_call" | custom-call | flops 125829120 | bytes 737280 | tf_op jit(solution)/shard_map/optimise/pallas_call | solution.py:273
  (294 shorter events, 149.3 us)
Async XLA Ops:
  5.4 14.9 %collective-permute-start.7 = (bf16[8,128,128]{2,1,0:T(8,128)(2,1)S(1)}, bf16[8,128,128]{2,1,0:T(8,128)(2,1)}, u32[]{:S(2)}, u32[]{:S(2)}) collective-permute-start(bf16[8,128,128]{2,1,0:T(8,128)(2,1)S(1)} %get-tuple-element.258.refs_1_), channel_id=1, source_target_pairs={{0,8},{4,12},{8,16},{12,20},{16,24},{20,28},{24,0},{28,4},{1,9},{5... | collective-permute-start | bytes 786440 | tf_op jit(solution)/shard_map/ppermute | solution.py:914
  7.0 18.9 %collective-permute-start.8 = (bf16[8,128,128]{2,1,0:T(8,128)(2,1)S(1)}, bf16[8,128,128]{2,1,0:T(8,128)(2,1)}, u32[]{:S(2)}, u32[]{:S(2)}) collective-permute-start(bf16[8,128,128]{2,1,0:T(8,128)(2,1)S(1)} %get-tuple-element.257.refs_2_), channel_id=1, source_target_pairs={{0,8},{4,12},{8,16},{12,20},{16,24},{20,28},{24,0},{28,4},{1,9},{5... | collective-permute-start | bytes 786440 | tf_op jit(solution)/shard_map/ppermute | solution.py:914
  8.6 17.4 %collective-permute-start.3 = (bf16[8,128,128]{2,1,0:T(8,128)(2,1)S(1)}, bf16[8,128,128]{2,1,0:T(8,128)(2,1)S(1)}, u32[]{:S(2)}, u32[]{:S(2)}) collective-permute-start(bf16[8,128,128]{2,1,0:T(8,128)(2,1)S(1)} %get-tuple-element.259.refs_0_), channel_id=1, source_target_pairs={{0,4},{4,0},{8,12},{12,8},{16,20},{20,16},{24,28},{28,24},{1,5},{5... | collective-permute-start | bytes 786440 | tf_op jit(solution)/shard_map/ppermute | solution.py:909
  10.8 17.5 %collective-permute-start.4 = (bf16[8,128,128]{2,1,0:T(8,128)(2,1)S(1)}, bf16[8,128,128]{2,1,0:T(8,128)(2,1)S(1)}, u32[]{:S(2)}, u32[]{:S(2)}) collective-permute-start(bf16[8,128,128]{2,1,0:T(8,128)(2,1)S(1)} %get-tuple-element.258.refs_1_), channel_id=1, source_target_pairs={{0,4},{4,0},{8,12},{12,8},{16,20},{20,16},{24,28},{28,24},{1,5},{5... | collective-permute-start | bytes 786440 | tf_op jit(solution)/shard_map/ppermute | solution.py:909
  14.7 15.8 %collective-permute-start.5 = (bf16[8,128,128]{2,1,0:T(8,128)(2,1)S(1)}, bf16[8,128,128]{2,1,0:T(8,128)(2,1)S(1)}, u32[]{:S(2)}, u32[]{:S(2)}) collective-permute-start(bf16[8,128,128]{2,1,0:T(8,128)(2,1)S(1)} %get-tuple-element.257.refs_2_), channel_id=1, source_target_pairs={{0,4},{4,0},{8,12},{12,8},{16,20},{20,16},{24,28},{28,24},{1,5},{5... | collective-permute-start | bytes 786440 | tf_op jit(solution)/shard_map/ppermute | solution.py:909
  20.3 12.4 %collective-permute-start.12 = (bf16[8,128,128]{2,1,0:T(8,128)(2,1)}, bf16[8,128,128]{2,1,0:T(8,128)(2,1)}, u32[]{:S(2)}, u32[]{:S(2)}) collective-permute-start(bf16[8,128,128]{2,1,0:T(8,128)(2,1)} %collective-permute-done.6.refs_6_), channel_id=1, source_target_pairs={{0,8},{4,12},{8,16},{12,20},{16,24},{20,28},{24,0},{28,4},{1,9},{5... | collective-permute-start | bytes 786440 | tf_op jit(solution)/shard_map/ppermute | solution.py:914
  26.7 15.3 %collective-permute-start.14 = (bf16[8,128,128]{2,1,0:T(8,128)(2,1)}, bf16[8,128,128]{2,1,0:T(8,128)(2,1)}, u32[]{:S(2)}, u32[]{:S(2)}) collective-permute-start(bf16[8,128,128]{2,1,0:T(8,128)(2,1)} %collective-permute-done.8.refs_8_), channel_id=1, source_target_pairs={{0,8},{4,12},{8,16},{12,20},{16,24},{20,28},{24,0},{28,4},{1,9},{5... | collective-permute-start | bytes 786440 | tf_op jit(solution)/shard_map/ppermute | solution.py:914
  28.9 14.5 %collective-permute-start.10 = (bf16[8,128,128]{2,1,0:T(8,128)(2,1)}, bf16[8,128,128]{2,1,0:T(8,128)(2,1)}, u32[]{:S(2)}, u32[]{:S(2)}) collective-permute-start(bf16[8,128,128]{2,1,0:T(8,128)(2,1)} %collective-permute-done.7.refs_7_), channel_id=1, source_target_pairs={{0,4},{4,0},{8,12},{12,8},{16,20},{20,16},{24,28},{28,24},{1,5},{5... | collective-permute-start | bytes 786440 | tf_op jit(solution)/shard_map/ppermute | solution.py:909
  31.1 21.0 %collective-permute-start.1 = (bf16[256,1024]{1,0:T(8,128)(2,1)S(1)}, bf16[256,1024]{1,0:T(8,128)(2,1)S(1)}, u32[]{:S(2)}, u32[]{:S(2)}) collective-permute-start(bf16[256,1024]{1,0:T(8,128)(2,1)S(1)} %copy-done.14), channel_id=1, source_target_pairs={{0,2},{1,3},{2,0},{3,1},{4,6},{5,7},{6,4},{7,5},{8,10},{9,11},{10,... | collective-permute-start | bytes 1572872 | tf_op jit(solution)/shard_map/ppermute | solution.py:909
  32.7 21.0 %collective-permute-start = (bf16[256,1024]{1,0:T(8,128)(2,1)S(1)}, bf16[256,1024]{1,0:T(8,128)(2,1)S(1)}, u32[]{:S(2)}, u32[]{:S(2)}) collective-permute-start(bf16[256,1024]{1,0:T(8,128)(2,1)S(1)} %copy-done.14), channel_id=1, source_target_pairs={{0,1},{1,0},{2,3},{3,2},{4,5},{5,4},{6,7},{7,6},{8,9},{9,8},{10,11... | collective-permute-start | bytes 1572872 | tf_op jit(solution)/shard_map/ppermute | solution.py:909
  45.5 20.8 %collective-permute-start.15 = (bf16[8,128,128]{2,1,0:T(8,128)(2,1)}, bf16[8,128,128]{2,1,0:T(8,128)(2,1)}, u32[]{:S(2)}, u32[]{:S(2)}) collective-permute-start(bf16[8,128,128]{2,1,0:T(8,128)(2,1)} %collective-permute-done.12.refs_12_), channel_id=1, source_target_pairs={{0,4},{4,0},{8,12},{12,8},{16,20},{20,16},{24,28},{28,24},{1,5},{5... | collective-permute-start | bytes 786440 | tf_op jit(solution)/shard_map/ppermute | solution.py:909
  52.1 14.3 %collective-permute-start.16 = (bf16[8,128,128]{2,1,0:T(8,128)(2,1)}, bf16[8,128,128]{2,1,0:T(8,128)(2,1)}, u32[]{:S(2)}, u32[]{:S(2)}) collective-permute-start(bf16[8,128,128]{2,1,0:T(8,128)(2,1)} %collective-permute-done.13.refs_13_), channel_id=1, source_target_pairs={{0,4},{4,0},{8,12},{12,8},{16,20},{20,16},{24,28},{28,24},{1,5},{5... | collective-permute-start | bytes 786440 | tf_op jit(solution)/shard_map/ppermute | solution.py:909
  54.9 14.6 %collective-permute-start.2 = (bf16[256,1024]{1,0:T(8,128)(2,1)S(1)}, bf16[256,1024]{1,0:T(8,128)(2,1)}, u32[]{:S(2)}, u32[]{:S(2)}) collective-permute-start(bf16[256,1024]{1,0:T(8,128)(2,1)S(1)} %collective-permute-done.1.rows_ref), channel_id=1, source_target_pairs={{0,1},{1,0},{2,3},{3,2},{4,5},{5,4},{6,7},{7,6},{8,9},{9,8},{10,11... | collective-permute-start | bytes 1572872 | tf_op jit(solution)/shard_map/ppermute | solution.py:909
  66.3 14.1 %collective-permute-start.22 = (bf16[8,128,128]{2,1,0:T(8,128)(2,1)}, bf16[8,128,128]{2,1,0:T(8,128)(2,1)S(1)}, u32[]{:S(2)}, u32[]{:S(2)}) collective-permute-start(bf16[8,128,128]{2,1,0:T(8,128)(2,1)} %collective-permute-done.19.refs_19_), channel_id=1, source_target_pairs={{0,4},{4,0},{8,12},{12,8},{16,20},{20,16},{24,28},{28,24},{1,5},{5... | collective-permute-start | bytes 786440 | tf_op jit(solution)/shard_map/ppermute | solution.py:909
  66.4 16.8 %collective-permute-start.23 = (bf16[8,128,128]{2,1,0:T(8,128)(2,1)}, bf16[8,128,128]{2,1,0:T(8,128)(2,1)S(1)}, u32[]{:S(2)}, u32[]{:S(2)}) collective-permute-start(bf16[8,128,128]{2,1,0:T(8,128)(2,1)} %collective-permute-done.20.refs_20_), channel_id=1, source_target_pairs={{0,4},{4,0},{8,12},{12,8},{16,20},{20,16},{24,28},{28,24},{1,5},{5... | collective-permute-start | bytes 786440 | tf_op jit(solution)/shard_map/ppermute | solution.py:909
  69.5 20.6 %collective-permute-start.24 = (bf16[256,1024]{1,0:T(8,128)(2,1)S(1)}, bf16[256,1024]{1,0:T(8,128)(2,1)S(1)}, u32[]{:S(2)}, u32[]{:S(2)}) collective-permute-start(bf16[256,1024]{1,0:T(8,128)(2,1)S(1)} %copy-done.33), channel_id=1, source_target_pairs={{0,2},{1,3},{2,0},{3,1},{4,6},{5,7},{6,4},{7,5},{8,10},{9,11},{10,... | collective-permute-start | bytes 1572872 | tf_op jit(solution)/shard_map/ppermute | solution.py:909
  103.2 14.2 %collective-permute-start.27 = (bf16[256,1024]{1,0:T(8,128)(2,1)}, bf16[256,1024]{1,0:T(8,128)(2,1)}, u32[]{:S(2)}, u32[]{:S(2)}) collective-permute-start(bf16[256,1024]{1,0:T(8,128)(2,1)} %get-tuple-element.141.chip_ref), channel_id=1, source_target_pairs={{0,2},{1,3},{2,0},{3,1},{4,6},{5,7},{6,4},{7,5},{8,10},{9,11},{10,... | collective-permute-start | bytes 1572872 | tf_op jit(solution)/shard_map/ppermute | solution.py:909
  120.1 14.3 %collective-permute-start.30 = (bf16[256,1024]{1,0:T(8,128)(2,1)S(1)}, bf16[256,1024]{1,0:T(8,128)(2,1)S(1)}, u32[]{:S(2)}, u32[]{:S(2)}) collective-permute-start(bf16[256,1024]{1,0:T(8,128)(2,1)S(1)} %get-tuple-element.140.chip_ref), channel_id=1, source_target_pairs={{0,2},{1,3},{2,0},{3,1},{4,6},{5,7},{6,4},{7,5},{8,10},{9,11},{10,... | collective-permute-start | bytes 1572872 | tf_op jit(solution)/shard_map/ppermute | solution.py:909
  148.0 13.9 %collective-permute-start.34 = (bf16[256,1024]{1,0:T(8,128)(2,1)S(1)}, bf16[256,1024]{1,0:T(8,128)(2,1)S(1)}, u32[]{:S(2)}, u32[]{:S(2)}) collective-permute-start(bf16[256,1024]{1,0:T(8,128)(2,1)S(1)} %get-tuple-element.152.chip_ref), channel_id=1, source_target_pairs={{0,2},{1,3},{2,0},{3,1},{4,6},{5,7},{6,4},{7,5},{8,10},{9,11},{10,... | collective-permute-start | bytes 1572872 | tf_op jit(solution)/shard_map/ppermute | solution.py:909
  164.6 14.3 %collective-permute-start.33 = (bf16[256,1024]{1,0:T(8,128)(2,1)S(1)}, bf16[256,1024]{1,0:T(8,128)(2,1)S(1)}, u32[]{:S(2)}, u32[]{:S(2)}) collective-permute-start(bf16[256,1024]{1,0:T(8,128)(2,1)S(1)} %get-tuple-element.159.chip_ref), channel_id=1, source_target_pairs={{0,2},{1,3},{2,0},{3,1},{4,6},{5,7},{6,4},{7,5},{8,10},{9,11},{10,... | collective-permute-start | bytes 1572872 | tf_op jit(solution)/shard_map/ppermute | solution.py:909
  190.3 14.3 %collective-permute-start.39 = (bf16[256,1024]{1,0:T(8,128)(2,1)S(1)}, bf16[256,1024]{1,0:T(8,128)(2,1)S(1)}, u32[]{:S(2)}, u32[]{:S(2)}) collective-permute-start(bf16[256,1024]{1,0:T(8,128)(2,1)S(1)} %get-tuple-element.182.chip_ref), channel_id=1, source_target_pairs={{0,2},{1,3},{2,0},{3,1},{4,6},{5,7},{6,4},{7,5},{8,10},{9,11},{10,... | collective-permute-start | bytes 1572872 | tf_op jit(solution)/shard_map/ppermute | solution.py:909
  205.7 14.3 %collective-permute-start.41 = (bf16[256,1024]{1,0:T(8,128)(2,1)S(1)}, bf16[256,1024]{1,0:T(8,128)(2,1)S(1)}, u32[]{:S(2)}, u32[]{:S(2)}) collective-permute-start(bf16[256,1024]{1,0:T(8,128)(2,1)S(1)} %get-tuple-element.181.chip_ref), channel_id=1, source_target_pairs={{0,2},{1,3},{2,0},{3,1},{4,6},{5,7},{6,4},{7,5},{8,10},{9,11},{10,... | collective-permute-start | bytes 1572872 | tf_op jit(solution)/shard_map/ppermute | solution.py:909
  243.7 25.3 %collective-permute-start.49 = (bf16[24,128,128]{2,1,0:T(8,128)(2,1)}, bf16[24,128,128]{2,1,0:T(8,128)(2,1)S(1)}, u32[]{:S(2)}, u32[]{:S(2)}) collective-permute-start(bf16[24,128,128]{2,1,0:T(8,128)(2,1)} %get-tuple-element.238), channel_id=1, source_target_pairs={{0,4},{4,0},{8,12},{12,8},{16,20},{20,16},{24,28},{28,24},{1,5},{5... | collective-permute-start | bytes 2359304 | tf_op jit(solution)/shard_map/ppermute | solution.py:909
  259.3 22.0 %collective-permute-start.48 = (bf16[24,128,128]{2,1,0:T(8,128)(2,1)}, bf16[24,128,128]{2,1,0:T(8,128)(2,1)}, u32[]{:S(2)}, u32[]{:S(2)}) collective-permute-start(bf16[24,128,128]{2,1,0:T(8,128)(2,1)} %copy-done.59), channel_id=1, source_target_pairs={{0,4},{4,0},{8,12},{12,8},{16,20},{20,16},{24,28},{28,24},{1,5},{5... | collective-permute-start | bytes 2359304 | tf_op jit(solution)/shard_map/ppermute | solution.py:909
  272.4 19.3 %collective-permute-start.54 = (bf16[24,128,128]{2,1,0:T(8,128)(2,1)}, bf16[24,128,128]{2,1,0:T(8,128)(2,1)S(1)}, u32[]{:S(2)}, u32[]{:S(2)}) collective-permute-start(bf16[24,128,128]{2,1,0:T(8,128)(2,1)} %get-tuple-element.240), channel_id=1, source_target_pairs={{0,8},{4,12},{8,16},{12,20},{16,24},{20,28},{24,0},{28,4},{1,9},{5... | collective-permute-start | bytes 2359304 | tf_op jit(solution)/shard_map/ppermute | solution.py:914
  273.2 26.8 %collective-permute-start.47 = (bf16[24,128,128]{2,1,0:T(8,128)(2,1)}, bf16[24,128,128]{2,1,0:T(8,128)(2,1)}, u32[]{:S(2)}, u32[]{:S(2)}) collective-permute-start(bf16[24,128,128]{2,1,0:T(8,128)(2,1)} %get-tuple-element.236), channel_id=1, source_target_pairs={{0,4},{4,0},{8,12},{12,8},{16,20},{20,16},{24,28},{28,24},{1,5},{5... | collective-permute-start | bytes 2359304 | tf_op jit(solution)/shard_map/ppermute | solution.py:909
  295.6 18.5 %collective-permute-start.55 = (bf16[24,128,128]{2,1,0:T(8,128)(2,1)}, bf16[24,128,128]{2,1,0:T(8,128)(2,1)}, u32[]{:S(2)}, u32[]{:S(2)}) collective-permute-start(bf16[24,128,128]{2,1,0:T(8,128)(2,1)} %get-tuple-element.242), channel_id=1, source_target_pairs={{0,8},{4,12},{8,16},{12,20},{16,24},{20,28},{24,0},{28,4},{1,9},{5... | collective-permute-start | bytes 2359304 | tf_op jit(solution)/shard_map/ppermute | solution.py:914
  295.8 21.2 %collective-permute-start.57 = (f32[16,1024]{1,0:T(8,128)S(1)}, f32[16,1024]{1,0:T(8,128)}, u32[]{:S(2)}, u32[]{:S(2)}) collective-permute-start(f32[16,1024]{1,0:T(8,128)S(1)} %copy-done.65), channel_id=1, source_target_pairs={{0,4},{4,0},{8,12},{12,8},{16,20},{20,16},{24,28},{28,24},{1,5},{5... | collective-permute-start | bytes 196616 | tf_op jit(solution)/shard_map/ppermute | solution.py:909
  297.1 26.9 %collective-permute-start.46 = (bf16[24,128,128]{2,1,0:T(8,128)(2,1)S(1)}, bf16[24,128,128]{2,1,0:T(8,128)(2,1)}, u32[]{:S(2)}, u32[]{:S(2)}) collective-permute-start(bf16[24,128,128]{2,1,0:T(8,128)(2,1)S(1)} %copy-done.58), channel_id=1, source_target_pairs={{0,4},{4,0},{8,12},{12,8},{16,20},{20,16},{24,28},{28,24},{1,5},{5... | collective-permute-start | bytes 2359304 | tf_op jit(solution)/shard_map/ppermute | solution.py:909
  298.5 23.1 %collective-permute-start.43 = (bf16[256,1024]{1,0:T(8,128)(2,1)}, bf16[256,1024]{1,0:T(8,128)(2,1)S(1)}, u32[]{:S(2)}, u32[]{:S(2)}) collective-permute-start(bf16[256,1024]{1,0:T(8,128)(2,1)} %get-tuple-element.227), channel_id=1, source_target_pairs={{0,1},{1,0},{2,3},{3,2},{4,5},{5,4},{6,7},{7,6},{8,9},{9,8},{10,11... | collective-permute-start | bytes 1572872 | tf_op jit(solution)/shard_map/ppermute | solution.py:909
  299.9 22.0 %collective-permute-start.45 = (bf16[256,1024]{1,0:T(8,128)(2,1)}, bf16[256,1024]{1,0:T(8,128)(2,1)}, u32[]{:S(2)}, u32[]{:S(2)}) collective-permute-start(bf16[256,1024]{1,0:T(8,128)(2,1)} %get-tuple-element.232), channel_id=1, source_target_pairs={{0,2},{1,3},{2,0},{3,1},{4,6},{5,7},{6,4},{7,5},{8,10},{9,11},{10,... | collective-permute-start | bytes 1572872 | tf_op jit(solution)/shard_map/ppermute | solution.py:909
  316.9 17.6 %collective-permute-start.56 = (bf16[24,128,128]{2,1,0:T(8,128)(2,1)}, bf16[24,128,128]{2,1,0:T(8,128)(2,1)}, u32[]{:S(2)}, u32[]{:S(2)}) collective-permute-start(bf16[24,128,128]{2,1,0:T(8,128)(2,1)} %get-tuple-element.244), channel_id=1, source_target_pairs={{0,8},{4,12},{8,16},{12,20},{16,24},{20,28},{24,0},{28,4},{1,9},{5... | collective-permute-start | bytes 2359304 | tf_op jit(solution)/shard_map/ppermute | solution.py:914
  (96 other events, 821.2 us)

commit v6 on v5

--- a/solution.py
+++ b/solution.py
@@ -217,8 +217,12 @@
 
 def optimise_kernel(slots_ref, rates_ref, *refs, count, adds):
     grads, states = refs[:adds], refs[adds : adds + 7]
-    outs = refs[-16:-9]
-    in_ref, out_ref, gram_ref, product_ref, inverse_ref, in_sems, out_sem, _ = refs[-8:]
+    outs = refs[-17:-10]
+    in_ref, out_ref, gram_ref, product_ref, inverse_ref, grad_ref, in_sems, out_sem, grad_sem = refs[
+        -9:
+    ]
+    for index, grad in enumerate(grads):
+        pltpu.make_async_copy(grad.at[0:count], grad_ref.at[index], grad_sem).start()
     for item in range(count):
         for index, state in enumerate(states):
             pltpu.make_async_copy(
@@ -226,15 +230,14 @@
             ).start()
 
     group = math.gcd(count, 4)
+    pltpu.make_async_copy(grad_ref, grad_ref, grad_sem).wait()
 
     def update(step, nothing):
         items = [step * group + index for index in range(group)]
         gradients = []
         for item in items:
             pltpu.make_async_copy(in_ref.at[item], in_ref.at[item], in_sems.at[item]).wait()
-            grad = grads[0][item].astype(single)
-            for other in grads[1:]:
-                grad = grad + other[item].astype(single)
+            grad = sum(grad_ref[index, item].astype(single) for index in range(adds))
             gradients.append(grad.astype(bfloat))
         results = adam_group(
             items, gradients, [[in_ref[item, index] for index in range(7)] for item in items],
@@ -275,8 +278,7 @@
         grid_spec=pltpu.PrefetchScalarGridSpec(
             num_scalar_prefetch=2,
             grid=(),
-            in_specs=[whole_spec()] * len(grads)
-            + [in_hbm()] * (7 + len(more))
+            in_specs=[in_hbm()] * (len(grads) + 7 + len(more))
             + [anywhere()] * len(after),
             out_specs=[in_hbm()] * 7 + [anywhere()],
             scratch_shapes=[
@@ -285,9 +287,10 @@
                 pltpu.VMEM((2 * count * BLK, BLK), single),
                 pltpu.VMEM((2 * count * BLK, BLK), single),
                 pltpu.VMEM((2 * count * PANEL, BLK), single),
+                pltpu.VMEM((len(grads), count, BLK, BLK), bfloat),
                 pltpu.SemaphoreType.DMA((count,)),
                 pltpu.SemaphoreType.DMA,
-                pltpu.SMEM((1,), jnp.int32),
+                pltpu.SemaphoreType.DMA,
             ],
         ),
         out_shape=[of((total, BLK, BLK), single)] * 7 + [token_of()],
@@ -538,7 +541,7 @@
             pltpu.VMEM((seq, width), single), pltpu.VMEM((seq, width), single),
         ],
         cost_estimate=cost(2 * 2 * rows * seq * width * 5 * heads, projected, *out_shape),
-        compiler_params=pltpu.CompilerParams(vmem_limit_bytes=32 * 2**20),
+        compiler_params=pltpu.CompilerParams(vmem_limit_bytes=28 * 2**20),
         name="attend_back",
     )(own, peer, w_out, projected, projected, projected, *attended, *lse, valid, *more, *after)
 
@@ -680,7 +683,7 @@
     )
 
 
-norm_tile = 64
+norm_tile = 128
 
 
 def norm_one_kernel(chip_ref, across_ref, rows_ref, vectors_ref, *refs):
@@ -779,7 +782,7 @@
         out_specs=[whole_spec()] * 4 + [anywhere()],
         out_shape=out_shape,
         cost_estimate=cost(8 * rows * D * w_qkv.shape[1], w_qkv, dk, *out_shape),
-        compiler_params=pltpu.CompilerParams(vmem_limit_bytes=24 * 2**20),
+        compiler_params=pltpu.CompilerParams(vmem_limit_bytes=12 * 2**20),
         name="token_back",
     )(dq_a, dq_b, dk, dv, w_qkv, *after)
 
@@ -846,7 +849,7 @@
             in_specs=[whole_spec()] * len(operands)
             + [in_hbm()] * len(more)
             + [anywhere()] * len(after),
-            out_specs=[in_hbm()] * len(regions) + [anywhere()],
+            out_specs=[anywhere()] * (len(regions) + 1),
             scratch_shapes=[
                 pltpu.VMEM((total, BLK, BLK), bfloat),
                 pltpu.SemaphoreType.DMA((len(regions),)),
@@ -855,7 +858,7 @@
         ),
         out_shape=[of((size, BLK, BLK), bfloat) for _, size in regions] + [token_of()],
         cost_estimate=cost(flops, *operands, of((blocks, BLK, BLK), bfloat)),
-        compiler_params=pltpu.CompilerParams(vmem_limit_bytes=40 * 2**20),
+        compiler_params=pltpu.CompilerParams(vmem_limit_bytes=28 * 2**20),
         name="pack",
     )(target, *operands, *more, *after)
 
@@ -888,6 +891,7 @@
         out_specs=[fixed(out.shape), anywhere()],
         out_shape=[out, token_of()],
         cost_estimate=cost(1, out),
+        compiler_params=pltpu.CompilerParams(vmem_limit_bytes=10 * 2**20),
         name="join",
     )(*operands, *after)
 
@@ -965,6 +969,7 @@
         ),
         out_shape=[of((16, D), single), token_of()],
         cost_estimate=cost(1, *operands),
+        compiler_params=pltpu.CompilerParams(vmem_limit_bytes=5 * 2**20),
         name="vector_rows",
     )(rank, *operands, *after)
 
@@ -1153,14 +1158,14 @@
         hidden[2 * part + 1] = peer_of(hidden[2 * part])
         return token
 
-    def feed_part(part, token):
+    def feed_part(part, token, arrived=()):
         block = 2 * part
         activation[block], slope[block], keep, token = feed(
             hidden[block], w_up, bias_row, w_down, single, [token]
         )
         block += 1
         activation[block], slope[block], send, token = feed(
-            hidden[block], w_up, bias_row, w_down, bfloat, [token]
+            hidden[block], w_up, bias_row, w_down, bfloat, [token, *arrived]
         )
         return keep, send, token
 
@@ -1169,7 +1174,7 @@
     token = norm_up(1, [token])
     chip_two[0], token = chip_sum(*sums, [token])
     other = [None, across(chip_two[0])]
-    *sums, token = feed_part(1, token)
+    *sums, token = feed_part(1, token, [other[1]])
     chip_two[1], token = chip_sum(*sums, [token])
     other[0] = across(chip_two[1])
 
@@ -1257,14 +1262,17 @@
         grad_value, [token],
     )
     vector_grad = hop_sum(vector_grad, "tensor", 1)
-    keep_a, send_a, keep_b, send_b, token = token_back(
-        grad_query[0], grad_query[1], grad_key, grad_value, w_qkv, [token]
-    )
     vector_grad = hop_sum(vector_grad, "tensor", 2)
-    chip_b = chip_sum(keep_b, send_b, [token])[0]
-    chip_a = chip_sum(keep_a, send_a, [token])[0]
-    over = across(chip_b)
-    token_grad = (chip_a.astype(single) + over.astype(single) + grad_summed).astype(bfloat)
+    def finish_tokens(token):
+        keep_a, send_a, keep_b, send_b, token = token_back(
+            grad_query[0], grad_query[1], grad_key, grad_value, w_qkv, [token]
+        )
+        chip_b = chip_sum(keep_b, send_b, [token])[0]
+        chip_a = chip_sum(keep_a, send_a, [token])[0]
+        over = across(chip_b)
+        token_grad = (chip_a.astype(single) + over.astype(single) + grad_summed).astype(bfloat)
+        return token_grad, token
+
     bits = []
     bit = 1
     while bit < data_ranks:
@@ -1277,12 +1285,16 @@
             vector_grad = hop_sum(vector_grad, "dp", bit)
             after.append(vector_grad)
         bits = bits[-1:]
-        for hop in range(hops - 1, -1, -1):
+        for hop in range(hops - 1, 0, -1):
             got = swap(leaving[hop], "dp", 1)
-            own_grad, token = join(hop, [[kept, got] + carried], after)
-            carried, after = [ring(own_grad)] if hop else [], [token]
+            total, token = join(hop, [[kept, got] + carried], after)
+            if hop == hops - 1:
+                token_grad, token = finish_tokens(token)
+            carried, after = [ring(total)], [token]
+        own_grad = [kept, swap(leaving[0], "dp", 1)] + carried
     else:
-        own_grad = lax.psum_scatter(kept, "dp", scatter_dimension=0, tiled=True)
+        token_grad, token = finish_tokens(token)
+        own_grad = [lax.psum_scatter(kept, "dp", scatter_dimension=0, tiled=True)]
     for bit in bits:
         vector_grad = hop_sum(vector_grad, "dp", bit)
     vector_sum = vector_grad[: 8 + FF // D].reshape(-1) * grad_scale
@@ -1292,7 +1304,7 @@
         first_moment[0], second_moment[0], master_blocks[0], left_stats[0], right_stats[0],
         left_basis[0], right_basis[0],
     ]
-    *fresh, _ = optimise(own_slots, rates, [own_grad], states)
+    *fresh, _ = optimise(own_slots, rates, own_grad, states)
     fresh_first, fresh_second, fresh_master, fresh_left, fresh_right, basis_left, basis_right = fresh
     vec_first = moment_decay * vector_first + (1.0 - moment_decay) * vector_sum
     vec_second = moment_decay * vector_second + (1.0 - moment_decay) * vector_sum * vector_sum

time: 369 us -> 346 us (0.938)
  Pallas kernels: 147 us -> 134 us
  local copies, waits for them, and re-layouts: 25.5 us -> 14.6 us
  waiting for transfers between devices: 127 us -> 131 us
    ppermute x46, waiting for transfers between devices: 66.3 us -> 86.9 us  [swap(): return lax.ppermute(value, axis, [(i, i ^ bit) for i in range(count)])]
    ppermute x12, waiting for transfers between devices: 60.7 us -> 44.2 us  [ring(): lax.ppermute(value, 'dp', [(i, (i + 2) % count) for i in range(count)])]
    unnamed x144 -> x100, local copies, waits for them, and re-layouts: 20.4 us -> 10.9 us
    pallas_call x4 -> x3, Pallas kernels: 11 us -> 3.89 us  [join(): pl.pallas_call(functools.partial(join_kernel, groups=[len(group) for grou...]
    pallas_call x2, Pallas kernels: 15.6 us -> 11 us  [pack(): pl.pallas_call(functools.partial(pack_kernel, jobs=jobs, scale=scale, reg...]
  transfers between devices with their start and end apart: 58 -> 58, of which waited for: 27 -> 32; matrix products, arithmetic and copies ran while one was open for 4% -> 3% of each run, Pallas kernels for 22% -> 21%
where the time goes in v6:
time: 346 us; the launch traced here: 343 us
  Pallas kernels  134 us (39%)
  waiting for transfers between devices  131 us (38%)
  starting transfers between devices  53 us (15%)
  local copies, waits for them, and re-layouts  14.6 us (4%)
  other arithmetic  6.18 us (2%)
    ppermute x46, waiting for transfers between devices, swap(): return lax.ppermute(value, axis, [(i, i ^ bit) for i in range(count)])  86.9 us
    ppermute x12, waiting for transfers between devices, ring(): lax.ppermute(value, 'dp', [(i, (i + 2) % count) for i in range(count)])  44.2 us
    ppermute x46, starting transfers between devices, swap(): return lax.ppermute(value, axis, [(i, i ^ bit) for i in range(count)])  43.6 us
    pallas_call x1, Pallas kernels, optimise(): pl.pallas_call(functools.partial(optimise_kernel, count=count, adds=len(g...  29.9 us
    pallas_call x4, Pallas kernels, feed(): pl.pallas_call(feed_kernel, grid=(hidden // step,), in_specs=[fixed(block...  20.3 us
    pallas_call x4, Pallas kernels, attend(): pl.pallas_call(functools.partial(attend_kernel, heads=heads, own=own), gr...  16.6 us
    pallas_call x4, Pallas kernels, feed_back(): pl.pallas_call(feed_back_kernel, grid=(hidden // step,), in_specs=[fixed(...  16.1 us
    pallas_call x2, Pallas kernels, attend_back(): pl.pallas_call(functools.partial(attend_back_kernel, heads=heads, first=f...  15.6 us
  transfers between devices with their start and end apart: 58, of which 32 were waited for; matrix products, arithmetic and copies ran while one was open for 3% of the time, Pallas kernels for 21%

profile of v6, /device:TPU:0, one launch (start us, length us, event | category | flops | bytes accessed | tf_op | source)
XLA Modules:
  0.0 342.8 jit_solution(9511470482228352210)
XLA Ops:
  16.4 3.9 %collective-permute-done.7.refs_7_ = bf16[8,128,128]{2,1,0:T(8,128)(2,1)} collective-permute-done((bf16[8,128,128]{2,1,0:T(8,128)(2,1)S(1)}, bf16[8,128,128]{2,1,0:T(8,128)(2,1)}, u32[]{:S(2)}, u32[]{:S(2)}) %collective-permute-start.7) | collective-permute-done | bytes 262176 | tf_op jit(solution)/shard_map/ppermute | solution.py:918
  20.3 5.6 %collective-permute-done.8.refs_8_ = bf16[8,128,128]{2,1,0:T(8,128)(2,1)} collective-permute-done((bf16[8,128,128]{2,1,0:T(8,128)(2,1)S(1)}, bf16[8,128,128]{2,1,0:T(8,128)(2,1)}, u32[]{:S(2)}, u32[]{:S(2)}) %collective-permute-start.8) | collective-permute-done | bytes 262176 | tf_op jit(solution)/shard_map/ppermute | solution.py:918
  46.7 4.7 %collective-permute-done.9.refs_9_ = bf16[8,128,128]{2,1,0:T(8,128)(2,1)S(1)} collective-permute-done((bf16[8,128,128]{2,1,0:T(8,128)(2,1)}, bf16[8,128,128]{2,1,0:T(8,128)(2,1)S(1)}, u32[]{:S(2)}, u32[]{:S(2)}) %collective-permute-start.9) | collective-permute-done | bytes 262176 | tf_op jit(solution)/shard_map/ppermute | solution.py:913
  55.1 6.5 %collective-permute-done.19.refs_19_ = bf16[8,128,128]{2,1,0:T(8,128)(2,1)} collective-permute-done((bf16[8,128,128]{2,1,0:T(8,128)(2,1)}, bf16[8,128,128]{2,1,0:T(8,128)(2,1)}, u32[]{:S(2)}, u32[]{:S(2)}) %collective-permute-start.19) | collective-permute-done | bytes 262176 | tf_op jit(solution)/shard_map/ppermute | solution.py:918
  72.2 4.5 %collective-permute-done.21.refs_21_ = bf16[8,128,128]{2,1,0:T(8,128)(2,1)S(1)} collective-permute-done((bf16[8,128,128]{2,1,0:T(8,128)(2,1)}, bf16[8,128,128]{2,1,0:T(8,128)(2,1)S(1)}, u32[]{:S(2)}, u32[]{:S(2)}) %collective-permute-start.21) | collective-permute-done | bytes 262176 | tf_op jit(solution)/shard_map/ppermute | solution.py:913
  83.3 4.2 %assemble.1 = (bf16[1024,768]{1,0:T(8,128)(2,1)S(1)}, bf16[256,1024]{1,0:T(8,128)(2,1)S(1)}, bf16[1024,1024]{1,0:T(8,128)(2,1)S(1)}, bf16[1024,1024]{1,0:T(8,128)(2,1)S(1)}) custom-call(s32[192]{0:T(256)S(1)} %get-tuple-element.270.source_ref, bf16[8,128,128]{2,1,0:T(8,128)(2,1)S(1)} %copy-done.23, bf16[8,128,128]{2,1,0:T(8,128)(2,1)S(1)} %copy-done.21, ...), custom_call_target="tpu_custom_call" | custom-call | tf_op jit(solution)/shard_map/assemble/pallas_call | solution.py:1005
  93.8 4.2 %attend.5 = (bf16[256,256]{1,0:T(8,128)(2,1)S(1)}, f32[4,256]{1,0:T(4,128)S(1)}, bf16[256,1024]{1,0:T(8,128)(2,1)}, f32[8,128]{1,0:T(8,128)S(1)}) custom-call(bf16[1024,768]{1,0:T(8,128)(2,1)S(1)} %add_convert_fusion.q_ref.k_ref.v_ref.refs_3_.refs_4_.refs_5_, bf16[1024,768]{1,0:T(8,128)(2,1)S(1)} %add_convert_fusion.q_ref.k_ref.v_ref.refs_3_.refs_4_.refs_5_, ...), custom_call_target="tpu_custom_call" | custom-call | flops 67108864 | bytes 139776 | tf_op jit(solution)/shard_map/attend/pallas_call | solution.py:400
  98.4 4.2 %attend.6 = (bf16[256,256]{1,0:T(8,128)(2,1)S(1)}, f32[4,256]{1,0:T(4,128)S(1)}, bf16[256,1024]{1,0:T(8,128)(2,1)}, f32[8,128]{1,0:T(8,128)S(1)}) custom-call(bf16[1024,768]{1,0:T(8,128)(2,1)S(1)} %add_convert_fusion.q_ref.k_ref.v_ref.refs_3_.refs_4_.refs_5_, bf16[1024,768]{1,0:T(8,128)(2,1)S(1)} %add_convert_fusion.q_ref.k_ref.v_ref.refs_3_.refs_4_.refs_5_, ...), custom_call_target="tpu_custom_call" | custom-call | flops 67108864 | bytes 139776 | tf_op jit(solution)/shard_map/attend/pallas_call | solution.py:400
  106.4 4.8 %attend.7 = (bf16[256,256]{1,0:T(8,128)(2,1)S(1)}, f32[4,256]{1,0:T(4,128)S(1)}, bf16[256,1024]{1,0:T(8,128)(2,1)S(1)}, f32[8,128]{1,0:T(8,128)S(1)}) custom-call(bf16[1024,768]{1,0:T(8,128)(2,1)S(1)} %add_convert_fusion.q_ref.k_ref.v_ref.refs_3_.refs_4_.refs_5_, bf16[1024,768]{1,0:T(8,128)(2,1)S(1)} %add_convert_fusion.q_ref.k_ref.v_ref.refs_3_.refs_4_.refs_5_, ...), custom_call_target="tpu_custom_call" | custom-call | flops 67108864 | bytes 139776 | tf_op jit(solution)/shard_map/attend/pallas_call | solution.py:400
  111.3 6.1 %collective-permute-done.27.across_ref = bf16[256,1024]{1,0:T(8,128)(2,1)} collective-permute-done((bf16[256,1024]{1,0:T(8,128)(2,1)}, bf16[256,1024]{1,0:T(8,128)(2,1)}, u32[]{:S(2)}, u32[]{:S(2)}) %collective-permute-start.27) | collective-permute-done | bytes 524320 | tf_op jit(solution)/shard_map/ppermute | solution.py:913
  120.8 5.1 %feed.4 = (bf16[256,1024]{1,0:T(8,128)(2,1)S(1)}, bf16[256,1024]{1,0:T(8,128)(2,1)S(1)}, f32[256,1024]{1,0:T(8,128)S(1)}, f32[8,128]{1,0:T(8,128)S(1)}) custom-call(bf16[256,1024]{1,0:T(8,128)(2,1)S(1)} %get-tuple-element.141.rows_ref.refs_0_, bf16[1024,1024]{1,0:T(8,128)(2,1)S(1)} %copy-done.1, f32[1,1024]{1,0:T(1,128)S(1)} %bitcast.32, ...), custom_call_target="tpu_custom_call" | custom-call | flops 67108864 | bytes 393472 | tf_op jit(solution)/shard_map/feed/pallas_call | solution.py:602
  125.9 5.1 %feed.5 = (bf16[256,1024]{1,0:T(8,128)(2,1)S(1)}, bf16[256,1024]{1,0:T(8,128)(2,1)S(1)}, bf16[256,1024]{1,0:T(8,128)(2,1)S(1)}, f32[8,128]{1,0:T(8,128)S(1)}) custom-call(bf16[256,1024]{1,0:T(8,128)(2,1)S(1)} %collective-permute-done.28.rows_ref.refs_1_, bf16[1024,1024]{1,0:T(8,128)(2,1)S(1)} %copy-done.1, f32[1,1024]{1,0:T(1,128)S(1)} %bitcast.33, ...), custom_call_target="tpu_custom_call" | custom-call | flops 67108864 | bytes 360704 | tf_op jit(solution)/shard_map/feed/pallas_call | solution.py:602
  137.0 5.1 %feed.6 = (bf16[256,1024]{1,0:T(8,128)(2,1)S(1)}, bf16[256,1024]{1,0:T(8,128)(2,1)S(1)}, f32[256,1024]{1,0:T(8,128)S(1)}, f32[8,128]{1,0:T(8,128)S(1)}) custom-call(bf16[256,1024]{1,0:T(8,128)(2,1)S(1)} %get-tuple-element.151.rows_ref.refs_2_, bf16[1024,1024]{1,0:T(8,128)(2,1)S(1)} %copy-done.1, f32[1,1024]{1,0:T(1,128)S(1)} %bitcast.34, ...), custom_call_target="tpu_custom_call" | custom-call | flops 67108864 | bytes 393472 | tf_op jit(solution)/shard_map/feed/pallas_call | solution.py:602
  142.1 7.5 %collective-permute-done.32.refs_1_.across_ref = bf16[256,1024]{1,0:T(8,128)(2,1)S(1)} collective-permute-done((bf16[256,1024]{1,0:T(8,128)(2,1)S(1)}, bf16[256,1024]{1,0:T(8,128)(2,1)S(1)}, u32[]{:S(2)}, u32[]{:S(2)}) %collective-permute-start.32) | collective-permute-done | bytes 524320 | tf_op jit(solution)/shard_map/ppermute | solution.py:913
  149.6 5.1 %feed.7 = (bf16[256,1024]{1,0:T(8,128)(2,1)S(1)}, bf16[256,1024]{1,0:T(8,128)(2,1)S(1)}, bf16[256,1024]{1,0:T(8,128)(2,1)S(1)}, f32[8,128]{1,0:T(8,128)S(1)}) custom-call(bf16[256,1024]{1,0:T(8,128)(2,1)S(1)} %collective-permute-done.31.rows_ref.refs_3_, bf16[1024,1024]{1,0:T(8,128)(2,1)S(1)} %copy-done.1, f32[1,1024]{1,0:T(1,128)S(1)} %bitcast.35, ...), custom_call_target="tpu_custom_call" | custom-call | flops 67108864 | bytes 360704 | tf_op jit(solution)/shard_map/feed/pallas_call | solution.py:602
  160.8 3.9 %feed_back.4 = (bf16[256,1024]{1,0:T(8,128)(2,1)S(1)}, f32[1,1024]{1,0:T(1,128)S(1)}, f32[256,1024]{1,0:T(8,128)S(1)}, f32[8,128]{1,0:T(8,128)S(1)}) custom-call(bf16[256,1024]{1,0:T(8,128)(2,1)S(1)} %get-tuple-element.161.rows_ref.refs_14_, bf16[1024,1024]{1,0:T(8,128)(2,1)S(1)} %copy-done.3, bf16[1024,1024]{1,0:T(8,128)(2,1)S(1)} %copy-done.1, ...), custom_call_target="tpu_custom_call" | custom-call | flops 67108864 | bytes 360960 | tf_op jit(solution)/shard_map/feed_back/pallas_call | solution.py:639
  164.7 3.9 %feed_back.5 = (bf16[256,1024]{1,0:T(8,128)(2,1)S(1)}, f32[1,1024]{1,0:T(1,128)S(1)}, bf16[256,1024]{1,0:T(8,128)(2,1)S(1)}, f32[8,128]{1,0:T(8,128)S(1)}) custom-call(bf16[256,1024]{1,0:T(8,128)(2,1)S(1)} %collective-permute-done.35.rows_ref.refs_15_, bf16[1024,1024]{1,0:T(8,128)(2,1)S(1)} %copy-done.3, bf16[1024,1024]{1,0:T(8,128)(2,1)S(1)} %copy-done.1, ...), custom_call_target="tpu_custom_call" | custom-call | flops 67108864 | bytes 328192 | tf_op jit(solution)/shard_map/feed_back/pallas_call | solution.py:639
  168.8 4.5 %collective-permute-done.34.across_ref = bf16[256,1024]{1,0:T(8,128)(2,1)S(1)} collective-permute-done((bf16[256,1024]{1,0:T(8,128)(2,1)S(1)}, bf16[256,1024]{1,0:T(8,128)(2,1)S(1)}, u32[]{:S(2)}, u32[]{:S(2)}) %collective-permute-start.34) | collective-permute-done | bytes 524320 | tf_op jit(solution)/shard_map/ppermute | solution.py:913
  175.4 3.9 %feed_back.6 = (bf16[256,1024]{1,0:T(8,128)(2,1)S(1)}, f32[1,1024]{1,0:T(1,128)S(1)}, f32[256,1024]{1,0:T(8,128)S(1)}, f32[8,128]{1,0:T(8,128)S(1)}) custom-call(bf16[256,1024]{1,0:T(8,128)(2,1)S(1)} %get-tuple-element.168.rows_ref.refs_12_, bf16[1024,1024]{1,0:T(8,128)(2,1)S(1)} %copy-done.3, bf16[1024,1024]{1,0:T(8,128)(2,1)S(1)} %copy-done.1, ...), custom_call_target="tpu_custom_call" | custom-call | flops 67108864 | bytes 360960 | tf_op jit(solution)/shard_map/feed_back/pallas_call | solution.py:639
  179.4 4.3 %feed_back.7 = (bf16[256,1024]{1,0:T(8,128)(2,1)S(1)}, f32[1,1024]{1,0:T(1,128)S(1)}, bf16[256,1024]{1,0:T(8,128)(2,1)S(1)}, f32[8,128]{1,0:T(8,128)S(1)}) custom-call(bf16[256,1024]{1,0:T(8,128)(2,1)S(1)} %collective-permute-done.37.rows_ref.refs_13_, bf16[1024,1024]{1,0:T(8,128)(2,1)S(1)} %copy-done.3, bf16[1024,1024]{1,0:T(8,128)(2,1)S(1)} %copy-done.1, ...), custom_call_target="tpu_custom_call" | custom-call | flops 67108864 | bytes 328192 | tf_op jit(solution)/shard_map/feed_back/pallas_call | solution.py:639
  186.2 5.7 %pack.2 = (bf16[192,128,128]{2,1,0:T(8,128)(2,1)S(1)}, f32[8,128]{1,0:T(8,128)S(1)}) custom-call(s32[192]{0:T(256)S(1)} %get-tuple-element.269.target_ref, bf16[256,1024]{1,0:T(8,128)(2,1)S(1)} %get-tuple-element.141.rows_ref.refs_0_, bf16[256,1024]{1,0:T(8,128)(2,1)S(1)} %collective-permute-done.28.rows_ref.refs_1_, ...), custom_call_target="tpu_custom_call" | custom-call | flops 268435456 | bytes 786432 | tf_op jit(solution)/shard_map/pack/pallas_call | solution.py:841
  191.9 6.3 %collective-permute-done.39.across_ref = bf16[256,1024]{1,0:T(8,128)(2,1)S(1)} collective-permute-done((bf16[256,1024]{1,0:T(8,128)(2,1)S(1)}, bf16[256,1024]{1,0:T(8,128)(2,1)S(1)}, u32[]{:S(2)}, u32[]{:S(2)}) %collective-permute-start.39) | collective-permute-done | bytes 524320 | tf_op jit(solution)/shard_map/ppermute | solution.py:913
  201.1 7.7 %attend_back.2 = (bf16[512,256]{1,0:T(8,128)(2,1)S(1)}, f32[1024,256]{1,0:T(8,128)S(1)}, f32[1024,256]{1,0:T(8,128)S(1)}, f32[8,128]{1,0:T(8,128)S(1)}) custom-call(bf16[256,1024]{1,0:T(8,128)(2,1)S(1)} %get-tuple-element.193.refs_0_.refs_9_, bf16[256,1024]{1,0:T(8,128)(2,1)S(1)} %collective-permute-done.40.refs_1_.refs_10_, ...), custom_call_target="tpu_custom_call" | custom-call | flops 335544320 | bytes 246016 | tf_op jit(solution)/shard_map/attend_back/pallas_call | solution.py:520
  208.8 4.7 %collective-permute-done.41.across_ref = bf16[256,1024]{1,0:T(8,128)(2,1)S(1)} collective-permute-done((bf16[256,1024]{1,0:T(8,128)(2,1)S(1)}, bf16[256,1024]{1,0:T(8,128)(2,1)S(1)}, u32[]{:S(2)}, u32[]{:S(2)}) %collective-permute-start.41) | collective-permute-done | bytes 524320 | tf_op jit(solution)/shard_map/ppermute | solution.py:913
  217.1 7.9 %attend_back.3 = (bf16[512,256]{1,0:T(8,128)(2,1)S(1)}, bf16[1024,256]{1,0:T(8,128)(2,1)S(1)}, bf16[1024,256]{1,0:T(8,128)(2,1)S(1)}, f32[8,128]{1,0:T(8,128)S(1)}) custom-call(bf16[256,1024]{1,0:T(8,128)(2,1)S(1)} %get-tuple-element.203.refs_0_.refs_11_, bf16[256,1024]{1,0:T(8,128)(2,1)S(1)} %collective-permute-done.42.refs_1_.refs_12_, ...), custom_call_target="tpu_custom_call" | custom-call | flops 335544320 | bytes 180480 | tf_op jit(solution)/shard_map/attend_back/pallas_call | solution.py:520
  224.9 5.2 %pack.3 = (bf16[96,128,128]{2,1,0:T(8,128)(2,1)S(1)}, bf16[24,128,128]{2,1,0:T(8,128)(2,1)S(1)}, bf16[24,128,128]{2,1,0:T(8,128)(2,1)}, bf16[24,128,128]{2,1,0:T...) custom-call(s32[192]{0:T(256)S(1)} %get-tuple-element.269.target_ref, ...), custom_call_target="tpu_custom_call" | custom-call | flops 134217728 | bytes 524288 | tf_op jit(solution)/shard_map/pack/pallas_call | solution.py:841
  237.9 4.3 %collective-permute-done.46 = f32[16,1024]{1,0:T(8,128)S(1)} collective-permute-done((f32[16,1024]{1,0:T(8,128)S(1)}, f32[16,1024]{1,0:T(8,128)S(1)}, u32[]{:S(2)}, u32[]{:S(2)}) %collective-permute-start.46) | collective-permute-done | bytes 65568 | tf_op jit(solution)/shard_map/ppermute | solution.py:913
  255.3 12.2 %collective-permute-done.53.refs_1_ = bf16[24,128,128]{2,1,0:T(8,128)(2,1)S(1)} collective-permute-done((bf16[24,128,128]{2,1,0:T(8,128)(2,1)S(1)}, bf16[24,128,128]{2,1,0:T(8,128)(2,1)S(1)}, u32[]{:S(2)}, u32[]{:S(2)}) %collective-permute-start.53) | collective-permute-done | bytes 786464 | tf_op jit(solution)/shard_map/ppermute | solution.py:913
  277.8 6.6 %collective-permute-done.52.refs_1_ = bf16[24,128,128]{2,1,0:T(8,128)(2,1)} collective-permute-done((bf16[24,128,128]{2,1,0:T(8,128)(2,1)}, bf16[24,128,128]{2,1,0:T(8,128)(2,1)}, u32[]{:S(2)}, u32[]{:S(2)}) %collective-permute-start.52) | collective-permute-done | bytes 786464 | tf_op jit(solution)/shard_map/ppermute | solution.py:913
  286.2 4.9 %collective-permute-done.55.refs_2_ = bf16[24,128,128]{2,1,0:T(8,128)(2,1)} collective-permute-done((bf16[24,128,128]{2,1,0:T(8,128)(2,1)}, bf16[24,128,128]{2,1,0:T(8,128)(2,1)}, u32[]{:S(2)}, u32[]{:S(2)}) %collective-permute-start.55) | collective-permute-done | bytes 786464 | tf_op jit(solution)/shard_map/ppermute | solution.py:918
  301.9 9.8 %collective-permute-done.56.refs_2_ = bf16[24,128,128]{2,1,0:T(8,128)(2,1)S(1)} collective-permute-done((bf16[24,128,128]{2,1,0:T(8,128)(2,1)}, bf16[24,128,128]{2,1,0:T(8,128)(2,1)S(1)}, u32[]{:S(2)}, u32[]{:S(2)}) %collective-permute-start.56) | collective-permute-done | bytes 786464 | tf_op jit(solution)/shard_map/ppermute | solution.py:918
  312.6 29.9 %optimise.1 = (f32[24,128,128]{2,1,0:T(8,128)}, f32[24,128,128]{2,1,0:T(8,128)}, f32[24,128,128]{2,1,0:T(8,128)}, f32[24,128,128]{2,1,0:T(8,128)}, f32[24,128,12...) custom-call(s32[24]{0:T(128)} %iota.22.slots_ref, ...), custom_call_target="tpu_custom_call" | custom-call | flops 125829120 | bytes 983040 | tf_op jit(solution)/shard_map/optimise/pallas_call | solution.py:276
  (249 shorter events, 138.0 us)
Async XLA Ops:
  5.4 14.9 %collective-permute-start.7 = (bf16[8,128,128]{2,1,0:T(8,128)(2,1)S(1)}, bf16[8,128,128]{2,1,0:T(8,128)(2,1)}, u32[]{:S(2)}, u32[]{:S(2)}) collective-permute-start(bf16[8,128,128]{2,1,0:T(8,128)(2,1)S(1)} %get-tuple-element.254.refs_1_), channel_id=1, source_target_pairs={{0,8},{4,12},{8,16},{12,20},{16,24},{20,28},{24,0},{28,4},{1,9},{5... | collective-permute-start | bytes 786440 | tf_op jit(solution)/shard_map/ppermute | solution.py:918
  7.0 18.9 %collective-permute-start.8 = (bf16[8,128,128]{2,1,0:T(8,128)(2,1)S(1)}, bf16[8,128,128]{2,1,0:T(8,128)(2,1)}, u32[]{:S(2)}, u32[]{:S(2)}) collective-permute-start(bf16[8,128,128]{2,1,0:T(8,128)(2,1)S(1)} %get-tuple-element.253.refs_2_), channel_id=1, source_target_pairs={{0,8},{4,12},{8,16},{12,20},{16,24},{20,28},{24,0},{28,4},{1,9},{5... | collective-permute-start | bytes 786440 | tf_op jit(solution)/shard_map/ppermute | solution.py:918
  8.6 17.4 %collective-permute-start.3 = (bf16[8,128,128]{2,1,0:T(8,128)(2,1)S(1)}, bf16[8,128,128]{2,1,0:T(8,128)(2,1)S(1)}, u32[]{:S(2)}, u32[]{:S(2)}) collective-permute-start(bf16[8,128,128]{2,1,0:T(8,128)(2,1)S(1)} %get-tuple-element.255.refs_0_), channel_id=1, source_target_pairs={{0,4},{4,0},{8,12},{12,8},{16,20},{20,16},{24,28},{28,24},{1,5},{5... | collective-permute-start | bytes 786440 | tf_op jit(solution)/shard_map/ppermute | solution.py:913
  10.8 17.5 %collective-permute-start.4 = (bf16[8,128,128]{2,1,0:T(8,128)(2,1)S(1)}, bf16[8,128,128]{2,1,0:T(8,128)(2,1)S(1)}, u32[]{:S(2)}, u32[]{:S(2)}) collective-permute-start(bf16[8,128,128]{2,1,0:T(8,128)(2,1)S(1)} %get-tuple-element.254.refs_1_), channel_id=1, source_target_pairs={{0,4},{4,0},{8,12},{12,8},{16,20},{20,16},{24,28},{28,24},{1,5},{5... | collective-permute-start | bytes 786440 | tf_op jit(solution)/shard_map/ppermute | solution.py:913
  14.7 15.8 %collective-permute-start.5 = (bf16[8,128,128]{2,1,0:T(8,128)(2,1)S(1)}, bf16[8,128,128]{2,1,0:T(8,128)(2,1)S(1)}, u32[]{:S(2)}, u32[]{:S(2)}) collective-permute-start(bf16[8,128,128]{2,1,0:T(8,128)(2,1)S(1)} %get-tuple-element.253.refs_2_), channel_id=1, source_target_pairs={{0,4},{4,0},{8,12},{12,8},{16,20},{20,16},{24,28},{28,24},{1,5},{5... | collective-permute-start | bytes 786440 | tf_op jit(solution)/shard_map/ppermute | solution.py:913
  20.3 12.4 %collective-permute-start.12 = (bf16[8,128,128]{2,1,0:T(8,128)(2,1)}, bf16[8,128,128]{2,1,0:T(8,128)(2,1)}, u32[]{:S(2)}, u32[]{:S(2)}) collective-permute-start(bf16[8,128,128]{2,1,0:T(8,128)(2,1)} %collective-permute-done.6.refs_6_), channel_id=1, source_target_pairs={{0,8},{4,12},{8,16},{12,20},{16,24},{20,28},{24,0},{28,4},{1,9},{5... | collective-permute-start | bytes 786440 | tf_op jit(solution)/shard_map/ppermute | solution.py:918
  26.7 15.3 %collective-permute-start.14 = (bf16[8,128,128]{2,1,0:T(8,128)(2,1)}, bf16[8,128,128]{2,1,0:T(8,128)(2,1)}, u32[]{:S(2)}, u32[]{:S(2)}) collective-permute-start(bf16[8,128,128]{2,1,0:T(8,128)(2,1)} %collective-permute-done.8.refs_8_), channel_id=1, source_target_pairs={{0,8},{4,12},{8,16},{12,20},{16,24},{20,28},{24,0},{28,4},{1,9},{5... | collective-permute-start | bytes 786440 | tf_op jit(solution)/shard_map/ppermute | solution.py:918
  28.9 14.5 %collective-permute-start.10 = (bf16[8,128,128]{2,1,0:T(8,128)(2,1)}, bf16[8,128,128]{2,1,0:T(8,128)(2,1)}, u32[]{:S(2)}, u32[]{:S(2)}) collective-permute-start(bf16[8,128,128]{2,1,0:T(8,128)(2,1)} %collective-permute-done.7.refs_7_), channel_id=1, source_target_pairs={{0,4},{4,0},{8,12},{12,8},{16,20},{20,16},{24,28},{28,24},{1,5},{5... | collective-permute-start | bytes 786440 | tf_op jit(solution)/shard_map/ppermute | solution.py:913
  31.1 21.0 %collective-permute-start.1 = (bf16[256,1024]{1,0:T(8,128)(2,1)S(1)}, bf16[256,1024]{1,0:T(8,128)(2,1)S(1)}, u32[]{:S(2)}, u32[]{:S(2)}) collective-permute-start(bf16[256,1024]{1,0:T(8,128)(2,1)S(1)} %copy-done.8), channel_id=1, source_target_pairs={{0,2},{1,3},{2,0},{3,1},{4,6},{5,7},{6,4},{7,5},{8,10},{9,11},{10,... | collective-permute-start | bytes 1572872 | tf_op jit(solution)/shard_map/ppermute | solution.py:913
  32.7 21.0 %collective-permute-start = (bf16[256,1024]{1,0:T(8,128)(2,1)S(1)}, bf16[256,1024]{1,0:T(8,128)(2,1)S(1)}, u32[]{:S(2)}, u32[]{:S(2)}) collective-permute-start(bf16[256,1024]{1,0:T(8,128)(2,1)S(1)} %copy-done.8), channel_id=1, source_target_pairs={{0,1},{1,0},{2,3},{3,2},{4,5},{5,4},{6,7},{7,6},{8,9},{9,8},{10,11... | collective-permute-start | bytes 1572872 | tf_op jit(solution)/shard_map/ppermute | solution.py:913
  45.5 20.8 %collective-permute-start.15 = (bf16[8,128,128]{2,1,0:T(8,128)(2,1)}, bf16[8,128,128]{2,1,0:T(8,128)(2,1)}, u32[]{:S(2)}, u32[]{:S(2)}) collective-permute-start(bf16[8,128,128]{2,1,0:T(8,128)(2,1)} %collective-permute-done.12.refs_12_), channel_id=1, source_target_pairs={{0,4},{4,0},{8,12},{12,8},{16,20},{20,16},{24,28},{28,24},{1,5},{5... | collective-permute-start | bytes 786440 | tf_op jit(solution)/shard_map/ppermute | solution.py:913
  52.1 14.3 %collective-permute-start.16 = (bf16[8,128,128]{2,1,0:T(8,128)(2,1)}, bf16[8,128,128]{2,1,0:T(8,128)(2,1)}, u32[]{:S(2)}, u32[]{:S(2)}) collective-permute-start(bf16[8,128,128]{2,1,0:T(8,128)(2,1)} %collective-permute-done.13.refs_13_), channel_id=1, source_target_pairs={{0,4},{4,0},{8,12},{12,8},{16,20},{20,16},{24,28},{28,24},{1,5},{5... | collective-permute-start | bytes 786440 | tf_op jit(solution)/shard_map/ppermute | solution.py:913
  54.9 14.6 %collective-permute-start.2 = (bf16[256,1024]{1,0:T(8,128)(2,1)S(1)}, bf16[256,1024]{1,0:T(8,128)(2,1)}, u32[]{:S(2)}, u32[]{:S(2)}) collective-permute-start(bf16[256,1024]{1,0:T(8,128)(2,1)S(1)} %collective-permute-done.1.rows_ref), channel_id=1, source_target_pairs={{0,1},{1,0},{2,3},{3,2},{4,5},{5,4},{6,7},{7,6},{8,9},{9,8},{10,11... | collective-permute-start | bytes 1572872 | tf_op jit(solution)/shard_map/ppermute | solution.py:913
  66.3 14.1 %collective-permute-start.22 = (bf16[8,128,128]{2,1,0:T(8,128)(2,1)}, bf16[8,128,128]{2,1,0:T(8,128)(2,1)S(1)}, u32[]{:S(2)}, u32[]{:S(2)}) collective-permute-start(bf16[8,128,128]{2,1,0:T(8,128)(2,1)} %collective-permute-done.19.refs_19_), channel_id=1, source_target_pairs={{0,4},{4,0},{8,12},{12,8},{16,20},{20,16},{24,28},{28,24},{1,5},{5... | collective-permute-start | bytes 786440 | tf_op jit(solution)/shard_map/ppermute | solution.py:913
  66.4 16.8 %collective-permute-start.23 = (bf16[8,128,128]{2,1,0:T(8,128)(2,1)}, bf16[8,128,128]{2,1,0:T(8,128)(2,1)S(1)}, u32[]{:S(2)}, u32[]{:S(2)}) collective-permute-start(bf16[8,128,128]{2,1,0:T(8,128)(2,1)} %collective-permute-done.20.refs_20_), channel_id=1, source_target_pairs={{0,4},{4,0},{8,12},{12,8},{16,20},{20,16},{24,28},{28,24},{1,5},{5... | collective-permute-start | bytes 786440 | tf_op jit(solution)/shard_map/ppermute | solution.py:913
  69.5 20.6 %collective-permute-start.24 = (bf16[256,1024]{1,0:T(8,128)(2,1)S(1)}, bf16[256,1024]{1,0:T(8,128)(2,1)S(1)}, u32[]{:S(2)}, u32[]{:S(2)}) collective-permute-start(bf16[256,1024]{1,0:T(8,128)(2,1)S(1)} %copy-done.24), channel_id=1, source_target_pairs={{0,2},{1,3},{2,0},{3,1},{4,6},{5,7},{6,4},{7,5},{8,10},{9,11},{10,... | collective-permute-start | bytes 1572872 | tf_op jit(solution)/shard_map/ppermute | solution.py:913
  103.2 14.2 %collective-permute-start.27 = (bf16[256,1024]{1,0:T(8,128)(2,1)}, bf16[256,1024]{1,0:T(8,128)(2,1)}, u32[]{:S(2)}, u32[]{:S(2)}) collective-permute-start(bf16[256,1024]{1,0:T(8,128)(2,1)} %get-tuple-element.139.chip_ref), channel_id=1, source_target_pairs={{0,2},{1,3},{2,0},{3,1},{4,6},{5,7},{6,4},{7,5},{8,10},{9,11},{10,... | collective-permute-start | bytes 1572872 | tf_op jit(solution)/shard_map/ppermute | solution.py:913
  119.0 14.3 %collective-permute-start.30 = (bf16[256,1024]{1,0:T(8,128)(2,1)S(1)}, bf16[256,1024]{1,0:T(8,128)(2,1)S(1)}, u32[]{:S(2)}, u32[]{:S(2)}) collective-permute-start(bf16[256,1024]{1,0:T(8,128)(2,1)S(1)} %get-tuple-element.138.chip_ref), channel_id=1, source_target_pairs={{0,2},{1,3},{2,0},{3,1},{4,6},{5,7},{6,4},{7,5},{8,10},{9,11},{10,... | collective-permute-start | bytes 1572872 | tf_op jit(solution)/shard_map/ppermute | solution.py:913
  135.2 14.4 %collective-permute-start.32 = (bf16[256,1024]{1,0:T(8,128)(2,1)S(1)}, bf16[256,1024]{1,0:T(8,128)(2,1)S(1)}, u32[]{:S(2)}, u32[]{:S(2)}) collective-permute-start(bf16[256,1024]{1,0:T(8,128)(2,1)S(1)} %get-tuple-element.150.chip_ref), channel_id=1, source_target_pairs={{0,2},{1,3},{2,0},{3,1},{4,6},{5,7},{6,4},{7,5},{8,10},{9,11},{10,... | collective-permute-start | bytes 1572872 | tf_op jit(solution)/shard_map/ppermute | solution.py:913
  159.0 14.2 %collective-permute-start.34 = (bf16[256,1024]{1,0:T(8,128)(2,1)S(1)}, bf16[256,1024]{1,0:T(8,128)(2,1)S(1)}, u32[]{:S(2)}, u32[]{:S(2)}) collective-permute-start(bf16[256,1024]{1,0:T(8,128)(2,1)S(1)} %get-tuple-element.157.chip_ref), channel_id=1, source_target_pairs={{0,2},{1,3},{2,0},{3,1},{4,6},{5,7},{6,4},{7,5},{8,10},{9,11},{10,... | collective-permute-start | bytes 1572872 | tf_op jit(solution)/shard_map/ppermute | solution.py:913
  184.3 13.9 %collective-permute-start.39 = (bf16[256,1024]{1,0:T(8,128)(2,1)S(1)}, bf16[256,1024]{1,0:T(8,128)(2,1)S(1)}, u32[]{:S(2)}, u32[]{:S(2)}) collective-permute-start(bf16[256,1024]{1,0:T(8,128)(2,1)S(1)} %get-tuple-element.180.chip_ref), channel_id=1, source_target_pairs={{0,2},{1,3},{2,0},{3,1},{4,6},{5,7},{6,4},{7,5},{8,10},{9,11},{10,... | collective-permute-start | bytes 1572872 | tf_op jit(solution)/shard_map/ppermute | solution.py:913
  199.2 14.3 %collective-permute-start.41 = (bf16[256,1024]{1,0:T(8,128)(2,1)S(1)}, bf16[256,1024]{1,0:T(8,128)(2,1)S(1)}, u32[]{:S(2)}, u32[]{:S(2)}) collective-permute-start(bf16[256,1024]{1,0:T(8,128)(2,1)S(1)} %get-tuple-element.179.chip_ref), channel_id=1, source_target_pairs={{0,2},{1,3},{2,0},{3,1},{4,6},{5,7},{6,4},{7,5},{8,10},{9,11},{10,... | collective-permute-start | bytes 1572872 | tf_op jit(solution)/shard_map/ppermute | solution.py:913
  230.2 20.4 %collective-permute-start.43 = (bf16[24,128,128]{2,1,0:T(8,128)(2,1)S(1)}, bf16[24,128,128]{2,1,0:T(8,128)(2,1)S(1)}, u32[]{:S(2)}, u32[]{:S(2)}) collective-permute-start(bf16[24,128,128]{2,1,0:T(8,128)(2,1)S(1)} %get-tuple-element.217), channel_id=1, source_target_pairs={{0,4},{4,0},{8,12},{12,8},{16,20},{20,16},{24,28},{28,24},{1,5},{5... | collective-permute-start | bytes 2359304 | tf_op jit(solution)/shard_map/ppermute | solution.py:913
  243.0 24.6 %collective-permute-start.53 = (bf16[24,128,128]{2,1,0:T(8,128)(2,1)S(1)}, bf16[24,128,128]{2,1,0:T(8,128)(2,1)S(1)}, u32[]{:S(2)}, u32[]{:S(2)}) collective-permute-start(bf16[24,128,128]{2,1,0:T(8,128)(2,1)S(1)} %get-tuple-element.238), channel_id=1, source_target_pairs={{0,4},{4,0},{8,12},{12,8},{16,20},{20,16},{24,28},{28,24},{1,5},{5... | collective-permute-start | bytes 2359304 | tf_op jit(solution)/shard_map/ppermute | solution.py:913
  250.8 19.8 %collective-permute-start.54 = (bf16[24,128,128]{2,1,0:T(8,128)(2,1)S(1)}, bf16[24,128,128]{2,1,0:T(8,128)(2,1)S(1)}, u32[]{:S(2)}, u32[]{:S(2)}) collective-permute-start(bf16[24,128,128]{2,1,0:T(8,128)(2,1)S(1)} %get-tuple-element.239), channel_id=1, source_target_pairs={{0,8},{4,12},{8,16},{12,20},{16,24},{20,28},{24,0},{28,4},{1,9},{5... | collective-permute-start | bytes 2359304 | tf_op jit(solution)/shard_map/ppermute | solution.py:918
  251.1 33.4 %collective-permute-start.52 = (bf16[24,128,128]{2,1,0:T(8,128)(2,1)}, bf16[24,128,128]{2,1,0:T(8,128)(2,1)}, u32[]{:S(2)}, u32[]{:S(2)}) collective-permute-start(bf16[24,128,128]{2,1,0:T(8,128)(2,1)} %get-tuple-element.237), channel_id=1, source_target_pairs={{0,4},{4,0},{8,12},{12,8},{16,20},{20,16},{24,28},{28,24},{1,5},{5... | collective-permute-start | bytes 2359304 | tf_op jit(solution)/shard_map/ppermute | solution.py:913
  271.8 19.2 %collective-permute-start.55 = (bf16[24,128,128]{2,1,0:T(8,128)(2,1)}, bf16[24,128,128]{2,1,0:T(8,128)(2,1)}, u32[]{:S(2)}, u32[]{:S(2)}) collective-permute-start(bf16[24,128,128]{2,1,0:T(8,128)(2,1)} %get-tuple-element.240), channel_id=1, source_target_pairs={{0,8},{4,12},{8,16},{12,20},{16,24},{20,28},{24,0},{28,4},{1,9},{5... | collective-permute-start | bytes 2359304 | tf_op jit(solution)/shard_map/ppermute | solution.py:918
  272.2 21.4 %collective-permute-start.57 = (f32[16,1024]{1,0:T(8,128)S(1)}, f32[16,1024]{1,0:T(8,128)S(1)}, u32[]{:S(2)}, u32[]{:S(2)}) collective-permute-start(f32[16,1024]{1,0:T(8,128)S(1)} %add.148.refs_4_), channel_id=1, source_target_pairs={{0,4},{4,0},{8,12},{12,8},{16,20},{20,16},{24,28},{28,24},{1,5},{5... | collective-permute-start | bytes 196616 | tf_op jit(solution)/shard_map/ppermute | solution.py:913
  274.5 27.5 %collective-permute-start.51 = (bf16[24,128,128]{2,1,0:T(8,128)(2,1)}, bf16[24,128,128]{2,1,0:T(8,128)(2,1)}, u32[]{:S(2)}, u32[]{:S(2)}) collective-permute-start(bf16[24,128,128]{2,1,0:T(8,128)(2,1)} %copy-done.38), channel_id=1, source_target_pairs={{0,4},{4,0},{8,12},{12,8},{16,20},{20,16},{24,28},{28,24},{1,5},{5... | collective-permute-start | bytes 2359304 | tf_op jit(solution)/shard_map/ppermute | solution.py:913
  274.8 19.6 %collective-permute-start.48 = (bf16[256,1024]{1,0:T(8,128)(2,1)}, bf16[256,1024]{1,0:T(8,128)(2,1)}, u32[]{:S(2)}, u32[]{:S(2)}) collective-permute-start(bf16[256,1024]{1,0:T(8,128)(2,1)} %copy-done.39), channel_id=1, source_target_pairs={{0,1},{1,0},{2,3},{3,2},{4,5},{5,4},{6,7},{7,6},{8,9},{9,8},{10,11... | collective-permute-start | bytes 1572872 | tf_op jit(solution)/shard_map/ppermute | solution.py:913
  284.5 12.7 %collective-permute-start.50 = (bf16[256,1024]{1,0:T(8,128)(2,1)}, bf16[256,1024]{1,0:T(8,128)(2,1)}, u32[]{:S(2)}, u32[]{:S(2)}) collective-permute-start(bf16[256,1024]{1,0:T(8,128)(2,1)} %get-tuple-element.234), channel_id=1, source_target_pairs={{0,2},{1,3},{2,0},{3,1},{4,6},{5,7},{6,4},{7,5},{8,10},{9,11},{10,... | collective-permute-start | bytes 1572872 | tf_op jit(solution)/shard_map/ppermute | solution.py:913
  293.6 18.1 %collective-permute-start.56 = (bf16[24,128,128]{2,1,0:T(8,128)(2,1)}, bf16[24,128,128]{2,1,0:T(8,128)(2,1)S(1)}, u32[]{:S(2)}, u32[]{:S(2)}) collective-permute-start(bf16[24,128,128]{2,1,0:T(8,128)(2,1)} %get-tuple-element.242), channel_id=1, source_target_pairs={{0,8},{4,12},{8,16},{12,20},{16,24},{20,28},{24,0},{28,4},{1,9},{5... | collective-permute-start | bytes 2359304 | tf_op jit(solution)/shard_map/ppermute | solution.py:918
  (74 other events, 749.4 us)

commit v7 on v6

--- a/solution.py
+++ b/solution.py
@@ -595,7 +595,7 @@
 
 def feed(block, w_up, bias, w_down, kind, after=()):
     rows, hidden = block.shape[0], w_up.shape[1]
-    step = 256
+    step = 512
     out_shape = [
         of((rows, hidden), bfloat), of((rows, hidden), bfloat), of((rows, D), kind), token_of()
     ]
@@ -632,7 +632,7 @@
 
 def feed_back(block, w_down, w_up, slope, kind, after=()):
     rows, hidden = block.shape[0], w_up.shape[1]
-    step = 256
+    step = 512
     out_shape = [
         of((rows, hidden), bfloat), of((1, hidden), single), of((rows, D), kind), token_of()
     ]

time: 346 us -> 341 us (0.986)
  Pallas kernels: 134 us -> 119 us
  waiting for transfers between devices: 131 us -> 140 us
    ppermute x46, waiting for transfers between devices: 86.9 us -> 96.4 us  [swap(): return lax.ppermute(value, axis, [(i, i ^ bit) for i in range(count)])]
    pallas_call x4, Pallas kernels: 20.3 us -> 12.5 us  [feed(): pl.pallas_call(feed_kernel, grid=(hidden // step,), in_specs=[fixed(block...]
    pallas_call x4, Pallas kernels: 16.1 us -> 8.72 us  [feed_back(): pl.pallas_call(feed_back_kernel, grid=(hidden // step,), in_specs=[fixed(...]
  transfers between devices with their start and end apart: 58 -> 58, of which waited for: 32 -> 32; matrix products, arithmetic and copies ran while one was open for 3% -> 3% of each run, Pallas kernels for 21% -> 18%
where the time goes in v7:
time: 341 us; the launch traced here: 337 us
  waiting for transfers between devices  140 us (41%)
  Pallas kernels  119 us (35%)
  starting transfers between devices  53 us (16%)
  local copies, waits for them, and re-layouts  14.6 us (4%)
  other arithmetic  6.18 us (2%)
    ppermute x46, waiting for transfers between devices, swap(): return lax.ppermute(value, axis, [(i, i ^ bit) for i in range(count)])  96.4 us
    ppermute x12, waiting for transfers between devices, ring(): lax.ppermute(value, 'dp', [(i, (i + 2) % count) for i in range(count)])  44 us
    ppermute x46, starting transfers between devices, swap(): return lax.ppermute(value, axis, [(i, i ^ bit) for i in range(count)])  43.7 us
    pallas_call x1, Pallas kernels, optimise(): pl.pallas_call(functools.partial(optimise_kernel, count=count, adds=len(g...  29.9 us
    pallas_call x4, Pallas kernels, attend(): pl.pallas_call(functools.partial(attend_kernel, heads=heads, own=own), gr...  16.6 us
    pallas_call x2, Pallas kernels, attend_back(): pl.pallas_call(functools.partial(attend_back_kernel, heads=heads, first=f...  15.6 us
    pallas_call x12, Pallas kernels, norm_call(): pl.pallas_call(kernel, grid=(rows // norm_tile,), in_specs=[by_row(value....  13.3 us
    pallas_call x4, Pallas kernels, feed(): pl.pallas_call(feed_kernel, grid=(hidden // step,), in_specs=[fixed(block...  12.5 us
  transfers between devices with their start and end apart: 58, of which 32 were waited for; matrix products, arithmetic and copies ran while one was open for 3% of the time, Pallas kernels for 18%

profile of v7, /device:TPU:0, one launch (start us, length us, event | category | flops | bytes accessed | tf_op | source)
XLA Modules:
  0.0 337.1 jit_solution(4121866138307694728)
XLA Ops:
  16.4 3.9 %collective-permute-done.7.refs_7_ = bf16[8,128,128]{2,1,0:T(8,128)(2,1)} collective-permute-done((bf16[8,128,128]{2,1,0:T(8,128)(2,1)S(1)}, bf16[8,128,128]{2,1,0:T(8,128)(2,1)}, u32[]{:S(2)}, u32[]{:S(2)}) %collective-permute-start.7) | collective-permute-done | bytes 262176 | tf_op jit(solution)/shard_map/ppermute | solution.py:918
  20.3 5.6 %collective-permute-done.8.refs_8_ = bf16[8,128,128]{2,1,0:T(8,128)(2,1)} collective-permute-done((bf16[8,128,128]{2,1,0:T(8,128)(2,1)S(1)}, bf16[8,128,128]{2,1,0:T(8,128)(2,1)}, u32[]{:S(2)}, u32[]{:S(2)}) %collective-permute-start.8) | collective-permute-done | bytes 262176 | tf_op jit(solution)/shard_map/ppermute | solution.py:918
  33.5 3.8 %collective-permute-done.13.refs_13_ = bf16[8,128,128]{2,1,0:T(8,128)(2,1)} collective-permute-done((bf16[8,128,128]{2,1,0:T(8,128)(2,1)}, bf16[8,128,128]{2,1,0:T(8,128)(2,1)}, u32[]{:S(2)}, u32[]{:S(2)}) %collective-permute-start.13) | collective-permute-done | bytes 262176 | tf_op jit(solution)/shard_map/ppermute | solution.py:918
  46.7 4.7 %collective-permute-done.9.refs_9_ = bf16[8,128,128]{2,1,0:T(8,128)(2,1)S(1)} collective-permute-done((bf16[8,128,128]{2,1,0:T(8,128)(2,1)}, bf16[8,128,128]{2,1,0:T(8,128)(2,1)S(1)}, u32[]{:S(2)}, u32[]{:S(2)}) %collective-permute-start.9) | collective-permute-done | bytes 262176 | tf_op jit(solution)/shard_map/ppermute | solution.py:913
  55.1 6.5 %collective-permute-done.19.refs_19_ = bf16[8,128,128]{2,1,0:T(8,128)(2,1)} collective-permute-done((bf16[8,128,128]{2,1,0:T(8,128)(2,1)}, bf16[8,128,128]{2,1,0:T(8,128)(2,1)}, u32[]{:S(2)}, u32[]{:S(2)}) %collective-permute-start.19) | collective-permute-done | bytes 262176 | tf_op jit(solution)/shard_map/ppermute | solution.py:918
  72.2 4.5 %collective-permute-done.21.refs_21_ = bf16[8,128,128]{2,1,0:T(8,128)(2,1)S(1)} collective-permute-done((bf16[8,128,128]{2,1,0:T(8,128)(2,1)}, bf16[8,128,128]{2,1,0:T(8,128)(2,1)S(1)}, u32[]{:S(2)}, u32[]{:S(2)}) %collective-permute-start.21) | collective-permute-done | bytes 262176 | tf_op jit(solution)/shard_map/ppermute | solution.py:913
  76.7 3.7 %collective-permute-done.22.refs_22_ = bf16[8,128,128]{2,1,0:T(8,128)(2,1)S(1)} collective-permute-done((bf16[8,128,128]{2,1,0:T(8,128)(2,1)}, bf16[8,128,128]{2,1,0:T(8,128)(2,1)S(1)}, u32[]{:S(2)}, u32[]{:S(2)}) %collective-permute-start.22) | collective-permute-done | bytes 262176 | tf_op jit(solution)/shard_map/ppermute | solution.py:913
  83.3 4.2 %assemble.1 = (bf16[1024,768]{1,0:T(8,128)(2,1)S(1)}, bf16[256,1024]{1,0:T(8,128)(2,1)S(1)}, bf16[1024,1024]{1,0:T(8,128)(2,1)S(1)}, bf16[1024,1024]{1,0:T(8,128)(2,1)S(1)}) custom-call(s32[192]{0:T(256)S(1)} %get-tuple-element.270.source_ref, bf16[8,128,128]{2,1,0:T(8,128)(2,1)S(1)} %copy-done.23, bf16[8,128,128]{2,1,0:T(8,128)(2,1)S(1)} %copy-done.21, ...), custom_call_target="tpu_custom_call" | custom-call | tf_op jit(solution)/shard_map/assemble/pallas_call | solution.py:1005
  90.3 3.4 %attend.4 = (bf16[256,256]{1,0:T(8,128)(2,1)S(1)}, f32[4,256]{1,0:T(4,128)S(1)}, bf16[256,1024]{1,0:T(8,128)(2,1)S(1)}, f32[8,128]{1,0:T(8,128)S(1)}) custom-call(bf16[1024,768]{1,0:T(8,128)(2,1)S(1)} %add_convert_fusion.q_ref.k_ref.v_ref.refs_3_.refs_4_.refs_5_, bf16[1024,768]{1,0:T(8,128)(2,1)S(1)} %add_convert_fusion.q_ref.k_ref.v_ref.refs_3_.refs_4_.refs_5_, ...), custom_call_target="tpu_custom_call" | custom-call | flops 67108864 | bytes 139776 | tf_op jit(solution)/shard_map/attend/pallas_call | solution.py:400
  93.8 4.2 %attend.5 = (bf16[256,256]{1,0:T(8,128)(2,1)S(1)}, f32[4,256]{1,0:T(4,128)S(1)}, bf16[256,1024]{1,0:T(8,128)(2,1)}, f32[8,128]{1,0:T(8,128)S(1)}) custom-call(bf16[1024,768]{1,0:T(8,128)(2,1)S(1)} %add_convert_fusion.q_ref.k_ref.v_ref.refs_3_.refs_4_.refs_5_, bf16[1024,768]{1,0:T(8,128)(2,1)S(1)} %add_convert_fusion.q_ref.k_ref.v_ref.refs_3_.refs_4_.refs_5_, ...), custom_call_target="tpu_custom_call" | custom-call | flops 67108864 | bytes 139776 | tf_op jit(solution)/shard_map/attend/pallas_call | solution.py:400
  98.4 4.2 %attend.6 = (bf16[256,256]{1,0:T(8,128)(2,1)S(1)}, f32[4,256]{1,0:T(4,128)S(1)}, bf16[256,1024]{1,0:T(8,128)(2,1)}, f32[8,128]{1,0:T(8,128)S(1)}) custom-call(bf16[1024,768]{1,0:T(8,128)(2,1)S(1)} %add_convert_fusion.q_ref.k_ref.v_ref.refs_3_.refs_4_.refs_5_, bf16[1024,768]{1,0:T(8,128)(2,1)S(1)} %add_convert_fusion.q_ref.k_ref.v_ref.refs_3_.refs_4_.refs_5_, ...), custom_call_target="tpu_custom_call" | custom-call | flops 67108864 | bytes 139776 | tf_op jit(solution)/shard_map/attend/pallas_call | solution.py:400
  106.4 4.8 %attend.7 = (bf16[256,256]{1,0:T(8,128)(2,1)S(1)}, f32[4,256]{1,0:T(4,128)S(1)}, bf16[256,1024]{1,0:T(8,128)(2,1)S(1)}, f32[8,128]{1,0:T(8,128)S(1)}) custom-call(bf16[1024,768]{1,0:T(8,128)(2,1)S(1)} %add_convert_fusion.q_ref.k_ref.v_ref.refs_3_.refs_4_.refs_5_, bf16[1024,768]{1,0:T(8,128)(2,1)S(1)} %add_convert_fusion.q_ref.k_ref.v_ref.refs_3_.refs_4_.refs_5_, ...), custom_call_target="tpu_custom_call" | custom-call | flops 67108864 | bytes 139776 | tf_op jit(solution)/shard_map/attend/pallas_call | solution.py:400
  111.3 6.1 %collective-permute-done.27.across_ref = bf16[256,1024]{1,0:T(8,128)(2,1)} collective-permute-done((bf16[256,1024]{1,0:T(8,128)(2,1)}, bf16[256,1024]{1,0:T(8,128)(2,1)}, u32[]{:S(2)}, u32[]{:S(2)}) %collective-permute-start.27) | collective-permute-done | bytes 524320 | tf_op jit(solution)/shard_map/ppermute | solution.py:913
  120.8 3.2 feed.4
  124.0 3.1 feed.5
  127.4 6.0 %collective-permute-done.30.across_ref = bf16[256,1024]{1,0:T(8,128)(2,1)S(1)} collective-permute-done((bf16[256,1024]{1,0:T(8,128)(2,1)S(1)}, bf16[256,1024]{1,0:T(8,128)(2,1)S(1)}, u32[]{:S(2)}, u32[]{:S(2)}) %collective-permute-start.30) | collective-permute-done | bytes 524320 | tf_op jit(solution)/shard_map/ppermute | solution.py:913
  140.2 9.4 %collective-permute-done.32.refs_1_.across_ref = bf16[256,1024]{1,0:T(8,128)(2,1)S(1)} collective-permute-done((bf16[256,1024]{1,0:T(8,128)(2,1)S(1)}, bf16[256,1024]{1,0:T(8,128)(2,1)S(1)}, u32[]{:S(2)}, u32[]{:S(2)}) %collective-permute-start.32) | collective-permute-done | bytes 524320 | tf_op jit(solution)/shard_map/ppermute | solution.py:913
  163.1 8.1 %collective-permute-done.34.across_ref = bf16[256,1024]{1,0:T(8,128)(2,1)S(1)} collective-permute-done((bf16[256,1024]{1,0:T(8,128)(2,1)S(1)}, bf16[256,1024]{1,0:T(8,128)(2,1)S(1)}, u32[]{:S(2)}, u32[]{:S(2)}) %collective-permute-start.34) | collective-permute-done | bytes 524320 | tf_op jit(solution)/shard_map/ppermute | solution.py:913
  180.5 5.7 %pack.2 = (bf16[192,128,128]{2,1,0:T(8,128)(2,1)S(1)}, f32[8,128]{1,0:T(8,128)S(1)}) custom-call(s32[192]{0:T(256)S(1)} %get-tuple-element.269.target_ref, bf16[256,1024]{1,0:T(8,128)(2,1)S(1)} %get-tuple-element.141.rows_ref.refs_0_, bf16[256,1024]{1,0:T(8,128)(2,1)S(1)} %collective-permute-done.28.rows_ref.refs_1_, ...), custom_call_target="tpu_custom_call" | custom-call | flops 268435456 | bytes 786432 | tf_op jit(solution)/shard_map/pack/pallas_call | solution.py:841
  186.3 6.3 %collective-permute-done.39.across_ref = bf16[256,1024]{1,0:T(8,128)(2,1)S(1)} collective-permute-done((bf16[256,1024]{1,0:T(8,128)(2,1)S(1)}, bf16[256,1024]{1,0:T(8,128)(2,1)S(1)}, u32[]{:S(2)}, u32[]{:S(2)}) %collective-permute-start.39) | collective-permute-done | bytes 524320 | tf_op jit(solution)/shard_map/ppermute | solution.py:913
  195.4 7.7 %attend_back.2 = (bf16[512,256]{1,0:T(8,128)(2,1)S(1)}, f32[1024,256]{1,0:T(8,128)S(1)}, f32[1024,256]{1,0:T(8,128)S(1)}, f32[8,128]{1,0:T(8,128)S(1)}) custom-call(bf16[256,1024]{1,0:T(8,128)(2,1)S(1)} %get-tuple-element.193.refs_0_.refs_9_, bf16[256,1024]{1,0:T(8,128)(2,1)S(1)} %collective-permute-done.40.refs_1_.refs_10_, ...), custom_call_target="tpu_custom_call" | custom-call | flops 335544320 | bytes 246016 | tf_op jit(solution)/shard_map/attend_back/pallas_call | solution.py:520
  203.2 4.7 %collective-permute-done.41.across_ref = bf16[256,1024]{1,0:T(8,128)(2,1)S(1)} collective-permute-done((bf16[256,1024]{1,0:T(8,128)(2,1)S(1)}, bf16[256,1024]{1,0:T(8,128)(2,1)S(1)}, u32[]{:S(2)}, u32[]{:S(2)}) %collective-permute-start.41) | collective-permute-done | bytes 524320 | tf_op jit(solution)/shard_map/ppermute | solution.py:913
  211.4 7.9 %attend_back.3 = (bf16[512,256]{1,0:T(8,128)(2,1)S(1)}, bf16[1024,256]{1,0:T(8,128)(2,1)S(1)}, bf16[1024,256]{1,0:T(8,128)(2,1)S(1)}, f32[8,128]{1,0:T(8,128)S(1)}) custom-call(bf16[256,1024]{1,0:T(8,128)(2,1)S(1)} %get-tuple-element.203.refs_0_.refs_11_, bf16[256,1024]{1,0:T(8,128)(2,1)S(1)} %collective-permute-done.42.refs_1_.refs_12_, ...), custom_call_target="tpu_custom_call" | custom-call | flops 335544320 | bytes 180480 | tf_op jit(solution)/shard_map/attend_back/pallas_call | solution.py:520
  219.3 5.2 %pack.3 = (bf16[96,128,128]{2,1,0:T(8,128)(2,1)S(1)}, bf16[24,128,128]{2,1,0:T(8,128)(2,1)S(1)}, bf16[24,128,128]{2,1,0:T(8,128)(2,1)}, bf16[24,128,128]{2,1,0:T...) custom-call(s32[192]{0:T(256)S(1)} %get-tuple-element.269.target_ref, ...), custom_call_target="tpu_custom_call" | custom-call | flops 134217728 | bytes 524288 | tf_op jit(solution)/shard_map/pack/pallas_call | solution.py:841
  232.3 4.3 %collective-permute-done.46 = f32[16,1024]{1,0:T(8,128)S(1)} collective-permute-done((f32[16,1024]{1,0:T(8,128)S(1)}, f32[16,1024]{1,0:T(8,128)S(1)}, u32[]{:S(2)}, u32[]{:S(2)}) %collective-permute-start.46) | collective-permute-done | bytes 65568 | tf_op jit(solution)/shard_map/ppermute | solution.py:913
  238.7 3.3 collective-permute-done.47
  249.7 12.2 %collective-permute-done.53.refs_1_ = bf16[24,128,128]{2,1,0:T(8,128)(2,1)S(1)} collective-permute-done((bf16[24,128,128]{2,1,0:T(8,128)(2,1)S(1)}, bf16[24,128,128]{2,1,0:T(8,128)(2,1)S(1)}, u32[]{:S(2)}, u32[]{:S(2)}) %collective-permute-start.53) | collective-permute-done | bytes 786464 | tf_op jit(solution)/shard_map/ppermute | solution.py:913
  261.9 3.1 collective-permute-done.54.refs_2_
  272.2 6.6 %collective-permute-done.52.refs_1_ = bf16[24,128,128]{2,1,0:T(8,128)(2,1)} collective-permute-done((bf16[24,128,128]{2,1,0:T(8,128)(2,1)}, bf16[24,128,128]{2,1,0:T(8,128)(2,1)}, u32[]{:S(2)}, u32[]{:S(2)}) %collective-permute-start.52) | collective-permute-done | bytes 786464 | tf_op jit(solution)/shard_map/ppermute | solution.py:913
  280.5 4.8 %collective-permute-done.55.refs_2_ = bf16[24,128,128]{2,1,0:T(8,128)(2,1)} collective-permute-done((bf16[24,128,128]{2,1,0:T(8,128)(2,1)}, bf16[24,128,128]{2,1,0:T(8,128)(2,1)}, u32[]{:S(2)}, u32[]{:S(2)}) %collective-permute-start.55) | collective-permute-done | bytes 786464 | tf_op jit(solution)/shard_map/ppermute | solution.py:918
  296.3 9.8 %collective-permute-done.56.refs_2_ = bf16[24,128,128]{2,1,0:T(8,128)(2,1)S(1)} collective-permute-done((bf16[24,128,128]{2,1,0:T(8,128)(2,1)}, bf16[24,128,128]{2,1,0:T(8,128)(2,1)S(1)}, u32[]{:S(2)}, u32[]{:S(2)}) %collective-permute-start.56) | collective-permute-done | bytes 786464 | tf_op jit(solution)/shard_map/ppermute | solution.py:918
  306.9 29.9 %optimise.1 = (f32[24,128,128]{2,1,0:T(8,128)}, f32[24,128,128]{2,1,0:T(8,128)}, f32[24,128,128]{2,1,0:T(8,128)}, f32[24,128,128]{2,1,0:T(8,128)}, f32[24,128,12...) custom-call(s32[24]{0:T(128)} %iota.22.slots_ref, ...), custom_call_target="tpu_custom_call" | custom-call | flops 125829120 | bytes 983040 | tf_op jit(solution)/shard_map/optimise/pallas_call | solution.py:276
  (249 shorter events, 133.6 us)
Async XLA Ops:
  5.4 14.9 %collective-permute-start.7 = (bf16[8,128,128]{2,1,0:T(8,128)(2,1)S(1)}, bf16[8,128,128]{2,1,0:T(8,128)(2,1)}, u32[]{:S(2)}, u32[]{:S(2)}) collective-permute-start(bf16[8,128,128]{2,1,0:T(8,128)(2,1)S(1)} %get-tuple-element.254.refs_1_), channel_id=1, source_target_pairs={{0,8},{4,12},{8,16},{12,20},{16,24},{20,28},{24,0},{28,4},{1,9},{5... | collective-permute-start | bytes 786440 | tf_op jit(solution)/shard_map/ppermute | solution.py:918
  7.0 18.9 %collective-permute-start.8 = (bf16[8,128,128]{2,1,0:T(8,128)(2,1)S(1)}, bf16[8,128,128]{2,1,0:T(8,128)(2,1)}, u32[]{:S(2)}, u32[]{:S(2)}) collective-permute-start(bf16[8,128,128]{2,1,0:T(8,128)(2,1)S(1)} %get-tuple-element.253.refs_2_), channel_id=1, source_target_pairs={{0,8},{4,12},{8,16},{12,20},{16,24},{20,28},{24,0},{28,4},{1,9},{5... | collective-permute-start | bytes 786440 | tf_op jit(solution)/shard_map/ppermute | solution.py:918
  8.6 17.4 %collective-permute-start.3 = (bf16[8,128,128]{2,1,0:T(8,128)(2,1)S(1)}, bf16[8,128,128]{2,1,0:T(8,128)(2,1)S(1)}, u32[]{:S(2)}, u32[]{:S(2)}) collective-permute-start(bf16[8,128,128]{2,1,0:T(8,128)(2,1)S(1)} %get-tuple-element.255.refs_0_), channel_id=1, source_target_pairs={{0,4},{4,0},{8,12},{12,8},{16,20},{20,16},{24,28},{28,24},{1,5},{5... | collective-permute-start | bytes 786440 | tf_op jit(solution)/shard_map/ppermute | solution.py:913
  10.8 17.5 %collective-permute-start.4 = (bf16[8,128,128]{2,1,0:T(8,128)(2,1)S(1)}, bf16[8,128,128]{2,1,0:T(8,128)(2,1)S(1)}, u32[]{:S(2)}, u32[]{:S(2)}) collective-permute-start(bf16[8,128,128]{2,1,0:T(8,128)(2,1)S(1)} %get-tuple-element.254.refs_1_), channel_id=1, source_target_pairs={{0,4},{4,0},{8,12},{12,8},{16,20},{20,16},{24,28},{28,24},{1,5},{5... | collective-permute-start | bytes 786440 | tf_op jit(solution)/shard_map/ppermute | solution.py:913
  14.7 15.8 %collective-permute-start.5 = (bf16[8,128,128]{2,1,0:T(8,128)(2,1)S(1)}, bf16[8,128,128]{2,1,0:T(8,128)(2,1)S(1)}, u32[]{:S(2)}, u32[]{:S(2)}) collective-permute-start(bf16[8,128,128]{2,1,0:T(8,128)(2,1)S(1)} %get-tuple-element.253.refs_2_), channel_id=1, source_target_pairs={{0,4},{4,0},{8,12},{12,8},{16,20},{20,16},{24,28},{28,24},{1,5},{5... | collective-permute-start | bytes 786440 | tf_op jit(solution)/shard_map/ppermute | solution.py:913
  20.3 12.4 %collective-permute-start.12 = (bf16[8,128,128]{2,1,0:T(8,128)(2,1)}, bf16[8,128,128]{2,1,0:T(8,128)(2,1)}, u32[]{:S(2)}, u32[]{:S(2)}) collective-permute-start(bf16[8,128,128]{2,1,0:T(8,128)(2,1)} %collective-permute-done.6.refs_6_), channel_id=1, source_target_pairs={{0,8},{4,12},{8,16},{12,20},{16,24},{20,28},{24,0},{28,4},{1,9},{5... | collective-permute-start | bytes 786440 | tf_op jit(solution)/shard_map/ppermute | solution.py:918
  26.7 15.3 %collective-permute-start.14 = (bf16[8,128,128]{2,1,0:T(8,128)(2,1)}, bf16[8,128,128]{2,1,0:T(8,128)(2,1)}, u32[]{:S(2)}, u32[]{:S(2)}) collective-permute-start(bf16[8,128,128]{2,1,0:T(8,128)(2,1)} %collective-permute-done.8.refs_8_), channel_id=1, source_target_pairs={{0,8},{4,12},{8,16},{12,20},{16,24},{20,28},{24,0},{28,4},{1,9},{5... | collective-permute-start | bytes 786440 | tf_op jit(solution)/shard_map/ppermute | solution.py:918
  28.9 14.5 %collective-permute-start.10 = (bf16[8,128,128]{2,1,0:T(8,128)(2,1)}, bf16[8,128,128]{2,1,0:T(8,128)(2,1)}, u32[]{:S(2)}, u32[]{:S(2)}) collective-permute-start(bf16[8,128,128]{2,1,0:T(8,128)(2,1)} %collective-permute-done.7.refs_7_), channel_id=1, source_target_pairs={{0,4},{4,0},{8,12},{12,8},{16,20},{20,16},{24,28},{28,24},{1,5},{5... | collective-permute-start | bytes 786440 | tf_op jit(solution)/shard_map/ppermute | solution.py:913
  31.1 21.0 %collective-permute-start.1 = (bf16[256,1024]{1,0:T(8,128)(2,1)S(1)}, bf16[256,1024]{1,0:T(8,128)(2,1)S(1)}, u32[]{:S(2)}, u32[]{:S(2)}) collective-permute-start(bf16[256,1024]{1,0:T(8,128)(2,1)S(1)} %copy-done.8), channel_id=1, source_target_pairs={{0,2},{1,3},{2,0},{3,1},{4,6},{5,7},{6,4},{7,5},{8,10},{9,11},{10,... | collective-permute-start | bytes 1572872 | tf_op jit(solution)/shard_map/ppermute | solution.py:913
  32.7 21.0 %collective-permute-start = (bf16[256,1024]{1,0:T(8,128)(2,1)S(1)}, bf16[256,1024]{1,0:T(8,128)(2,1)S(1)}, u32[]{:S(2)}, u32[]{:S(2)}) collective-permute-start(bf16[256,1024]{1,0:T(8,128)(2,1)S(1)} %copy-done.8), channel_id=1, source_target_pairs={{0,1},{1,0},{2,3},{3,2},{4,5},{5,4},{6,7},{7,6},{8,9},{9,8},{10,11... | collective-permute-start | bytes 1572872 | tf_op jit(solution)/shard_map/ppermute | solution.py:913
  45.5 20.8 %collective-permute-start.15 = (bf16[8,128,128]{2,1,0:T(8,128)(2,1)}, bf16[8,128,128]{2,1,0:T(8,128)(2,1)}, u32[]{:S(2)}, u32[]{:S(2)}) collective-permute-start(bf16[8,128,128]{2,1,0:T(8,128)(2,1)} %collective-permute-done.12.refs_12_), channel_id=1, source_target_pairs={{0,4},{4,0},{8,12},{12,8},{16,20},{20,16},{24,28},{28,24},{1,5},{5... | collective-permute-start | bytes 786440 | tf_op jit(solution)/shard_map/ppermute | solution.py:913
  52.1 14.3 %collective-permute-start.16 = (bf16[8,128,128]{2,1,0:T(8,128)(2,1)}, bf16[8,128,128]{2,1,0:T(8,128)(2,1)}, u32[]{:S(2)}, u32[]{:S(2)}) collective-permute-start(bf16[8,128,128]{2,1,0:T(8,128)(2,1)} %collective-permute-done.13.refs_13_), channel_id=1, source_target_pairs={{0,4},{4,0},{8,12},{12,8},{16,20},{20,16},{24,28},{28,24},{1,5},{5... | collective-permute-start | bytes 786440 | tf_op jit(solution)/shard_map/ppermute | solution.py:913
  54.9 14.6 %collective-permute-start.2 = (bf16[256,1024]{1,0:T(8,128)(2,1)S(1)}, bf16[256,1024]{1,0:T(8,128)(2,1)}, u32[]{:S(2)}, u32[]{:S(2)}) collective-permute-start(bf16[256,1024]{1,0:T(8,128)(2,1)S(1)} %collective-permute-done.1.rows_ref), channel_id=1, source_target_pairs={{0,1},{1,0},{2,3},{3,2},{4,5},{5,4},{6,7},{7,6},{8,9},{9,8},{10,11... | collective-permute-start | bytes 1572872 | tf_op jit(solution)/shard_map/ppermute | solution.py:913
  66.3 14.1 %collective-permute-start.22 = (bf16[8,128,128]{2,1,0:T(8,128)(2,1)}, bf16[8,128,128]{2,1,0:T(8,128)(2,1)S(1)}, u32[]{:S(2)}, u32[]{:S(2)}) collective-permute-start(bf16[8,128,128]{2,1,0:T(8,128)(2,1)} %collective-permute-done.19.refs_19_), channel_id=1, source_target_pairs={{0,4},{4,0},{8,12},{12,8},{16,20},{20,16},{24,28},{28,24},{1,5},{5... | collective-permute-start | bytes 786440 | tf_op jit(solution)/shard_map/ppermute | solution.py:913
  66.4 16.8 %collective-permute-start.23 = (bf16[8,128,128]{2,1,0:T(8,128)(2,1)}, bf16[8,128,128]{2,1,0:T(8,128)(2,1)S(1)}, u32[]{:S(2)}, u32[]{:S(2)}) collective-permute-start(bf16[8,128,128]{2,1,0:T(8,128)(2,1)} %collective-permute-done.20.refs_20_), channel_id=1, source_target_pairs={{0,4},{4,0},{8,12},{12,8},{16,20},{20,16},{24,28},{28,24},{1,5},{5... | collective-permute-start | bytes 786440 | tf_op jit(solution)/shard_map/ppermute | solution.py:913
  69.5 20.6 %collective-permute-start.24 = (bf16[256,1024]{1,0:T(8,128)(2,1)S(1)}, bf16[256,1024]{1,0:T(8,128)(2,1)S(1)}, u32[]{:S(2)}, u32[]{:S(2)}) collective-permute-start(bf16[256,1024]{1,0:T(8,128)(2,1)S(1)} %copy-done.24), channel_id=1, source_target_pairs={{0,2},{1,3},{2,0},{3,1},{4,6},{5,7},{6,4},{7,5},{8,10},{9,11},{10,... | collective-permute-start | bytes 1572872 | tf_op jit(solution)/shard_map/ppermute | solution.py:913
  103.2 14.2 %collective-permute-start.27 = (bf16[256,1024]{1,0:T(8,128)(2,1)}, bf16[256,1024]{1,0:T(8,128)(2,1)}, u32[]{:S(2)}, u32[]{:S(2)}) collective-permute-start(bf16[256,1024]{1,0:T(8,128)(2,1)} %get-tuple-element.139.chip_ref), channel_id=1, source_target_pairs={{0,2},{1,3},{2,0},{3,1},{4,6},{5,7},{6,4},{7,5},{8,10},{9,11},{10,... | collective-permute-start | bytes 1572872 | tf_op jit(solution)/shard_map/ppermute | solution.py:913
  119.0 14.3 %collective-permute-start.30 = (bf16[256,1024]{1,0:T(8,128)(2,1)S(1)}, bf16[256,1024]{1,0:T(8,128)(2,1)S(1)}, u32[]{:S(2)}, u32[]{:S(2)}) collective-permute-start(bf16[256,1024]{1,0:T(8,128)(2,1)S(1)} %get-tuple-element.138.chip_ref), channel_id=1, source_target_pairs={{0,2},{1,3},{2,0},{3,1},{4,6},{5,7},{6,4},{7,5},{8,10},{9,11},{10,... | collective-permute-start | bytes 1572872 | tf_op jit(solution)/shard_map/ppermute | solution.py:913
  135.2 14.4 %collective-permute-start.32 = (bf16[256,1024]{1,0:T(8,128)(2,1)S(1)}, bf16[256,1024]{1,0:T(8,128)(2,1)S(1)}, u32[]{:S(2)}, u32[]{:S(2)}) collective-permute-start(bf16[256,1024]{1,0:T(8,128)(2,1)S(1)} %get-tuple-element.150.chip_ref), channel_id=1, source_target_pairs={{0,2},{1,3},{2,0},{3,1},{4,6},{5,7},{6,4},{7,5},{8,10},{9,11},{10,... | collective-permute-start | bytes 1572872 | tf_op jit(solution)/shard_map/ppermute | solution.py:913
  157.1 14.2 %collective-permute-start.34 = (bf16[256,1024]{1,0:T(8,128)(2,1)S(1)}, bf16[256,1024]{1,0:T(8,128)(2,1)S(1)}, u32[]{:S(2)}, u32[]{:S(2)}) collective-permute-start(bf16[256,1024]{1,0:T(8,128)(2,1)S(1)} %get-tuple-element.157.chip_ref), channel_id=1, source_target_pairs={{0,2},{1,3},{2,0},{3,1},{4,6},{5,7},{6,4},{7,5},{8,10},{9,11},{10,... | collective-permute-start | bytes 1572872 | tf_op jit(solution)/shard_map/ppermute | solution.py:913
  178.6 13.9 %collective-permute-start.39 = (bf16[256,1024]{1,0:T(8,128)(2,1)S(1)}, bf16[256,1024]{1,0:T(8,128)(2,1)S(1)}, u32[]{:S(2)}, u32[]{:S(2)}) collective-permute-start(bf16[256,1024]{1,0:T(8,128)(2,1)S(1)} %get-tuple-element.180.chip_ref), channel_id=1, source_target_pairs={{0,2},{1,3},{2,0},{3,1},{4,6},{5,7},{6,4},{7,5},{8,10},{9,11},{10,... | collective-permute-start | bytes 1572872 | tf_op jit(solution)/shard_map/ppermute | solution.py:913
  193.5 14.3 %collective-permute-start.41 = (bf16[256,1024]{1,0:T(8,128)(2,1)S(1)}, bf16[256,1024]{1,0:T(8,128)(2,1)S(1)}, u32[]{:S(2)}, u32[]{:S(2)}) collective-permute-start(bf16[256,1024]{1,0:T(8,128)(2,1)S(1)} %get-tuple-element.179.chip_ref), channel_id=1, source_target_pairs={{0,2},{1,3},{2,0},{3,1},{4,6},{5,7},{6,4},{7,5},{8,10},{9,11},{10,... | collective-permute-start | bytes 1572872 | tf_op jit(solution)/shard_map/ppermute | solution.py:913
  224.6 20.5 %collective-permute-start.43 = (bf16[24,128,128]{2,1,0:T(8,128)(2,1)S(1)}, bf16[24,128,128]{2,1,0:T(8,128)(2,1)S(1)}, u32[]{:S(2)}, u32[]{:S(2)}) collective-permute-start(bf16[24,128,128]{2,1,0:T(8,128)(2,1)S(1)} %get-tuple-element.217), channel_id=1, source_target_pairs={{0,4},{4,0},{8,12},{12,8},{16,20},{20,16},{24,28},{28,24},{1,5},{5... | collective-permute-start | bytes 2359304 | tf_op jit(solution)/shard_map/ppermute | solution.py:913
  237.3 24.5 %collective-permute-start.53 = (bf16[24,128,128]{2,1,0:T(8,128)(2,1)S(1)}, bf16[24,128,128]{2,1,0:T(8,128)(2,1)S(1)}, u32[]{:S(2)}, u32[]{:S(2)}) collective-permute-start(bf16[24,128,128]{2,1,0:T(8,128)(2,1)S(1)} %get-tuple-element.238), channel_id=1, source_target_pairs={{0,4},{4,0},{8,12},{12,8},{16,20},{20,16},{24,28},{28,24},{1,5},{5... | collective-permute-start | bytes 2359304 | tf_op jit(solution)/shard_map/ppermute | solution.py:913
  245.2 19.8 %collective-permute-start.54 = (bf16[24,128,128]{2,1,0:T(8,128)(2,1)S(1)}, bf16[24,128,128]{2,1,0:T(8,128)(2,1)S(1)}, u32[]{:S(2)}, u32[]{:S(2)}) collective-permute-start(bf16[24,128,128]{2,1,0:T(8,128)(2,1)S(1)} %get-tuple-element.239), channel_id=1, source_target_pairs={{0,8},{4,12},{8,16},{12,20},{16,24},{20,28},{24,0},{28,4},{1,9},{5... | collective-permute-start | bytes 2359304 | tf_op jit(solution)/shard_map/ppermute | solution.py:918
  245.4 33.4 %collective-permute-start.52 = (bf16[24,128,128]{2,1,0:T(8,128)(2,1)}, bf16[24,128,128]{2,1,0:T(8,128)(2,1)}, u32[]{:S(2)}, u32[]{:S(2)}) collective-permute-start(bf16[24,128,128]{2,1,0:T(8,128)(2,1)} %get-tuple-element.237), channel_id=1, source_target_pairs={{0,4},{4,0},{8,12},{12,8},{16,20},{20,16},{24,28},{28,24},{1,5},{5... | collective-permute-start | bytes 2359304 | tf_op jit(solution)/shard_map/ppermute | solution.py:913
  266.2 19.2 %collective-permute-start.55 = (bf16[24,128,128]{2,1,0:T(8,128)(2,1)}, bf16[24,128,128]{2,1,0:T(8,128)(2,1)}, u32[]{:S(2)}, u32[]{:S(2)}) collective-permute-start(bf16[24,128,128]{2,1,0:T(8,128)(2,1)} %get-tuple-element.240), channel_id=1, source_target_pairs={{0,8},{4,12},{8,16},{12,20},{16,24},{20,28},{24,0},{28,4},{1,9},{5... | collective-permute-start | bytes 2359304 | tf_op jit(solution)/shard_map/ppermute | solution.py:918
  266.5 21.4 %collective-permute-start.57 = (f32[16,1024]{1,0:T(8,128)S(1)}, f32[16,1024]{1,0:T(8,128)S(1)}, u32[]{:S(2)}, u32[]{:S(2)}) collective-permute-start(f32[16,1024]{1,0:T(8,128)S(1)} %add.148.refs_4_), channel_id=1, source_target_pairs={{0,4},{4,0},{8,12},{12,8},{16,20},{20,16},{24,28},{28,24},{1,5},{5... | collective-permute-start | bytes 196616 | tf_op jit(solution)/shard_map/ppermute | solution.py:913
  268.8 27.5 %collective-permute-start.51 = (bf16[24,128,128]{2,1,0:T(8,128)(2,1)}, bf16[24,128,128]{2,1,0:T(8,128)(2,1)}, u32[]{:S(2)}, u32[]{:S(2)}) collective-permute-start(bf16[24,128,128]{2,1,0:T(8,128)(2,1)} %copy-done.38), channel_id=1, source_target_pairs={{0,4},{4,0},{8,12},{12,8},{16,20},{20,16},{24,28},{28,24},{1,5},{5... | collective-permute-start | bytes 2359304 | tf_op jit(solution)/shard_map/ppermute | solution.py:913
  269.2 19.5 %collective-permute-start.48 = (bf16[256,1024]{1,0:T(8,128)(2,1)}, bf16[256,1024]{1,0:T(8,128)(2,1)}, u32[]{:S(2)}, u32[]{:S(2)}) collective-permute-start(bf16[256,1024]{1,0:T(8,128)(2,1)} %copy-done.39), channel_id=1, source_target_pairs={{0,1},{1,0},{2,3},{3,2},{4,5},{5,4},{6,7},{7,6},{8,9},{9,8},{10,11... | collective-permute-start | bytes 1572872 | tf_op jit(solution)/shard_map/ppermute | solution.py:913
  278.8 12.7 %collective-permute-start.50 = (bf16[256,1024]{1,0:T(8,128)(2,1)}, bf16[256,1024]{1,0:T(8,128)(2,1)}, u32[]{:S(2)}, u32[]{:S(2)}) collective-permute-start(bf16[256,1024]{1,0:T(8,128)(2,1)} %get-tuple-element.234), channel_id=1, source_target_pairs={{0,2},{1,3},{2,0},{3,1},{4,6},{5,7},{6,4},{7,5},{8,10},{9,11},{10,... | collective-permute-start | bytes 1572872 | tf_op jit(solution)/shard_map/ppermute | solution.py:913
  287.9 18.1 %collective-permute-start.56 = (bf16[24,128,128]{2,1,0:T(8,128)(2,1)}, bf16[24,128,128]{2,1,0:T(8,128)(2,1)S(1)}, u32[]{:S(2)}, u32[]{:S(2)}) collective-permute-start(bf16[24,128,128]{2,1,0:T(8,128)(2,1)} %get-tuple-element.242), channel_id=1, source_target_pairs={{0,8},{4,12},{8,16},{12,20},{16,24},{20,28},{24,0},{28,4},{1,9},{5... | collective-permute-start | bytes 2359304 | tf_op jit(solution)/shard_map/ppermute | solution.py:918
  (74 other events, 751.5 us)
